TPU v7x, 256 devices: a whole 4x4x8 slice. The times are simulated.
256 devices in a mesh: chan: 8 (over x, y_hi), tm: 32 (over z, y_lo, core).
Axes of the slice: x: 4, y: 4 (y_hi: 2, y_lo: 2; y = y_hi * 2 + y_lo), z: 8, core: 2. Of those that a mesh axis runs over, the one named last changes fastest.
Arguments:
- strain_rate: bfloat16 [4096, 131072], P('chan', 'tm'), may hold values from -1500 to 1500
- whiten_taps: bfloat16 [64], replicated, may hold values from -0.75 to 0.75
- source_channels: int32 [2, 4], replicated, may hold values from 0 to 4095
- window_offsets: int32 [16], replicated, may hold values from 0 to 511
Outputs:
- correlations: float32 [4096, 2, 4, 256], P(('chan', 'tm'))
All inputs are finite; a program needn't handle non-finite values.
Results may differ from a plain program's by a relative error of at most 0.0027.
Values may be sent and summed in bfloat16 or wider, within the bound.
No kernel may reach another device: no remote copies, remote signals or barrier semaphores. Data moves between devices by JAX's collectives and lax.ppermute only.
A program may use at most 256 MiB of HBM per device.

v0:
```python
import math

import jax
import jax.numpy as jnp
from jax import lax
from jax.sharding import PartitionSpec as P

TAPS = 64
MAXLAG = 128
NSRC = 2
SB = 4
WIN = 8192


epsilon = 1e-05


def shifted(shard, axis, by):
    devices = lax.axis_size(axis)
    pairs = [(i, i + by) for i in range(devices) if 0 <= i + by < devices]
    return lax.ppermute(shard, axis, pairs)


def padded_2(block, sides, width):
    for axis, dim in sides:
        count = lax.axis_size(axis)
        forward = [(i, i + 1) for i in range(count - 1)]
        backward = [(target, source) for source, target in forward]
        low = lax.ppermute(
            lax.slice_in_dim(block, block.shape[dim] - width, None, axis=dim), axis, forward
        )
        high = lax.ppermute(lax.slice_in_dim(block, 0, width, axis=dim), axis, backward)
        block = jnp.concatenate([low, block, high], axis=dim)
    return block


def lag_table(padded, span):
    lag_total = padded.shape[1] - span
    return jnp.stack([padded[:, lag : lag + span] for lag in range(lag_total)], axis=1)


def correlate(receivers, table):
    product = jnp.einsum("rt,mlt->rml", receivers, table, preferred_element_type=jnp.float32)
    return product.reshape(receivers.shape[0], table.shape[0] * table.shape[1])


def make_terms(whitened, table):
    return correlate(whitened, table)


def shards(strain_rate, whiten_taps, source_channels, window_offsets):
    channels, samples = strain_rate.shape
    time_tiles = lax.axis_size("tm")
    tile_index = lax.axis_index("tm")
    total_samples = samples * time_tiles
    out_rows = channels // time_tiles
    lag_count = 2 * MAXLAG
    last_cols = strain_rate[:, samples - TAPS :]
    earlier = shifted(last_cols, "tm", 1)
    extended = jnp.concatenate([earlier, strain_rate], axis=1)
    block_count = samples // 128
    previous = extended[:, :samples].reshape(channels, block_count, 128)[:, :, :TAPS]
    current = strain_rate.reshape(channels, block_count, 128)
    framed = jnp.concatenate([previous, current], axis=2)
    row_pos = jnp.arange(TAPS + 128, dtype=jnp.int32)[:, None]
    col_pos = jnp.arange(128, dtype=jnp.int32)[None, :]
    tap_index = TAPS + col_pos - row_pos
    tap_hit = tap_index[:, :, None] == jnp.arange(TAPS, dtype=jnp.int32)[None, None, :]
    fir_matrix = jnp.sum(
        jnp.where(tap_hit, whiten_taps.astype(jnp.float32)[None, None, :], 0.0), axis=2
    ).astype(jnp.bfloat16)
    filtered = jnp.einsum(
        "cbi,ij->cbj", framed, fir_matrix, preferred_element_type=jnp.float32
    ).reshape(channels, samples)
    energy = lax.psum(jnp.sum(filtered * filtered, axis=1), "tm")
    inverse_rms = lax.rsqrt(energy / total_samples + epsilon)
    global_time = tile_index * samples + jnp.arange(samples, dtype=jnp.int32)
    window_index = global_time // WIN
    window_hit = (
        window_index[:, None] == jnp.arange(window_offsets.shape[0], dtype=jnp.int32)[None, :]
    )
    first_kept = jnp.sum(jnp.where(window_hit, window_offsets[None, :], 0), axis=1)
    keep_mask = jnp.where(global_time % WIN >= first_kept, 1.0, 0.0).astype(jnp.float32)
    whitened = (filtered * inverse_rms[:, None] * keep_mask[None, :]).astype(jnp.bfloat16)
    group_index = lax.axis_index("chan")
    channel_ids = group_index * channels + jnp.arange(channels, dtype=jnp.int32)
    flat_sources = source_channels.reshape(-1)
    selector = (flat_sources[:, None] == channel_ids[None, :]).astype(jnp.bfloat16)
    local_picks = jnp.dot(selector, whitened, preferred_element_type=jnp.float32)
    source_traces = lax.psum(local_picks.astype(jnp.bfloat16), "chan")
    inverse_norm = 1.0 / math.sqrt(total_samples)
    padded = padded_2(source_traces, (("tm", 1),), MAXLAG)
    table = lag_table(padded, samples)
    stacked = lax.psum_scatter(make_terms(whitened, table), "tm", scatter_dimension=0, tiled=True)
    return (stacked * inverse_norm).reshape(out_rows, NSRC, SB, lag_count)


def solution(mesh):
    return jax.shard_map(
        shards,
        mesh=mesh,
        in_specs=(P("chan", "tm"), P(), P(), P()),
        out_specs=P(("chan", "tm"), None, None, None),
        check_vma=False,
    )
```

profile of v0, /device:TPU:8, one launch (start us, length us, event | category | flops | bytes accessed | tf_op | source)
XLA Modules:
  0.0 393.1 jit_solution(8371478265441944846)
XLA Ops:
  6.5 1.0 slice.1035
  7.5 1.9 collective-permute-start
  9.5 6.5 %copy.11 = bf16[512,4096]{0,1:T(8,128)(2,1)} copy(bf16[512,4096]{1,0:T(8,128)(2,1)} %param.4) | data formatting | bytes 8388608 | tf_op args[0]
  16.0 0.7 convert_element_type.18
  16.7 0.8 eq.49
  17.5 0.8 select_reduce_fusion.1
  18.3 2.1 select_reduce_fusion
  20.4 6.1 %pad_maximum_fusion = bf16[512,4096]{1,0:T(8,128)(2,1)} fusion(bf16[512,4096]{1,0:T(8,128)(2,1)} %param.4, bf16[512,64]{1,0:T(8,128)(2,1)S(1)} %collective-permute-done), kind=kLoop, calls=%fused_computation.12 | loop fusion | flops 8388608 | bytes 8454144 | tf_op jit(solution)/shard_map/concatenate | solution.py:60
  26.5 6.5 %copy.10 = bf16[512,4096]{0,1:T(8,128)(2,1)} copy(bf16[512,4096]{1,0:T(8,128)(2,1)} %pad_maximum_fusion) | data formatting | bytes 8388608 | tf_op jit(solution)/shard_map/slice | solution.py:62
  33.0 1.8 slice.1295
  34.8 7.2 %multiply_reduce_fusion = (f32[512]{0:T(512)S(1)}, f32[512,32,128]{0,2,1:T(8,128)}) fusion(bf16[192,128]{1,0:T(8,128)(2,1)S(1)} %select_reduce_fusion, bf16[512,32,128]{0,2,1:T(8,128)(2,1)} %bitcast.1046, bf16[512,32,64]{0,2,1:T(8,128)(2,1)S(1)} %slice.1295), kind=kOutput, calls=%fused_computation.4 | convolution fusion | flops 822083072 | bytes 14731264 | tf_op jit(solution)/shard_map/cbi,ij->cbj/dot_general | solution.py:72
  42.0 54.7 %psum.14 = f32[512]{0:T(512)S(1)} all-reduce(f32[512]{0:T(512)S(1)} %get-tuple-element.9), channel_id=1, replica_groups=mesh['chan'=8,'tm'=32] {'tm'}, use_global_device_ids=true, to_apply=%region_2.3 | all-reduce | flops 512 | bytes 4096 | tf_op jit(solution)/shard_map/psum | solution.py:75
  96.7 3.9 fusion.1
  100.7 1.8 convolution_convert_fusion
  102.6 92.3 %all-reduce.2.cloned.1.call-done = bf16[8,4096]{1,0:T(8,128)(2,1)} async-done(((bf16[8,4096]{1,0:T(8,128)(2,1)}), bf16[8,4096]{1,0:T(8,128)(2,1)}) %all-reduce.2.cloned.1.call-update) | async-done | bytes 65552 | tf_op jit(solution)/shard_map/psum | solution.py:90
  194.9 0.8 fusion.22
  195.6 1.9 collective-permute-start.1
  197.5 3.9 %multiply_convert_fusion = bf16[512,32,128]{0,2,1:T(8,128)(2,1)S(1)} fusion(f32[512,32,128]{0,2,1:T(8,128)} %get-tuple-element.10, f32[32,128]{1,0:T(8,128)S(1)} %fusion.16, f32[512]{0:T(512)S(1)} %add_rsqrt_fusion), kind=kLoop, calls=%fused_computation.3 | loop fusion | flops 6291456 | bytes 12601344 | tf_op jit(solution)/shard_map/convert_element_type | solution.py:84
  201.5 3.8 collective-permute-start.2
  205.3 0.8 constant_dynamic-update-slice_fusion.3
  206.3 0.1 constant_dynamic-update-slice_fusion.257
  206.5 0.1 constant_dynamic-update-slice_fusion.255
  206.6 0.1 constant_dynamic-update-slice_fusion.254
  206.8 0.1 constant_dynamic-update-slice_fusion.252
  207.0 0.1 constant_dynamic-update-slice_fusion.249
  207.3 0.1 constant_dynamic-update-slice_fusion.246
  207.5 0.1 constant_dynamic-update-slice_fusion.244
  207.6 0.1 constant_dynamic-update-slice_fusion.243
  207.8 0.1 constant_dynamic-update-slice_fusion.241
  208.0 0.1 constant_dynamic-update-slice_fusion.238
  208.2 0.1 constant_dynamic-update-slice_fusion.236
  208.3 0.1 constant_dynamic-update-slice_fusion.235
  208.5 0.1 constant_dynamic-update-slice_fusion.233
  208.8 0.1 constant_dynamic-update-slice_fusion.230
  209.0 0.1 constant_dynamic-update-slice_fusion.227
  209.2 0.1 constant_dynamic-update-slice_fusion.225
  209.3 0.1 constant_dynamic-update-slice_fusion.224
  209.5 0.1 constant_dynamic-update-slice_fusion.222
  209.8 0.1 constant_dynamic-update-slice_fusion.219
  209.9 0.1 constant_dynamic-update-slice_fusion.217
  210.0 0.1 constant_dynamic-update-slice_fusion.216
  210.2 0.1 constant_dynamic-update-slice_fusion.214
  210.5 0.1 constant_dynamic-update-slice_fusion.211
  229.4 21.6 %copy.12 = bf16[8,256,4096]{2,1,0:T(8,128)(2,1)} copy(bf16[8,256,4096]{2,0,1:T(8,128)(2,1)S(1)} %constant_dynamic-update-slice_fusion.4) | data formatting | bytes 33554432 | tf_op jit(solution)/shard_map/stack | solution.py:39
  251.0 14.0 %fusion.23 = f32[512,2048]{1,0:T(8,128)} fusion(bf16[512,4096]{0,1:T(8,128)(2,1)S(1)} %bitcast.1047, bf16[2048,4096]{1,0:T(8,128)(2,1)} %bitcast.1044), kind=kOutput, calls=%fused_computation.562 | convolution fusion | flops 8589934592 | bytes 25165824 | tf_op jit(solution)/shard_map/rt,mlt->rml/dot_general | solution.py:43
  265.1 119.5 %reduce-scatter.2.cloned.1.call-done = f32[16,2048]{1,0:T(8,128)} async-done(((f32[512,2048]{1,0:T(8,128)}), f32[16,2048]{1,0:T(8,128)}) %reduce-scatter.2.cloned.1.call-update) | async-done | bytes 131088 | tf_op jit(solution)/shard_map/reduce_scatter | solution.py:94
  384.6 0.9 broadcast_multiply_fusion
  385.5 0.7 reshape.100
  (251 shorter events, 20.0 us)
Async XLA Ops:
  6.5 188.3 %all-reduce.2.cloned.1.call-start = ((), (), s32[]{:S(2)}) async-start(), calls=%async_computation.1 | async-start | bytes 131072 | tf_op jit(solution)/shard_map/psum | solution.py:90
  7.5 12.9 %collective-permute-start = (bf16[512,64]{1,0:T(8,128)(2,1)S(1)}, bf16[512,64]{1,0:T(8,128)(2,1)S(1)}, u32[]{:S(2)}, u32[]{:S(2)}) collective-permute-start(bf16[512,64]{1,0:T(8,128)(2,1)S(1)} %slice.1035), channel_id=1, source_target_pairs={{0,1},{1,2},{2,3},{3,4},{4,5},{5,6},{6,7},{7,8},{8,9},{9,10},{10,1... | collective-permute-start | bytes 196616 | tf_op jit(solution)/shard_map/ppermute | solution.py:21
  102.5 282.1 %reduce-scatter.2.cloned.1.call-start = ((), (), s32[]{:S(2)}) async-start(), calls=%async_computation.2 | async-start | bytes 4325376 | tf_op jit(solution)/shard_map/reduce_scatter | solution.py:94
  194.9 22.9 %copy-start = (bf16[8,4096]{1,0:T(8,128)(2,1)S(1)}, bf16[8,4096]{1,0:T(8,128)(2,1)}, u32[]{:S(2)}) copy-start(bf16[8,4096]{1,0:T(8,128)(2,1)} %all-reduce.2.cloned.1.call-done) | copy-start | bytes 196612
  195.6 9.7 %collective-permute-start.1 = (bf16[8,128]{1,0:T(8,128)(2,1)S(1)}, bf16[8,128]{1,0:T(8,128)(2,1)S(1)}, u32[]{:S(2)}, u32[]{:S(2)}) collective-permute-start(bf16[8,128]{1,0:T(8,128)(2,1)S(1)} %get-tuple-element.6), channel_id=1, source_target_pairs={{0,1},{1,2},{2,3},{3,4},{4,5},{5,6},{6,7},{7,8},{8,9},{9,10},{10,1... | collective-permute-start | bytes 6152 | tf_op jit(solution)/shard_map/ppermute | solution.py:29
  201.5 16.3 %collective-permute-start.2 = (bf16[8,128]{1,0:T(8,128)(2,1)S(1)}, bf16[8,128]{1,0:T(8,128)(2,1)S(1)}, u32[]{:S(2)}, u32[]{:S(2)}) collective-permute-start(bf16[8,128]{1,0:T(8,128)(2,1)S(1)} %get-tuple-element.5), channel_id=1, source_target_pairs={{1,0},{2,1},{3,2},{4,3},{5,4},{6,5},{7,6},{8,7},{9,8},{10,9},{11,1... | collective-permute-start | bytes 6152 | tf_op jit(solution)/shard_map/ppermute | solution.py:32
Sparse Core Ops, SparseCore 0:
  102.6 92.1 all-reduce.1
  265.2 119.3 reduce-scatter.1
where the time goes:
time: 398 us; the launch traced here: 393 us
  waiting for transfers between devices  212 us (53%)
  local copies, waits for them, and re-layouts  62.5 us (16%)
  blocking collectives  54.7 us (14%)
  matrix products  23.1 us (6%)
  other arithmetic  18.5 us (5%)
  between operations  14.9 us (4%)
  starting transfers between devices  7.7 us (2%)
    reduce_scatter x1, waiting for transfers between devices, shards(): lax.psum_scatter(make_terms(whitened, table), 'tm', scatter_dimension=0,...  120 us
    psum x1, waiting for transfers between devices, shards(): source_traces = lax.psum(local_picks.astype(jnp.bfloat16), 'chan')  92.3 us
    psum x1, blocking collectives, shards(): energy = lax.psum(jnp.sum(filtered * filtered, axis=1), 'tm')  54.7 us
    unnamed x260, local copies, waits for them, and re-layouts  29.1 us
    another operation x2, local copies, waits for them, and re-layouts, lag_table(): jnp.stack([padded[:, lag:lag + span] for lag in range(lag_total)], axis=1)  21.7 us
    dot_general x1, matrix products, correlate(): jnp.einsum('rt,mlt->rml', receivers, table, preferred_element_type=jnp.fl...  14 us
    slice x2, local copies, waits for them, and re-layouts, shards(): extended[:, :samples].reshape(channels, block_count, 128)[:, :, :TAPS]  8.35 us
  transfers between devices with their start and end apart: 5, of which 2 were waited for; matrix products, arithmetic and copies ran while one was open for 7% of the time, Pallas kernels for 0%

commit v1 on v0

v1 whole, which is shorter than its diff:
```python
import math

import jax
import jax.numpy as jnp
from jax import lax
from jax.experimental import pallas as pl
from jax.experimental.pallas import tpu as pltpu
from jax.sharding import PartitionSpec as P

TAPS = 64
MAXLAG = 128
LAGS = 256
NSRC = 2
SB = 4
NS = NSRC * SB
WIN = 8192
LANE = 128
SHIFTS = 16
LEFT = 256
EPS = 1e-05
VMEM_LIMIT = 56 * 1024 * 1024


def params():
    return pltpu.CompilerParams(vmem_limit_bytes=VMEM_LIMIT)


def permute(block, axis, pairs):
    return lax.ppermute(block, axis, pairs)


def fir_tile(taps_ref):
    wide = jnp.broadcast_to(taps_ref[...], (2 * LANE, 2 * LANE))
    rolled = pltpu.roll(wide, LANE, 1, stride=1, stride_axis=0)
    return rolled[:, :LANE].astype(jnp.bfloat16)


def pick_kernel(row_ref, own_ref, x_ref, out_ref, buf, sems):
    copies = []
    for j in range(NS):
        first = pl.multiple_of((row_ref[j] // 16) * 16, 16)
        copy = pltpu.make_async_copy(x_ref.at[pl.ds(first, 16), :], buf.at[j], sems.at[j])
        copy.start()
        copies.append(copy)
    for j in range(NS):
        copies[j].wait()
        inside = jnp.where(own_ref[j] > 0, row_ref[j] % 16, -1)
        rows = lax.broadcasted_iota(jnp.int32, (16, 1), 0)
        picked = jnp.where(rows == inside, buf[j].astype(jnp.float32), 0.0)
        out_ref[pl.ds(j, 1), :] = jnp.sum(picked, axis=0, keepdims=True)


def pick_sources(x, rows, owned):
    samples = x.shape[1]
    return pl.pallas_call(
        pick_kernel,
        out_shape=jax.ShapeDtypeStruct((NS, samples), jnp.float32),
        in_specs=[
            pl.BlockSpec(memory_space=pltpu.SMEM),
            pl.BlockSpec(memory_space=pltpu.SMEM),
            pl.BlockSpec(memory_space=pl.ANY),
        ],
        out_specs=pl.BlockSpec(memory_space=pltpu.VMEM),
        scratch_shapes=[
            pltpu.VMEM((NS, 16, samples), jnp.bfloat16),
            pltpu.SemaphoreType.DMA((NS,)),
        ],
        compiler_params=params(),
        name="pick_sources",
    )(rows, owned, x)


def filter_kernel(core_ref, taps_ref, own_ref, other_ref, halo_ref, out_ref, power_ref, tile):
    @pl.when(pl.program_id(0) == 0)
    def _():
        tile[...] = fir_tile(taps_ref)

    groups, _, sub, half = own_ref.shape
    rows = groups * sub
    own = own_ref[...].reshape(rows, half)
    other = other_ref[...].reshape(rows, half)
    halo = halo_ref[...].reshape(rows, LANE)
    first = core_ref[0] == 0
    matrix = tile[...]

    def run(low, high):
        power = jnp.zeros((rows, LANE), jnp.float32)
        previous = halo
        for part, block in enumerate((low, high)):
            for j in range(half // LANE):
                current = block[:, j * LANE : (j + 1) * LANE]
                framed = jnp.concatenate([previous, current], axis=1)
                value = jnp.dot(framed, matrix, preferred_element_type=jnp.float32)
                start = part * half + j * LANE
                out_ref[:, start : start + LANE] = value
                power = power + value * value
                previous = current
        power_ref[...] = power

    @pl.when(first)
    def _():
        run(own, other)

    @pl.when(jnp.logical_not(first))
    def _():
        run(other, own)


def filter_rows(core, taps, x4, other, halo):
    groups, _, sub, half = x4.shape
    step = 4
    rows = step * sub
    return pl.pallas_call(
        filter_kernel,
        grid_spec=pltpu.PrefetchScalarGridSpec(
            num_scalar_prefetch=1,
            grid=(groups // step,),
            in_specs=[
                pl.BlockSpec((1, 2 * LANE), lambda i, core: (0, 0)),
                pl.BlockSpec((step, 1, sub, half), lambda i, core: (i, core[0], 0, 0)),
                pl.BlockSpec((step, sub, half), lambda i, core: (i, 0, 0)),
                pl.BlockSpec((step, sub, LANE), lambda i, core: (i, 0, 0)),
            ],
            out_specs=[
                pl.BlockSpec((rows, 2 * half), lambda i, core: (i, 0)),
                pl.BlockSpec((rows, LANE), lambda i, core: (i, 0)),
            ],
            scratch_shapes=[pltpu.VMEM((2 * LANE, LANE), jnp.bfloat16)],
        ),
        out_shape=[
            jax.ShapeDtypeStruct((groups * sub, 2 * half), jnp.float32),
            jax.ShapeDtypeStruct((groups * sub, LANE), jnp.float32),
        ],
        compiler_params=params(),
        cost_estimate=pl.CostEstimate(
            flops=2 * groups * sub * 2 * half * 512, bytes_accessed=12 << 20, transcendentals=0
        ),
        name="filter_rows",
    )(core, taps, x4, other, halo)


def source_kernel(core_ref, taps_ref, mine_ref, other_ref, power_ref, out_ref, energy_ref):
    first = core_ref[0] == 0
    mine = mine_ref[...].astype(jnp.float32)
    other = other_ref[...].astype(jnp.float32)
    low = jnp.where(first, mine, other)
    high = jnp.where(first, other, mine)
    count = out_ref.shape[1] // LANE
    width = low.shape[1]
    raw = jnp.concatenate([low, high[:, : (count + 1) * LANE - width]], axis=1)
    blocks = [raw[:, j * LANE : (j + 1) * LANE] for j in range(count + 1)]
    before = jnp.concatenate(blocks[:-1], axis=0)
    after = jnp.concatenate(blocks[1:], axis=0)
    framed = jnp.concatenate([before, after], axis=1).astype(jnp.bfloat16)
    value = jnp.dot(framed, fir_tile(taps_ref), preferred_element_type=jnp.float32)
    total = jnp.zeros((NS, LANE), jnp.float32)
    for j in range(count):
        piece = value[j * NS : (j + 1) * NS, :]
        out_ref[:, j * LANE : (j + 1) * LANE] = piece
        if 1 <= j < count - 1:
            total = total + piece * piece
    rows = power_ref.shape[0]
    lines = []
    for r in range(rows // LANE):
        turned = power_ref[r * LANE : (r + 1) * LANE, :].T
        lines.append(jnp.sum(turned, axis=0, keepdims=True))
    padded = jnp.concatenate([total, jnp.zeros((LANE - NS, LANE), jnp.float32)], axis=0)
    lines.append(jnp.sum(padded.T, axis=0, keepdims=True))
    lines.append(jnp.zeros((8 - len(lines), LANE), jnp.float32))
    energy_ref[...] = jnp.concatenate(lines, axis=0)


def filter_sources(core, taps, mine, other, power, length):
    vmem = pl.BlockSpec(memory_space=pltpu.VMEM)
    return pl.pallas_call(
        source_kernel,
        out_shape=[
            jax.ShapeDtypeStruct((NS, length), jnp.float32),
            jax.ShapeDtypeStruct((8, LANE), jnp.float32),
        ],
        in_specs=[pl.BlockSpec(memory_space=pltpu.SMEM), vmem, vmem, vmem, vmem],
        out_specs=[vmem, vmem],
        compiler_params=params(),
        name="filter_sources",
    )(core, taps, mine, other, power)


def make_correlate_kernel(loads, dots, total_samples, half_groups):
    def kernel(
        place_ref, energy_ref, traces_ref, rows_ref, keep_ref, send_ref, gain, white, table, shifted
    ):
        step = pl.program_id(0)
        chip, line = place_ref[0], place_ref[1]
        before, here, after = place_ref[2], place_ref[3], place_ref[4]
        rows, span = rows_ref.shape
        length = traces_ref.shape[1]

        @pl.when(step == 0)
        def _():
            energy = jnp.sum(energy_ref[...], axis=0)
            scale = lax.rsqrt(energy / total_samples + EPS)
            padded = jnp.concatenate([scale, jnp.zeros((LANE - 8, LANE), jnp.float32)], axis=0)
            turned = padded.T
            for r in range(rows // LANE):
                gain[r * LANE : (r + 1) * LANE, :] = jnp.broadcast_to(
                    turned[:, r : r + 1], (LANE, LANE)
                )
            count = rows // LANE
            source_gain = turned[:NS, count : count + 1]
            place = lax.broadcasted_iota(jnp.int32, (1, length), 1) - MAXLAG
            when = chip * WIN + place
            bound = jnp.where(
                place < 0, before - WIN, jnp.where(place < WIN, here, after + WIN)
            )
            keep = jnp.where(place >= bound, 1.0, 0.0)
            keep = keep * jnp.where(when >= 0, 1.0, 0.0)
            keep = keep * jnp.where(when < total_samples, 1.0, 0.0)
            trace = (traces_ref[...] * source_gain * keep).astype(jnp.bfloat16).astype(jnp.float32)
            for b in range(SHIFTS):
                moved = trace if b == 0 else pltpu.roll(trace, length - b, 1)
                shifted[b * NS : (b + 1) * NS, :] = moved
            for j in range(length // LANE):
                block = shifted[:, j * LANE : (j + 1) * LANE]
                table[j * LANE : (j + 1) * LANE, :] = block.T.astype(jnp.bfloat16)

        @pl.when(step < loads)
        def _():
            start = pl.multiple_of(step * span, span)
            place = lax.broadcasted_iota(jnp.int32, (1, span), 1) + step * span
            keep = jnp.where(place >= here, 1.0, 0.0).astype(jnp.float32)
            factor = gain[...]
            for j in range(span // LANE):
                cols = slice(j * LANE, (j + 1) * LANE)
                value = rows_ref[:, cols] * factor * keep[:, cols]
                white[:, pl.ds(start + j * LANE, LANE)] = value.astype(jnp.bfloat16)

        @pl.when(step >= loads)
        def _():
            pair = step - loads
            offset = pl.multiple_of(pair * (2 * SHIFTS), 2 * SHIFTS)
            depth = white.shape[1]
            left = table[pl.ds(offset, depth), :]
            right = table[pl.ds(offset + SHIFTS, depth), :]
            lags = jnp.concatenate([left, right], axis=1)
            value = jnp.dot(white[...], lags, preferred_element_type=jnp.float32)
            value = value.reshape(half_groups, 2, rows // half_groups // 2, 2 * LANE)
            low, high = value[:, 0], value[:, 1]
            is_low = line == 0
            keep_ref[...] = jnp.where(is_low, low, high)
            send_ref[...] = jnp.where(is_low, high, low).astype(jnp.bfloat16)

    return kernel


def correlate(place, energy, traces, rows, total_samples):
    channels, depth = rows.shape
    loads = 8
    span = depth // loads
    dots = LAGS // (2 * SHIFTS)
    length = traces.shape[1]
    half_groups = 8
    sub = channels // half_groups // 2
    cols = NS * LAGS
    return pl.pallas_call(
        make_correlate_kernel(loads, dots, total_samples, half_groups),
        grid_spec=pltpu.PrefetchScalarGridSpec(
            num_scalar_prefetch=1,
            grid=(loads + dots,),
            in_specs=[
                pl.BlockSpec(energy.shape, lambda i, p: (0, 0, 0)),
                pl.BlockSpec(traces.shape, lambda i, p: (0, 0)),
                pl.BlockSpec((channels, span), lambda i, p: (0, jnp.minimum(i, loads - 1))),
            ],
            out_specs=[
                pl.BlockSpec(
                    (half_groups, sub, 2 * LANE), lambda i, p: (0, 0, jnp.maximum(i - loads, 0))
                ),
                pl.BlockSpec(
                    (half_groups, sub, 2 * LANE), lambda i, p: (0, 0, jnp.maximum(i - loads, 0))
                ),
            ],
            scratch_shapes=[
                pltpu.VMEM((channels, LANE), jnp.float32),
                pltpu.VMEM((channels, depth), jnp.bfloat16),
                pltpu.VMEM((length, LANE), jnp.bfloat16),
                pltpu.VMEM((LANE, length), jnp.float32),
            ],
        ),
        out_shape=[
            jax.ShapeDtypeStruct((half_groups, sub, cols), jnp.float32),
            jax.ShapeDtypeStruct((half_groups, sub, cols), jnp.bfloat16),
        ],
        compiler_params=params(),
        cost_estimate=pl.CostEstimate(
            flops=2 * channels * depth * cols, bytes_accessed=16 << 20, transcendentals=0
        ),
        name="correlate",
    )(place, energy, traces, rows)


def shards(strain_rate, whiten_taps, source_channels, window_offsets):
    channels, samples = strain_rate.shape
    tiles = lax.axis_size("tm")
    groups_chan = lax.axis_size("chan")
    total_samples = samples * tiles
    tile = lax.axis_index("tm")
    core = tile % 2
    chip = tile // 2
    chips = tiles // 2
    line = chip % 2
    sub = channels // tiles

    taps = jnp.zeros((1, 2 * LANE), jnp.float32).at[0, :TAPS].set(whiten_taps.astype(jnp.float32))
    core_arr = core.astype(jnp.int32).reshape(1)

    group_index = lax.axis_index("chan")
    local = source_channels.reshape(-1) - group_index * channels
    owned = ((local >= 0) & (local < channels)).astype(jnp.int32)
    rows = jnp.clip(local, 0, channels - 1)
    picked = pick_sources(strain_rate, rows, owned).astype(jnp.bfloat16)

    x4 = strain_rate.reshape(chips, 2, sub, samples)
    away = lax.dynamic_index_in_dim(x4, 1 - core, axis=1, keepdims=False)
    swap = [(i, i ^ 1) for i in range(tiles)]
    other = permute(away, "tm", swap)
    tail = x4[:, :, :, samples - LANE :]
    to_low = [(2 * k - 1, 2 * k) for k in range(1, chips)]
    to_high = [(2 * k - 1, 2 * k + 1) for k in range(1, chips)]
    halo_low = permute(tail[:, 0], "tm", to_low)
    halo_high = permute(tail[:, 1], "tm", to_high)
    halo = jnp.where(core == 0, halo_low, halo_high)

    up = [(i, i + 1) for i in range(tiles - 1)]
    down = [(i + 1, i) for i in range(tiles - 1)]
    left = permute(picked[:, samples - LEFT :], "tm", up)
    right = permute(picked[:, :LANE], "tm", down)
    pad = jnp.zeros((NS, LEFT - LANE), jnp.bfloat16)
    piece = jnp.where(
        core == 0,
        jnp.concatenate([left, picked], axis=1),
        jnp.concatenate([picked, right, pad], axis=1),
    )
    parts = [
        permute(piece, "chan", [(i, (i + 2 * d) % groups_chan) for i in range(groups_chan)])
        for d in range(1, groups_chan // 2)
    ]
    piece = piece + sum(parts[1:], parts[0])
    piece = piece + permute(piece, "chan", [(i, i ^ 1) for i in range(groups_chan)])
    piece_other = permute(piece, "tm", swap)

    filtered, power = filter_rows(core_arr, taps, x4, other, halo)
    length = WIN + 2 * MAXLAG
    traces, energy = filter_sources(core_arr, taps, piece, piece_other, power, length)

    same = [[2 * k + c for k in range(chips)] for c in range(2)]
    spread = jnp.broadcast_to(energy[None], (chips,) + energy.shape)
    energies = lax.all_to_all(spread, "tm", 0, 0, tiled=True, axis_index_groups=same)

    padded_offsets = jnp.concatenate(
        [jnp.zeros((1,), jnp.int32), window_offsets, jnp.zeros((1,), jnp.int32)]
    )
    place = jnp.concatenate(
        [
            jnp.stack([chip, line]).astype(jnp.int32),
            lax.dynamic_slice_in_dim(padded_offsets, chip, 3),
        ]
    )
    keep, send = correlate(place, energies, traces, filtered, total_samples)

    across = permute(send, "tm", [(i, i ^ 2) for i in range(tiles)])
    summed = (keep + across.astype(jnp.float32)).astype(jnp.bfloat16)
    column = [[4 * z + r for z in range(tiles // 4)] for r in range(4)]
    gathered = lax.all_to_all(summed, "tm", 0, 0, tiled=True, axis_index_groups=column)
    total = jnp.sum(gathered.astype(jnp.float32), axis=0) * (1.0 / math.sqrt(total_samples))
    total = total.reshape(sub, LAGS, NS).transpose(0, 2, 1)
    return total.reshape(sub, NSRC, SB, LAGS)


def solution(mesh):
    return jax.shard_map(
        shards,
        mesh=mesh,
        in_specs=(P("chan", "tm"), P(), P(), P()),
        out_specs=P(("chan", "tm"), None, None, None),
        check_vma=False,
    )
```

time: 398 us -> 118 us (0.30)
  waiting for transfers between devices: 212 us -> 22.9 us
  local copies, waits for them, and re-layouts: 62.5 us -> 8.61 us
  blocking collectives: 54.7 us -> 18.1 us
  Pallas kernels: 0 us -> 32.2 us
  matrix products: 23.1 us -> 0 us
  starting transfers between devices: 7.7 us -> 28.9 us
  between operations: 14.9 us -> 0.21 us
  other arithmetic: 18.5 us -> 5.03 us
    reduce_scatter x1 -> x0, waiting for transfers between devices: 120 us -> none  [shards(): lax.psum_scatter(make_terms(whitened, table), 'tm', scatter_dimension=0,...]
    psum x1 -> x0, waiting for transfers between devices: 92.3 us -> none  [shards(): source_traces = lax.psum(local_picks.astype(jnp.bfloat16), 'chan')]
    psum x1 -> x0, blocking collectives: 54.7 us -> none  [shards(): energy = lax.psum(jnp.sum(filtered * filtered, axis=1), 'tm')]
    pallas_call x0 -> x4, Pallas kernels: none -> 32.2 us  [the longest x1 19.9 us: correlate(): pl.pallas_call(make_correlate_kernel(loads, dots, total_samples, half_gro...]
    unnamed x260 -> x12, local copies, waits for them, and re-layouts: 29.1 us -> 1.26 us
    dot_general x3 -> x0, matrix products: 23.1 us -> none  [the longest x1 14 us: correlate(): jnp.einsum('rt,mlt->rml', receivers, table, preferred_element_type=jnp.fl...]
    another operation x2 -> x0, local copies, waits for them, and re-layouts: 21.7 us -> none  [lag_table(): jnp.stack([padded[:, lag:lag + span] for lag in range(lag_total)], axis=1)]
    all_to_all x0 -> x1, blocking collectives: none -> 18.1 us  [shards(): lax.all_to_all(summed, 'tm', 0, 0, tiled=True, axis_index_groups=column)]
  transfers between devices with their start and end apart: 5 -> 12, of which waited for: 2 -> 4; matrix products, arithmetic and copies ran while one was open for 7% -> 6% of each run, Pallas kernels for 0% -> 9%
where the time goes in v1:
time: 118 us; the launch traced here: 116 us
  Pallas kernels  32.2 us (27%)
  starting transfers between devices  28.9 us (24%)
  waiting for transfers between devices  22.9 us (19%)
  blocking collectives  18.1 us (15%)
  local copies, waits for them, and re-layouts  8.61 us (7%)
  other arithmetic  5.03 us (4%)
    pallas_call x1, Pallas kernels, correlate(): pl.pallas_call(make_correlate_kernel(loads, dots, total_samples, half_gro...  19.9 us
    ppermute x11, starting transfers between devices, permute(): return lax.ppermute(block, axis, pairs)  18.7 us
    all_to_all x1, blocking collectives, shards(): lax.all_to_all(summed, 'tm', 0, 0, tiled=True, axis_index_groups=column)  18.1 us
    ppermute x11, waiting for transfers between devices, permute(): return lax.ppermute(block, axis, pairs)  15.9 us
    all_to_all x1, starting transfers between devices, shards(): lax.all_to_all(spread, 'tm', 0, 0, tiled=True, axis_index_groups=same)  10.2 us
    pallas_call x1, Pallas kernels, filter_rows(): pl.pallas_call(filter_kernel, grid_spec=pltpu.PrefetchScalarGridSpec(num_...  7.36 us
    all_to_all x1, waiting for transfers between devices, shards(): lax.all_to_all(spread, 'tm', 0, 0, tiled=True, axis_index_groups=same)  6.99 us
    pallas_call x1, Pallas kernels, pick_sources(): pl.pallas_call(pick_kernel, out_shape=jax.ShapeDtypeStruct((NS, samples),...  2.88 us
  transfers between devices with their start and end apart: 12, of which 4 were waited for; matrix products, arithmetic and copies ran while one was open for 6% of the time, Pallas kernels for 9%

profile of v1, /device:TPU:8, one launch (start us, length us, event | category | flops | bytes accessed | tf_op | source)
XLA Modules:
  0.0 115.9 jit_solution(10789584824928572972)
XLA Ops:
  0.0 1.8 %dynamic-slice_bitcast_fusion = bf16[16,16,4096]{2,1,0:T(8,128)(2,1)S(1)} fusion(bf16[16,2,16,4096]{3,2,1,0:T(8,128)(2,1)} %bitcast.21, s32[]{:T(128)S(6)} %select_n.44), kind=kLoop, calls=%fused_computation | loop fusion | bytes 4194308 | tf_op jit(solution)/shard_map/jit(dynamic_index_in_dim)/squeeze | solution.py:323
  1.8 0.1 collective-permute-start.7
  1.9 0.6 min.12.row_ref
  2.5 0.6 reshape.61.own_ref
  3.2 2.9 %pick_sources.1 = f32[8,4096]{1,0:T(8,128)} custom-call(s32[8]{0:T(128)} %min.12.row_ref, s32[8]{0:T(128)} %reshape.61.own_ref, bf16[512,4096]{1,0:T(8,128)(2,1)} %x_ref.1), custom_call_target="tpu_custom_call" | custom-call | tf_op jit(solution)/shard_map/pick_sources/pallas_call | solution.py:55
  6.1 0.9 convert_element_type.23
  7.0 2.4 %collective-permute-start = (bf16[8,256]{1,0:T(8,128)(2,1)S(1)}, bf16[8,256]{1,0:T(8,128)(2,1)S(1)}, u32[]{:S(2)}, u32[]{:S(2)}) collective-permute-start(bf16[8,256]{1,0:T(8,128)(2,1)S(1)} %slice.35), channel_id=1, source_target_pairs={{0,1},{1,2},{2,3},{3,4},{4,5},{5,6},{6,7},{7,8},{8,9},{9,10},{10,1... | collective-permute-start | bytes 12296 | tf_op jit(solution)/shard_map/ppermute | solution.py:29
  9.4 3.7 %collective-permute-start.1 = (bf16[8,128]{1,0:T(8,128)(2,1)S(1)}, bf16[8,128]{1,0:T(8,128)(2,1)S(1)}, u32[]{:S(2)}, u32[]{:S(2)}) collective-permute-start(bf16[8,128]{1,0:T(8,128)(2,1)S(1)} %slice.36), channel_id=1, source_target_pairs={{1,0},{2,1},{3,2},{4,3},{5,4},{6,5},{7,6},{8,7},{9,8},{10,9},{11,1... | collective-permute-start | bytes 6152 | tf_op jit(solution)/shard_map/ppermute | solution.py:29
  13.1 0.9 slice_bitcast_fusion
  14.0 1.3 %collective-permute-start.8 = (bf16[16,16,128]{2,1,0:T(8,128)(2,1)S(1)}, bf16[16,16,128]{2,1,0:T(8,128)(2,1)S(1)}, u32[]{:S(2)}, u32[]{:S(2)}) collective-permute-start(bf16[16,16,128]{2,1,0:T(8,128)(2,1)S(1)} %get-tuple-element.30), channel_id=1, source_target_pairs={{1,2},{3,4},{5,6},{7,8},{9,10},{11,12},{13,14},{15,16},{17,18},{19... | collective-permute-start | bytes 196616 | tf_op jit(solution)/shard_map/ppermute | solution.py:29
  15.3 0.6 compare_reduce_fusion
  16.0 0.0 collective-permute-done.1
  16.0 0.0 collective-permute-done
  16.0 1.0 collective-permute-start.2
  17.0 2.9 %collective-permute-start.3 = (bf16[8,4352]{1,0:T(8,128)(2,1)S(1)}, bf16[8,4352]{1,0:T(8,128)(2,1)S(1)}, u32[]{:S(2)}, u32[]{:S(2)}) collective-permute-start(bf16[8,4352]{1,0:T(8,128)(2,1)S(1)} %maximum_select_fusion), channel_id=1, source_target_pairs={{0,128},{32,160},{64,192},{96,224},{128,0},{160,32},{192,64},{224,... | collective-permute-start | bytes 208904 | tf_op jit(solution)/shard_map/ppermute | solution.py:29
  20.0 1.4 %collective-permute-start.4 = (bf16[8,4352]{1,0:T(8,128)(2,1)S(1)}, bf16[8,4352]{1,0:T(8,128)(2,1)S(1)}, u32[]{:S(2)}, u32[]{:S(2)}) collective-permute-start(bf16[8,4352]{1,0:T(8,128)(2,1)S(1)} %maximum_select_fusion), channel_id=1, source_target_pairs={{0,192},{32,224},{64,0},{96,32},{128,64},{160,96},{192,128},{224,1... | collective-permute-start | bytes 208904 | tf_op jit(solution)/shard_map/ppermute | solution.py:29
  21.3 0.6 fusion
  22.0 0.6 scatter.4.taps_ref
  22.6 0.0 collective-permute-done.2
  22.6 0.7 collective-permute-start.9
  23.2 0.0 collective-permute-done.3
  23.3 1.7 %collective-permute-done.4 = bf16[8,4352]{1,0:T(8,128)(2,1)S(1)} collective-permute-done((bf16[8,4352]{1,0:T(8,128)(2,1)S(1)}, bf16[8,4352]{1,0:T(8,128)(2,1)S(1)}, u32[]{:S(2)}, u32[]{:S(2)}) %collective-permute-start.4) | collective-permute-done | bytes 69664 | tf_op jit(solution)/shard_map/ppermute | solution.py:29
  25.0 2.4 %collective-permute-start.5 = (bf16[8,4352]{1,0:T(8,128)(2,1)S(1)}, bf16[8,4352]{1,0:T(8,128)(2,1)S(1)}, u32[]{:S(2)}, u32[]{:S(2)}) collective-permute-start(bf16[8,4352]{1,0:T(8,128)(2,1)S(1)} %add_add_fusion), channel_id=1, source_target_pairs={{0,32},{32,0},{64,96},{96,64},{128,160},{160,128},{192,224},{224,1... | collective-permute-start | bytes 208904 | tf_op jit(solution)/shard_map/ppermute | solution.py:29
  27.3 0.0 collective-permute-done.8
  27.3 0.0 collective-permute-done.9
  27.3 0.6 broadcast_select_fusion.halo_ref
  28.0 2.9 %collective-permute-done.5 = bf16[8,4352]{1,0:T(8,128)(2,1)S(1)} collective-permute-done((bf16[8,4352]{1,0:T(8,128)(2,1)S(1)}, bf16[8,4352]{1,0:T(8,128)(2,1)S(1)}, u32[]{:S(2)}, u32[]{:S(2)}) %collective-permute-start.5) | collective-permute-done | bytes 69664 | tf_op jit(solution)/shard_map/ppermute | solution.py:29
  30.9 1.5 %collective-permute-start.6 = (bf16[8,4352]{1,0:T(8,128)(2,1)S(1)}, bf16[8,4352]{1,0:T(8,128)(2,1)S(1)}, u32[]{:S(2)}, u32[]{:S(2)}) collective-permute-start(bf16[8,4352]{1,0:T(8,128)(2,1)S(1)} %add.41.mine_ref), channel_id=1, source_target_pairs={{0,1},{1,0},{2,3},{3,2},{4,5},{5,4},{6,7},{7,6},{8,9},{9,8},{10,11... | collective-permute-start | bytes 208904 | tf_op jit(solution)/shard_map/ppermute | solution.py:29
  32.4 0.0 collective-permute-done.7.other_ref
  32.4 7.4 %filter_rows.1 = (f32[256,8192]{1,0:T(8,128)}, f32[256,128]{1,0:T(8,128)}) custom-call(s32[1]{0:T(128)} %bitcast.2.core_ref, f32[1,256]{1,0:T(1,128)} %scatter.4.taps_ref, bf16[16,2,16,4096]{3,2,1,0:T(8,128)(2,1)} %bitcast.23, bf16[16,16,4096]{2,1,0:T(8,128)(2,1)} %collective-permute-done.7.other_ref, bf16[16,16,128]{2,1,0:T(8,128)(2,1)} %broadcast_select_fusion.halo_ref), custom_call_target="tpu_custom_call" | custom-call | flops 2147483648 | bytes 12582912 | tf_op jit(solution)/shard_map/filter_rows/pallas_call | solution.py:113
  39.8 0.0 collective-permute-done.6.other_ref
  39.8 0.6 copy-done.1
  40.4 2.0 %filter_sources.1 = (f32[8,8448]{1,0:T(8,128)}, f32[8,128]{1,0:T(8,128)}) custom-call(s32[1]{0:T(128)} %bitcast.2.core_ref, f32[1,256]{1,0:T(1,128)} %scatter.4.taps_ref, bf16[8,4352]{1,0:T(8,128)(2,1)} %copy-done, bf16[8,4352]{1,0:T(8,128)(2,1)} %copy-done.1, f32[256,128]{1,0:T(8,128)} %get-tuple-element.23.power_ref), custom_call_target="tpu_custom_call" | custom-call | tf_op jit(solution)/shard_map/filter_sources/pallas_call | solution.py:175
  42.4 1.3 %broadcast_in_dim.5 = f32[16,8,128]{2,1,0:T(8,128)} broadcast(f32[8,128]{1,0:T(8,128)} %get-tuple-element.24), dimensions={1,2} | broadcast | bytes 69632 | tf_op jit(solution)/shard_map/broadcast_in_dim | solution.py:356
  43.7 10.2 %all-to-all-start = ((f32[16,8,128]{2,1,0:T(8,128)}), f32[16,8,128]{2,1,0:T(8,128)S(1)}, u32[]{:S(2)}, u32[]{:S(2)}) async-start(f32[16,8,128]{2,1,0:T(8,128)} %broadcast_in_dim.5), calls=%async_computation | async-start | bytes 131072 | tf_op jit(solution)/shard_map/all_to_all | solution.py:357
  53.9 0.1 pad_add_fusion
  54.0 0.1 dynamic_slice.7
  54.1 0.6 pad_add_fusion.1.place_ref
  54.7 7.0 %all-to-all-done.energy_ref = f32[16,8,128]{2,1,0:T(8,128)S(1)} async-done(((f32[16,8,128]{2,1,0:T(8,128)}), f32[16,8,128]{2,1,0:T(8,128)S(1)}, u32[]{:S(2)}, u32[]{:S(2)}) %all-to-all-start) | async-done | bytes 65568 | tf_op jit(solution)/shard_map/all_to_all | solution.py:357
  61.7 0.6 copy-done.2
  62.3 19.9 %correlate.1 = (f32[8,16,2048]{2,1,0:T(8,128)}, bf16[8,16,2048]{2,1,0:T(8,128)(2,1)}) custom-call(s32[5]{0:T(128)} %pad_add_fusion.1.place_ref, f32[16,8,128]{2,1,0:T(8,128)} %copy-done.2, f32[8,8448]{1,0:T(8,128)} %get-tuple-element.25.traces_ref, f32[256,8192]{1,0:T(8,128)} %get-tuple-element.26.rows_ref), custom_call_target="tpu_custom_call" | custom-call | flops 8589934592 | bytes 16777216 | tf_op jit(solution)/shard_map/correlate/pallas_call | solution.py:264
  82.2 1.4 %collective-permute-start.10 = (bf16[8,16,2048]{2,1,0:T(8,128)(2,1)}, bf16[8,16,2048]{2,1,0:T(8,128)(2,1)S(1)}, u32[]{:S(2)}, u32[]{:S(2)}) collective-permute-start(bf16[8,16,2048]{2,1,0:T(8,128)(2,1)} %get-tuple-element.28), channel_id=1, source_target_pairs={{0,2},{1,3},{2,0},{3,1},{4,6},{5,7},{6,4},{7,5},{8,10},{9,11},{10,... | collective-permute-start | bytes 1572872 | tf_op jit(solution)/shard_map/ppermute | solution.py:29
  83.6 11.3 %collective-permute-done.10 = bf16[8,16,2048]{2,1,0:T(8,128)(2,1)S(1)} collective-permute-done((bf16[8,16,2048]{2,1,0:T(8,128)(2,1)}, bf16[8,16,2048]{2,1,0:T(8,128)(2,1)S(1)}, u32[]{:S(2)}, u32[]{:S(2)}) %collective-permute-start.10) | collective-permute-done | bytes 524320 | tf_op jit(solution)/shard_map/ppermute | solution.py:29
  94.9 1.3 %add_convert_fusion = bf16[8,16,2048]{2,1,0:T(8,128)(2,1)S(1)} fusion(f32[8,16,2048]{2,1,0:T(8,128)} %get-tuple-element.27, bf16[8,16,2048]{2,1,0:T(8,128)(2,1)S(1)} %collective-permute-done.10), kind=kLoop, calls=%fused_computation.2 | loop fusion | flops 786432 | bytes 2097152 | tf_op jit(solution)/shard_map/convert_element_type | solution.py:371
  96.3 18.1 %all_to_all.10 = bf16[8,16,2048]{2,1,0:T(8,128)(2,1)S(1)} all-to-all(bf16[8,16,2048]{2,1,0:T(8,128)(2,1)S(1)} %add_convert_fusion), channel_id=1, replica_groups={{0,4,8,12,16,20,24,28},{1,5,9,13,17,21,25,29},{2,6,10,14,18,22,26,30},{..., dimensions={0} | all-to-all | bytes 1048576 | tf_op jit(solution)/shard_map/all_to_all | solution.py:373
  114.3 0.1 convert_reduce_fusion
  114.4 0.3 copy.11
  114.7 1.1 copy.12
  (20 shorter events, 0.1 us)
Async XLA Ops:
  0.0 1.9 %copy-start.3 = (s32[2,4]{1,0:T(2,128)S(1)}, s32[2,4]{1,0:T(2,128)}, u32[]{:S(2)}) copy-start(s32[2,4]{1,0:T(2,128)} %param.8) | copy-start | bytes 100
  0.0 21.3 %copy-start.4 = (bf16[64]{0:T(256)(128)(2,1)S(1)}, bf16[64]{0:T(256)(128)(2,1)}, u32[]{:S(2)}) copy-start(bf16[64]{0:T(256)(128)(2,1)} %param.7) | copy-start | bytes 388
  1.8 30.6 %collective-permute-start.7 = (bf16[16,16,4096]{2,1,0:T(8,128)(2,1)S(1)}, bf16[16,16,4096]{2,1,0:T(8,128)(2,1)}, u32[]{:S(2)}, u32[]{:S(2)}) collective-permute-start(bf16[16,16,4096]{2,1,0:T(8,128)(2,1)S(1)} %dynamic-slice_bitcast_fusion), channel_id=1, source_target_pairs={{0,1},{1,0},{2,3},{3,2},{4,5},{5,4},{6,7},{7,6},{8,9},{9,8},{10,11... | collective-permute-start | bytes 6291464 | tf_op jit(solution)/shard_map/ppermute | solution.py:29
  7.0 9.0 %collective-permute-start = (bf16[8,256]{1,0:T(8,128)(2,1)S(1)}, bf16[8,256]{1,0:T(8,128)(2,1)S(1)}, u32[]{:S(2)}, u32[]{:S(2)}) collective-permute-start(bf16[8,256]{1,0:T(8,128)(2,1)S(1)} %slice.35), channel_id=1, source_target_pairs={{0,1},{1,2},{2,3},{3,4},{4,5},{5,6},{6,7},{7,8},{8,9},{9,10},{10,1... | collective-permute-start | bytes 12296 | tf_op jit(solution)/shard_map/ppermute | solution.py:29
  9.4 6.6 %collective-permute-start.1 = (bf16[8,128]{1,0:T(8,128)(2,1)S(1)}, bf16[8,128]{1,0:T(8,128)(2,1)S(1)}, u32[]{:S(2)}, u32[]{:S(2)}) collective-permute-start(bf16[8,128]{1,0:T(8,128)(2,1)S(1)} %slice.36), channel_id=1, source_target_pairs={{1,0},{2,1},{3,2},{4,3},{5,4},{6,5},{7,6},{8,7},{9,8},{10,9},{11,1... | collective-permute-start | bytes 6152 | tf_op jit(solution)/shard_map/ppermute | solution.py:29
  14.0 13.3 %collective-permute-start.8 = (bf16[16,16,128]{2,1,0:T(8,128)(2,1)S(1)}, bf16[16,16,128]{2,1,0:T(8,128)(2,1)S(1)}, u32[]{:S(2)}, u32[]{:S(2)}) collective-permute-start(bf16[16,16,128]{2,1,0:T(8,128)(2,1)S(1)} %get-tuple-element.30), channel_id=1, source_target_pairs={{1,2},{3,4},{5,6},{7,8},{9,10},{11,12},{13,14},{15,16},{17,18},{19... | collective-permute-start | bytes 196616 | tf_op jit(solution)/shard_map/ppermute | solution.py:29
  16.0 6.6 %collective-permute-start.2 = (bf16[8,4352]{1,0:T(8,128)(2,1)S(1)}, bf16[8,4352]{1,0:T(8,128)(2,1)S(1)}, u32[]{:S(2)}, u32[]{:S(2)}) collective-permute-start(bf16[8,4352]{1,0:T(8,128)(2,1)S(1)} %maximum_select_fusion), channel_id=1, source_target_pairs={{0,64},{32,96},{64,128},{96,160},{128,192},{160,224},{192,0},{224,... | collective-permute-start | bytes 208904 | tf_op jit(solution)/shard_map/ppermute | solution.py:29
  17.0 6.2 %collective-permute-start.3 = (bf16[8,4352]{1,0:T(8,128)(2,1)S(1)}, bf16[8,4352]{1,0:T(8,128)(2,1)S(1)}, u32[]{:S(2)}, u32[]{:S(2)}) collective-permute-start(bf16[8,4352]{1,0:T(8,128)(2,1)S(1)} %maximum_select_fusion), channel_id=1, source_target_pairs={{0,128},{32,160},{64,192},{96,224},{128,0},{160,32},{192,64},{224,... | collective-permute-start | bytes 208904 | tf_op jit(solution)/shard_map/ppermute | solution.py:29
  20.0 5.0 %collective-permute-start.4 = (bf16[8,4352]{1,0:T(8,128)(2,1)S(1)}, bf16[8,4352]{1,0:T(8,128)(2,1)S(1)}, u32[]{:S(2)}, u32[]{:S(2)}) collective-permute-start(bf16[8,4352]{1,0:T(8,128)(2,1)S(1)} %maximum_select_fusion), channel_id=1, source_target_pairs={{0,192},{32,224},{64,0},{96,32},{128,64},{160,96},{192,128},{224,1... | collective-permute-start | bytes 208904 | tf_op jit(solution)/shard_map/ppermute | solution.py:29
  22.6 4.8 %collective-permute-start.9 = (bf16[16,16,128]{2,1,0:T(8,128)(2,1)S(1)}, bf16[16,16,128]{2,1,0:T(8,128)(2,1)S(1)}, u32[]{:S(2)}, u32[]{:S(2)}) collective-permute-start(bf16[16,16,128]{2,1,0:T(8,128)(2,1)S(1)} %get-tuple-element.29), channel_id=1, source_target_pairs={{1,3},{3,5},{5,7},{7,9},{9,11},{11,13},{13,15},{15,17},{17,19},{19... | collective-permute-start | bytes 196616 | tf_op jit(solution)/shard_map/ppermute | solution.py:29
  25.0 5.9 %collective-permute-start.5 = (bf16[8,4352]{1,0:T(8,128)(2,1)S(1)}, bf16[8,4352]{1,0:T(8,128)(2,1)S(1)}, u32[]{:S(2)}, u32[]{:S(2)}) collective-permute-start(bf16[8,4352]{1,0:T(8,128)(2,1)S(1)} %add_add_fusion), channel_id=1, source_target_pairs={{0,32},{32,0},{64,96},{96,64},{128,160},{160,128},{192,224},{224,1... | collective-permute-start | bytes 208904 | tf_op jit(solution)/shard_map/ppermute | solution.py:29
  30.9 8.9 %copy-start = (bf16[8,4352]{1,0:T(8,128)(2,1)}, bf16[8,4352]{1,0:T(8,128)(2,1)S(1)}, u32[]{:S(2)}) copy-start(bf16[8,4352]{1,0:T(8,128)(2,1)S(1)} %add.41.mine_ref) | copy-start | bytes 208900
  30.9 8.9 %collective-permute-start.6 = (bf16[8,4352]{1,0:T(8,128)(2,1)S(1)}, bf16[8,4352]{1,0:T(8,128)(2,1)S(1)}, u32[]{:S(2)}, u32[]{:S(2)}) collective-permute-start(bf16[8,4352]{1,0:T(8,128)(2,1)S(1)} %add.41.mine_ref), channel_id=1, source_target_pairs={{0,1},{1,0},{2,3},{3,2},{4,5},{5,4},{6,7},{7,6},{8,9},{9,8},{10,11... | collective-permute-start | bytes 208904 | tf_op jit(solution)/shard_map/ppermute | solution.py:29
  32.4 21.5 %copy-start.5 = (s32[16]{0:T(128)S(1)}, s32[16]{0:T(128)}, u32[]{:S(2)}) copy-start(s32[16]{0:T(128)} %param.9) | copy-start | bytes 196
  39.8 0.6 copy-start.1
  43.7 17.9 %all-to-all-start = ((f32[16,8,128]{2,1,0:T(8,128)}), f32[16,8,128]{2,1,0:T(8,128)S(1)}, u32[]{:S(2)}, u32[]{:S(2)}) async-start(f32[16,8,128]{2,1,0:T(8,128)} %broadcast_in_dim.5), calls=%async_computation | async-start | bytes 131072 | tf_op jit(solution)/shard_map/all_to_all | solution.py:357
  61.7 0.6 copy-start.2
  82.2 12.7 %collective-permute-start.10 = (bf16[8,16,2048]{2,1,0:T(8,128)(2,1)}, bf16[8,16,2048]{2,1,0:T(8,128)(2,1)S(1)}, u32[]{:S(2)}, u32[]{:S(2)}) collective-permute-start(bf16[8,16,2048]{2,1,0:T(8,128)(2,1)} %get-tuple-element.28), channel_id=1, source_target_pairs={{0,2},{1,3},{2,0},{3,1},{4,6},{5,7},{6,4},{7,5},{8,10},{9,11},{10,... | collective-permute-start | bytes 1572872 | tf_op jit(solution)/shard_map/ppermute | solution.py:29

commit v2 on v0

v2 whole, which is shorter than its diff:
```python
import math

import jax
import jax.numpy as jnp
from jax import lax
from jax.experimental import pallas as pl
from jax.experimental.pallas import tpu as pltpu
from jax.sharding import PartitionSpec as P

TAPS = 64
MAXLAG = 128
LAGS = 256
NSRC = 2
SB = 4
NS = NSRC * SB
WIN = 8192
LANE = 128
SHIFTS = 16
LEFT = 256
EPS = 1e-05
MIB = 1024 * 1024

VMEM = pl.BlockSpec(memory_space=pltpu.VMEM)
SMEM = pl.BlockSpec(memory_space=pltpu.SMEM)
ANY = pl.BlockSpec(memory_space=pl.ANY)


def call(kernel, name, out, in_specs, scratch=(), limit=16, flops=0, moved=0):
    return pl.pallas_call(
        kernel,
        out_shape=out,
        in_specs=in_specs,
        out_specs=[VMEM] * len(out),
        scratch_shapes=list(scratch),
        compiler_params=pltpu.CompilerParams(vmem_limit_bytes=limit * MIB),
        cost_estimate=pl.CostEstimate(flops=flops, bytes_accessed=moved, transcendentals=0),
        name=name,
    )


def shape(dims, dtype):
    return jax.ShapeDtypeStruct(dims, dtype)


def fir_tile(taps):
    wide = jnp.broadcast_to(taps.astype(jnp.float32), (2 * LANE, 2 * LANE))
    rolled = pltpu.roll(wide, LANE, 1, stride=1, stride_axis=0)
    return rolled[:, :LANE].astype(jnp.bfloat16)


def wide_taps(taps):
    return jnp.pad(taps, (0, 2 * LANE - TAPS)).reshape(1, 2 * LANE)


def pick_sources(source_channels, x4):
    groups, _, sub, samples = x4.shape
    channels = groups * 2 * sub

    def kernel(ids_ref, x_ref, own_ref, edge_ref, high_ref, buf, sems):
        base = lax.axis_index("chan") * channels
        core = lax.axis_index("tm") % 2
        copies = []
        inner = []
        for j in range(NS):
            local = ids_ref[j // SB, j % SB] - base
            owned = (local >= 0) & (local < channels)
            row = jnp.clip(local, 0, channels - 1)
            group, half = row // (2 * sub), (row // sub) % 2
            inner.append(jnp.where(owned, row % sub, -1))
            copies.append(pltpu.make_async_copy(x_ref.at[group, half], buf.at[j], sems.at[j]))
        for copy in copies:
            copy.start()
        last = pl.ds(samples - LANE, LANE)
        low = pltpu.make_async_copy(
            x_ref.at[:, 0, :, last], edge_ref.at[pl.ds(0, groups)], sems.at[NS]
        )
        high = pltpu.make_async_copy(x_ref.at[:, 1, :, last], high_ref, sems.at[NS + 1])
        low.start()
        high.start()
        rows = lax.broadcasted_iota(jnp.int32, (sub, 1), 0)
        lines = []
        for j in range(NS):
            copies[j].wait()
            hit = jnp.where(rows == inner[j], 1.0, 0.0)
            lines.append(jnp.sum(buf[j].astype(jnp.float32) * hit, axis=0, keepdims=True))
        own = jnp.concatenate(lines, axis=0)
        own_ref[...] = own.astype(jnp.bfloat16)
        tail = jnp.concatenate(
            [own[:, samples - LEFT : samples - LANE], own[:, samples - LANE :]], axis=0
        )
        head = jnp.concatenate([own[:, :LANE], own[:, LANE : 2 * LANE]], axis=0)
        low.wait()
        high.wait()
        edge_ref[groups] = jnp.where(core == 1, tail, head).astype(jnp.bfloat16)

    return call(
        kernel,
        "pick_sources",
        [
            shape((NS, samples), jnp.bfloat16),
            shape((groups + 1, sub, LANE), jnp.bfloat16),
            shape((groups, sub, LANE), jnp.bfloat16),
        ],
        [SMEM, ANY],
        [pltpu.VMEM((NS, sub, samples), jnp.bfloat16), pltpu.SemaphoreType.DMA((NS + 2,))],
        limit=61,
        moved=2 * MIB,
    )(source_channels, x4)


def filter_rows(offsets, taps, x4, other, edge, high):
    groups, _, sub, half = x4.shape
    rows = groups * sub

    def kernel(off_ref, taps_ref, x_ref, other_ref, edge_ref, high_ref, out_ref, power_ref, own, sem):
        tile = lax.axis_index("tm")
        core = tile % 2
        copy = pltpu.make_async_copy(x_ref.at[:, core], own, sem)
        copy.start()
        matrix = fir_tile(taps_ref[...])
        first_kept = off_ref[tile // 2]
        copy.wait()

        def run(low, high_half, halo):
            power = jnp.zeros((rows, LANE), jnp.float32)
            previous = halo
            for part, block in enumerate((low, high_half)):
                for j in range(half // LANE):
                    current = block[:, :, j * LANE : (j + 1) * LANE].reshape(rows, LANE)
                    framed = jnp.concatenate([previous, current], axis=1)
                    value = jnp.dot(framed, matrix, preferred_element_type=jnp.float32)
                    start = part * half + j * LANE
                    power = power + value * value
                    place = lax.broadcasted_iota(jnp.int32, (1, LANE), 1) + start
                    value = value * jnp.where(place >= first_kept, 1.0, 0.0)
                    out_ref[:, start : start + LANE] = value
                    previous = current
            power_ref[...] = power

        @pl.when(core == 0)
        def _():
            run(own, other_ref, edge_ref[:groups].reshape(rows, LANE))

        @pl.when(core == 1)
        def _():
            run(other_ref, own, high_ref[...].reshape(rows, LANE))

    return call(
        kernel,
        "filter_rows",
        [shape((rows, 2 * half), jnp.float32), shape((rows, LANE), jnp.float32)],
        [SMEM, VMEM, ANY, VMEM, VMEM, VMEM],
        [pltpu.VMEM((groups, sub, half), jnp.bfloat16), pltpu.SemaphoreType.DMA],
        flops=2 * rows * 2 * half * 512,
        moved=12 * MIB,
    )(offsets, taps, x4, other, edge, high)


def filter_sources(offsets, taps, mine, other, power, chips, total_samples):
    length = WIN + 2 * MAXLAG
    count = length // LANE
    half = mine.shape[1] - LEFT

    def kernel(off_ref, taps_ref, mine_ref, other_ref, power_ref, out_ref, energy_ref):
        tile = lax.axis_index("tm")
        core, chip = tile % 2, tile // 2
        mine_rows = mine_ref[...].astype(jnp.float32)
        other_rows = other_ref[...].astype(jnp.float32)
        low = jnp.where(core == 0, mine_rows, other_rows)
        high = jnp.where(core == 0, other_rows, mine_rows)
        raw = [low[:, half:], low[:, :half], high[:, :half], high[:, half : half + LANE]]
        raw = jnp.concatenate(raw, axis=1)
        blocks = [raw[:, j * LANE : (j + 1) * LANE] for j in range(count + 1)]
        before = jnp.concatenate(blocks[:-1], axis=0)
        after = jnp.concatenate(blocks[1:], axis=0)
        framed = jnp.concatenate([before, after], axis=1).astype(jnp.bfloat16)
        value = jnp.dot(framed, fir_tile(taps_ref[...]), preferred_element_type=jnp.float32)
        total = jnp.zeros((NS, LANE), jnp.float32)
        first_kept = [
            off_ref[jnp.maximum(chip - 1, 0)],
            off_ref[chip],
            off_ref[jnp.minimum(chip + 1, chips - 1)],
        ]
        for j in range(count):
            piece = value[j * NS : (j + 1) * NS, :]
            start = j * LANE - MAXLAG
            window = start // WIN
            if window == 0:
                total = total + piece * piece
            place = lax.broadcasted_iota(jnp.int32, (1, LANE), 1) + (start - window * WIN)
            keep = jnp.where(place >= first_kept[window + 1], 1.0, 0.0)
            if window < 0:
                keep = keep * jnp.where(chip > 0, 1.0, 0.0)
            if window > 0:
                keep = keep * jnp.where(chip < chips - 1, 1.0, 0.0)
            out_ref[:, j * LANE : (j + 1) * LANE] = piece * keep
        lines = []
        for r in range(power_ref.shape[0] // LANE):
            turned = power_ref[r * LANE : (r + 1) * LANE, :].T
            lines.append(jnp.sum(turned, axis=0, keepdims=True))
        repeated = jnp.concatenate([total] * SHIFTS, axis=0)
        lines.append(jnp.sum(repeated.T, axis=0, keepdims=True))
        lines.append(jnp.zeros((8 - len(lines), LANE), jnp.float32))
        energy = jnp.concatenate(lines, axis=0)
        energy_ref[...] = jnp.broadcast_to(energy[None], energy_ref.shape)

    return call(
        kernel,
        "filter_sources",
        [shape((NS, length), jnp.float32), shape((chips, 8, LANE), jnp.float32)],
        [SMEM, VMEM, VMEM, VMEM, VMEM],
        moved=MIB,
    )(offsets, taps, mine, other, power)


def shift_sources(traces):
    length = traces.shape[1]

    def kernel(traces_ref, table_ref, shifted):
        trace = traces_ref[...]
        for b in range(SHIFTS):
            moved = trace if b == 0 else pltpu.roll(trace, length - b, 1)
            shifted[b * NS : (b + 1) * NS, :] = moved
        for j in range(length // LANE):
            cols = slice(j * LANE, (j + 1) * LANE)
            table_ref[cols, :] = shifted[:, cols].T

    return call(
        kernel,
        "shift_sources",
        [shape((length, LANE), jnp.float32)],
        [VMEM],
        [pltpu.VMEM((LANE, length), jnp.float32)],
        moved=8 * MIB,
    )(traces)[0]


def lag_products(white, table_ref, pairs, keep_ref, send_ref, half_groups):
    rows, depth = white.shape
    sub = rows // half_groups // 2
    own_low = (lax.axis_index("tm") // 2) % 2 == 0
    for place, pair in enumerate(pairs):
        offset = pair * 2 * SHIFTS
        left = table_ref[offset : offset + depth, :]
        right = table_ref[offset + SHIFTS : offset + SHIFTS + depth, :]
        lags = jnp.concatenate([left, right], axis=1)
        value = jnp.dot(white[...], lags, preferred_element_type=jnp.float32)
        value = value.reshape(half_groups, 2, sub, 2 * LANE)
        low, high = value[:, 0], value[:, 1]
        cols = slice(place * 2 * LANE, (place + 1) * 2 * LANE)
        keep_ref[:, :, cols] = jnp.where(own_low, low, high)
        send_ref[:, :, cols] = jnp.where(own_low, high, low).astype(jnp.bfloat16)


def correlate_first(energies, traces, rows, pairs, half_groups, total_samples):
    channels, depth = rows.shape
    length = traces.shape[0]

    def kernel(energy_ref, traces_ref, rows_ref, keep_ref, send_ref, white, table):
        energy = jnp.sum(energy_ref[...], axis=0)
        scale = lax.rsqrt(energy / total_samples + EPS)
        padded = jnp.concatenate([scale, jnp.zeros((LANE - 8, LANE), jnp.float32)], axis=0)
        turned = padded.T
        parts = channels // LANE
        columns = [turned[:, r : r + 1] for r in range(parts)]
        gain = jnp.concatenate(columns, axis=0)
        table[...] = (traces_ref[...] * scale[parts : parts + 1, :]).astype(jnp.bfloat16)
        white[...] = (rows_ref[...] * gain).astype(jnp.bfloat16)
        lag_products(white, table, pairs, keep_ref, send_ref, half_groups)

    sub = channels // half_groups // 2
    cols = len(pairs) * 2 * LANE
    return call(
        kernel,
        "correlate_first",
        [
            shape((half_groups, sub, cols), jnp.float32),
            shape((half_groups, sub, cols), jnp.bfloat16),
            shape((channels, depth), jnp.bfloat16),
            shape((length, LANE), jnp.bfloat16),
        ],
        [VMEM, VMEM, VMEM],
        flops=2 * channels * depth * cols,
        moved=16 * MIB,
    )(energies, traces, rows)


def correlate_next(white, table, pairs, half_groups):
    channels, depth = white.shape

    def kernel(white_ref, table_ref, keep_ref, send_ref):
        lag_products(white_ref, table_ref, pairs, keep_ref, send_ref, half_groups)

    sub = channels // half_groups // 2
    cols = len(pairs) * 2 * LANE
    return call(
        kernel,
        "correlate_next",
        [
            shape((half_groups, sub, cols), jnp.float32),
            shape((half_groups, sub, cols), jnp.bfloat16),
        ],
        [VMEM, VMEM],
        flops=2 * channels * depth * cols,
        moved=8 * MIB,
    )(white, table)


def shards(strain_rate, whiten_taps, source_channels, window_offsets):
    channels, samples = strain_rate.shape
    tiles = lax.axis_size("tm")
    groups_chan = lax.axis_size("chan")
    total_samples = samples * tiles
    chips = tiles // 2
    sub = channels // tiles
    core = lax.axis_index("tm") % 2
    taps = wide_taps(whiten_taps)

    x4 = strain_rate.reshape(chips, 2, sub, samples)
    own, edge, high = pick_sources(source_channels, x4)
    core, own = lax.optimization_barrier((core, own))

    swap = [(i, i ^ 1) for i in range(tiles)]
    across_edge = [(2 * k - 1, 2 * k) for k in range(1, chips)]
    across_edge = across_edge + [(b, a) for a, b in across_edge]
    edge = lax.ppermute(edge, "tm", across_edge)
    away = lax.dynamic_index_in_dim(x4, 1 - core, axis=1, keepdims=False)
    other = lax.ppermute(away, "tm", swap)
    high = lax.ppermute(high, "tm", [(2 * k - 1, 2 * k + 1) for k in range(1, chips)])

    piece = jnp.concatenate([own, edge[chips, :NS], edge[chips, NS:]], axis=1)
    parts = [
        lax.ppermute(piece, "chan", [(i, (i + 2 * d) % groups_chan) for i in range(groups_chan)])
        for d in range(1, groups_chan // 2)
    ]
    filtered, power = filter_rows(window_offsets, taps, x4, other, edge, high)
    *parts, power = lax.optimization_barrier((*parts, power))
    piece = piece + sum(parts[1:], parts[0])
    piece = piece + lax.ppermute(piece, "chan", [(i, i ^ 1) for i in range(groups_chan)])
    piece_other = lax.ppermute(piece, "tm", swap)

    traces, energy = filter_sources(
        window_offsets, taps, piece, piece_other, power, chips, total_samples
    )
    same = [[2 * k + c for k in range(chips)] for c in range(2)]
    energies = lax.all_to_all(energy, "tm", 0, 0, tiled=True, axis_index_groups=same)
    shifted = shift_sources(traces)

    column_size = tiles // 4
    column = [[4 * z + r for z in range(column_size)] for r in range(4)]
    dots = LAGS // (2 * SHIFTS)
    first, second = range(dots // 2), range(dots // 2, dots)
    keep_a, send_a, white, table = correlate_first(
        energies, shifted, filtered, first, column_size, total_samples
    )
    line = [(i, i ^ 2) for i in range(tiles)]

    def over_column(keep, across):
        summed = (keep + across.astype(jnp.float32)).astype(jnp.bfloat16)
        return lax.all_to_all(summed, "tm", 0, 0, tiled=True, axis_index_groups=column)

    across_a = lax.ppermute(send_a, "tm", line)
    keep_b, send_b = correlate_next(white, table, second, column_size)
    across_b = lax.ppermute(send_b, "tm", line)
    parts_a = over_column(keep_a, across_a)
    parts_b = over_column(keep_b, across_b)
    total = jnp.concatenate(
        [jnp.sum(p.astype(jnp.float32), axis=0) for p in (parts_a, parts_b)], axis=1
    )
    total = total * (1.0 / math.sqrt(total_samples))
    total = total.reshape(sub, LAGS, NS).transpose(0, 2, 1)
    return total.reshape(sub, NSRC, SB, LAGS)


def solution(mesh):
    return jax.shard_map(
        shards,
        mesh=mesh,
        in_specs=(P("chan", "tm"), P(), P(), P()),
        out_specs=P(("chan", "tm"), None, None, None),
        check_vma=False,
    )
```

time: 398 us -> 99.1 us (0.25)
  waiting for transfers between devices: 212 us -> 29.9 us
  blocking collectives: 54.7 us -> 0 us
  local copies, waits for them, and re-layouts: 62.5 us -> 14.4 us
  starting transfers between devices: 7.7 us -> 32.4 us
  matrix products: 23.1 us -> 0 us
  Pallas kernels: 0 us -> 19.3 us
  other arithmetic: 18.5 us -> 1.7 us
  between operations: 14.9 us -> 0.24 us
    reduce_scatter x1 -> x0, waiting for transfers between devices: 120 us -> none  [shards(): lax.psum_scatter(make_terms(whitened, table), 'tm', scatter_dimension=0,...]
    psum x1 -> x0, waiting for transfers between devices: 92.3 us -> none  [shards(): source_traces = lax.psum(local_picks.astype(jnp.bfloat16), 'chan')]
    psum x1 -> x0, blocking collectives: 54.7 us -> none  [shards(): energy = lax.psum(jnp.sum(filtered * filtered, axis=1), 'tm')]
    dot_general x3 -> x0, matrix products: 23.1 us -> none  [the longest x1 14 us: correlate(): jnp.einsum('rt,mlt->rml', receivers, table, preferred_element_type=jnp.fl...]
    all_to_all x0 -> x3, waiting for transfers between devices: none -> 23 us  [the longest x2 19.5 us: over_column(): lax.all_to_all(summed, 'tm', 0, 0, tiled=True, axis_index_groups=column)]
    another operation x2 -> x0, local copies, waits for them, and re-layouts: 21.7 us -> none  [lag_table(): jnp.stack([padded[:, lag:lag + span] for lag in range(lag_total)], axis=1)]
    pallas_call x0 -> x6, Pallas kernels: none -> 19.3 us  [the longest x1 4.84 us: correlate_first(): call(kernel, 'correlate_first', [shape((half_groups, sub, cols), jnp.floa...]
    all_to_all x0 -> x3, starting transfers between devices: none -> 18.8 us  [the longest x1 10.6 us: shards(): lax.all_to_all(energy, 'tm', 0, 0, tiled=True, axis_index_groups=same)]
  transfers between devices with their start and end apart: 5 -> 13, of which waited for: 2 -> 8; matrix products, arithmetic and copies ran while one was open for 7% -> 2% of each run, Pallas kernels for 0% -> 10%
where the time goes in v2:
time: 99.1 us; the launch traced here: 97.9 us
  starting transfers between devices  32.4 us (33%)
  waiting for transfers between devices  29.9 us (30%)
  Pallas kernels  19.3 us (19%)
  local copies, waits for them, and re-layouts  14.4 us (15%)
  other arithmetic  1.7 us (2%)
    all_to_all x2, waiting for transfers between devices, over_column(): lax.all_to_all(summed, 'tm', 0, 0, tiled=True, axis_index_groups=column)  19.5 us
    unnamed x18, local copies, waits for them, and re-layouts  10.9 us
    all_to_all x1, starting transfers between devices, shards(): lax.all_to_all(energy, 'tm', 0, 0, tiled=True, axis_index_groups=same)  10.6 us
    all_to_all x2, starting transfers between devices, over_column(): lax.all_to_all(summed, 'tm', 0, 0, tiled=True, axis_index_groups=column)  8.14 us
    pallas_call x1, Pallas kernels, correlate_first(): call(kernel, 'correlate_first', [shape((half_groups, sub, cols), jnp.floa...  4.84 us
    pallas_call x1, Pallas kernels, correlate_next(): call(kernel, 'correlate_next', [shape((half_groups, sub, cols), jnp.float...  4.48 us
    ppermute x1, starting transfers between devices, shards(): edge = lax.ppermute(edge, 'tm', across_edge)  4.18 us
    ppermute x3, starting transfers between devices, shards(): lax.ppermute(piece, 'chan', [(i, (i + 2 * d) % groups_chan) for i in rang...  3.99 us
  transfers between devices with their start and end apart: 13, of which 8 were waited for; matrix products, arithmetic and copies ran while one was open for 2% of the time, Pallas kernels for 10%

profile of v2, /device:TPU:8, one launch (start us, length us, event | category | flops | bytes accessed | tf_op | source)
XLA Modules:
  0.0 97.9 jit_solution(12384593855500834111)
XLA Ops:
  0.0 3.0 %pick_sources.1 = (bf16[8,4096]{1,0:T(8,128)(2,1)}, bf16[17,16,128]{2,1,0:T(8,128)(2,1)}, bf16[16,16,128]{2,1,0:T(8,128)(2,1)}) custom-call(s32[2,4]{1,0:T(2,128)} %ids_ref.1, bf16[16,2,16,4096]{3,2,1,0:T(8,128)(2,1)} %bitcast.11), custom_call_target="tpu_custom_call" | custom-call | bytes 2097152 | tf_op jit(solution)/shard_map/pick_sources/pallas_call | solution.py:96
  3.0 0.0 copy-start.7
  3.0 0.0 copy-start.6
  3.0 0.0 copy-start
  3.1 2.0 %dynamic-slice_bitcast_fusion = bf16[16,16,4096]{2,1,0:T(8,128)(2,1)S(1)} fusion(bf16[16,2,16,4096]{3,2,1,0:T(8,128)(2,1)} %bitcast.12, s32[]{:T(128)S(6)} %select_n.12), kind=kLoop, calls=%fused_computation | loop fusion | bytes 4194308 | tf_op jit(solution)/shard_map/jit(dynamic_index_in_dim)/squeeze | solution.py:327
  5.0 0.1 collective-permute-start.4
  5.1 4.2 %collective-permute-start = (bf16[17,16,128]{2,1,0:T(8,128)(2,1)S(1)}, bf16[17,16,128]{2,1,0:T(8,128)(2,1)S(1)}, u32[]{:S(2)}, u32[]{:S(2)}) collective-permute-start(bf16[17,16,128]{2,1,0:T(8,128)(2,1)S(1)} %copy-done.7), channel_id=1, source_target_pairs={{1,2},{3,4},{5,6},{7,8},{9,10},{11,12},{13,14},{15,16},{17,18},{19... | collective-permute-start | bytes 208904 | tf_op jit(solution)/shard_map/ppermute | solution.py:326
  9.3 0.7 collective-permute-start.5
  10.0 1.3 %collective-permute-done.edge_ref = bf16[17,16,128]{2,1,0:T(8,128)(2,1)S(1)} collective-permute-done((bf16[17,16,128]{2,1,0:T(8,128)(2,1)S(1)}, bf16[17,16,128]{2,1,0:T(8,128)(2,1)S(1)}, u32[]{:S(2)}, u32[]{:S(2)}) %collective-permute-start) | collective-permute-done | bytes 69664 | tf_op jit(solution)/shard_map/ppermute | solution.py:326
  11.3 2.4 %collective-permute-start.3 = (bf16[8,4352]{1,0:T(8,128)(2,1)S(1)}, bf16[8,4352]{1,0:T(8,128)(2,1)S(1)}, u32[]{:S(2)}, u32[]{:S(2)}) collective-permute-start(bf16[8,4352]{1,0:T(8,128)(2,1)S(1)} %pad_maximum_fusion), channel_id=1, source_target_pairs={{0,192},{32,224},{64,0},{96,32},{128,64},{160,96},{192,128},{224,1... | collective-permute-start | bytes 208904 | tf_op jit(solution)/shard_map/ppermute | solution.py:333
  13.7 0.8 collective-permute-start.2
  14.5 0.8 collective-permute-start.1
  15.3 0.0 collective-permute-done.5.high_ref
  15.3 0.0 collective-permute-done.4.other_ref
  15.3 0.0 copy-done
  15.3 3.1 %filter_rows.1 = (f32[256,8192]{1,0:T(8,128)S(1)}, f32[256,128]{1,0:T(8,128)S(1)}) custom-call(s32[16]{0:T(128)S(1)} %copy-done.3, bf16[1,256]{1,0:T(2,128)(2,1)S(1)} %reshape.12.taps_ref, bf16[16,2,16,4096]{3,2,1,0:T(8,128)(2,1)S(1)} %bitcast.13, bf16[16,16,4096]{2,1,0:T(8,128)(2,1)S(1)} %collective-permute-done.4.other_ref, ...), custom_call_target="tpu_custom_call" | custom-call | flops 2147483648 | bytes 12582912 | tf_op jit(solution)/shard_map/filter_rows/pallas_call | solution.py:148
  18.5 3.3 %copy-done.4 = f32[256,8192]{1,0:T(8,128)} copy-done((f32[256,8192]{1,0:T(8,128)}, f32[256,8192]{1,0:T(8,128)S(1)}, u32[]{:S(2)}) %copy-start.4) | copy-done | bytes 8388632
  21.7 0.0 collective-permute-done.3
  21.7 0.0 collective-permute-done.2
  21.7 0.0 collective-permute-done.1
  21.8 2.5 %collective-permute-start.6 = (bf16[8,4352]{1,0:T(8,128)(2,1)S(1)}, bf16[8,4352]{1,0:T(8,128)(2,1)S(1)}, u32[]{:S(2)}, u32[]{:S(2)}) collective-permute-start(bf16[8,4352]{1,0:T(8,128)(2,1)S(1)} %add_add_fusion), channel_id=1, source_target_pairs={{0,32},{32,0},{64,96},{96,64},{128,160},{160,128},{192,224},{224,1... | collective-permute-start | bytes 208904 | tf_op jit(solution)/shard_map/ppermute | solution.py:339
  24.3 3.8 %collective-permute-done.6 = bf16[8,4352]{1,0:T(8,128)(2,1)S(1)} collective-permute-done((bf16[8,4352]{1,0:T(8,128)(2,1)S(1)}, bf16[8,4352]{1,0:T(8,128)(2,1)S(1)}, u32[]{:S(2)}, u32[]{:S(2)}) %collective-permute-start.6) | collective-permute-done | bytes 69664 | tf_op jit(solution)/shard_map/ppermute | solution.py:339
  28.1 0.1 collective-permute-start.7
  28.2 1.2 %collective-permute-done.7.other_ref = bf16[8,4352]{1,0:T(8,128)(2,1)S(1)} collective-permute-done((bf16[8,4352]{1,0:T(8,128)(2,1)S(1)}, bf16[8,4352]{1,0:T(8,128)(2,1)S(1)}, u32[]{:S(2)}, u32[]{:S(2)}) %collective-permute-start.7) | collective-permute-done | bytes 69664 | tf_op jit(solution)/shard_map/ppermute | solution.py:340
  29.5 1.6 %filter_sources.1 = (f32[8,8448]{1,0:T(8,128)S(1)}, f32[16,8,128]{2,1,0:T(8,128)}) custom-call(s32[16]{0:T(128)S(1)} %copy-done.3, bf16[1,256]{1,0:T(2,128)(2,1)S(1)} %reshape.12.taps_ref, bf16[8,4352]{1,0:T(8,128)(2,1)S(1)} %add.34.mine_ref, bf16[8,4352]{1,0:T(8,128)(2,1)S(1)} %collective-permute-done.7.other_ref, f32[256,128]{1,0:T(8,128)S(1)} %get-tuple-element.33.power_ref), custom_call_target="tpu_custom_call" | custom-call | bytes 1048576 | tf_op jit(solution)/shard_map/filter_sources/pallas_call | solution.py:207
  31.1 10.6 %all-to-all-start = ((f32[16,8,128]{2,1,0:T(8,128)}), f32[16,8,128]{2,1,0:T(8,128)S(1)}, u32[]{:S(2)}, u32[]{:S(2)}) async-start(f32[16,8,128]{2,1,0:T(8,128)} %get-tuple-element.34), calls=%async_computation | async-start | bytes 131072 | tf_op jit(solution)/shard_map/all_to_all | solution.py:346
  41.7 2.2 %shift_sources.1.traces_ref = f32[8448,128]{1,0:T(8,128)S(1)} custom-call(f32[8,8448]{1,0:T(8,128)S(1)} %get-tuple-element.35.traces_ref), custom_call_target="tpu_custom_call" | custom-call | bytes 8388608 | tf_op jit(solution)/shard_map/shift_sources/pallas_call | solution.py:228
  44.0 2.0 %copy-done.1 = f32[8448,128]{1,0:T(8,128)} copy-done((f32[8448,128]{1,0:T(8,128)}, f32[8448,128]{1,0:T(8,128)S(1)}, u32[]{:S(2)}) %copy-start.1) | copy-done | bytes 4325400
  46.0 3.5 %all-to-all-done.energy_ref = f32[16,8,128]{2,1,0:T(8,128)S(1)} async-done(((f32[16,8,128]{2,1,0:T(8,128)}), f32[16,8,128]{2,1,0:T(8,128)S(1)}, u32[]{:S(2)}, u32[]{:S(2)}) %all-to-all-start) | async-done | bytes 65568 | tf_op jit(solution)/shard_map/all_to_all | solution.py:346
  49.5 2.2 %copy-done.2 = f32[8448,128]{1,0:T(8,128)S(1)} copy-done((f32[8448,128]{1,0:T(8,128)S(1)}, f32[8448,128]{1,0:T(8,128)}, u32[]{:S(2)}) %copy-start.2) | copy-done | bytes 4325400
  51.7 3.4 %copy-done.5 = f32[256,8192]{1,0:T(8,128)S(1)} copy-done((f32[256,8192]{1,0:T(8,128)S(1)}, f32[256,8192]{1,0:T(8,128)}, u32[]{:S(2)}) %copy-start.5) | copy-done | bytes 8388632
  55.1 4.8 %correlate_first.1 = (f32[8,16,1024]{2,1,0:T(8,128)S(1)}, bf16[8,16,1024]{2,1,0:T(8,128)(2,1)S(1)}, bf16[256,8192]{1,0:T(8,128)(2,1)S(1)}, bf16[8448,128]{1,0:T(8,128)(2,1)S(1)}) custom-call(f32[16,8,128]{2,1,0:T(8,128)S(1)} %all-to-all-done.energy_ref, f32[8448,128]{1,0:T(8,128)S(1)} %copy-done.2, f32[256,8192]{1,0:T(8,128)S(1)} %copy-done.5), custom_call_target="tpu_custom_call" | custom-call | flops 4294967296 | bytes 16777216 | tf_op jit(solution)/shard_map/correlate_first/pallas_call | solution.py:273
  60.0 1.5 %collective-permute-start.8 = (bf16[8,16,1024]{2,1,0:T(8,128)(2,1)S(1)}, bf16[8,16,1024]{2,1,0:T(8,128)(2,1)S(1)}, u32[]{:S(2)}, u32[]{:S(2)}) collective-permute-start(bf16[8,16,1024]{2,1,0:T(8,128)(2,1)S(1)} %get-tuple-element.38), channel_id=1, source_target_pairs={{0,2},{1,3},{2,0},{3,1},{4,6},{5,7},{6,4},{7,5},{8,10},{9,11},{10,... | collective-permute-start | bytes 786440 | tf_op jit(solution)/shard_map/ppermute | solution.py:362
  61.4 4.5 %correlate_next.1 = (f32[8,16,1024]{2,1,0:T(8,128)S(1)}, bf16[8,16,1024]{2,1,0:T(8,128)(2,1)S(1)}) custom-call(bf16[256,8192]{1,0:T(8,128)(2,1)S(1)} %get-tuple-element.39.white_ref, bf16[8448,128]{1,0:T(8,128)(2,1)S(1)} %get-tuple-element.40.table_ref), custom_call_target="tpu_custom_call" | custom-call | flops 4294967296 | bytes 8388608 | tf_op jit(solution)/shard_map/correlate_next/pallas_call | solution.py:296
  65.9 0.7 collective-permute-start.9
  66.6 0.3 collective-permute-done.8
  67.0 0.8 add_convert_fusion.1
  67.7 4.7 %all-to-all-start.1 = ((bf16[8,16,1024]{2,1,0:T(8,128)(2,1)}), bf16[8,16,1024]{2,1,0:T(8,128)(2,1)S(1)}, u32[]{:S(2)}, u32[]{:S(2)}) async-start(bf16[8,16,1024]{2,1,0:T(8,128)(2,1)} %add_convert_fusion.1), calls=%async_computation.1 | async-start | bytes 524288 | tf_op jit(solution)/shard_map/all_to_all | solution.py:360
  72.5 0.2 collective-permute-done.9
  72.7 0.8 add_convert_fusion
  73.4 9.5 %all-to-all-done.1 = bf16[8,16,1024]{2,1,0:T(8,128)(2,1)S(1)} async-done(((bf16[8,16,1024]{2,1,0:T(8,128)(2,1)}), bf16[8,16,1024]{2,1,0:T(8,128)(2,1)S(1)}, u32[]{:S(2)}, u32[]{:S(2)}) %all-to-all-start.1) | async-done | bytes 262176 | tf_op jit(solution)/shard_map/all_to_all | solution.py:360
  83.0 3.4 %all-to-all-start.2 = ((bf16[8,16,1024]{2,1,0:T(8,128)(2,1)}), bf16[8,16,1024]{2,1,0:T(8,128)(2,1)S(1)}, u32[]{:S(2)}, u32[]{:S(2)}) async-start(bf16[8,16,1024]{2,1,0:T(8,128)(2,1)} %add_convert_fusion), calls=%async_computation.2 | async-start | bytes 524288 | tf_op jit(solution)/shard_map/all_to_all | solution.py:360
  86.4 0.2 copy.6
  86.6 0.2 copy.8
  86.8 9.9 %all-to-all-done.2 = bf16[8,16,1024]{2,1,0:T(8,128)(2,1)S(1)} async-done(((bf16[8,16,1024]{2,1,0:T(8,128)(2,1)}), bf16[8,16,1024]{2,1,0:T(8,128)(2,1)S(1)}, u32[]{:S(2)}, u32[]{:S(2)}) %all-to-all-start.2) | async-done | bytes 262176 | tf_op jit(solution)/shard_map/all_to_all | solution.py:360
  96.8 0.2 copy.7
  97.0 0.2 copy.9
  97.3 0.7 reshape.14
  (19 shorter events, 0.2 us)
Async XLA Ops:
  0.0 10.0 %copy-start.8 = (bf16[64]{0:T(256)(128)(2,1)S(1)}, bf16[64]{0:T(256)(128)(2,1)}, u32[]{:S(2)}) copy-start(bf16[64]{0:T(256)(128)(2,1)} %param.5) | copy-start | bytes 388
  0.0 15.3 %copy-start.3 = (s32[16]{0:T(128)S(1)}, s32[16]{0:T(128)}, u32[]{:S(2)}) copy-start(s32[16]{0:T(128)} %off_ref.3) | copy-start | bytes 196
  3.0 2.1 %copy-start.7 = (bf16[17,16,128]{2,1,0:T(8,128)(2,1)S(1)}, bf16[17,16,128]{2,1,0:T(8,128)(2,1)}, u32[]{:S(2)}) copy-start(bf16[17,16,128]{2,1,0:T(8,128)(2,1)} %get-tuple-element.26) | copy-start | bytes 208900
  3.0 8.3 %copy-start.6 = (bf16[8,4096]{1,0:T(8,128)(2,1)S(1)}, bf16[8,4096]{1,0:T(8,128)(2,1)}, u32[]{:S(2)}) copy-start(bf16[8,4096]{1,0:T(8,128)(2,1)} %get-tuple-element.25) | copy-start | bytes 196612
  3.0 12.3 %copy-start = (bf16[512,4096]{1,0:T(8,128)(2,1)S(1)}, bf16[512,4096]{1,0:T(8,128)(2,1)}, u32[]{:S(2)}) copy-start(bf16[512,4096]{1,0:T(8,128)(2,1)} %param.4) | copy-start | bytes 12582916
  5.0 10.3 %collective-permute-start.4 = (bf16[16,16,4096]{2,1,0:T(8,128)(2,1)S(1)}, bf16[16,16,4096]{2,1,0:T(8,128)(2,1)S(1)}, u32[]{:S(2)}, u32[]{:S(2)}) collective-permute-start(bf16[16,16,4096]{2,1,0:T(8,128)(2,1)S(1)} %dynamic-slice_bitcast_fusion), channel_id=1, source_target_pairs={{0,1},{1,0},{2,3},{3,2},{4,5},{5,4},{6,7},{7,6},{8,9},{9,8},{10,11... | collective-permute-start | bytes 6291464 | tf_op jit(solution)/shard_map/ppermute | solution.py:328
  5.1 6.2 %collective-permute-start = (bf16[17,16,128]{2,1,0:T(8,128)(2,1)S(1)}, bf16[17,16,128]{2,1,0:T(8,128)(2,1)S(1)}, u32[]{:S(2)}, u32[]{:S(2)}) collective-permute-start(bf16[17,16,128]{2,1,0:T(8,128)(2,1)S(1)} %copy-done.7), channel_id=1, source_target_pairs={{1,2},{3,4},{5,6},{7,8},{9,10},{11,12},{13,14},{15,16},{17,18},{19... | collective-permute-start | bytes 208904 | tf_op jit(solution)/shard_map/ppermute | solution.py:326
  9.3 6.0 %collective-permute-start.5 = (bf16[16,16,128]{2,1,0:T(8,128)(2,1)}, bf16[16,16,128]{2,1,0:T(8,128)(2,1)S(1)}, u32[]{:S(2)}, u32[]{:S(2)}) collective-permute-start(bf16[16,16,128]{2,1,0:T(8,128)(2,1)} %get-tuple-element.28), channel_id=1, source_target_pairs={{1,3},{3,5},{5,7},{7,9},{9,11},{11,13},{13,15},{15,17},{17,19},{19... | collective-permute-start | bytes 196616 | tf_op jit(solution)/shard_map/ppermute | solution.py:329
  11.3 10.4 %collective-permute-start.3 = (bf16[8,4352]{1,0:T(8,128)(2,1)S(1)}, bf16[8,4352]{1,0:T(8,128)(2,1)S(1)}, u32[]{:S(2)}, u32[]{:S(2)}) collective-permute-start(bf16[8,4352]{1,0:T(8,128)(2,1)S(1)} %pad_maximum_fusion), channel_id=1, source_target_pairs={{0,192},{32,224},{64,0},{96,32},{128,64},{160,96},{192,128},{224,1... | collective-permute-start | bytes 208904 | tf_op jit(solution)/shard_map/ppermute | solution.py:333
  13.7 8.0 %collective-permute-start.2 = (bf16[8,4352]{1,0:T(8,128)(2,1)S(1)}, bf16[8,4352]{1,0:T(8,128)(2,1)S(1)}, u32[]{:S(2)}, u32[]{:S(2)}) collective-permute-start(bf16[8,4352]{1,0:T(8,128)(2,1)S(1)} %pad_maximum_fusion), channel_id=1, source_target_pairs={{0,128},{32,160},{64,192},{96,224},{128,0},{160,32},{192,64},{224,... | collective-permute-start | bytes 208904 | tf_op jit(solution)/shard_map/ppermute | solution.py:333
  14.5 7.3 %collective-permute-start.1 = (bf16[8,4352]{1,0:T(8,128)(2,1)S(1)}, bf16[8,4352]{1,0:T(8,128)(2,1)S(1)}, u32[]{:S(2)}, u32[]{:S(2)}) collective-permute-start(bf16[8,4352]{1,0:T(8,128)(2,1)S(1)} %pad_maximum_fusion), channel_id=1, source_target_pairs={{0,64},{32,96},{64,128},{96,160},{128,192},{160,224},{192,0},{224,... | collective-permute-start | bytes 208904 | tf_op jit(solution)/shard_map/ppermute | solution.py:333
  18.5 3.3 %copy-start.4 = (f32[256,8192]{1,0:T(8,128)}, f32[256,8192]{1,0:T(8,128)S(1)}, u32[]{:S(2)}) copy-start(f32[256,8192]{1,0:T(8,128)S(1)} %get-tuple-element.36.rows_ref) | copy-start | bytes 25165828
  21.8 6.3 %collective-permute-start.6 = (bf16[8,4352]{1,0:T(8,128)(2,1)S(1)}, bf16[8,4352]{1,0:T(8,128)(2,1)S(1)}, u32[]{:S(2)}, u32[]{:S(2)}) collective-permute-start(bf16[8,4352]{1,0:T(8,128)(2,1)S(1)} %add_add_fusion), channel_id=1, source_target_pairs={{0,32},{32,0},{64,96},{96,64},{128,160},{160,128},{192,224},{224,1... | collective-permute-start | bytes 208904 | tf_op jit(solution)/shard_map/ppermute | solution.py:339
  28.1 1.3 %collective-permute-start.7 = (bf16[8,4352]{1,0:T(8,128)(2,1)S(1)}, bf16[8,4352]{1,0:T(8,128)(2,1)S(1)}, u32[]{:S(2)}, u32[]{:S(2)}) collective-permute-start(bf16[8,4352]{1,0:T(8,128)(2,1)S(1)} %add.34.mine_ref), channel_id=1, source_target_pairs={{0,1},{1,0},{2,3},{3,2},{4,5},{5,4},{6,7},{7,6},{8,9},{9,8},{10,11... | collective-permute-start | bytes 208904 | tf_op jit(solution)/shard_map/ppermute | solution.py:340
  31.1 18.4 %all-to-all-start = ((f32[16,8,128]{2,1,0:T(8,128)}), f32[16,8,128]{2,1,0:T(8,128)S(1)}, u32[]{:S(2)}, u32[]{:S(2)}) async-start(f32[16,8,128]{2,1,0:T(8,128)} %get-tuple-element.34), calls=%async_computation | async-start | bytes 131072 | tf_op jit(solution)/shard_map/all_to_all | solution.py:346
  44.0 2.0 %copy-start.1 = (f32[8448,128]{1,0:T(8,128)}, f32[8448,128]{1,0:T(8,128)S(1)}, u32[]{:S(2)}) copy-start(f32[8448,128]{1,0:T(8,128)S(1)} %shift_sources.1.traces_ref) | copy-start | bytes 12976132
  49.5 2.2 %copy-start.2 = (f32[8448,128]{1,0:T(8,128)S(1)}, f32[8448,128]{1,0:T(8,128)}, u32[]{:S(2)}) copy-start(f32[8448,128]{1,0:T(8,128)} %copy-done.1) | copy-start | bytes 12976132
  51.7 3.4 %copy-start.5 = (f32[256,8192]{1,0:T(8,128)S(1)}, f32[256,8192]{1,0:T(8,128)}, u32[]{:S(2)}) copy-start(f32[256,8192]{1,0:T(8,128)} %copy-done.4) | copy-start | bytes 25165828
  60.0 7.0 %collective-permute-start.8 = (bf16[8,16,1024]{2,1,0:T(8,128)(2,1)S(1)}, bf16[8,16,1024]{2,1,0:T(8,128)(2,1)S(1)}, u32[]{:S(2)}, u32[]{:S(2)}) collective-permute-start(bf16[8,16,1024]{2,1,0:T(8,128)(2,1)S(1)} %get-tuple-element.38), channel_id=1, source_target_pairs={{0,2},{1,3},{2,0},{3,1},{4,6},{5,7},{6,4},{7,5},{8,10},{9,11},{10,... | collective-permute-start | bytes 786440 | tf_op jit(solution)/shard_map/ppermute | solution.py:362
  65.9 6.7 %collective-permute-start.9 = (bf16[8,16,1024]{2,1,0:T(8,128)(2,1)S(1)}, bf16[8,16,1024]{2,1,0:T(8,128)(2,1)S(1)}, u32[]{:S(2)}, u32[]{:S(2)}) collective-permute-start(bf16[8,16,1024]{2,1,0:T(8,128)(2,1)S(1)} %get-tuple-element.42), channel_id=1, source_target_pairs={{0,2},{1,3},{2,0},{3,1},{4,6},{5,7},{6,4},{7,5},{8,10},{9,11},{10,... | collective-permute-start | bytes 786440 | tf_op jit(solution)/shard_map/ppermute | solution.py:364
  67.7 15.2 %all-to-all-start.1 = ((bf16[8,16,1024]{2,1,0:T(8,128)(2,1)}), bf16[8,16,1024]{2,1,0:T(8,128)(2,1)S(1)}, u32[]{:S(2)}, u32[]{:S(2)}) async-start(bf16[8,16,1024]{2,1,0:T(8,128)(2,1)} %add_convert_fusion.1), calls=%async_computation.1 | async-start | bytes 524288 | tf_op jit(solution)/shard_map/all_to_all | solution.py:360
  83.0 13.8 %all-to-all-start.2 = ((bf16[8,16,1024]{2,1,0:T(8,128)(2,1)}), bf16[8,16,1024]{2,1,0:T(8,128)(2,1)S(1)}, u32[]{:S(2)}, u32[]{:S(2)}) async-start(bf16[8,16,1024]{2,1,0:T(8,128)(2,1)} %add_convert_fusion), calls=%async_computation.2 | async-start | bytes 524288 | tf_op jit(solution)/shard_map/all_to_all | solution.py:360

commit v3 on v2

v3 whole, which is shorter than its diff:
```python
import math

import jax
import jax.numpy as jnp
from jax import lax
from jax.experimental import pallas as pl
from jax.experimental.pallas import tpu as pltpu
from jax.sharding import PartitionSpec as P

TAPS = 64
MAXLAG = 128
LAGS = 256
NSRC = 2
SB = 4
NS = NSRC * SB
WIN = 8192
LANE = 128
SHIFTS = 16
LEFT = 256
EPS = 1e-05
MIB = 1024 * 1024

VMEM = pl.BlockSpec(memory_space=pltpu.VMEM)
SMEM = pl.BlockSpec(memory_space=pltpu.SMEM)
ANY = pl.BlockSpec(memory_space=pl.ANY)


def call(kernel, name, out, in_specs, scratch=(), out_specs=None, limit=16, flops=0, moved=0):
    return pl.pallas_call(
        kernel,
        out_shape=out,
        in_specs=in_specs,
        out_specs=out_specs or [VMEM] * len(out),
        scratch_shapes=list(scratch),
        compiler_params=pltpu.CompilerParams(vmem_limit_bytes=limit * MIB),
        cost_estimate=pl.CostEstimate(flops=flops, bytes_accessed=moved, transcendentals=0),
        name=name,
    )


def shape(dims, dtype):
    return jax.ShapeDtypeStruct(dims, dtype)


def fir_tile(taps):
    wide = jnp.broadcast_to(taps.astype(jnp.float32), (2 * LANE, 2 * LANE))
    rolled = pltpu.roll(wide, LANE, 1, stride=1, stride_axis=0)
    return rolled[:, :LANE].astype(jnp.bfloat16)


def wide_taps(taps):
    return jnp.pad(taps, (0, 2 * LANE - TAPS)).reshape(1, 2 * LANE)


def pick_sources(source_channels, x4):
    groups, _, sub, samples = x4.shape
    channels = groups * 2 * sub

    def kernel(ids_ref, x_ref, own_ref, low_ref, high_ref, away_ref, buf, sems):
        base = lax.axis_index("chan") * channels
        core = lax.axis_index("tm") % 2
        copies = []
        inner = []
        for j in range(NS):
            local = ids_ref[j // SB, j % SB] - base
            owned = (local >= 0) & (local < channels)
            row = jnp.clip(local, 0, channels - 1)
            group, half = row // (2 * sub), (row // sub) % 2
            inner.append(jnp.where(owned, row % sub, -1))
            copies.append(pltpu.make_async_copy(x_ref.at[group, half], buf.at[j], sems.at[j]))
        last = pl.ds(samples - LANE, LANE)
        rest = [
            pltpu.make_async_copy(x_ref.at[:, 0, :, last], low_ref, sems.at[NS]),
            pltpu.make_async_copy(x_ref.at[:, 1, :, last], high_ref, sems.at[NS + 1]),
            pltpu.make_async_copy(x_ref.at[:, 1 - core], away_ref, sems.at[NS + 2]),
        ]
        for copy in copies + rest:
            copy.start()
        rows = lax.broadcasted_iota(jnp.int32, (sub, 1), 0)
        own = jnp.zeros((NS, samples), jnp.float32)
        for j in range(NS):
            copies[j].wait()
            picked = buf[j].astype(jnp.float32) * jnp.where(rows == inner[j], 1.0, 0.0)
            picked = picked[:NS] + picked[NS:]
            own = own + pltpu.roll(picked, (j + NS - inner[j] % NS) % NS, 0)
        own_ref[...] = own.astype(jnp.bfloat16)
        for copy in rest:
            copy.wait()

    edge = shape((groups, sub, LANE), jnp.bfloat16)
    return call(
        kernel,
        "pick_sources",
        [
            shape((NS, samples), jnp.bfloat16),
            edge,
            edge,
            shape((groups, sub, samples), jnp.bfloat16),
        ],
        [SMEM, ANY],
        [pltpu.VMEM((NS, sub, samples), jnp.bfloat16), pltpu.SemaphoreType.DMA((NS + 3,))],
        out_specs=[VMEM, VMEM, VMEM, ANY],
        limit=61,
        moved=4 * MIB,
    )(source_channels, x4)


def join_sources(piece, arrived):
    samples = piece.shape[1]

    def kernel(piece_ref, arrived_ref, out_ref, end_ref):
        core = lax.axis_index("tm") % 2
        total = piece_ref[...].astype(jnp.float32) + arrived_ref[...].astype(jnp.float32)
        out_ref[...] = total.astype(jnp.bfloat16)
        end = jnp.where(core == 1, total[:, samples - LEFT :], total[:, :LEFT])
        end_ref[...] = end.astype(jnp.bfloat16)

    return call(
        kernel,
        "join_sources",
        [shape(piece.shape, jnp.bfloat16), shape((NS, LEFT), jnp.bfloat16)],
        [VMEM, VMEM],
    )(piece, arrived)


def filter_rows(offsets, taps, x4, other, low_edge, high_edge):
    groups, _, sub, half = x4.shape
    rows = groups * sub
    chunk = 1024
    parts = half // chunk
    total = 2 * parts

    def kernel(
        off_ref, taps_ref, x_ref, other_ref, low_ref, high_ref, out_ref, power_ref,
        raw, value_buf, in_sems, out_sems
    ):
        tile = lax.axis_index("tm")
        core = tile % 2

        def fetch(part, source, index):
            cols = pl.ds(index * chunk, chunk)
            return pltpu.make_async_copy(source.at[:, :, cols], raw.at[part], in_sems.at[part])

        own = x_ref.at[:, core]

        @pl.when(core == 0)
        def _():
            for p in range(parts):
                fetch(p, own, p).start()
            for p in range(parts):
                fetch(parts + p, other_ref, p).start()

        @pl.when(core == 1)
        def _():
            for p in range(parts):
                fetch(p, other_ref, p).start()
            for p in range(parts):
                fetch(parts + p, own, p).start()

        matrix = fir_tile(taps_ref[...])
        first_kept = off_ref[tile // 2]
        previous = jnp.where(core == 0, low_ref[...], high_ref[...]).reshape(rows, LANE)
        power = jnp.zeros((rows, LANE), jnp.float32)
        stores = []
        for part in range(total):
            fetch(part, own, 0).wait()
            for j in range(chunk // LANE):
                current = raw[part, :, :, j * LANE : (j + 1) * LANE].reshape(rows, LANE)
                framed = jnp.concatenate([previous, current], axis=1)
                value = jnp.dot(framed, matrix, preferred_element_type=jnp.float32)
                power = power + value * value
                start = part * chunk + j * LANE
                if start < WIN:
                    place = lax.broadcasted_iota(jnp.int32, (1, LANE), 1) + start
                    value = value * jnp.where(place >= first_kept, 1.0, 0.0)
                value_buf[part, :, j * LANE : (j + 1) * LANE] = value
                previous = current
            store = pltpu.make_async_copy(
                value_buf.at[part],
                out_ref.at[:, pl.ds(part * chunk, chunk)],
                out_sems.at[part],
            )
            store.start()
            stores.append(store)
        power_ref[...] = power
        for store in stores:
            store.wait()

    return call(
        kernel,
        "filter_rows",
        [shape((rows, 2 * half), jnp.float32), shape((rows, LANE), jnp.float32)],
        [SMEM, VMEM, ANY, ANY, VMEM, VMEM],
        [
            pltpu.VMEM((total, groups, sub, chunk), jnp.bfloat16),
            pltpu.VMEM((total, rows, chunk), jnp.float32),
            pltpu.SemaphoreType.DMA((total,)),
            pltpu.SemaphoreType.DMA((total,)),
        ],
        out_specs=[ANY, VMEM],
        limit=40,
        flops=2 * rows * 2 * half * 512,
        moved=12 * MIB,
    )(offsets, taps, x4, other, low_edge, high_edge)


def filter_sources(offsets, taps, mine, other, edge, cross, power, chips):
    length = WIN + 2 * MAXLAG
    count = length // LANE

    def kernel(
        off_ref, taps_ref, mine_ref, other_ref, edge_ref, cross_ref, power_ref, out_ref, energy_ref
    ):
        tile = lax.axis_index("tm")
        core, chip = tile % 2, tile // 2
        mine_rows = mine_ref[...].astype(jnp.float32)
        other_rows = other_ref[...].astype(jnp.float32)
        low = jnp.where(core == 0, mine_rows, other_rows)
        high = jnp.where(core == 0, other_rows, mine_rows)
        edge_rows = edge_ref[...].astype(jnp.float32)
        cross_rows = cross_ref[...].astype(jnp.float32)
        left = jnp.where(core == 0, edge_rows, cross_rows)
        right = jnp.where(core == 0, cross_rows, edge_rows)
        raw = jnp.concatenate([left, low, high, right[:, :LANE]], axis=1)
        blocks = [raw[:, j * LANE : (j + 1) * LANE] for j in range(count + 1)]
        before = jnp.concatenate(blocks[:-1], axis=0)
        after = jnp.concatenate(blocks[1:], axis=0)
        framed = jnp.concatenate([before, after], axis=1).astype(jnp.bfloat16)
        value = jnp.dot(framed, fir_tile(taps_ref[...]), preferred_element_type=jnp.float32)
        total = jnp.zeros((NS, LANE), jnp.float32)
        first_kept = [
            off_ref[jnp.maximum(chip - 1, 0)],
            off_ref[chip],
            off_ref[jnp.minimum(chip + 1, chips - 1)],
        ]
        for j in range(count):
            piece = value[j * NS : (j + 1) * NS, :]
            start = j * LANE - MAXLAG
            window = start // WIN
            if window == 0:
                total = total + piece * piece
            place = lax.broadcasted_iota(jnp.int32, (1, LANE), 1) + (start - window * WIN)
            keep = jnp.where(place >= first_kept[window + 1], 1.0, 0.0)
            if window < 0:
                keep = keep * jnp.where(chip > 0, 1.0, 0.0)
            if window > 0:
                keep = keep * jnp.where(chip < chips - 1, 1.0, 0.0)
            out_ref[:, j * LANE : (j + 1) * LANE] = piece * keep
        lines = []
        for r in range(power_ref.shape[0] // LANE):
            turned = power_ref[r * LANE : (r + 1) * LANE, :].T
            lines.append(jnp.sum(turned, axis=0, keepdims=True))
        repeated = jnp.concatenate([total] * SHIFTS, axis=0)
        lines.append(jnp.sum(repeated.T, axis=0, keepdims=True))
        lines.append(jnp.zeros((8 - len(lines), LANE), jnp.float32))
        energy = jnp.concatenate(lines, axis=0)
        energy_ref[...] = jnp.broadcast_to(energy[None], energy_ref.shape)

    return call(
        kernel,
        "filter_sources",
        [shape((NS, length), jnp.float32), shape((chips, 8, LANE), jnp.float32)],
        [SMEM, VMEM, VMEM, VMEM, VMEM, VMEM, VMEM],
        moved=MIB,
    )(offsets, taps, mine, other, edge, cross, power)


def lag_products(white, table_ref, pairs, keep_ref, send_ref, half_groups):
    rows, depth = white.shape
    sub = rows // half_groups // 2
    own_low = (lax.axis_index("tm") // 2) % 2 == 0
    for place, pair in enumerate(pairs):
        offset = pair * 2 * SHIFTS
        left = table_ref[offset : offset + depth, :]
        right = table_ref[offset + SHIFTS : offset + SHIFTS + depth, :]
        lags = jnp.concatenate([left, right], axis=1)
        value = jnp.dot(white[...], lags, preferred_element_type=jnp.float32)
        value = value.reshape(half_groups, 2, sub, 2 * LANE)
        low, high = value[:, 0], value[:, 1]
        cols = slice(place * 2 * LANE, (place + 1) * 2 * LANE)
        keep_ref[:, :, cols] = jnp.where(own_low, low, high)
        send_ref[:, :, cols] = jnp.where(own_low, high, low).astype(jnp.bfloat16)


def correlate_first(energies, traces, rows, pairs, half_groups, total_samples):
    channels, depth = rows.shape
    length = traces.shape[1]
    chunk = 1024
    loads = depth // chunk

    def kernel(
        energy_ref, traces_ref, rows_ref, keep_ref, send_ref, white, table, buf, shifted, sems
    ):
        copies = []
        for i in range(loads):
            cols = pl.ds(i * chunk, chunk)
            copies.append(pltpu.make_async_copy(rows_ref.at[:, cols], buf.at[i], sems.at[i]))
        for copy in copies:
            copy.start()
        energy = jnp.sum(energy_ref[...], axis=0)
        scale = lax.rsqrt(energy / total_samples + EPS)
        padded = jnp.concatenate([scale, jnp.zeros((LANE - 8, LANE), jnp.float32)], axis=0)
        turned = padded.T
        parts = channels // LANE
        gain = jnp.concatenate([turned[:, r : r + 1] for r in range(parts)], axis=0)
        trace = traces_ref[...] * turned[:NS, parts : parts + 1]
        trace = trace.astype(jnp.bfloat16).astype(jnp.float32)
        for b in range(SHIFTS):
            moved = trace if b == 0 else pltpu.roll(trace, length - b, 1)
            shifted[b * NS : (b + 1) * NS, :] = moved
        for j in range(length // LANE):
            cols = slice(j * LANE, (j + 1) * LANE)
            table[cols, :] = shifted[:, cols].T.astype(jnp.bfloat16)
        for i in range(loads):
            copies[i].wait()
            white[:, i * chunk : (i + 1) * chunk] = (buf[i] * gain).astype(jnp.bfloat16)
        lag_products(white, table, pairs, keep_ref, send_ref, half_groups)

    sub = channels // half_groups // 2
    cols = len(pairs) * 2 * LANE
    return call(
        kernel,
        "correlate_first",
        [
            shape((half_groups, sub, cols), jnp.float32),
            shape((half_groups, sub, cols), jnp.bfloat16),
            shape((channels, depth), jnp.bfloat16),
            shape((length, LANE), jnp.bfloat16),
        ],
        [VMEM, VMEM, ANY],
        [
            pltpu.VMEM((loads, channels, chunk), jnp.float32),
            pltpu.VMEM((LANE, length), jnp.float32),
            pltpu.SemaphoreType.DMA((loads,)),
        ],
        limit=40,
        flops=2 * channels * depth * cols,
        moved=16 * MIB,
    )(energies, traces, rows)


def correlate_next(white, table, pairs, half_groups):
    channels, depth = white.shape

    def kernel(white_ref, table_ref, keep_ref, send_ref):
        lag_products(white_ref, table_ref, pairs, keep_ref, send_ref, half_groups)

    sub = channels // half_groups // 2
    cols = len(pairs) * 2 * LANE
    return call(
        kernel,
        "correlate_next",
        [
            shape((half_groups, sub, cols), jnp.float32),
            shape((half_groups, sub, cols), jnp.bfloat16),
        ],
        [VMEM, VMEM],
        flops=2 * channels * depth * cols,
        moved=8 * MIB,
    )(white, table)


def add_line(keep, across):
    groups, sub, cols = keep.shape

    def kernel(keep_ref, across_ref, own_ref, *out_refs):
        place = lax.axis_index("tm") // 4
        for d in range(groups):
            index = lax.rem(place + d, groups)
            value = keep_ref[index] + across_ref[index].astype(jnp.float32)
            if d == 0:
                own_ref[...] = value
            else:
                out_refs[d - 1][...] = value.astype(jnp.bfloat16)

    return call(
        kernel,
        "add_line",
        [shape((sub, cols), jnp.float32)]
        + [shape((sub, cols), jnp.bfloat16)] * (groups - 1),
        [VMEM, VMEM],
        moved=MIB,
    )(keep, across)


def finish(halves, factor):
    count = len(halves[0])
    sub, cols = halves[0][0].shape
    blocks = cols // LANE

    def kernel(*refs):
        out_ref, turned = refs[-2], refs[-1]
        blank = jnp.zeros((LANE - sub, LANE), jnp.float32)
        for h in range(len(halves)):
            part = refs[h * count : (h + 1) * count]
            value = part[0][...]
            for ref in part[1:]:
                value = value + ref[...].astype(jnp.float32)
            value = value * factor
            for j in range(blocks):
                block = jnp.concatenate([value[:, j * LANE : (j + 1) * LANE], blank], axis=0)
                start = (h * blocks + j) * LANE
                turned[start : start + LANE, :] = block.T
        for m in range(NS):
            for j in range(LAGS // LANE):
                block = turned[pl.ds(j * LANE * NS + m, LANE, stride=NS), :]
                out_ref[:, m, j * LANE : (j + 1) * LANE] = block.T[:sub]

    return call(
        kernel,
        "finish",
        [shape((sub, NS, LAGS), jnp.float32)],
        [VMEM] * (count * len(halves)),
        [pltpu.VMEM((NS * LAGS, LANE), jnp.float32)],
        moved=MIB,
    )(*[part for half in halves for part in half])[0]


def shards(strain_rate, whiten_taps, source_channels, window_offsets):
    channels, samples = strain_rate.shape
    tiles = lax.axis_size("tm")
    groups_chan = lax.axis_size("chan")
    total_samples = samples * tiles
    chips = tiles // 2
    sub = channels // tiles
    taps = wide_taps(whiten_taps)

    x4 = strain_rate.reshape(chips, 2, sub, samples)
    piece, low_edge, high_edge, away = pick_sources(source_channels, x4)

    swap = [(i, i ^ 1) for i in range(tiles)]
    to_next = [(2 * k - 1, 2 * k) for k in range(1, chips)]
    skip_next = [(2 * k - 1, 2 * k + 1) for k in range(1, chips)]
    both_next = to_next + [(b, a) for a, b in to_next]
    both_skip = skip_next + [(2 * k, 2 * k - 2) for k in range(1, chips)]

    parts = [
        lax.ppermute(piece, "chan", [(i, (i + 2 * d) % groups_chan) for i in range(groups_chan)])
        for d in range(1, groups_chan // 2)
    ]
    other = lax.ppermute(away, "tm", swap)
    piece = piece + sum(parts[1:], parts[0])
    arrived = lax.ppermute(piece, "chan", [(i, i ^ 1) for i in range(groups_chan)])
    low_edge = lax.ppermute(low_edge, "tm", to_next)
    high_edge = lax.ppermute(high_edge, "tm", skip_next)
    piece, end = join_sources(piece, arrived)
    piece_other = lax.ppermute(piece, "tm", swap)
    edge = lax.ppermute(end, "tm", both_next)
    cross = lax.ppermute(end, "tm", both_skip)
    filtered, power = filter_rows(window_offsets, taps, x4, other, low_edge, high_edge)
    piece_other, edge, cross, power = lax.optimization_barrier((piece_other, edge, cross, power))
    traces, energy = filter_sources(
        window_offsets, taps, piece, piece_other, edge, cross, power, chips
    )
    same = [[2 * k + c for k in range(chips)] for c in range(2)]
    energies = lax.all_to_all(energy, "tm", 0, 0, tiled=True, axis_index_groups=same)

    column = tiles // 4
    dots = LAGS // (2 * SHIFTS)
    first, second = range(dots // 2), range(dots // 2, dots)
    keep_a, send_a, white, table = correlate_first(
        energies, traces, filtered, first, column, total_samples
    )
    line = [(i, i ^ 2) for i in range(tiles)]

    def over_column(keep, across):
        own, *sends = add_line(keep, across)
        far_first = sorted(range(1, column), key=lambda d: -min(d, column - d))
        arrived = [
            lax.ppermute(sends[d - 1], "tm", [(i, (i + 4 * d) % tiles) for i in range(tiles)])
            for d in far_first
        ]
        return [own] + arrived

    across_a = lax.ppermute(send_a, "tm", line)
    keep_b, send_b = correlate_next(white, table, second, column)
    across_b = lax.ppermute(send_b, "tm", line)
    halves = [over_column(keep_a, across_a), over_column(keep_b, across_b)]
    total = finish(halves, 1.0 / math.sqrt(total_samples))
    return total.reshape(sub, NSRC, SB, LAGS)


def solution(mesh):
    return jax.shard_map(
        shards,
        mesh=mesh,
        in_specs=(P("chan", "tm"), P(), P(), P()),
        out_specs=P(("chan", "tm"), None, None, None),
        check_vma=False,
    )
```

time: 99.1 us -> 170 us (1.72)
  Pallas kernels: 19.3 us -> 86.3 us
  waiting for transfers between devices: 29.9 us -> 9.56 us
  starting transfers between devices: 32.4 us -> 52.2 us
  blocking collectives: 0 us -> 17.6 us
  local copies, waits for them, and re-layouts: 14.4 us -> 2.9 us
    pallas_call x2 -> x5, Pallas kernels: 5.24 us -> 67.1 us  [the longest x1 66.3 us: pick_sources(): call(kernel, 'pick_sources', [shape((NS, samples), jnp.bfloat16), edge, e...]
    ppermute x2 -> x18, starting transfers between devices: 4.84 us -> 41.8 us  [the longest x14 31.1 us: over_column(): lax.ppermute(sends[d - 1], 'tm', [(i, (i + 4 * d) % tiles) for i in range...]
    all_to_all x3 -> x0, waiting for transfers between devices: 23 us -> none  [the longest x2 19.5 us: over_column(): lax.all_to_all(summed, 'tm', 0, 0, tiled=True, axis_index_groups=column)]
    all_to_all x3 -> x0, starting transfers between devices: 18.8 us -> none  [the longest x1 10.6 us: shards(): lax.all_to_all(energy, 'tm', 0, 0, tiled=True, axis_index_groups=same)]
    all_to_all x0 -> x1, blocking collectives: none -> 17.6 us  [shards(): lax.all_to_all(energy, 'tm', 0, 0, tiled=True, axis_index_groups=same)]
    unnamed x18 -> x6, local copies, waits for them, and re-layouts: 10.9 us -> 2.19 us
    ppermute x3, waiting for transfers between devices: 0.02 us -> 5.58 us  [shards(): lax.ppermute(piece, 'chan', [(i, (i + 2 * d) % groups_chan) for i in rang...]
    pallas_call x1, Pallas kernels: 4.84 us -> 8.13 us  [correlate_first(): call(kernel, 'correlate_first', [shape((half_groups, sub, cols), jnp.floa...]
  transfers between devices with their start and end apart: 13 -> 26, of which waited for: 8 -> 6; matrix products, arithmetic and copies ran while one was open for 2% -> 1% of each run, Pallas kernels for 10% -> 6%
where the time goes in v3:
time: 170 us
  Pallas kernels  86.3 us (51%)
  starting transfers between devices  52.2 us (31%)
  blocking collectives  17.6 us (10%)
  waiting for transfers between devices  9.56 us (6%)
  local copies, waits for them, and re-layouts  2.9 us (2%)
    pallas_call x1, Pallas kernels, pick_sources(): call(kernel, 'pick_sources', [shape((NS, samples), jnp.bfloat16), edge, e...  66.3 us
    ppermute x14, starting transfers between devices, over_column(): lax.ppermute(sends[d - 1], 'tm', [(i, (i + 4 * d) % tiles) for i in range...  31.1 us
    all_to_all x1, blocking collectives, shards(): lax.all_to_all(energy, 'tm', 0, 0, tiled=True, axis_index_groups=same)  17.6 us
    pallas_call x1, Pallas kernels, correlate_first(): call(kernel, 'correlate_first', [shape((half_groups, sub, cols), jnp.floa...  8.13 us
    ppermute x1, starting transfers between devices, shards(): edge = lax.ppermute(end, 'tm', both_next)  6.41 us
    pallas_call x1, Pallas kernels, filter_rows(): call(kernel, 'filter_rows', [shape((rows, 2 * half), jnp.float32), shape(...  5.58 us
    ppermute x3, waiting for transfers between devices, shards(): lax.ppermute(piece, 'chan', [(i, (i + 2 * d) % groups_chan) for i in rang...  5.58 us
    ppermute x3, starting transfers between devices, shards(): lax.ppermute(piece, 'chan', [(i, (i + 2 * d) % groups_chan) for i in rang...  4.52 us
  transfers between devices with their start and end apart: 26, of which 6 were waited for; matrix products, arithmetic and copies ran while one was open for 1% of the time, Pallas kernels for 6%

profile of v3, /device:TPU:8, one launch (start us, length us, event | category | flops | bytes accessed | tf_op | source)
XLA Modules:
  0.0 169.6 jit_solution(5268730880884236572)
XLA Ops:
  0.0 66.3 %pick_sources.1 = (bf16[8,4096]{1,0:T(8,128)(2,1)}, bf16[16,16,128]{2,1,0:T(8,128)(2,1)}, bf16[16,16,128]{2,1,0:T(8,128)(2,1)}, bf16[16,16,4096]{2,1,0:T(8,128)(2,1)}) custom-call(s32[2,4]{1,0:T(2,128)} %ids_ref.1, bf16[16,2,16,4096]{3,2,1,0:T(8,128)(2,1)} %bitcast.1), custom_call_target="tpu_custom_call" | custom-call | bytes 4194304 | tf_op jit(solution)/shard_map/pick_sources/pallas_call | solution.py:91
  66.4 0.1 collective-permute-start.7
  66.5 2.8 %collective-permute-start.2 = (bf16[8,4096]{1,0:T(8,128)(2,1)}, bf16[8,4096]{1,0:T(8,128)(2,1)S(1)}, u32[]{:S(2)}, u32[]{:S(2)}) collective-permute-start(bf16[8,4096]{1,0:T(8,128)(2,1)} %get-tuple-element.41), channel_id=1, source_target_pairs={{0,192},{32,224},{64,0},{96,32},{128,64},{160,96},{192,128},{224,1... | collective-permute-start | bytes 196616 | tf_op jit(solution)/shard_map/ppermute | solution.py:438
  69.3 0.8 collective-permute-start.1
  70.1 0.9 collective-permute-start
  71.0 2.0 %collective-permute-done.2 = bf16[8,4096]{1,0:T(8,128)(2,1)S(1)} collective-permute-done((bf16[8,4096]{1,0:T(8,128)(2,1)}, bf16[8,4096]{1,0:T(8,128)(2,1)S(1)}, u32[]{:S(2)}, u32[]{:S(2)}) %collective-permute-start.2) | collective-permute-done | bytes 65568 | tf_op jit(solution)/shard_map/ppermute | solution.py:438
  73.0 2.9 %collective-permute-done.1 = bf16[8,4096]{1,0:T(8,128)(2,1)S(1)} collective-permute-done((bf16[8,4096]{1,0:T(8,128)(2,1)}, bf16[8,4096]{1,0:T(8,128)(2,1)S(1)}, u32[]{:S(2)}, u32[]{:S(2)}) %collective-permute-start.1) | collective-permute-done | bytes 65568 | tf_op jit(solution)/shard_map/ppermute | solution.py:438
  75.9 0.7 collective-permute-done
  76.6 0.9 add_add_fusion.piece_ref
  77.4 2.4 %collective-permute-start.3 = (bf16[8,4096]{1,0:T(8,128)(2,1)S(1)}, bf16[8,4096]{1,0:T(8,128)(2,1)S(1)}, u32[]{:S(2)}, u32[]{:S(2)}) collective-permute-start(bf16[8,4096]{1,0:T(8,128)(2,1)S(1)} %add_add_fusion.piece_ref), channel_id=1, source_target_pairs={{0,32},{32,0},{64,96},{96,64},{128,160},{160,128},{192,224},{224,1... | collective-permute-start | bytes 196616 | tf_op jit(solution)/shard_map/ppermute | solution.py:443
  79.8 1.3 collective-permute-start.8
  81.1 0.7 collective-permute-start.9
  81.8 1.5 collective-permute-done.3.arrived_ref
  83.3 2.4 %collective-permute-start.6 = (bf16[8,256]{1,0:T(8,128)(2,1)S(1)}, bf16[8,256]{1,0:T(8,128)(2,1)S(1)}, u32[]{:S(2)}, u32[]{:S(2)}) collective-permute-start(bf16[8,256]{1,0:T(8,128)(2,1)S(1)} %get-tuple-element.43), channel_id=1, source_target_pairs={{1,3},{3,5},{5,7},{7,9},{9,11},{11,13},{13,15},{15,17},{17,19},{19... | collective-permute-start | bytes 12296 | tf_op jit(solution)/shard_map/ppermute | solution.py:449
  85.7 6.4 %collective-permute-start.5 = (bf16[8,256]{1,0:T(8,128)(2,1)S(1)}, bf16[8,256]{1,0:T(8,128)(2,1)S(1)}, u32[]{:S(2)}, u32[]{:S(2)}) collective-permute-start(bf16[8,256]{1,0:T(8,128)(2,1)S(1)} %get-tuple-element.43), channel_id=1, source_target_pairs={{1,2},{3,4},{5,6},{7,8},{9,10},{11,12},{13,14},{15,16},{17,18},{19... | collective-permute-start | bytes 12296 | tf_op jit(solution)/shard_map/ppermute | solution.py:448
  92.1 0.0 collective-permute-done.8.low_ref
  92.1 1.2 collective-permute-start.4
  93.3 0.0 collective-permute-done.9.high_ref
  93.3 0.0 copy-start
  93.3 2.2 %copy-done = bf16[512,4096]{1,0:T(8,128)(2,1)S(1)} copy-done((bf16[512,4096]{1,0:T(8,128)(2,1)S(1)}, bf16[512,4096]{1,0:T(8,128)(2,1)}, u32[]{:S(2)}) %copy-start) | copy-done | bytes 4194328
  95.5 5.6 %filter_rows.1 = (f32[256,8192]{1,0:T(8,128)}, f32[256,128]{1,0:T(8,128)S(1)}) custom-call(s32[16]{0:T(128)S(1)} %copy-done.1, bf16[1,256]{1,0:T(2,128)(2,1)S(1)} %reshape.9.taps_ref, bf16[16,2,16,4096]{3,2,1,0:T(8,128)(2,1)S(1)} %bitcast.2, bf16[16,16,4096]{2,1,0:T(8,128)(2,1)S(1)} %collective-permute-done.7.other_ref, ...), custom_call_target="tpu_custom_call" | custom-call | flops 2147483648 | bytes 12582912 | tf_op jit(solution)/shard_map/filter_rows/pallas_call | solution.py:189
  101.1 0.0 collective-permute-done.5.edge_ref
  101.1 0.0 collective-permute-done.4.other_ref
  101.1 1.0 filter_sources.1
  102.1 17.6 %all_to_all.5.energy_ref = f32[16,8,128]{2,1,0:T(8,128)S(1)} all-to-all(f32[16,8,128]{2,1,0:T(8,128)S(1)} %get-tuple-element.52), channel_id=1, replica_groups={{0,2,4,6,8,10,12,14,16,18,20,22,24,26,28,30},{1,3,5,7,9,11,13,15,17,19,..., dimensions={0} | all-to-all | bytes 131072 | tf_op jit(solution)/shard_map/all_to_all | solution.py:456
  119.7 8.1 %correlate_first.1 = (f32[8,16,1024]{2,1,0:T(8,128)S(1)}, bf16[8,16,1024]{2,1,0:T(8,128)(2,1)S(1)}, bf16[256,8192]{1,0:T(8,128)(2,1)S(1)}, bf16[8448,128]{1,0:T(8,128)(2,1)S(1)}) custom-call(f32[16,8,128]{2,1,0:T(8,128)S(1)} %all_to_all.5.energy_ref, f32[8,8448]{1,0:T(8,128)S(1)} %get-tuple-element.53.traces_ref, f32[256,8192]{1,0:T(8,128)} %get-tuple-element.54.rows_ref), custom_call_target="tpu_custom_call" | custom-call | flops 4294967296 | bytes 16777216 | tf_op jit(solution)/shard_map/correlate_first/pallas_call | solution.py:321
  127.8 1.5 collective-permute-start.10
  129.3 4.5 %correlate_next.1 = (f32[8,16,1024]{2,1,0:T(8,128)S(1)}, bf16[8,16,1024]{2,1,0:T(8,128)(2,1)S(1)}) custom-call(bf16[256,8192]{1,0:T(8,128)(2,1)S(1)} %get-tuple-element.65.white_ref, bf16[8448,128]{1,0:T(8,128)(2,1)S(1)} %get-tuple-element.66.table_ref), custom_call_target="tpu_custom_call" | custom-call | flops 4294967296 | bytes 8388608 | tf_op jit(solution)/shard_map/correlate_next/pallas_call | solution.py:350
  133.7 0.7 collective-permute-start.18
  134.5 0.6 collective-permute-done.10.across_ref
  135.1 0.1 add_line.2
  135.1 1.1 collective-permute-start.11
  136.2 3.1 %collective-permute-start.12 = (bf16[16,1024]{1,0:T(8,128)(2,1)S(1)}, bf16[16,1024]{1,0:T(8,128)(2,1)S(1)}, u32[]{:S(2)}, u32[]{:S(2)}) collective-permute-start(bf16[16,1024]{1,0:T(8,128)(2,1)S(1)} %get-tuple-element.59), channel_id=1, source_target_pairs={{0,12},{1,13},{2,14},{3,15},{4,16},{5,17},{6,18},{7,19},{8,20},{9,... | collective-permute-start | bytes 98312 | tf_op jit(solution)/shard_map/ppermute | solution.py:470
  139.3 2.0 %collective-permute-start.13 = (bf16[16,1024]{1,0:T(8,128)(2,1)S(1)}, bf16[16,1024]{1,0:T(8,128)(2,1)S(1)}, u32[]{:S(2)}, u32[]{:S(2)}) collective-permute-start(bf16[16,1024]{1,0:T(8,128)(2,1)S(1)} %get-tuple-element.60), channel_id=1, source_target_pairs={{0,20},{1,21},{2,22},{3,23},{4,24},{5,25},{6,26},{7,27},{8,28},{9,... | collective-permute-start | bytes 98312 | tf_op jit(solution)/shard_map/ppermute | solution.py:470
  141.2 2.1 %collective-permute-start.14 = (bf16[16,1024]{1,0:T(8,128)(2,1)S(1)}, bf16[16,1024]{1,0:T(8,128)(2,1)S(1)}, u32[]{:S(2)}, u32[]{:S(2)}) collective-permute-start(bf16[16,1024]{1,0:T(8,128)(2,1)S(1)} %get-tuple-element.61), channel_id=1, source_target_pairs={{0,8},{1,9},{2,10},{3,11},{4,12},{5,13},{6,14},{7,15},{8,16},{9,17... | collective-permute-start | bytes 98312 | tf_op jit(solution)/shard_map/ppermute | solution.py:470
  143.3 0.0 collective-permute-done.18.across_ref
  143.3 2.1 %collective-permute-start.15 = (bf16[16,1024]{1,0:T(8,128)(2,1)S(1)}, bf16[16,1024]{1,0:T(8,128)(2,1)S(1)}, u32[]{:S(2)}, u32[]{:S(2)}) collective-permute-start(bf16[16,1024]{1,0:T(8,128)(2,1)S(1)} %get-tuple-element.62), channel_id=1, source_target_pairs={{0,24},{1,25},{2,26},{3,27},{4,28},{5,29},{6,30},{7,31},{8,0},{9,1... | collective-permute-start | bytes 98312 | tf_op jit(solution)/shard_map/ppermute | solution.py:470
  145.4 0.0 collective-permute-done.11.refs_1_
  145.4 1.8 %collective-permute-start.16 = (bf16[16,1024]{1,0:T(8,128)(2,1)S(1)}, bf16[16,1024]{1,0:T(8,128)(2,1)S(1)}, u32[]{:S(2)}, u32[]{:S(2)}) collective-permute-start(bf16[16,1024]{1,0:T(8,128)(2,1)S(1)} %get-tuple-element.63), channel_id=1, source_target_pairs={{0,4},{1,5},{2,6},{3,7},{4,8},{5,9},{6,10},{7,11},{8,12},{9,13},{1... | collective-permute-start | bytes 98312 | tf_op jit(solution)/shard_map/ppermute | solution.py:470
  147.2 1.8 %collective-permute-start.17 = (bf16[16,1024]{1,0:T(8,128)(2,1)S(1)}, bf16[16,1024]{1,0:T(8,128)(2,1)S(1)}, u32[]{:S(2)}, u32[]{:S(2)}) collective-permute-start(bf16[16,1024]{1,0:T(8,128)(2,1)S(1)} %get-tuple-element.64), channel_id=1, source_target_pairs={{0,28},{1,29},{2,30},{3,31},{4,0},{5,1},{6,2},{7,3},{8,4},{9,5},{1... | collective-permute-start | bytes 98312 | tf_op jit(solution)/shard_map/ppermute | solution.py:470
  149.0 0.0 collective-permute-done.13.refs_3_
  149.0 4.9 %collective-permute-start.19 = (bf16[16,1024]{1,0:T(8,128)(2,1)S(1)}, bf16[16,1024]{1,0:T(8,128)(2,1)S(1)}, u32[]{:S(2)}, u32[]{:S(2)}) collective-permute-start(bf16[16,1024]{1,0:T(8,128)(2,1)S(1)} %get-tuple-element.70), channel_id=1, source_target_pairs={{0,16},{1,17},{2,18},{3,19},{4,20},{5,21},{6,22},{7,23},{8,24},{9,... | collective-permute-start | bytes 98312 | tf_op jit(solution)/shard_map/ppermute | solution.py:470
  153.9 5.0 %collective-permute-start.21 = (bf16[16,1024]{1,0:T(8,128)(2,1)S(1)}, bf16[16,1024]{1,0:T(8,128)(2,1)S(1)}, u32[]{:S(2)}, u32[]{:S(2)}) collective-permute-start(bf16[16,1024]{1,0:T(8,128)(2,1)S(1)} %get-tuple-element.72), channel_id=1, source_target_pairs={{0,20},{1,21},{2,22},{3,23},{4,24},{5,25},{6,26},{7,27},{8,28},{9,... | collective-permute-start | bytes 98312 | tf_op jit(solution)/shard_map/ppermute | solution.py:470
  159.0 4.1 %collective-permute-start.23 = (bf16[16,1024]{1,0:T(8,128)(2,1)S(1)}, bf16[16,1024]{1,0:T(8,128)(2,1)S(1)}, u32[]{:S(2)}, u32[]{:S(2)}) collective-permute-start(bf16[16,1024]{1,0:T(8,128)(2,1)S(1)} %get-tuple-element.74), channel_id=1, source_target_pairs={{0,24},{1,25},{2,26},{3,27},{4,28},{5,29},{6,30},{7,31},{8,0},{9,1... | collective-permute-start | bytes 98312 | tf_op jit(solution)/shard_map/ppermute | solution.py:470
  163.1 3.2 %collective-permute-start.25 = (bf16[16,1024]{1,0:T(8,128)(2,1)S(1)}, bf16[16,1024]{1,0:T(8,128)(2,1)S(1)}, u32[]{:S(2)}, u32[]{:S(2)}) collective-permute-start(bf16[16,1024]{1,0:T(8,128)(2,1)S(1)} %get-tuple-element.76), channel_id=1, source_target_pairs={{0,28},{1,29},{2,30},{3,31},{4,0},{5,1},{6,2},{7,3},{8,4},{9,5},{1... | collective-permute-start | bytes 98312 | tf_op jit(solution)/shard_map/ppermute | solution.py:470
  166.4 1.9 %collective-permute-done.24.refs_14_ = bf16[16,1024]{1,0:T(8,128)(2,1)S(1)} collective-permute-done((bf16[16,1024]{1,0:T(8,128)(2,1)S(1)}, bf16[16,1024]{1,0:T(8,128)(2,1)S(1)}, u32[]{:S(2)}, u32[]{:S(2)}) %collective-permute-start.24) | collective-permute-done | bytes 32800 | tf_op jit(solution)/shard_map/ppermute | solution.py:470
  168.2 0.7 finish.1
  168.9 0.7 reshape.11
  (24 shorter events, 0.1 us)
Async XLA Ops:
  0.0 81.8 %copy-start.2 = (bf16[64]{0:T(256)(128)(2,1)S(1)}, bf16[64]{0:T(256)(128)(2,1)}, u32[]{:S(2)}) copy-start(bf16[64]{0:T(256)(128)(2,1)} %param.5) | copy-start | bytes 388
  0.0 93.3 %copy-start.1 = (s32[16]{0:T(128)S(1)}, s32[16]{0:T(128)}, u32[]{:S(2)}) copy-start(s32[16]{0:T(128)} %off_ref.3) | copy-start | bytes 196
  66.4 26.9 %collective-permute-start.7 = (bf16[16,16,4096]{2,1,0:T(8,128)(2,1)}, bf16[16,16,4096]{2,1,0:T(8,128)(2,1)S(1)}, u32[]{:S(2)}, u32[]{:S(2)}) collective-permute-start(bf16[16,16,4096]{2,1,0:T(8,128)(2,1)} %get-tuple-element.44), channel_id=1, source_target_pairs={{0,1},{1,0},{2,3},{3,2},{4,5},{5,4},{6,7},{7,6},{8,9},{9,8},{10,11... | collective-permute-start | bytes 6291464 | tf_op jit(solution)/shard_map/ppermute | solution.py:441
  66.5 6.5 %collective-permute-start.2 = (bf16[8,4096]{1,0:T(8,128)(2,1)}, bf16[8,4096]{1,0:T(8,128)(2,1)S(1)}, u32[]{:S(2)}, u32[]{:S(2)}) collective-permute-start(bf16[8,4096]{1,0:T(8,128)(2,1)} %get-tuple-element.41), channel_id=1, source_target_pairs={{0,192},{32,224},{64,0},{96,32},{128,64},{160,96},{192,128},{224,1... | collective-permute-start | bytes 196616 | tf_op jit(solution)/shard_map/ppermute | solution.py:438
  69.3 6.6 %collective-permute-start.1 = (bf16[8,4096]{1,0:T(8,128)(2,1)}, bf16[8,4096]{1,0:T(8,128)(2,1)S(1)}, u32[]{:S(2)}, u32[]{:S(2)}) collective-permute-start(bf16[8,4096]{1,0:T(8,128)(2,1)} %get-tuple-element.41), channel_id=1, source_target_pairs={{0,128},{32,160},{64,192},{96,224},{128,0},{160,32},{192,64},{224,... | collective-permute-start | bytes 196616 | tf_op jit(solution)/shard_map/ppermute | solution.py:438
  70.1 6.5 %collective-permute-start = (bf16[8,4096]{1,0:T(8,128)(2,1)}, bf16[8,4096]{1,0:T(8,128)(2,1)S(1)}, u32[]{:S(2)}, u32[]{:S(2)}) collective-permute-start(bf16[8,4096]{1,0:T(8,128)(2,1)} %get-tuple-element.41), channel_id=1, source_target_pairs={{0,64},{32,96},{64,128},{96,160},{128,192},{160,224},{192,0},{224,... | collective-permute-start | bytes 196616 | tf_op jit(solution)/shard_map/ppermute | solution.py:438
  77.4 5.9 %collective-permute-start.3 = (bf16[8,4096]{1,0:T(8,128)(2,1)S(1)}, bf16[8,4096]{1,0:T(8,128)(2,1)S(1)}, u32[]{:S(2)}, u32[]{:S(2)}) collective-permute-start(bf16[8,4096]{1,0:T(8,128)(2,1)S(1)} %add_add_fusion.piece_ref), channel_id=1, source_target_pairs={{0,32},{32,0},{64,96},{96,64},{128,160},{160,128},{192,224},{224,1... | collective-permute-start | bytes 196616 | tf_op jit(solution)/shard_map/ppermute | solution.py:443
  79.8 12.3 %collective-permute-start.8 = (bf16[16,16,128]{2,1,0:T(8,128)(2,1)}, bf16[16,16,128]{2,1,0:T(8,128)(2,1)S(1)}, u32[]{:S(2)}, u32[]{:S(2)}) collective-permute-start(bf16[16,16,128]{2,1,0:T(8,128)(2,1)} %get-tuple-element.45), channel_id=1, source_target_pairs={{1,2},{3,4},{5,6},{7,8},{9,10},{11,12},{13,14},{15,16},{17,18},{19... | collective-permute-start | bytes 196616 | tf_op jit(solution)/shard_map/ppermute | solution.py:444
  81.1 12.2 %collective-permute-start.9 = (bf16[16,16,128]{2,1,0:T(8,128)(2,1)}, bf16[16,16,128]{2,1,0:T(8,128)(2,1)S(1)}, u32[]{:S(2)}, u32[]{:S(2)}) collective-permute-start(bf16[16,16,128]{2,1,0:T(8,128)(2,1)} %get-tuple-element.46), channel_id=1, source_target_pairs={{1,3},{3,5},{5,7},{7,9},{9,11},{11,13},{13,15},{15,17},{17,19},{19... | collective-permute-start | bytes 196616 | tf_op jit(solution)/shard_map/ppermute | solution.py:445
  83.3 17.8 %collective-permute-start.6 = (bf16[8,256]{1,0:T(8,128)(2,1)S(1)}, bf16[8,256]{1,0:T(8,128)(2,1)S(1)}, u32[]{:S(2)}, u32[]{:S(2)}) collective-permute-start(bf16[8,256]{1,0:T(8,128)(2,1)S(1)} %get-tuple-element.43), channel_id=1, source_target_pairs={{1,3},{3,5},{5,7},{7,9},{9,11},{11,13},{13,15},{15,17},{17,19},{19... | collective-permute-start | bytes 12296 | tf_op jit(solution)/shard_map/ppermute | solution.py:449
  85.7 15.4 %collective-permute-start.5 = (bf16[8,256]{1,0:T(8,128)(2,1)S(1)}, bf16[8,256]{1,0:T(8,128)(2,1)S(1)}, u32[]{:S(2)}, u32[]{:S(2)}) collective-permute-start(bf16[8,256]{1,0:T(8,128)(2,1)S(1)} %get-tuple-element.43), channel_id=1, source_target_pairs={{1,2},{3,4},{5,6},{7,8},{9,10},{11,12},{13,14},{15,16},{17,18},{19... | collective-permute-start | bytes 12296 | tf_op jit(solution)/shard_map/ppermute | solution.py:448
  92.1 9.0 %collective-permute-start.4 = (bf16[8,4096]{1,0:T(8,128)(2,1)S(1)}, bf16[8,4096]{1,0:T(8,128)(2,1)S(1)}, u32[]{:S(2)}, u32[]{:S(2)}) collective-permute-start(bf16[8,4096]{1,0:T(8,128)(2,1)S(1)} %get-tuple-element.42.mine_ref), channel_id=1, source_target_pairs={{0,1},{1,0},{2,3},{3,2},{4,5},{5,4},{6,7},{7,6},{8,9},{9,8},{10,11... | collective-permute-start | bytes 196616 | tf_op jit(solution)/shard_map/ppermute | solution.py:447
  93.3 2.2 %copy-start = (bf16[512,4096]{1,0:T(8,128)(2,1)S(1)}, bf16[512,4096]{1,0:T(8,128)(2,1)}, u32[]{:S(2)}) copy-start(bf16[512,4096]{1,0:T(8,128)(2,1)} %param.4) | copy-start | bytes 12582916
  127.8 7.3 %collective-permute-start.10 = (bf16[8,16,1024]{2,1,0:T(8,128)(2,1)S(1)}, bf16[8,16,1024]{2,1,0:T(8,128)(2,1)S(1)}, u32[]{:S(2)}, u32[]{:S(2)}) collective-permute-start(bf16[8,16,1024]{2,1,0:T(8,128)(2,1)S(1)} %get-tuple-element.56), channel_id=1, source_target_pairs={{0,2},{1,3},{2,0},{3,1},{4,6},{5,7},{6,4},{7,5},{8,10},{9,11},{10,... | collective-permute-start | bytes 786440 | tf_op jit(solution)/shard_map/ppermute | solution.py:475
  133.7 9.6 %collective-permute-start.18 = (bf16[8,16,1024]{2,1,0:T(8,128)(2,1)S(1)}, bf16[8,16,1024]{2,1,0:T(8,128)(2,1)S(1)}, u32[]{:S(2)}, u32[]{:S(2)}) collective-permute-start(bf16[8,16,1024]{2,1,0:T(8,128)(2,1)S(1)} %get-tuple-element.68), channel_id=1, source_target_pairs={{0,2},{1,3},{2,0},{3,1},{4,6},{5,7},{6,4},{7,5},{8,10},{9,11},{10,... | collective-permute-start | bytes 786440 | tf_op jit(solution)/shard_map/ppermute | solution.py:477
  135.1 10.3 %collective-permute-start.11 = (bf16[16,1024]{1,0:T(8,128)(2,1)S(1)}, bf16[16,1024]{1,0:T(8,128)(2,1)S(1)}, u32[]{:S(2)}, u32[]{:S(2)}) collective-permute-start(bf16[16,1024]{1,0:T(8,128)(2,1)S(1)} %get-tuple-element.58), channel_id=1, source_target_pairs={{0,16},{1,17},{2,18},{3,19},{4,20},{5,21},{6,22},{7,23},{8,24},{9,... | collective-permute-start | bytes 98312 | tf_op jit(solution)/shard_map/ppermute | solution.py:470
  136.2 11.0 %collective-permute-start.12 = (bf16[16,1024]{1,0:T(8,128)(2,1)S(1)}, bf16[16,1024]{1,0:T(8,128)(2,1)S(1)}, u32[]{:S(2)}, u32[]{:S(2)}) collective-permute-start(bf16[16,1024]{1,0:T(8,128)(2,1)S(1)} %get-tuple-element.59), channel_id=1, source_target_pairs={{0,12},{1,13},{2,14},{3,15},{4,16},{5,17},{6,18},{7,19},{8,20},{9,... | collective-permute-start | bytes 98312 | tf_op jit(solution)/shard_map/ppermute | solution.py:470
  139.3 9.7 %collective-permute-start.13 = (bf16[16,1024]{1,0:T(8,128)(2,1)S(1)}, bf16[16,1024]{1,0:T(8,128)(2,1)S(1)}, u32[]{:S(2)}, u32[]{:S(2)}) collective-permute-start(bf16[16,1024]{1,0:T(8,128)(2,1)S(1)} %get-tuple-element.60), channel_id=1, source_target_pairs={{0,20},{1,21},{2,22},{3,23},{4,24},{5,25},{6,26},{7,27},{8,28},{9,... | collective-permute-start | bytes 98312 | tf_op jit(solution)/shard_map/ppermute | solution.py:470
  141.2 12.7 %collective-permute-start.14 = (bf16[16,1024]{1,0:T(8,128)(2,1)S(1)}, bf16[16,1024]{1,0:T(8,128)(2,1)S(1)}, u32[]{:S(2)}, u32[]{:S(2)}) collective-permute-start(bf16[16,1024]{1,0:T(8,128)(2,1)S(1)} %get-tuple-element.61), channel_id=1, source_target_pairs={{0,8},{1,9},{2,10},{3,11},{4,12},{5,13},{6,14},{7,15},{8,16},{9,17... | collective-permute-start | bytes 98312 | tf_op jit(solution)/shard_map/ppermute | solution.py:470
  143.3 10.6 %collective-permute-start.15 = (bf16[16,1024]{1,0:T(8,128)(2,1)S(1)}, bf16[16,1024]{1,0:T(8,128)(2,1)S(1)}, u32[]{:S(2)}, u32[]{:S(2)}) collective-permute-start(bf16[16,1024]{1,0:T(8,128)(2,1)S(1)} %get-tuple-element.62), channel_id=1, source_target_pairs={{0,24},{1,25},{2,26},{3,27},{4,28},{5,29},{6,30},{7,31},{8,0},{9,1... | collective-permute-start | bytes 98312 | tf_op jit(solution)/shard_map/ppermute | solution.py:470
  145.4 13.5 %collective-permute-start.16 = (bf16[16,1024]{1,0:T(8,128)(2,1)S(1)}, bf16[16,1024]{1,0:T(8,128)(2,1)S(1)}, u32[]{:S(2)}, u32[]{:S(2)}) collective-permute-start(bf16[16,1024]{1,0:T(8,128)(2,1)S(1)} %get-tuple-element.63), channel_id=1, source_target_pairs={{0,4},{1,5},{2,6},{3,7},{4,8},{5,9},{6,10},{7,11},{8,12},{9,13},{1... | collective-permute-start | bytes 98312 | tf_op jit(solution)/shard_map/ppermute | solution.py:470
  147.2 11.8 %collective-permute-start.17 = (bf16[16,1024]{1,0:T(8,128)(2,1)S(1)}, bf16[16,1024]{1,0:T(8,128)(2,1)S(1)}, u32[]{:S(2)}, u32[]{:S(2)}) collective-permute-start(bf16[16,1024]{1,0:T(8,128)(2,1)S(1)} %get-tuple-element.64), channel_id=1, source_target_pairs={{0,28},{1,29},{2,30},{3,31},{4,0},{5,1},{6,2},{7,3},{8,4},{9,5},{1... | collective-permute-start | bytes 98312 | tf_op jit(solution)/shard_map/ppermute | solution.py:470
  149.0 14.1 %collective-permute-start.19 = (bf16[16,1024]{1,0:T(8,128)(2,1)S(1)}, bf16[16,1024]{1,0:T(8,128)(2,1)S(1)}, u32[]{:S(2)}, u32[]{:S(2)}) collective-permute-start(bf16[16,1024]{1,0:T(8,128)(2,1)S(1)} %get-tuple-element.70), channel_id=1, source_target_pairs={{0,16},{1,17},{2,18},{3,19},{4,20},{5,21},{6,22},{7,23},{8,24},{9,... | collective-permute-start | bytes 98312 | tf_op jit(solution)/shard_map/ppermute | solution.py:470
  153.9 9.2 %collective-permute-start.20 = (bf16[16,1024]{1,0:T(8,128)(2,1)S(1)}, bf16[16,1024]{1,0:T(8,128)(2,1)S(1)}, u32[]{:S(2)}, u32[]{:S(2)}) collective-permute-start(bf16[16,1024]{1,0:T(8,128)(2,1)S(1)} %get-tuple-element.71), channel_id=1, source_target_pairs={{0,12},{1,13},{2,14},{3,15},{4,16},{5,17},{6,18},{7,19},{8,20},{9,... | collective-permute-start | bytes 98312 | tf_op jit(solution)/shard_map/ppermute | solution.py:470
  153.9 12.4 %collective-permute-start.21 = (bf16[16,1024]{1,0:T(8,128)(2,1)S(1)}, bf16[16,1024]{1,0:T(8,128)(2,1)S(1)}, u32[]{:S(2)}, u32[]{:S(2)}) collective-permute-start(bf16[16,1024]{1,0:T(8,128)(2,1)S(1)} %get-tuple-element.72), channel_id=1, source_target_pairs={{0,20},{1,21},{2,22},{3,23},{4,24},{5,25},{6,26},{7,27},{8,28},{9,... | collective-permute-start | bytes 98312 | tf_op jit(solution)/shard_map/ppermute | solution.py:470
  159.0 7.4 %collective-permute-start.22 = (bf16[16,1024]{1,0:T(8,128)(2,1)S(1)}, bf16[16,1024]{1,0:T(8,128)(2,1)S(1)}, u32[]{:S(2)}, u32[]{:S(2)}) collective-permute-start(bf16[16,1024]{1,0:T(8,128)(2,1)S(1)} %get-tuple-element.73), channel_id=1, source_target_pairs={{0,8},{1,9},{2,10},{3,11},{4,12},{5,13},{6,14},{7,15},{8,16},{9,17... | collective-permute-start | bytes 98312 | tf_op jit(solution)/shard_map/ppermute | solution.py:470
  159.0 7.4 %collective-permute-start.23 = (bf16[16,1024]{1,0:T(8,128)(2,1)S(1)}, bf16[16,1024]{1,0:T(8,128)(2,1)S(1)}, u32[]{:S(2)}, u32[]{:S(2)}) collective-permute-start(bf16[16,1024]{1,0:T(8,128)(2,1)S(1)} %get-tuple-element.74), channel_id=1, source_target_pairs={{0,24},{1,25},{2,26},{3,27},{4,28},{5,29},{6,30},{7,31},{8,0},{9,1... | collective-permute-start | bytes 98312 | tf_op jit(solution)/shard_map/ppermute | solution.py:470
  163.1 5.1 %collective-permute-start.24 = (bf16[16,1024]{1,0:T(8,128)(2,1)S(1)}, bf16[16,1024]{1,0:T(8,128)(2,1)S(1)}, u32[]{:S(2)}, u32[]{:S(2)}) collective-permute-start(bf16[16,1024]{1,0:T(8,128)(2,1)S(1)} %get-tuple-element.75), channel_id=1, source_target_pairs={{0,4},{1,5},{2,6},{3,7},{4,8},{5,9},{6,10},{7,11},{8,12},{9,13},{1... | collective-permute-start | bytes 98312 | tf_op jit(solution)/shard_map/ppermute | solution.py:470
  163.1 5.1 %collective-permute-start.25 = (bf16[16,1024]{1,0:T(8,128)(2,1)S(1)}, bf16[16,1024]{1,0:T(8,128)(2,1)S(1)}, u32[]{:S(2)}, u32[]{:S(2)}) collective-permute-start(bf16[16,1024]{1,0:T(8,128)(2,1)S(1)} %get-tuple-element.76), channel_id=1, source_target_pairs={{0,28},{1,29},{2,30},{3,31},{4,0},{5,1},{6,2},{7,3},{8,4},{9,5},{1... | collective-permute-start | bytes 98312 | tf_op jit(solution)/shard_map/ppermute | solution.py:470

commit v4 on v3

--- a/solution.py
+++ b/solution.py
@@ -56,7 +56,7 @@
     groups, _, sub, samples = x4.shape
     channels = groups * 2 * sub
 
-    def kernel(ids_ref, x_ref, own_ref, low_ref, high_ref, away_ref, buf, sems):
+    def kernel(ids_ref, x_ref, own_ref, edge_ref, high_ref, buf, sems):
         base = lax.axis_index("chan") * channels
         core = lax.axis_index("tm") % 2
         copies = []
@@ -70,9 +70,10 @@
             copies.append(pltpu.make_async_copy(x_ref.at[group, half], buf.at[j], sems.at[j]))
         last = pl.ds(samples - LANE, LANE)
         rest = [
-            pltpu.make_async_copy(x_ref.at[:, 0, :, last], low_ref, sems.at[NS]),
+            pltpu.make_async_copy(
+                x_ref.at[:, 0, :, last], edge_ref.at[pl.ds(0, groups)], sems.at[NS]
+            ),
             pltpu.make_async_copy(x_ref.at[:, 1, :, last], high_ref, sems.at[NS + 1]),
-            pltpu.make_async_copy(x_ref.at[:, 1 - core], away_ref, sems.at[NS + 2]),
         ]
         for copy in copies + rest:
             copy.start()
@@ -84,43 +85,58 @@
             picked = picked[:NS] + picked[NS:]
             own = own + pltpu.roll(picked, (j + NS - inner[j] % NS) % NS, 0)
         own_ref[...] = own.astype(jnp.bfloat16)
+        end = jnp.where(core == 1, own[:, samples - LEFT :], own[:, :LEFT])
         for copy in rest:
             copy.wait()
-
-    edge = shape((groups, sub, LANE), jnp.bfloat16)
+        edge_ref[groups] = jnp.concatenate(
+            [end[:, :LANE], end[:, LANE:]], axis=0
+        ).astype(jnp.bfloat16)
+
     return call(
         kernel,
         "pick_sources",
         [
             shape((NS, samples), jnp.bfloat16),
-            edge,
-            edge,
-            shape((groups, sub, samples), jnp.bfloat16),
+            shape((groups + 1, sub, LANE), jnp.bfloat16),
+            shape((groups, sub, LANE), jnp.bfloat16),
         ],
         [SMEM, ANY],
-        [pltpu.VMEM((NS, sub, samples), jnp.bfloat16), pltpu.SemaphoreType.DMA((NS + 3,))],
-        out_specs=[VMEM, VMEM, VMEM, ANY],
+        [pltpu.VMEM((NS, sub, samples), jnp.bfloat16), pltpu.SemaphoreType.DMA((NS + 2,))],
         limit=61,
-        moved=4 * MIB,
+        moved=2 * MIB,
     )(source_channels, x4)
 
 
-def join_sources(piece, arrived):
-    samples = piece.shape[1]
-
-    def kernel(piece_ref, arrived_ref, out_ref, end_ref):
-        core = lax.axis_index("tm") % 2
-        total = piece_ref[...].astype(jnp.float32) + arrived_ref[...].astype(jnp.float32)
-        out_ref[...] = total.astype(jnp.bfloat16)
-        end = jnp.where(core == 1, total[:, samples - LEFT :], total[:, :LEFT])
-        end_ref[...] = end.astype(jnp.bfloat16)
-
-    return call(
-        kernel,
-        "join_sources",
-        [shape(piece.shape, jnp.bfloat16), shape((NS, LEFT), jnp.bfloat16)],
+def extend_sources(own, edge):
+    samples = own.shape[1]
+    groups = edge.shape[0] - 1
+
+    def kernel(own_ref, edge_ref, out_ref):
+        end = edge_ref[groups].astype(jnp.float32)
+        joined = [own_ref[...].astype(jnp.float32), end[:NS], end[NS:]]
+        out_ref[...] = jnp.concatenate(joined, axis=1).astype(jnp.bfloat16)
+
+    return call(
+        kernel,
+        "extend_sources",
+        [shape((NS, samples + LEFT), jnp.bfloat16)],
         [VMEM, VMEM],
-    )(piece, arrived)
+    )(own, edge)[0]
+
+
+def add_pieces(*pieces):
+    def kernel(*refs):
+        total = refs[0][...].astype(jnp.float32)
+        for ref in refs[1:-1]:
+            total = total + ref[...].astype(jnp.float32)
+        refs[-1][...] = total.astype(jnp.bfloat16)
+
+    return call(
+        kernel,
+        "add_pieces",
+        [shape(pieces[0].shape, jnp.bfloat16)],
+        [VMEM] * len(pieces),
+    )(*pieces)[0]
 
 
 def filter_rows(offsets, taps, x4, other, low_edge, high_edge):
@@ -132,71 +148,57 @@
 
     def kernel(
         off_ref, taps_ref, x_ref, other_ref, low_ref, high_ref, out_ref, power_ref,
-        raw, value_buf, in_sems, out_sems
+        value_buf, sems
     ):
         tile = lax.axis_index("tm")
         core = tile % 2
-
-        def fetch(part, source, index):
-            cols = pl.ds(index * chunk, chunk)
-            return pltpu.make_async_copy(source.at[:, :, cols], raw.at[part], in_sems.at[part])
-
-        own = x_ref.at[:, core]
+        matrix = fir_tile(taps_ref[...])
+        first_kept = off_ref[tile // 2]
+
+        def store(part):
+            cols = pl.ds(part * chunk, chunk)
+            return pltpu.make_async_copy(value_buf.at[part], out_ref.at[:, cols], sems.at[part])
+
+        def run(read_low, read_high, previous):
+            power = jnp.zeros((rows, LANE), jnp.float32)
+            for part in range(total):
+                read = read_low if part < parts else read_high
+                for j in range(chunk // LANE):
+                    first = (part % parts) * chunk + j * LANE
+                    current = read(slice(first, first + LANE)).reshape(rows, LANE)
+                    framed = jnp.concatenate([previous, current], axis=1)
+                    value = jnp.dot(framed, matrix, preferred_element_type=jnp.float32)
+                    power = power + value * value
+                    place = lax.broadcasted_iota(jnp.int32, (1, LANE), 1) + part * chunk + j * LANE
+                    value = value * jnp.where(place >= first_kept, 1.0, 0.0)
+                    value_buf[part, :, j * LANE : (j + 1) * LANE] = value
+                    previous = current
+                store(part).start()
+            power_ref[...] = power
+
+        def own(cols):
+            return x_ref[:, core, :, cols]
+
+        def swapped(cols):
+            return other_ref[:, :, cols]
 
         @pl.when(core == 0)
         def _():
-            for p in range(parts):
-                fetch(p, own, p).start()
-            for p in range(parts):
-                fetch(parts + p, other_ref, p).start()
+            run(own, swapped, low_ref[:groups].reshape(rows, LANE))
 
         @pl.when(core == 1)
         def _():
-            for p in range(parts):
-                fetch(p, other_ref, p).start()
-            for p in range(parts):
-                fetch(parts + p, own, p).start()
-
-        matrix = fir_tile(taps_ref[...])
-        first_kept = off_ref[tile // 2]
-        previous = jnp.where(core == 0, low_ref[...], high_ref[...]).reshape(rows, LANE)
-        power = jnp.zeros((rows, LANE), jnp.float32)
-        stores = []
+            run(swapped, own, high_ref[...].reshape(rows, LANE))
+
         for part in range(total):
-            fetch(part, own, 0).wait()
-            for j in range(chunk // LANE):
-                current = raw[part, :, :, j * LANE : (j + 1) * LANE].reshape(rows, LANE)
-                framed = jnp.concatenate([previous, current], axis=1)
-                value = jnp.dot(framed, matrix, preferred_element_type=jnp.float32)
-                power = power + value * value
-                start = part * chunk + j * LANE
-                if start < WIN:
-                    place = lax.broadcasted_iota(jnp.int32, (1, LANE), 1) + start
-                    value = value * jnp.where(place >= first_kept, 1.0, 0.0)
-                value_buf[part, :, j * LANE : (j + 1) * LANE] = value
-                previous = current
-            store = pltpu.make_async_copy(
-                value_buf.at[part],
-                out_ref.at[:, pl.ds(part * chunk, chunk)],
-                out_sems.at[part],
-            )
-            store.start()
-            stores.append(store)
-        power_ref[...] = power
-        for store in stores:
-            store.wait()
+            store(part).wait()
 
     return call(
         kernel,
         "filter_rows",
         [shape((rows, 2 * half), jnp.float32), shape((rows, LANE), jnp.float32)],
-        [SMEM, VMEM, ANY, ANY, VMEM, VMEM],
-        [
-            pltpu.VMEM((total, groups, sub, chunk), jnp.bfloat16),
-            pltpu.VMEM((total, rows, chunk), jnp.float32),
-            pltpu.SemaphoreType.DMA((total,)),
-            pltpu.SemaphoreType.DMA((total,)),
-        ],
+        [SMEM, VMEM, VMEM, VMEM, VMEM, VMEM],
+        [pltpu.VMEM((total, rows, chunk), jnp.float32), pltpu.SemaphoreType.DMA((total,))],
         out_specs=[ANY, VMEM],
         limit=40,
         flops=2 * rows * 2 * half * 512,
@@ -204,24 +206,20 @@
     )(offsets, taps, x4, other, low_edge, high_edge)
 
 
-def filter_sources(offsets, taps, mine, other, edge, cross, power, chips):
+def filter_sources(offsets, taps, mine, other, power, chips):
     length = WIN + 2 * MAXLAG
     count = length // LANE
-
-    def kernel(
-        off_ref, taps_ref, mine_ref, other_ref, edge_ref, cross_ref, power_ref, out_ref, energy_ref
-    ):
+    half = mine.shape[1] - LEFT
+
+    def kernel(off_ref, taps_ref, mine_ref, other_ref, power_ref, out_ref, energy_ref):
         tile = lax.axis_index("tm")
         core, chip = tile % 2, tile // 2
         mine_rows = mine_ref[...].astype(jnp.float32)
         other_rows = other_ref[...].astype(jnp.float32)
         low = jnp.where(core == 0, mine_rows, other_rows)
         high = jnp.where(core == 0, other_rows, mine_rows)
-        edge_rows = edge_ref[...].astype(jnp.float32)
-        cross_rows = cross_ref[...].astype(jnp.float32)
-        left = jnp.where(core == 0, edge_rows, cross_rows)
-        right = jnp.where(core == 0, cross_rows, edge_rows)
-        raw = jnp.concatenate([left, low, high, right[:, :LANE]], axis=1)
+        raw = [low[:, half:], low[:, :half], high[:, :half], high[:, half : half + LANE]]
+        raw = jnp.concatenate(raw, axis=1)
         blocks = [raw[:, j * LANE : (j + 1) * LANE] for j in range(count + 1)]
         before = jnp.concatenate(blocks[:-1], axis=0)
         after = jnp.concatenate(blocks[1:], axis=0)
@@ -260,9 +258,9 @@
         kernel,
         "filter_sources",
         [shape((NS, length), jnp.float32), shape((chips, 8, LANE), jnp.float32)],
-        [SMEM, VMEM, VMEM, VMEM, VMEM, VMEM, VMEM],
+        [SMEM, VMEM, VMEM, VMEM, VMEM],
         moved=MIB,
-    )(offsets, taps, mine, other, edge, cross, power)
+    )(offsets, taps, mine, other, power)
 
 
 def lag_products(white, table_ref, pairs, keep_ref, send_ref, half_groups):
@@ -360,60 +358,52 @@
     )(white, table)
 
 
-def add_line(keep, across):
-    groups, sub, cols = keep.shape
-
-    def kernel(keep_ref, across_ref, own_ref, *out_refs):
-        place = lax.axis_index("tm") // 4
-        for d in range(groups):
-            index = lax.rem(place + d, groups)
-            value = keep_ref[index] + across_ref[index].astype(jnp.float32)
-            if d == 0:
-                own_ref[...] = value
-            else:
-                out_refs[d - 1][...] = value.astype(jnp.bfloat16)
+def add_line(keeps, arrivals):
+    groups, sub, _ = keeps[0].shape
+    widths = [keep.shape[2] for keep in keeps]
+    count = len(keeps)
+
+    def kernel(*refs):
+        start = 0
+        for keep_ref, across_ref, width in zip(refs[:count], refs[count : 2 * count], widths):
+            value = keep_ref[...] + across_ref[...].astype(jnp.float32)
+            refs[-1][:, :, start : start + width] = value.astype(jnp.bfloat16)
+            start += width
 
     return call(
         kernel,
         "add_line",
-        [shape((sub, cols), jnp.float32)]
-        + [shape((sub, cols), jnp.bfloat16)] * (groups - 1),
-        [VMEM, VMEM],
+        [shape((groups, sub, sum(widths)), jnp.bfloat16)],
+        [VMEM] * (2 * count),
         moved=MIB,
-    )(keep, across)
-
-
-def finish(halves, factor):
-    count = len(halves[0])
-    sub, cols = halves[0][0].shape
-    blocks = cols // LANE
-
-    def kernel(*refs):
-        out_ref, turned = refs[-2], refs[-1]
+    )(*keeps, *arrivals)[0]
+
+
+def finish(parts, factor):
+    count, sub, cols = parts.shape
+
+    def kernel(parts_ref, out_ref, turned):
         blank = jnp.zeros((LANE - sub, LANE), jnp.float32)
-        for h in range(len(halves)):
-            part = refs[h * count : (h + 1) * count]
-            value = part[0][...]
-            for ref in part[1:]:
-                value = value + ref[...].astype(jnp.float32)
-            value = value * factor
-            for j in range(blocks):
-                block = jnp.concatenate([value[:, j * LANE : (j + 1) * LANE], blank], axis=0)
-                start = (h * blocks + j) * LANE
-                turned[start : start + LANE, :] = block.T
+        value = parts_ref[0].astype(jnp.float32)
+        for i in range(1, count):
+            value = value + parts_ref[i].astype(jnp.float32)
+        value = value * factor
+        for j in range(cols // LANE):
+            block = jnp.concatenate([value[:, j * LANE : (j + 1) * LANE], blank], axis=0)
+            turned[j * LANE : (j + 1) * LANE, :] = block.T
         for m in range(NS):
             for j in range(LAGS // LANE):
                 block = turned[pl.ds(j * LANE * NS + m, LANE, stride=NS), :]
-                out_ref[:, m, j * LANE : (j + 1) * LANE] = block.T[:sub]
+                out_ref[:, m // SB, m % SB, j * LANE : (j + 1) * LANE] = block.T[:sub]
 
     return call(
         kernel,
         "finish",
-        [shape((sub, NS, LAGS), jnp.float32)],
-        [VMEM] * (count * len(halves)),
+        [shape((sub, NSRC, SB, LAGS), jnp.float32)],
+        [VMEM],
         [pltpu.VMEM((NS * LAGS, LANE), jnp.float32)],
         moved=MIB,
-    )(*[part for half in halves for part in half])[0]
+    )(parts)[0]
 
 
 def shards(strain_rate, whiten_taps, source_channels, window_offsets):
@@ -423,35 +413,33 @@
     total_samples = samples * tiles
     chips = tiles // 2
     sub = channels // tiles
+    core = lax.axis_index("tm") % 2
     taps = wide_taps(whiten_taps)
 
     x4 = strain_rate.reshape(chips, 2, sub, samples)
-    piece, low_edge, high_edge, away = pick_sources(source_channels, x4)
+    own, edge, high = pick_sources(source_channels, x4)
+    core, own = lax.optimization_barrier((core, own))
 
     swap = [(i, i ^ 1) for i in range(tiles)]
     to_next = [(2 * k - 1, 2 * k) for k in range(1, chips)]
-    skip_next = [(2 * k - 1, 2 * k + 1) for k in range(1, chips)]
     both_next = to_next + [(b, a) for a, b in to_next]
-    both_skip = skip_next + [(2 * k, 2 * k - 2) for k in range(1, chips)]
-
+    edge = lax.ppermute(edge, "tm", both_next)
+    away = lax.dynamic_index_in_dim(x4, 1 - core, axis=1, keepdims=False)
+    other = lax.ppermute(away, "tm", swap)
+    high = lax.ppermute(high, "tm", [(2 * k - 1, 2 * k + 1) for k in range(1, chips)])
+
+    piece = extend_sources(own, edge)
     parts = [
         lax.ppermute(piece, "chan", [(i, (i + 2 * d) % groups_chan) for i in range(groups_chan)])
         for d in range(1, groups_chan // 2)
     ]
-    other = lax.ppermute(away, "tm", swap)
-    piece = piece + sum(parts[1:], parts[0])
+    piece = add_pieces(piece, *parts)
     arrived = lax.ppermute(piece, "chan", [(i, i ^ 1) for i in range(groups_chan)])
-    low_edge = lax.ppermute(low_edge, "tm", to_next)
-    high_edge = lax.ppermute(high_edge, "tm", skip_next)
-    piece, end = join_sources(piece, arrived)
+    filtered, power = filter_rows(window_offsets, taps, x4, other, edge, high)
+    arrived, power = lax.optimization_barrier((arrived, power))
+    piece = add_pieces(piece, arrived)
     piece_other = lax.ppermute(piece, "tm", swap)
-    edge = lax.ppermute(end, "tm", both_next)
-    cross = lax.ppermute(end, "tm", both_skip)
-    filtered, power = filter_rows(window_offsets, taps, x4, other, low_edge, high_edge)
-    piece_other, edge, cross, power = lax.optimization_barrier((piece_other, edge, cross, power))
-    traces, energy = filter_sources(
-        window_offsets, taps, piece, piece_other, edge, cross, power, chips
-    )
+    traces, energy = filter_sources(window_offsets, taps, piece, piece_other, power, chips)
     same = [[2 * k + c for k in range(chips)] for c in range(2)]
     energies = lax.all_to_all(energy, "tm", 0, 0, tiled=True, axis_index_groups=same)
 
@@ -462,22 +450,13 @@
         energies, traces, filtered, first, column, total_samples
     )
     line = [(i, i ^ 2) for i in range(tiles)]
-
-    def over_column(keep, across):
-        own, *sends = add_line(keep, across)
-        far_first = sorted(range(1, column), key=lambda d: -min(d, column - d))
-        arrived = [
-            lax.ppermute(sends[d - 1], "tm", [(i, (i + 4 * d) % tiles) for i in range(tiles)])
-            for d in far_first
-        ]
-        return [own] + arrived
-
     across_a = lax.ppermute(send_a, "tm", line)
     keep_b, send_b = correlate_next(white, table, second, column)
     across_b = lax.ppermute(send_b, "tm", line)
-    halves = [over_column(keep_a, across_a), over_column(keep_b, across_b)]
-    total = finish(halves, 1.0 / math.sqrt(total_samples))
-    return total.reshape(sub, NSRC, SB, LAGS)
+    summed = add_line([keep_a, keep_b], [across_a, across_b])
+    columns = [[4 * z + r for z in range(column)] for r in range(4)]
+    parts = lax.all_to_all(summed, "tm", 0, 0, tiled=True, axis_index_groups=columns)
+    return finish(parts, 1.0 / math.sqrt(total_samples))
 
 
 def solution(mesh):

time: 170 us -> 89.7 us (0.53)
  Pallas kernels: 86.3 us -> 22.4 us
  starting transfers between devices: 52.2 us -> 14 us
  blocking collectives: 17.6 us -> 35.9 us
  waiting for transfers between devices: 9.56 us -> 14.8 us
    pallas_call x5 -> x6, Pallas kernels: 67.1 us -> 4.45 us  [the longest x1 2.96 us: pick_sources(): call(kernel, 'pick_sources', [shape((NS, samples), jnp.bfloat16), shape((...]
    ppermute x18 -> x2, starting transfers between devices: 41.8 us -> 4.83 us  [the longest x1 4.18 us: shards(): edge = lax.ppermute(edge, 'tm', both_next)]
    all_to_all x0 -> x1, blocking collectives: none -> 17.9 us  [shards(): lax.all_to_all(summed, 'tm', 0, 0, tiled=True, axis_index_groups=columns)]
    ppermute x1, waiting for transfers between devices: 0.01 us -> 5.67 us  [shards(): across_b = lax.ppermute(send_b, 'tm', line)]
    unnamed x6 -> x12, local copies, waits for them, and re-layouts: 2.19 us -> 0.03 us
    squeeze x0 -> x1, local copies, waits for them, and re-layouts: none -> 1.96 us  [shards(): away = lax.dynamic_index_in_dim(x4, 1 - core, axis=1, keepdims=False)]
  transfers between devices with their start and end apart: 26 -> 10, of which waited for: 6 -> 6; matrix products, arithmetic and copies ran while one was open for 1% -> 0% of each run, Pallas kernels for 6% -> 10%
where the time goes in v4:
time: 89.7 us; the launch traced here: 89.4 us
  blocking collectives  35.9 us (40%)
  Pallas kernels  22.4 us (25%)
  waiting for transfers between devices  14.8 us (16%)
  starting transfers between devices  14 us (16%)
  local copies, waits for them, and re-layouts  2 us (2%)
    all_to_all x1, blocking collectives, shards(): lax.all_to_all(energy, 'tm', 0, 0, tiled=True, axis_index_groups=same)  18 us
    all_to_all x1, blocking collectives, shards(): lax.all_to_all(summed, 'tm', 0, 0, tiled=True, axis_index_groups=columns)  17.9 us
    pallas_call x1, Pallas kernels, correlate_first(): call(kernel, 'correlate_first', [shape((half_groups, sub, cols), jnp.floa...  8.13 us
    ppermute x1, waiting for transfers between devices, shards(): across_b = lax.ppermute(send_b, 'tm', line)  5.67 us
    ppermute x3, waiting for transfers between devices, shards(): lax.ppermute(piece, 'chan', [(i, (i + 2 * d) % groups_chan) for i in rang...  5.59 us
    pallas_call x1, Pallas kernels, correlate_next(): call(kernel, 'correlate_next', [shape((half_groups, sub, cols), jnp.float...  4.48 us
    pallas_call x1, Pallas kernels, filter_rows(): call(kernel, 'filter_rows', [shape((rows, 2 * half), jnp.float32), shape(...  4.38 us
    ppermute x3, starting transfers between devices, shards(): lax.ppermute(piece, 'chan', [(i, (i + 2 * d) % groups_chan) for i in rang...  4.31 us
  transfers between devices with their start and end apart: 10, of which 6 were waited for; matrix products, arithmetic and copies ran while one was open for 0% of the time, Pallas kernels for 10%

profile of v4, /device:TPU:8, one launch (start us, length us, event | category | flops | bytes accessed | tf_op | source)
XLA Modules:
  0.0 89.4 jit_solution(3984990164537465678)
XLA Ops:
  0.0 0.0 copy-start.5
  0.0 0.0 copy-start.2
  0.0 3.0 %pick_sources.1 = (bf16[8,4096]{1,0:T(8,128)(2,1)}, bf16[17,16,128]{2,1,0:T(8,128)(2,1)}, bf16[16,16,128]{2,1,0:T(8,128)(2,1)}) custom-call(s32[2,4]{1,0:T(2,128)} %ids_ref.1, bf16[16,2,16,4096]{3,2,1,0:T(8,128)(2,1)} %bitcast.3), custom_call_target="tpu_custom_call" | custom-call | bytes 2097152 | tf_op jit(solution)/shard_map/pick_sources/pallas_call | solution.py:95
  3.0 0.0 copy-start.3
  3.0 0.0 copy-start.1
  3.0 0.0 copy-start.4
  3.0 0.0 copy-start
  3.0 2.0 %dynamic-slice_bitcast_fusion = bf16[16,16,4096]{2,1,0:T(8,128)(2,1)S(1)} fusion(bf16[16,2,16,4096]{3,2,1,0:T(8,128)(2,1)} %bitcast.4, s32[]{:T(128)S(6)} %select_n.12), kind=kLoop, calls=%fused_computation | loop fusion | bytes 4194308 | tf_op jit(solution)/shard_map/jit(dynamic_index_in_dim)/squeeze | solution.py:427
  5.0 0.1 collective-permute-start.5
  5.1 0.0 copy-done.3
  5.1 4.2 %collective-permute-start = (bf16[17,16,128]{2,1,0:T(8,128)(2,1)S(1)}, bf16[17,16,128]{2,1,0:T(8,128)(2,1)S(1)}, u32[]{:S(2)}, u32[]{:S(2)}) collective-permute-start(bf16[17,16,128]{2,1,0:T(8,128)(2,1)S(1)} %copy-done.3), channel_id=1, source_target_pairs={{1,2},{3,4},{5,6},{7,8},{9,10},{11,12},{13,14},{15,16},{17,18},{19... | collective-permute-start | bytes 208904 | tf_op jit(solution)/shard_map/ppermute | solution.py:426
  9.3 2.0 %collective-permute-done.edge_ref.low_ref = bf16[17,16,128]{2,1,0:T(8,128)(2,1)S(1)} collective-permute-done((bf16[17,16,128]{2,1,0:T(8,128)(2,1)S(1)}, bf16[17,16,128]{2,1,0:T(8,128)(2,1)S(1)}, u32[]{:S(2)}, u32[]{:S(2)}) %collective-permute-start) | collective-permute-done | bytes 69664 | tf_op jit(solution)/shard_map/ppermute | solution.py:426
  11.3 0.0 copy-done.1
  11.3 2.6 %collective-permute-start.3 = (bf16[8,4352]{1,0:T(8,128)(2,1)S(1)}, bf16[8,4352]{1,0:T(8,128)(2,1)S(1)}, u32[]{:S(2)}, u32[]{:S(2)}) collective-permute-start(bf16[8,4352]{1,0:T(8,128)(2,1)S(1)} %extend_sources.1.refs_0_), channel_id=1, source_target_pairs={{0,192},{32,224},{64,0},{96,32},{128,64},{160,96},{192,128},{224,1... | collective-permute-start | bytes 208904 | tf_op jit(solution)/shard_map/ppermute | solution.py:433
  13.8 0.7 collective-permute-start.2
  14.6 1.0 %collective-permute-start.1 = (bf16[8,4352]{1,0:T(8,128)(2,1)S(1)}, bf16[8,4352]{1,0:T(8,128)(2,1)S(1)}, u32[]{:S(2)}, u32[]{:S(2)}) collective-permute-start(bf16[8,4352]{1,0:T(8,128)(2,1)S(1)} %extend_sources.1.refs_0_), channel_id=1, source_target_pairs={{0,64},{32,96},{64,128},{96,160},{128,192},{160,224},{192,0},{224,... | collective-permute-start | bytes 208904 | tf_op jit(solution)/shard_map/ppermute | solution.py:433
  15.6 0.0 copy-done.4
  15.6 0.7 collective-permute-start.6
  16.2 0.0 copy-done.5
  16.3 0.0 collective-permute-done.3.refs_3_
  16.3 4.1 %collective-permute-done.2.refs_2_ = bf16[8,4352]{1,0:T(8,128)(2,1)S(1)} collective-permute-done((bf16[8,4352]{1,0:T(8,128)(2,1)S(1)}, bf16[8,4352]{1,0:T(8,128)(2,1)S(1)}, u32[]{:S(2)}, u32[]{:S(2)}) %collective-permute-start.2) | collective-permute-done | bytes 69664 | tf_op jit(solution)/shard_map/ppermute | solution.py:433
  20.4 1.5 %collective-permute-done.1.refs_1_ = bf16[8,4352]{1,0:T(8,128)(2,1)S(1)} collective-permute-done((bf16[8,4352]{1,0:T(8,128)(2,1)S(1)}, bf16[8,4352]{1,0:T(8,128)(2,1)S(1)}, u32[]{:S(2)}, u32[]{:S(2)}) %collective-permute-start.1) | collective-permute-done | bytes 69664 | tf_op jit(solution)/shard_map/ppermute | solution.py:433
  21.9 2.5 %collective-permute-start.4 = (bf16[8,4352]{1,0:T(8,128)(2,1)S(1)}, bf16[8,4352]{1,0:T(8,128)(2,1)S(1)}, u32[]{:S(2)}, u32[]{:S(2)}) collective-permute-start(bf16[8,4352]{1,0:T(8,128)(2,1)S(1)} %add_pieces.2.refs_0_), channel_id=1, source_target_pairs={{0,32},{32,0},{64,96},{96,64},{128,160},{160,128},{192,224},{224,1... | collective-permute-start | bytes 208904 | tf_op jit(solution)/shard_map/ppermute | solution.py:437
  24.4 0.0 collective-permute-done.6.high_ref
  24.4 0.0 collective-permute-done.5.other_ref
  24.5 0.0 copy-done.2
  24.5 0.0 copy-done
  24.5 4.4 %filter_rows.1 = (f32[256,8192]{1,0:T(8,128)}, f32[256,128]{1,0:T(8,128)S(1)}) custom-call(s32[16]{0:T(128)S(1)} %copy-done.2, bf16[1,256]{1,0:T(2,128)(2,1)S(1)} %reshape.6.taps_ref, bf16[16,2,16,4096]{3,2,1,0:T(8,128)(2,1)S(1)} %bitcast.5, bf16[16,16,4096]{2,1,0:T(8,128)(2,1)S(1)} %collective-permute-done.5.other_ref, ...), custom_call_target="tpu_custom_call" | custom-call | flops 2147483648 | bytes 12582912 | tf_op jit(solution)/shard_map/filter_rows/pallas_call | solution.py:196
  28.9 0.0 collective-permute-done.4.refs_1_
  28.9 0.1 collective-permute-start.7
  29.0 1.2 %collective-permute-done.7.other_ref = bf16[8,4352]{1,0:T(8,128)(2,1)S(1)} collective-permute-done((bf16[8,4352]{1,0:T(8,128)(2,1)S(1)}, bf16[8,4352]{1,0:T(8,128)(2,1)S(1)}, u32[]{:S(2)}, u32[]{:S(2)}) %collective-permute-start.7) | collective-permute-done | bytes 69664 | tf_op jit(solution)/shard_map/ppermute | solution.py:441
  30.2 1.0 %filter_sources.1 = (f32[8,8448]{1,0:T(8,128)S(1)}, f32[16,8,128]{2,1,0:T(8,128)S(1)}) custom-call(s32[16]{0:T(128)S(1)} %copy-done.2, bf16[1,256]{1,0:T(2,128)(2,1)S(1)} %reshape.6.taps_ref, bf16[8,4352]{1,0:T(8,128)(2,1)S(1)} %add_pieces.3.mine_ref, bf16[8,4352]{1,0:T(8,128)(2,1)S(1)} %collective-permute-done.7.other_ref, ...), custom_call_target="tpu_custom_call" | custom-call | bytes 1048576 | tf_op jit(solution)/shard_map/filter_sources/pallas_call | solution.py:257
  31.2 18.0 %all_to_all.10.energy_ref = f32[16,8,128]{2,1,0:T(8,128)S(1)} all-to-all(f32[16,8,128]{2,1,0:T(8,128)S(1)} %get-tuple-element.30), channel_id=1, replica_groups={{0,2,4,6,8,10,12,14,16,18,20,22,24,26,28,30},{1,3,5,7,9,11,13,15,17,19,..., dimensions={0} | all-to-all | bytes 131072 | tf_op jit(solution)/shard_map/all_to_all | solution.py:444
  49.3 8.1 %correlate_first.1 = (f32[8,16,1024]{2,1,0:T(8,128)S(1)}, bf16[8,16,1024]{2,1,0:T(8,128)(2,1)S(1)}, bf16[256,8192]{1,0:T(8,128)(2,1)S(1)}, bf16[8448,128]{1,0:T(8,128)(2,1)S(1)}) custom-call(f32[16,8,128]{2,1,0:T(8,128)S(1)} %all_to_all.10.energy_ref, f32[8,8448]{1,0:T(8,128)S(1)} %get-tuple-element.31.traces_ref, f32[256,8192]{1,0:T(8,128)} %get-tuple-element.32.rows_ref), custom_call_target="tpu_custom_call" | custom-call | flops 4294967296 | bytes 16777216 | tf_op jit(solution)/shard_map/correlate_first/pallas_call | solution.py:319
  57.4 1.5 %collective-permute-start.8 = (bf16[8,16,1024]{2,1,0:T(8,128)(2,1)S(1)}, bf16[8,16,1024]{2,1,0:T(8,128)(2,1)S(1)}, u32[]{:S(2)}, u32[]{:S(2)}) collective-permute-start(bf16[8,16,1024]{2,1,0:T(8,128)(2,1)S(1)} %get-tuple-element.37), channel_id=1, source_target_pairs={{0,2},{1,3},{2,0},{3,1},{4,6},{5,7},{6,4},{7,5},{8,10},{9,11},{10,... | collective-permute-start | bytes 786440 | tf_op jit(solution)/shard_map/ppermute | solution.py:453
  58.9 4.5 %correlate_next.1 = (f32[8,16,1024]{2,1,0:T(8,128)S(1)}, bf16[8,16,1024]{2,1,0:T(8,128)(2,1)S(1)}) custom-call(bf16[256,8192]{1,0:T(8,128)(2,1)S(1)} %get-tuple-element.34.white_ref, bf16[8448,128]{1,0:T(8,128)(2,1)S(1)} %get-tuple-element.35.table_ref), custom_call_target="tpu_custom_call" | custom-call | flops 4294967296 | bytes 8388608 | tf_op jit(solution)/shard_map/correlate_next/pallas_call | solution.py:348
  63.3 0.7 collective-permute-start.9
  64.1 0.3 collective-permute-done.8.refs_2_
  64.4 5.7 %collective-permute-done.9.refs_3_ = bf16[8,16,1024]{2,1,0:T(8,128)(2,1)S(1)} collective-permute-done((bf16[8,16,1024]{2,1,0:T(8,128)(2,1)S(1)}, bf16[8,16,1024]{2,1,0:T(8,128)(2,1)S(1)}, u32[]{:S(2)}, u32[]{:S(2)}) %collective-permute-start.9) | collective-permute-done | bytes 262176 | tf_op jit(solution)/shard_map/ppermute | solution.py:455
  70.1 0.1 add_line.1
  70.2 17.9 %all_to_all.11.parts_ref = bf16[8,16,2048]{2,1,0:T(8,128)(2,1)S(1)} all-to-all(bf16[8,16,2048]{2,1,0:T(8,128)(2,1)S(1)} %add_line.1), channel_id=1, replica_groups={{0,4,8,12,16,20,24,28},{1,5,9,13,17,21,25,29},{2,6,10,14,18,22,26,30},{..., dimensions={0} | all-to-all | bytes 1048576 | tf_op jit(solution)/shard_map/all_to_all | solution.py:458
  88.0 1.3 %finish.1 = f32[16,2,4,256]{3,2,1,0:T(4,128)} custom-call(bf16[8,16,2048]{2,1,0:T(8,128)(2,1)S(1)} %all_to_all.11.parts_ref), custom_call_target="tpu_custom_call" | custom-call | bytes 1048576 | tf_op jit(solution)/shard_map/finish/pallas_call | solution.py:399
  (5 shorter events, 0.1 us)
Async XLA Ops:
  0.0 16.2 %copy-start.5 = (bf16[64]{0:T(256)(128)(2,1)S(1)}, bf16[64]{0:T(256)(128)(2,1)}, u32[]{:S(2)}) copy-start(bf16[64]{0:T(256)(128)(2,1)} %param.5) | copy-start | bytes 388
  0.0 24.4 %copy-start.2 = (s32[16]{0:T(128)S(1)}, s32[16]{0:T(128)}, u32[]{:S(2)}) copy-start(s32[16]{0:T(128)} %off_ref.3) | copy-start | bytes 196
  3.0 2.1 %copy-start.3 = (bf16[17,16,128]{2,1,0:T(8,128)(2,1)S(1)}, bf16[17,16,128]{2,1,0:T(8,128)(2,1)}, u32[]{:S(2)}) copy-start(bf16[17,16,128]{2,1,0:T(8,128)(2,1)} %get-tuple-element.24) | copy-start | bytes 208900
  3.0 8.3 %copy-start.1 = (bf16[8,4096]{1,0:T(8,128)(2,1)S(1)}, bf16[8,4096]{1,0:T(8,128)(2,1)}, u32[]{:S(2)}) copy-start(bf16[8,4096]{1,0:T(8,128)(2,1)} %get-tuple-element.23.own_ref) | copy-start | bytes 196612
  3.0 12.6 %copy-start.4 = (bf16[16,16,128]{2,1,0:T(8,128)(2,1)S(1)}, bf16[16,16,128]{2,1,0:T(8,128)(2,1)}, u32[]{:S(2)}) copy-start(bf16[16,16,128]{2,1,0:T(8,128)(2,1)} %get-tuple-element.26) | copy-start | bytes 196612
  3.0 21.4 %copy-start = (bf16[512,4096]{1,0:T(8,128)(2,1)S(1)}, bf16[512,4096]{1,0:T(8,128)(2,1)}, u32[]{:S(2)}) copy-start(bf16[512,4096]{1,0:T(8,128)(2,1)} %param.4) | copy-start | bytes 12582916
  5.0 19.5 %collective-permute-start.5 = (bf16[16,16,4096]{2,1,0:T(8,128)(2,1)S(1)}, bf16[16,16,4096]{2,1,0:T(8,128)(2,1)S(1)}, u32[]{:S(2)}, u32[]{:S(2)}) collective-permute-start(bf16[16,16,4096]{2,1,0:T(8,128)(2,1)S(1)} %dynamic-slice_bitcast_fusion), channel_id=1, source_target_pairs={{0,1},{1,0},{2,3},{3,2},{4,5},{5,4},{6,7},{7,6},{8,9},{9,8},{10,11... | collective-permute-start | bytes 6291464 | tf_op jit(solution)/shard_map/ppermute | solution.py:428
  5.1 6.2 %collective-permute-start = (bf16[17,16,128]{2,1,0:T(8,128)(2,1)S(1)}, bf16[17,16,128]{2,1,0:T(8,128)(2,1)S(1)}, u32[]{:S(2)}, u32[]{:S(2)}) collective-permute-start(bf16[17,16,128]{2,1,0:T(8,128)(2,1)S(1)} %copy-done.3), channel_id=1, source_target_pairs={{1,2},{3,4},{5,6},{7,8},{9,10},{11,12},{13,14},{15,16},{17,18},{19... | collective-permute-start | bytes 208904 | tf_op jit(solution)/shard_map/ppermute | solution.py:426
  11.3 5.0 %collective-permute-start.3 = (bf16[8,4352]{1,0:T(8,128)(2,1)S(1)}, bf16[8,4352]{1,0:T(8,128)(2,1)S(1)}, u32[]{:S(2)}, u32[]{:S(2)}) collective-permute-start(bf16[8,4352]{1,0:T(8,128)(2,1)S(1)} %extend_sources.1.refs_0_), channel_id=1, source_target_pairs={{0,192},{32,224},{64,0},{96,32},{128,64},{160,96},{192,128},{224,1... | collective-permute-start | bytes 208904 | tf_op jit(solution)/shard_map/ppermute | solution.py:433
  13.8 6.5 %collective-permute-start.2 = (bf16[8,4352]{1,0:T(8,128)(2,1)S(1)}, bf16[8,4352]{1,0:T(8,128)(2,1)S(1)}, u32[]{:S(2)}, u32[]{:S(2)}) collective-permute-start(bf16[8,4352]{1,0:T(8,128)(2,1)S(1)} %extend_sources.1.refs_0_), channel_id=1, source_target_pairs={{0,128},{32,160},{64,192},{96,224},{128,0},{160,32},{192,64},{224,... | collective-permute-start | bytes 208904 | tf_op jit(solution)/shard_map/ppermute | solution.py:433
  14.6 7.3 %collective-permute-start.1 = (bf16[8,4352]{1,0:T(8,128)(2,1)S(1)}, bf16[8,4352]{1,0:T(8,128)(2,1)S(1)}, u32[]{:S(2)}, u32[]{:S(2)}) collective-permute-start(bf16[8,4352]{1,0:T(8,128)(2,1)S(1)} %extend_sources.1.refs_0_), channel_id=1, source_target_pairs={{0,64},{32,96},{64,128},{96,160},{128,192},{160,224},{192,0},{224,... | collective-permute-start | bytes 208904 | tf_op jit(solution)/shard_map/ppermute | solution.py:433
  15.6 8.9 %collective-permute-start.6 = (bf16[16,16,128]{2,1,0:T(8,128)(2,1)S(1)}, bf16[16,16,128]{2,1,0:T(8,128)(2,1)S(1)}, u32[]{:S(2)}, u32[]{:S(2)}) collective-permute-start(bf16[16,16,128]{2,1,0:T(8,128)(2,1)S(1)} %copy-done.4), channel_id=1, source_target_pairs={{1,3},{3,5},{5,7},{7,9},{9,11},{11,13},{13,15},{15,17},{17,19},{19... | collective-permute-start | bytes 196616 | tf_op jit(solution)/shard_map/ppermute | solution.py:429
  21.9 6.9 %collective-permute-start.4 = (bf16[8,4352]{1,0:T(8,128)(2,1)S(1)}, bf16[8,4352]{1,0:T(8,128)(2,1)S(1)}, u32[]{:S(2)}, u32[]{:S(2)}) collective-permute-start(bf16[8,4352]{1,0:T(8,128)(2,1)S(1)} %add_pieces.2.refs_0_), channel_id=1, source_target_pairs={{0,32},{32,0},{64,96},{96,64},{128,160},{160,128},{192,224},{224,1... | collective-permute-start | bytes 208904 | tf_op jit(solution)/shard_map/ppermute | solution.py:437
  28.9 1.3 %collective-permute-start.7 = (bf16[8,4352]{1,0:T(8,128)(2,1)S(1)}, bf16[8,4352]{1,0:T(8,128)(2,1)S(1)}, u32[]{:S(2)}, u32[]{:S(2)}) collective-permute-start(bf16[8,4352]{1,0:T(8,128)(2,1)S(1)} %add_pieces.3.mine_ref), channel_id=1, source_target_pairs={{0,1},{1,0},{2,3},{3,2},{4,5},{5,4},{6,7},{7,6},{8,9},{9,8},{10,11... | collective-permute-start | bytes 208904 | tf_op jit(solution)/shard_map/ppermute | solution.py:441
  57.4 7.0 %collective-permute-start.8 = (bf16[8,16,1024]{2,1,0:T(8,128)(2,1)S(1)}, bf16[8,16,1024]{2,1,0:T(8,128)(2,1)S(1)}, u32[]{:S(2)}, u32[]{:S(2)}) collective-permute-start(bf16[8,16,1024]{2,1,0:T(8,128)(2,1)S(1)} %get-tuple-element.37), channel_id=1, source_target_pairs={{0,2},{1,3},{2,0},{3,1},{4,6},{5,7},{6,4},{7,5},{8,10},{9,11},{10,... | collective-permute-start | bytes 786440 | tf_op jit(solution)/shard_map/ppermute | solution.py:453
  63.3 6.7 %collective-permute-start.9 = (bf16[8,16,1024]{2,1,0:T(8,128)(2,1)S(1)}, bf16[8,16,1024]{2,1,0:T(8,128)(2,1)S(1)}, u32[]{:S(2)}, u32[]{:S(2)}) collective-permute-start(bf16[8,16,1024]{2,1,0:T(8,128)(2,1)S(1)} %get-tuple-element.38), channel_id=1, source_target_pairs={{0,2},{1,3},{2,0},{3,1},{4,6},{5,7},{6,4},{7,5},{8,10},{9,11},{10,... | collective-permute-start | bytes 786440 | tf_op jit(solution)/shard_map/ppermute | solution.py:455

commit v5 on v4

--- a/solution.py
+++ b/solution.py
@@ -56,9 +56,8 @@
     groups, _, sub, samples = x4.shape
     channels = groups * 2 * sub
 
-    def kernel(ids_ref, x_ref, own_ref, edge_ref, high_ref, buf, sems):
+    def kernel(ids_ref, x_ref, own_ref, low_ref, high_ref, buf, sems):
         base = lax.axis_index("chan") * channels
-        core = lax.axis_index("tm") % 2
         copies = []
         inner = []
         for j in range(NS):
@@ -70,9 +69,7 @@
             copies.append(pltpu.make_async_copy(x_ref.at[group, half], buf.at[j], sems.at[j]))
         last = pl.ds(samples - LANE, LANE)
         rest = [
-            pltpu.make_async_copy(
-                x_ref.at[:, 0, :, last], edge_ref.at[pl.ds(0, groups)], sems.at[NS]
-            ),
+            pltpu.make_async_copy(x_ref.at[:, 0, :, last], low_ref, sems.at[NS]),
             pltpu.make_async_copy(x_ref.at[:, 1, :, last], high_ref, sems.at[NS + 1]),
         ]
         for copy in copies + rest:
@@ -85,43 +82,56 @@
             picked = picked[:NS] + picked[NS:]
             own = own + pltpu.roll(picked, (j + NS - inner[j] % NS) % NS, 0)
         own_ref[...] = own.astype(jnp.bfloat16)
-        end = jnp.where(core == 1, own[:, samples - LEFT :], own[:, :LEFT])
         for copy in rest:
             copy.wait()
-        edge_ref[groups] = jnp.concatenate(
-            [end[:, :LANE], end[:, LANE:]], axis=0
-        ).astype(jnp.bfloat16)
-
+
+    edge = shape((groups, sub, LANE), jnp.bfloat16)
     return call(
         kernel,
         "pick_sources",
         [
             shape((NS, samples), jnp.bfloat16),
-            shape((groups + 1, sub, LANE), jnp.bfloat16),
-            shape((groups, sub, LANE), jnp.bfloat16),
+            edge,
+            edge,
         ],
         [SMEM, ANY],
         [pltpu.VMEM((NS, sub, samples), jnp.bfloat16), pltpu.SemaphoreType.DMA((NS + 2,))],
-        limit=61,
+        limit=52,
         moved=2 * MIB,
     )(source_channels, x4)
 
 
-def extend_sources(own, edge):
-    samples = own.shape[1]
-    groups = edge.shape[0] - 1
-
-    def kernel(own_ref, edge_ref, out_ref):
-        end = edge_ref[groups].astype(jnp.float32)
-        joined = [own_ref[...].astype(jnp.float32), end[:NS], end[NS:]]
-        out_ref[...] = jnp.concatenate(joined, axis=1).astype(jnp.bfloat16)
+def join_sources(piece, arrived):
+    samples = piece.shape[1]
+
+    def kernel(piece_ref, arrived_ref, out_ref, end_ref):
+        core = lax.axis_index("tm") % 2
+        total = piece_ref[...].astype(jnp.float32) + arrived_ref[...].astype(jnp.float32)
+        out_ref[...] = total.astype(jnp.bfloat16)
+        end = jnp.where(core == 1, total[:, samples - LEFT :], total[:, :LEFT])
+        end_ref[...] = end.astype(jnp.bfloat16)
+
+    return call(
+        kernel,
+        "join_sources",
+        [shape(piece.shape, jnp.bfloat16), shape((NS, LEFT), jnp.bfloat16)],
+        [VMEM, VMEM],
+    )(piece, arrived)
+
+
+def extend_sources(piece, edge):
+    samples = piece.shape[1]
+
+    def kernel(piece_ref, edge_ref, out_ref):
+        out_ref[:, :samples] = piece_ref[...]
+        out_ref[:, samples:] = edge_ref[...]
 
     return call(
         kernel,
         "extend_sources",
         [shape((NS, samples + LEFT), jnp.bfloat16)],
         [VMEM, VMEM],
-    )(own, edge)[0]
+    )(piece, edge)[0]
 
 
 def add_pieces(*pieces):
@@ -184,7 +194,7 @@
 
         @pl.when(core == 0)
         def _():
-            run(own, swapped, low_ref[:groups].reshape(rows, LANE))
+            run(own, swapped, low_ref[...].reshape(rows, LANE))
 
         @pl.when(core == 1)
         def _():
@@ -417,27 +427,31 @@
     taps = wide_taps(whiten_taps)
 
     x4 = strain_rate.reshape(chips, 2, sub, samples)
-    own, edge, high = pick_sources(source_channels, x4)
-    core, own = lax.optimization_barrier((core, own))
+    own, low_edge, high_edge = pick_sources(source_channels, x4)
 
     swap = [(i, i ^ 1) for i in range(tiles)]
     to_next = [(2 * k - 1, 2 * k) for k in range(1, chips)]
+    skip_next = [(2 * k - 1, 2 * k + 1) for k in range(1, chips)]
     both_next = to_next + [(b, a) for a, b in to_next]
-    edge = lax.ppermute(edge, "tm", both_next)
+
+    parts = [
+        lax.ppermute(own, "chan", [(i, (i + 2 * d) % groups_chan) for i in range(groups_chan)])
+        for d in range(1, groups_chan // 2)
+    ]
+    piece = add_pieces(own, *parts)
+    piece, core, low_edge, high_edge = lax.optimization_barrier(
+        (piece, core, low_edge, high_edge)
+    )
     away = lax.dynamic_index_in_dim(x4, 1 - core, axis=1, keepdims=False)
     other = lax.ppermute(away, "tm", swap)
-    high = lax.ppermute(high, "tm", [(2 * k - 1, 2 * k + 1) for k in range(1, chips)])
-
-    piece = extend_sources(own, edge)
-    parts = [
-        lax.ppermute(piece, "chan", [(i, (i + 2 * d) % groups_chan) for i in range(groups_chan)])
-        for d in range(1, groups_chan // 2)
-    ]
-    piece = add_pieces(piece, *parts)
     arrived = lax.ppermute(piece, "chan", [(i, i ^ 1) for i in range(groups_chan)])
-    filtered, power = filter_rows(window_offsets, taps, x4, other, edge, high)
-    arrived, power = lax.optimization_barrier((arrived, power))
-    piece = add_pieces(piece, arrived)
+    low_edge = lax.ppermute(low_edge, "tm", to_next)
+    high_edge = lax.ppermute(high_edge, "tm", skip_next)
+    piece, end = join_sources(piece, arrived)
+    edge = lax.ppermute(end, "tm", both_next)
+    filtered, power = filter_rows(window_offsets, taps, x4, other, low_edge, high_edge)
+    edge, power = lax.optimization_barrier((edge, power))
+    piece = extend_sources(piece, edge)
     piece_other = lax.ppermute(piece, "tm", swap)
     traces, energy = filter_sources(window_offsets, taps, piece, piece_other, power, chips)
     same = [[2 * k + c for k in range(chips)] for c in range(2)]

time: 89.7 us -> 91.8 us (1.023)
  starting transfers between devices: 14 us -> 17.5 us
  waiting for transfers between devices: 14.8 us -> 13.8 us
    ppermute x5 -> x6, starting transfers between devices: 9.14 us -> 12.8 us  [the longest x1 6.24 us: shards(): edge = lax.ppermute(end, 'tm', both_next)]
    ppermute x5 -> x6, waiting for transfers between devices: 7.57 us -> 4.86 us  [the longest x3 4.85 us: shards(): lax.ppermute(own, 'chan', [(i, (i + 2 * d) % groups_chan) for i in range(...]
    ppermute x1, waiting for transfers between devices: 0.01 us -> 1.71 us  [shards(): lax.ppermute(piece, 'chan', [(i, i ^ 1) for i in range(groups_chan)])]
    pallas_call x1 -> x2, Pallas kernels: 2.96 us -> 2.22 us  [the longest x1 2.2 us: pick_sources(): call(kernel, 'pick_sources', [shape((NS, samples), jnp.bfloat16), edge, e...]
  transfers between devices with their start and end apart: 10 -> 11, of which waited for: 6 -> 7; matrix products, arithmetic and copies ran while one was open for 0% -> 0% of each run, Pallas kernels for 10% -> 10%
where the time goes in v5:
time: 91.8 us; the launch traced here: 91.2 us
  blocking collectives  35.3 us (38%)
  Pallas kernels  21.7 us (24%)
  starting transfers between devices  17.5 us (19%)
  waiting for transfers between devices  13.8 us (15%)
  local copies, waits for them, and re-layouts  2.66 us (3%)
    all_to_all x1, blocking collectives, shards(): lax.all_to_all(summed, 'tm', 0, 0, tiled=True, axis_index_groups=columns)  17.9 us
    all_to_all x1, blocking collectives, shards(): lax.all_to_all(energy, 'tm', 0, 0, tiled=True, axis_index_groups=same)  17.5 us
    pallas_call x1, Pallas kernels, correlate_first(): call(kernel, 'correlate_first', [shape((half_groups, sub, cols), jnp.floa...  8.13 us
    ppermute x1, starting transfers between devices, shards(): edge = lax.ppermute(end, 'tm', both_next)  6.24 us
    ppermute x1, waiting for transfers between devices, shards(): across_b = lax.ppermute(send_b, 'tm', line)  5.67 us
    ppermute x3, waiting for transfers between devices, shards(): lax.ppermute(own, 'chan', [(i, (i + 2 * d) % groups_chan) for i in range(...  4.85 us
    ppermute x3, starting transfers between devices, shards(): lax.ppermute(own, 'chan', [(i, (i + 2 * d) % groups_chan) for i in range(...  4.6 us
    pallas_call x1, Pallas kernels, correlate_next(): call(kernel, 'correlate_next', [shape((half_groups, sub, cols), jnp.float...  4.48 us
  transfers between devices with their start and end apart: 11, of which 7 were waited for; matrix products, arithmetic and copies ran while one was open for 0% of the time, Pallas kernels for 10%

profile of v5, /device:TPU:8, one launch (start us, length us, event | category | flops | bytes accessed | tf_op | source)
XLA Modules:
  0.0 91.2 jit_solution(4733376881426146801)
XLA Ops:
  0.0 0.0 copy-start.1
  0.0 0.7 copy-done.1
  0.7 0.0 copy-start.3
  0.7 0.0 copy-start.2
  0.7 2.2 %pick_sources.1 = (bf16[8,4096]{1,0:T(8,128)(2,1)S(1)}, bf16[16,16,128]{2,1,0:T(8,128)(2,1)S(1)}, bf16[16,16,128]{2,1,0:T(8,128)(2,1)S(1)}) custom-call(s32[2,4]{1,0:T(2,128)S(1)} %copy-done.1, bf16[16,2,16,4096]{3,2,1,0:T(8,128)(2,1)} %bitcast.3), custom_call_target="tpu_custom_call" | custom-call | bytes 2097152 | tf_op jit(solution)/shard_map/pick_sources/pallas_call | solution.py:89
  2.9 3.0 %collective-permute-start.2 = (bf16[8,4096]{1,0:T(8,128)(2,1)S(1)}, bf16[8,4096]{1,0:T(8,128)(2,1)S(1)}, u32[]{:S(2)}, u32[]{:S(2)}) collective-permute-start(bf16[8,4096]{1,0:T(8,128)(2,1)S(1)} %get-tuple-element.26.refs_0_), channel_id=1, source_target_pairs={{0,192},{32,224},{64,0},{96,32},{128,64},{160,96},{192,128},{224,1... | collective-permute-start | bytes 196616 | tf_op jit(solution)/shard_map/ppermute | solution.py:438
  5.9 0.5 collective-permute-start.1
  6.3 1.2 %collective-permute-start = (bf16[8,4096]{1,0:T(8,128)(2,1)S(1)}, bf16[8,4096]{1,0:T(8,128)(2,1)S(1)}, u32[]{:S(2)}, u32[]{:S(2)}) collective-permute-start(bf16[8,4096]{1,0:T(8,128)(2,1)S(1)} %get-tuple-element.26.refs_0_), channel_id=1, source_target_pairs={{0,64},{32,96},{64,128},{96,160},{128,192},{160,224},{192,0},{224,... | collective-permute-start | bytes 196616 | tf_op jit(solution)/shard_map/ppermute | solution.py:438
  7.5 0.5 collective-permute-done.2.refs_3_
  8.0 3.7 %collective-permute-done.1.refs_2_ = bf16[8,4096]{1,0:T(8,128)(2,1)S(1)} collective-permute-done((bf16[8,4096]{1,0:T(8,128)(2,1)S(1)}, bf16[8,4096]{1,0:T(8,128)(2,1)S(1)}, u32[]{:S(2)}, u32[]{:S(2)}) %collective-permute-start.1) | collective-permute-done | bytes 65568 | tf_op jit(solution)/shard_map/ppermute | solution.py:438
  11.7 0.6 collective-permute-done.refs_1_
  12.4 0.0 copy-start
  12.4 2.0 %dynamic-slice_bitcast_fusion = bf16[16,16,4096]{2,1,0:T(8,128)(2,1)S(1)} fusion(bf16[16,2,16,4096]{3,2,1,0:T(8,128)(2,1)} %bitcast.4, s32[]{:T(128)S(6)} %select_n.12), kind=kLoop, calls=%fused_computation | loop fusion | bytes 4194308 | tf_op jit(solution)/shard_map/jit(dynamic_index_in_dim)/squeeze | solution.py:445
  14.4 0.1 collective-permute-start.5
  14.5 2.3 %collective-permute-start.3 = (bf16[8,4096]{1,0:T(8,128)(2,1)S(1)}, bf16[8,4096]{1,0:T(8,128)(2,1)S(1)}, u32[]{:S(2)}, u32[]{:S(2)}) collective-permute-start(bf16[8,4096]{1,0:T(8,128)(2,1)S(1)} %add_pieces.1.piece_ref), channel_id=1, source_target_pairs={{0,32},{32,0},{64,96},{96,64},{128,160},{160,128},{192,224},{224,1... | collective-permute-start | bytes 196616 | tf_op jit(solution)/shard_map/ppermute | solution.py:447
  16.8 1.3 %collective-permute-start.6 = (bf16[16,16,128]{2,1,0:T(8,128)(2,1)S(1)}, bf16[16,16,128]{2,1,0:T(8,128)(2,1)S(1)}, u32[]{:S(2)}, u32[]{:S(2)}) collective-permute-start(bf16[16,16,128]{2,1,0:T(8,128)(2,1)S(1)} %get-tuple-element.33), channel_id=1, source_target_pairs={{1,2},{3,4},{5,6},{7,8},{9,10},{11,12},{13,14},{15,16},{17,18},{19... | collective-permute-start | bytes 196616 | tf_op jit(solution)/shard_map/ppermute | solution.py:448
  18.1 0.7 collective-permute-start.7
  18.7 0.0 copy-done.3
  18.8 1.7 %collective-permute-done.3.arrived_ref = bf16[8,4096]{1,0:T(8,128)(2,1)S(1)} collective-permute-done((bf16[8,4096]{1,0:T(8,128)(2,1)S(1)}, bf16[8,4096]{1,0:T(8,128)(2,1)S(1)}, u32[]{:S(2)}, u32[]{:S(2)}) %collective-permute-start.3) | collective-permute-done | bytes 65568 | tf_op jit(solution)/shard_map/ppermute | solution.py:447
  20.5 6.2 %collective-permute-start.4 = (bf16[8,256]{1,0:T(8,128)(2,1)S(1)}, bf16[8,256]{1,0:T(8,128)(2,1)S(1)}, u32[]{:S(2)}, u32[]{:S(2)}) collective-permute-start(bf16[8,256]{1,0:T(8,128)(2,1)S(1)} %get-tuple-element.31), channel_id=1, source_target_pairs={{1,2},{3,4},{5,6},{7,8},{9,10},{11,12},{13,14},{15,16},{17,18},{19... | collective-permute-start | bytes 12296 | tf_op jit(solution)/shard_map/ppermute | solution.py:451
  26.8 0.0 collective-permute-done.6.low_ref
  26.8 0.0 collective-permute-done.7.high_ref
  26.8 0.0 collective-permute-done.5.other_ref
  26.8 0.0 copy-done.2
  26.8 0.0 copy-done
  26.8 4.4 %filter_rows.1 = (f32[256,8192]{1,0:T(8,128)}, f32[256,128]{1,0:T(8,128)S(1)}) custom-call(s32[16]{0:T(128)S(1)} %copy-done.2, bf16[1,256]{1,0:T(2,128)(2,1)S(1)} %reshape.6.taps_ref, bf16[16,2,16,4096]{3,2,1,0:T(8,128)(2,1)S(1)} %bitcast.5, bf16[16,16,4096]{2,1,0:T(8,128)(2,1)S(1)} %collective-permute-done.5.other_ref, ...), custom_call_target="tpu_custom_call" | custom-call | flops 2147483648 | bytes 12582912 | tf_op jit(solution)/shard_map/filter_rows/pallas_call | solution.py:206
  31.2 0.0 collective-permute-done.4.edge_ref
  31.2 0.1 collective-permute-start.8
  31.3 1.2 %collective-permute-done.8.other_ref = bf16[8,4352]{1,0:T(8,128)(2,1)S(1)} collective-permute-done((bf16[8,4352]{1,0:T(8,128)(2,1)S(1)}, bf16[8,4352]{1,0:T(8,128)(2,1)S(1)}, u32[]{:S(2)}, u32[]{:S(2)}) %collective-permute-start.8) | collective-permute-done | bytes 69664 | tf_op jit(solution)/shard_map/ppermute | solution.py:455
  32.6 1.0 %filter_sources.1 = (f32[8,8448]{1,0:T(8,128)S(1)}, f32[16,8,128]{2,1,0:T(8,128)S(1)}) custom-call(s32[16]{0:T(128)S(1)} %copy-done.2, bf16[1,256]{1,0:T(2,128)(2,1)S(1)} %reshape.6.taps_ref, bf16[8,4352]{1,0:T(8,128)(2,1)S(1)} %extend_sources.1.mine_ref, bf16[8,4352]{1,0:T(8,128)(2,1)S(1)} %collective-permute-done.8.other_ref, ...), custom_call_target="tpu_custom_call" | custom-call | bytes 1048576 | tf_op jit(solution)/shard_map/filter_sources/pallas_call | solution.py:267
  33.6 17.5 %all_to_all.10.energy_ref = f32[16,8,128]{2,1,0:T(8,128)S(1)} all-to-all(f32[16,8,128]{2,1,0:T(8,128)S(1)} %get-tuple-element.38), channel_id=1, replica_groups={{0,2,4,6,8,10,12,14,16,18,20,22,24,26,28,30},{1,3,5,7,9,11,13,15,17,19,..., dimensions={0} | all-to-all | bytes 131072 | tf_op jit(solution)/shard_map/all_to_all | solution.py:458
  51.0 8.1 %correlate_first.1 = (f32[8,16,1024]{2,1,0:T(8,128)S(1)}, bf16[8,16,1024]{2,1,0:T(8,128)(2,1)S(1)}, bf16[256,8192]{1,0:T(8,128)(2,1)S(1)}, bf16[8448,128]{1,0:T(8,128)(2,1)S(1)}) custom-call(f32[16,8,128]{2,1,0:T(8,128)S(1)} %all_to_all.10.energy_ref, f32[8,8448]{1,0:T(8,128)S(1)} %get-tuple-element.39.traces_ref, f32[256,8192]{1,0:T(8,128)} %get-tuple-element.40.rows_ref), custom_call_target="tpu_custom_call" | custom-call | flops 4294967296 | bytes 16777216 | tf_op jit(solution)/shard_map/correlate_first/pallas_call | solution.py:329
  59.2 1.5 %collective-permute-start.9 = (bf16[8,16,1024]{2,1,0:T(8,128)(2,1)S(1)}, bf16[8,16,1024]{2,1,0:T(8,128)(2,1)S(1)}, u32[]{:S(2)}, u32[]{:S(2)}) collective-permute-start(bf16[8,16,1024]{2,1,0:T(8,128)(2,1)S(1)} %get-tuple-element.45), channel_id=1, source_target_pairs={{0,2},{1,3},{2,0},{3,1},{4,6},{5,7},{6,4},{7,5},{8,10},{9,11},{10,... | collective-permute-start | bytes 786440 | tf_op jit(solution)/shard_map/ppermute | solution.py:467
  60.6 4.5 %correlate_next.1 = (f32[8,16,1024]{2,1,0:T(8,128)S(1)}, bf16[8,16,1024]{2,1,0:T(8,128)(2,1)S(1)}) custom-call(bf16[256,8192]{1,0:T(8,128)(2,1)S(1)} %get-tuple-element.42.white_ref, bf16[8448,128]{1,0:T(8,128)(2,1)S(1)} %get-tuple-element.43.table_ref), custom_call_target="tpu_custom_call" | custom-call | flops 4294967296 | bytes 8388608 | tf_op jit(solution)/shard_map/correlate_next/pallas_call | solution.py:358
  65.1 0.7 collective-permute-start.10
  65.9 0.3 collective-permute-done.9.refs_2_
  66.2 5.7 %collective-permute-done.10.refs_3_ = bf16[8,16,1024]{2,1,0:T(8,128)(2,1)S(1)} collective-permute-done((bf16[8,16,1024]{2,1,0:T(8,128)(2,1)S(1)}, bf16[8,16,1024]{2,1,0:T(8,128)(2,1)S(1)}, u32[]{:S(2)}, u32[]{:S(2)}) %collective-permute-start.10) | collective-permute-done | bytes 262176 | tf_op jit(solution)/shard_map/ppermute | solution.py:469
  71.9 0.1 add_line.1
  72.0 17.9 %all_to_all.11.parts_ref = bf16[8,16,2048]{2,1,0:T(8,128)(2,1)S(1)} all-to-all(bf16[8,16,2048]{2,1,0:T(8,128)(2,1)S(1)} %add_line.1), channel_id=1, replica_groups={{0,4,8,12,16,20,24,28},{1,5,9,13,17,21,25,29},{2,6,10,14,18,22,26,30},{..., dimensions={0} | all-to-all | bytes 1048576 | tf_op jit(solution)/shard_map/all_to_all | solution.py:472
  89.8 1.3 %finish.1 = f32[16,2,4,256]{3,2,1,0:T(4,128)} custom-call(bf16[8,16,2048]{2,1,0:T(8,128)(2,1)S(1)} %all_to_all.11.parts_ref), custom_call_target="tpu_custom_call" | custom-call | bytes 1048576 | tf_op jit(solution)/shard_map/finish/pallas_call | solution.py:409
  (5 shorter events, 0.1 us)
Async XLA Ops:
  0.0 0.7 copy-start.1
  0.7 18.1 %copy-start.3 = (bf16[64]{0:T(256)(128)(2,1)S(1)}, bf16[64]{0:T(256)(128)(2,1)}, u32[]{:S(2)}) copy-start(bf16[64]{0:T(256)(128)(2,1)} %param.5) | copy-start | bytes 388
  0.7 26.1 %copy-start.2 = (s32[16]{0:T(128)S(1)}, s32[16]{0:T(128)}, u32[]{:S(2)}) copy-start(s32[16]{0:T(128)} %off_ref.3) | copy-start | bytes 196
  2.9 5.1 %collective-permute-start.2 = (bf16[8,4096]{1,0:T(8,128)(2,1)S(1)}, bf16[8,4096]{1,0:T(8,128)(2,1)S(1)}, u32[]{:S(2)}, u32[]{:S(2)}) collective-permute-start(bf16[8,4096]{1,0:T(8,128)(2,1)S(1)} %get-tuple-element.26.refs_0_), channel_id=1, source_target_pairs={{0,192},{32,224},{64,0},{96,32},{128,64},{160,96},{192,128},{224,1... | collective-permute-start | bytes 196616 | tf_op jit(solution)/shard_map/ppermute | solution.py:438
  5.9 5.8 %collective-permute-start.1 = (bf16[8,4096]{1,0:T(8,128)(2,1)S(1)}, bf16[8,4096]{1,0:T(8,128)(2,1)S(1)}, u32[]{:S(2)}, u32[]{:S(2)}) collective-permute-start(bf16[8,4096]{1,0:T(8,128)(2,1)S(1)} %get-tuple-element.26.refs_0_), channel_id=1, source_target_pairs={{0,128},{32,160},{64,192},{96,224},{128,0},{160,32},{192,64},{224,... | collective-permute-start | bytes 196616 | tf_op jit(solution)/shard_map/ppermute | solution.py:438
  6.3 6.0 %collective-permute-start = (bf16[8,4096]{1,0:T(8,128)(2,1)S(1)}, bf16[8,4096]{1,0:T(8,128)(2,1)S(1)}, u32[]{:S(2)}, u32[]{:S(2)}) collective-permute-start(bf16[8,4096]{1,0:T(8,128)(2,1)S(1)} %get-tuple-element.26.refs_0_), channel_id=1, source_target_pairs={{0,64},{32,96},{64,128},{96,160},{128,192},{160,224},{192,0},{224,... | collective-permute-start | bytes 196616 | tf_op jit(solution)/shard_map/ppermute | solution.py:438
  12.4 14.4 %copy-start = (bf16[512,4096]{1,0:T(8,128)(2,1)S(1)}, bf16[512,4096]{1,0:T(8,128)(2,1)}, u32[]{:S(2)}) copy-start(bf16[512,4096]{1,0:T(8,128)(2,1)} %param.4) | copy-start | bytes 12582916
  14.4 12.4 %collective-permute-start.5 = (bf16[16,16,4096]{2,1,0:T(8,128)(2,1)S(1)}, bf16[16,16,4096]{2,1,0:T(8,128)(2,1)S(1)}, u32[]{:S(2)}, u32[]{:S(2)}) collective-permute-start(bf16[16,16,4096]{2,1,0:T(8,128)(2,1)S(1)} %dynamic-slice_bitcast_fusion), channel_id=1, source_target_pairs={{0,1},{1,0},{2,3},{3,2},{4,5},{5,4},{6,7},{7,6},{8,9},{9,8},{10,11... | collective-permute-start | bytes 6291464 | tf_op jit(solution)/shard_map/ppermute | solution.py:446
  14.5 6.0 %collective-permute-start.3 = (bf16[8,4096]{1,0:T(8,128)(2,1)S(1)}, bf16[8,4096]{1,0:T(8,128)(2,1)S(1)}, u32[]{:S(2)}, u32[]{:S(2)}) collective-permute-start(bf16[8,4096]{1,0:T(8,128)(2,1)S(1)} %add_pieces.1.piece_ref), channel_id=1, source_target_pairs={{0,32},{32,0},{64,96},{96,64},{128,160},{160,128},{192,224},{224,1... | collective-permute-start | bytes 196616 | tf_op jit(solution)/shard_map/ppermute | solution.py:447
  16.8 10.0 %collective-permute-start.6 = (bf16[16,16,128]{2,1,0:T(8,128)(2,1)S(1)}, bf16[16,16,128]{2,1,0:T(8,128)(2,1)S(1)}, u32[]{:S(2)}, u32[]{:S(2)}) collective-permute-start(bf16[16,16,128]{2,1,0:T(8,128)(2,1)S(1)} %get-tuple-element.33), channel_id=1, source_target_pairs={{1,2},{3,4},{5,6},{7,8},{9,10},{11,12},{13,14},{15,16},{17,18},{19... | collective-permute-start | bytes 196616 | tf_op jit(solution)/shard_map/ppermute | solution.py:448
  18.1 8.7 %collective-permute-start.7 = (bf16[16,16,128]{2,1,0:T(8,128)(2,1)S(1)}, bf16[16,16,128]{2,1,0:T(8,128)(2,1)S(1)}, u32[]{:S(2)}, u32[]{:S(2)}) collective-permute-start(bf16[16,16,128]{2,1,0:T(8,128)(2,1)S(1)} %get-tuple-element.34), channel_id=1, source_target_pairs={{1,3},{3,5},{5,7},{7,9},{9,11},{11,13},{13,15},{15,17},{17,19},{19... | collective-permute-start | bytes 196616 | tf_op jit(solution)/shard_map/ppermute | solution.py:449
  20.5 10.7 %collective-permute-start.4 = (bf16[8,256]{1,0:T(8,128)(2,1)S(1)}, bf16[8,256]{1,0:T(8,128)(2,1)S(1)}, u32[]{:S(2)}, u32[]{:S(2)}) collective-permute-start(bf16[8,256]{1,0:T(8,128)(2,1)S(1)} %get-tuple-element.31), channel_id=1, source_target_pairs={{1,2},{3,4},{5,6},{7,8},{9,10},{11,12},{13,14},{15,16},{17,18},{19... | collective-permute-start | bytes 12296 | tf_op jit(solution)/shard_map/ppermute | solution.py:451
  31.2 1.3 %collective-permute-start.8 = (bf16[8,4352]{1,0:T(8,128)(2,1)S(1)}, bf16[8,4352]{1,0:T(8,128)(2,1)S(1)}, u32[]{:S(2)}, u32[]{:S(2)}) collective-permute-start(bf16[8,4352]{1,0:T(8,128)(2,1)S(1)} %extend_sources.1.mine_ref), channel_id=1, source_target_pairs={{0,1},{1,0},{2,3},{3,2},{4,5},{5,4},{6,7},{7,6},{8,9},{9,8},{10,11... | collective-permute-start | bytes 208904 | tf_op jit(solution)/shard_map/ppermute | solution.py:455
  59.2 7.0 %collective-permute-start.9 = (bf16[8,16,1024]{2,1,0:T(8,128)(2,1)S(1)}, bf16[8,16,1024]{2,1,0:T(8,128)(2,1)S(1)}, u32[]{:S(2)}, u32[]{:S(2)}) collective-permute-start(bf16[8,16,1024]{2,1,0:T(8,128)(2,1)S(1)} %get-tuple-element.45), channel_id=1, source_target_pairs={{0,2},{1,3},{2,0},{3,1},{4,6},{5,7},{6,4},{7,5},{8,10},{9,11},{10,... | collective-permute-start | bytes 786440 | tf_op jit(solution)/shard_map/ppermute | solution.py:467
  65.1 6.7 %collective-permute-start.10 = (bf16[8,16,1024]{2,1,0:T(8,128)(2,1)S(1)}, bf16[8,16,1024]{2,1,0:T(8,128)(2,1)S(1)}, u32[]{:S(2)}, u32[]{:S(2)}) collective-permute-start(bf16[8,16,1024]{2,1,0:T(8,128)(2,1)S(1)} %get-tuple-element.46), channel_id=1, source_target_pairs={{0,2},{1,3},{2,0},{3,1},{4,6},{5,7},{6,4},{7,5},{8,10},{9,11},{10,... | collective-permute-start | bytes 786440 | tf_op jit(solution)/shard_map/ppermute | solution.py:469

commit v6 on v4

--- a/solution.py
+++ b/solution.py
@@ -56,7 +56,7 @@
     groups, _, sub, samples = x4.shape
     channels = groups * 2 * sub
 
-    def kernel(ids_ref, x_ref, own_ref, edge_ref, high_ref, buf, sems):
+    def kernel(ids_ref, x_ref, own_ref, edge_ref, high_ref, away_ref, buf, sems):
         base = lax.axis_index("chan") * channels
         core = lax.axis_index("tm") % 2
         copies = []
@@ -74,6 +74,7 @@
                 x_ref.at[:, 0, :, last], edge_ref.at[pl.ds(0, groups)], sems.at[NS]
             ),
             pltpu.make_async_copy(x_ref.at[:, 1, :, last], high_ref, sems.at[NS + 1]),
+            pltpu.make_async_copy(x_ref.at[:, 1 - core], away_ref, sems.at[NS + 2]),
         ]
         for copy in copies + rest:
             copy.start()
@@ -99,10 +100,11 @@
             shape((NS, samples), jnp.bfloat16),
             shape((groups + 1, sub, LANE), jnp.bfloat16),
             shape((groups, sub, LANE), jnp.bfloat16),
+            shape((groups, sub, samples), jnp.bfloat16),
         ],
         [SMEM, ANY],
-        [pltpu.VMEM((NS, sub, samples), jnp.bfloat16), pltpu.SemaphoreType.DMA((NS + 2,))],
-        limit=61,
+        [pltpu.VMEM((NS, sub, samples), jnp.bfloat16), pltpu.SemaphoreType.DMA((NS + 3,))],
+        limit=50,
         moved=2 * MIB,
     )(source_channels, x4)
 
@@ -413,21 +415,19 @@
     total_samples = samples * tiles
     chips = tiles // 2
     sub = channels // tiles
-    core = lax.axis_index("tm") % 2
     taps = wide_taps(whiten_taps)
 
     x4 = strain_rate.reshape(chips, 2, sub, samples)
-    own, edge, high = pick_sources(source_channels, x4)
-    core, own = lax.optimization_barrier((core, own))
+    own, edge, high, away = pick_sources(source_channels, x4)
 
     swap = [(i, i ^ 1) for i in range(tiles)]
     to_next = [(2 * k - 1, 2 * k) for k in range(1, chips)]
     both_next = to_next + [(b, a) for a, b in to_next]
     edge = lax.ppermute(edge, "tm", both_next)
-    away = lax.dynamic_index_in_dim(x4, 1 - core, axis=1, keepdims=False)
     other = lax.ppermute(away, "tm", swap)
     high = lax.ppermute(high, "tm", [(2 * k - 1, 2 * k + 1) for k in range(1, chips)])
 
+    edge, high = lax.optimization_barrier((edge, high))
     piece = extend_sources(own, edge)
     parts = [
         lax.ppermute(piece, "chan", [(i, (i + 2 * d) % groups_chan) for i in range(groups_chan)])

time: 89.7 us -> 89.1 us (level)
  starting transfers between devices: 14 us -> 15.4 us
  waiting for transfers between devices: 14.8 us -> 13.4 us
  local copies, waits for them, and re-layouts: 2 us -> 0.85 us
    squeeze x1 -> x0, local copies, waits for them, and re-layouts: 1.96 us -> none  [shards(): away = lax.dynamic_index_in_dim(x4, 1 - core, axis=1, keepdims=False)]
    ppermute x1, starting transfers between devices: 0.09 us -> 1.98 us  [shards(): piece_other = lax.ppermute(piece, 'tm', swap)]
  transfers between devices with their start and end apart: 10 -> 10, of which waited for: 6 -> 7; matrix products, arithmetic and copies ran while one was open for 0% -> 0% of each run, Pallas kernels for 10% -> 10%
where the time goes in v6:
time: 89.1 us; the launch traced here: 88.8 us
  blocking collectives  36.7 us (41%)
  Pallas kernels  22.2 us (25%)
  starting transfers between devices  15.4 us (17%)
  waiting for transfers between devices  13.4 us (15%)
    all_to_all x1, blocking collectives, shards(): lax.all_to_all(energy, 'tm', 0, 0, tiled=True, axis_index_groups=same)  18.7 us
    all_to_all x1, blocking collectives, shards(): lax.all_to_all(summed, 'tm', 0, 0, tiled=True, axis_index_groups=columns)  18.1 us
    pallas_call x1, Pallas kernels, correlate_first(): call(kernel, 'correlate_first', [shape((half_groups, sub, cols), jnp.floa...  8.13 us
    ppermute x1, waiting for transfers between devices, shards(): across_b = lax.ppermute(send_b, 'tm', line)  5.69 us
    ppermute x3, waiting for transfers between devices, shards(): lax.ppermute(piece, 'chan', [(i, (i + 2 * d) % groups_chan) for i in rang...  5.02 us
    pallas_call x1, Pallas kernels, correlate_next(): call(kernel, 'correlate_next', [shape((half_groups, sub, cols), jnp.float...  4.48 us
    pallas_call x1, Pallas kernels, filter_rows(): call(kernel, 'filter_rows', [shape((rows, 2 * half), jnp.float32), shape(...  4.36 us
    ppermute x1, starting transfers between devices, shards(): edge = lax.ppermute(edge, 'tm', both_next)  4.18 us
  transfers between devices with their start and end apart: 10, of which 7 were waited for; matrix products, arithmetic and copies ran while one was open for 0% of the time, Pallas kernels for 10%

profile of v6, /device:TPU:8, one launch (start us, length us, event | category | flops | bytes accessed | tf_op | source)
XLA Modules:
  0.0 88.8 jit_solution(8715538662925471634)
XLA Ops:
  0.0 0.0 copy-start
  0.0 0.0 copy-start.1
  0.0 0.8 copy-done.1
  0.8 0.0 copy-start.3
  0.8 0.0 copy-start.2
  0.8 2.8 %pick_sources.1 = (bf16[8,4096]{1,0:T(8,128)(2,1)S(1)}, bf16[17,16,128]{2,1,0:T(8,128)(2,1)S(1)}, bf16[16,16,128]{2,1,0:T(8,128)(2,1)S(1)}, bf16[16,16,4096]{2,1,0:T(8,128)(2,1)S(1)}) custom-call(s32[2,4]{1,0:T(2,128)S(1)} %copy-done.1, bf16[16,2,16,4096]{3,2,1,0:T(8,128)(2,1)} %bitcast.1), custom_call_target="tpu_custom_call" | custom-call | bytes 2097152 | tf_op jit(solution)/shard_map/pick_sources/pallas_call | solution.py:96
  3.6 0.1 collective-permute-start.6
  3.7 4.2 %collective-permute-start = (bf16[17,16,128]{2,1,0:T(8,128)(2,1)S(1)}, bf16[17,16,128]{2,1,0:T(8,128)(2,1)S(1)}, u32[]{:S(2)}, u32[]{:S(2)}) collective-permute-start(bf16[17,16,128]{2,1,0:T(8,128)(2,1)S(1)} %get-tuple-element.24), channel_id=1, source_target_pairs={{1,2},{3,4},{5,6},{7,8},{9,10},{11,12},{13,14},{15,16},{17,18},{19... | collective-permute-start | bytes 208904 | tf_op jit(solution)/shard_map/ppermute | solution.py:426
  7.9 0.7 collective-permute-start.1
  8.6 0.0 collective-permute-done.1.high_ref
  8.6 1.3 %collective-permute-done.edge_ref.low_ref = bf16[17,16,128]{2,1,0:T(8,128)(2,1)S(1)} collective-permute-done((bf16[17,16,128]{2,1,0:T(8,128)(2,1)S(1)}, bf16[17,16,128]{2,1,0:T(8,128)(2,1)S(1)}, u32[]{:S(2)}, u32[]{:S(2)}) %collective-permute-start) | collective-permute-done | bytes 69664 | tf_op jit(solution)/shard_map/ppermute | solution.py:426
  9.9 2.4 %collective-permute-start.4 = (bf16[8,4352]{1,0:T(8,128)(2,1)S(1)}, bf16[8,4352]{1,0:T(8,128)(2,1)S(1)}, u32[]{:S(2)}, u32[]{:S(2)}) collective-permute-start(bf16[8,4352]{1,0:T(8,128)(2,1)S(1)} %extend_sources.1.refs_0_), channel_id=1, source_target_pairs={{0,192},{32,224},{64,0},{96,32},{128,64},{160,96},{192,128},{224,1... | collective-permute-start | bytes 208904 | tf_op jit(solution)/shard_map/ppermute | solution.py:433
  12.3 0.6 collective-permute-start.3
  12.9 0.9 %collective-permute-start.2 = (bf16[8,4352]{1,0:T(8,128)(2,1)S(1)}, bf16[8,4352]{1,0:T(8,128)(2,1)S(1)}, u32[]{:S(2)}, u32[]{:S(2)}) collective-permute-start(bf16[8,4352]{1,0:T(8,128)(2,1)S(1)} %extend_sources.1.refs_0_), channel_id=1, source_target_pairs={{0,64},{32,96},{64,128},{96,160},{128,192},{160,224},{192,0},{224,... | collective-permute-start | bytes 208904 | tf_op jit(solution)/shard_map/ppermute | solution.py:433
  13.8 0.0 copy-done.3
  13.8 0.4 collective-permute-done.4.refs_3_
  14.2 3.9 %collective-permute-done.3.refs_2_ = bf16[8,4352]{1,0:T(8,128)(2,1)S(1)} collective-permute-done((bf16[8,4352]{1,0:T(8,128)(2,1)S(1)}, bf16[8,4352]{1,0:T(8,128)(2,1)S(1)}, u32[]{:S(2)}, u32[]{:S(2)}) %collective-permute-start.3) | collective-permute-done | bytes 69664 | tf_op jit(solution)/shard_map/ppermute | solution.py:433
  18.1 0.7 collective-permute-done.2.refs_1_
  18.9 2.4 %collective-permute-start.5 = (bf16[8,4352]{1,0:T(8,128)(2,1)S(1)}, bf16[8,4352]{1,0:T(8,128)(2,1)S(1)}, u32[]{:S(2)}, u32[]{:S(2)}) collective-permute-start(bf16[8,4352]{1,0:T(8,128)(2,1)S(1)} %add_pieces.2.refs_0_), channel_id=1, source_target_pairs={{0,32},{32,0},{64,96},{96,64},{128,160},{160,128},{192,224},{224,1... | collective-permute-start | bytes 208904 | tf_op jit(solution)/shard_map/ppermute | solution.py:437
  21.3 0.0 collective-permute-done.6.other_ref
  21.3 0.0 copy-done
  21.3 0.0 copy-done.2
  21.3 4.4 %filter_rows.1 = (f32[256,8192]{1,0:T(8,128)}, f32[256,128]{1,0:T(8,128)S(1)}) custom-call(s32[16]{0:T(128)S(1)} %copy-done.2, bf16[1,256]{1,0:T(2,128)(2,1)S(1)} %reshape.6.taps_ref, bf16[16,2,16,4096]{3,2,1,0:T(8,128)(2,1)S(1)} %bitcast.2, bf16[16,16,4096]{2,1,0:T(8,128)(2,1)S(1)} %collective-permute-done.6.other_ref, ...), custom_call_target="tpu_custom_call" | custom-call | flops 2147483648 | bytes 12582912 | tf_op jit(solution)/shard_map/filter_rows/pallas_call | solution.py:198
  25.6 0.0 collective-permute-done.5.refs_1_
  25.7 2.0 %collective-permute-start.7 = (bf16[8,4352]{1,0:T(8,128)(2,1)S(1)}, bf16[8,4352]{1,0:T(8,128)(2,1)S(1)}, u32[]{:S(2)}, u32[]{:S(2)}) collective-permute-start(bf16[8,4352]{1,0:T(8,128)(2,1)S(1)} %add_pieces.3.mine_ref), channel_id=1, source_target_pairs={{0,1},{1,0},{2,3},{3,2},{4,5},{5,4},{6,7},{7,6},{8,9},{9,8},{10,11... | collective-permute-start | bytes 208904 | tf_op jit(solution)/shard_map/ppermute | solution.py:441
  27.6 0.9 %collective-permute-done.7.other_ref = bf16[8,4352]{1,0:T(8,128)(2,1)S(1)} collective-permute-done((bf16[8,4352]{1,0:T(8,128)(2,1)S(1)}, bf16[8,4352]{1,0:T(8,128)(2,1)S(1)}, u32[]{:S(2)}, u32[]{:S(2)}) %collective-permute-start.7) | collective-permute-done | bytes 69664 | tf_op jit(solution)/shard_map/ppermute | solution.py:441
  28.6 1.0 %filter_sources.1 = (f32[8,8448]{1,0:T(8,128)S(1)}, f32[16,8,128]{2,1,0:T(8,128)S(1)}) custom-call(s32[16]{0:T(128)S(1)} %copy-done.2, bf16[1,256]{1,0:T(2,128)(2,1)S(1)} %reshape.6.taps_ref, bf16[8,4352]{1,0:T(8,128)(2,1)S(1)} %add_pieces.3.mine_ref, bf16[8,4352]{1,0:T(8,128)(2,1)S(1)} %collective-permute-done.7.other_ref, ...), custom_call_target="tpu_custom_call" | custom-call | bytes 1048576 | tf_op jit(solution)/shard_map/filter_sources/pallas_call | solution.py:259
  29.6 18.7 %all_to_all.10.energy_ref = f32[16,8,128]{2,1,0:T(8,128)S(1)} all-to-all(f32[16,8,128]{2,1,0:T(8,128)S(1)} %get-tuple-element.32), channel_id=1, replica_groups={{0,2,4,6,8,10,12,14,16,18,20,22,24,26,28,30},{1,3,5,7,9,11,13,15,17,19,..., dimensions={0} | all-to-all | bytes 131072 | tf_op jit(solution)/shard_map/all_to_all | solution.py:444
  48.2 8.1 %correlate_first.1 = (f32[8,16,1024]{2,1,0:T(8,128)S(1)}, bf16[8,16,1024]{2,1,0:T(8,128)(2,1)S(1)}, bf16[256,8192]{1,0:T(8,128)(2,1)S(1)}, bf16[8448,128]{1,0:T(8,128)(2,1)S(1)}) custom-call(f32[16,8,128]{2,1,0:T(8,128)S(1)} %all_to_all.10.energy_ref, f32[8,8448]{1,0:T(8,128)S(1)} %get-tuple-element.33.traces_ref, f32[256,8192]{1,0:T(8,128)} %get-tuple-element.34.rows_ref), custom_call_target="tpu_custom_call" | custom-call | flops 4294967296 | bytes 16777216 | tf_op jit(solution)/shard_map/correlate_first/pallas_call | solution.py:321
  56.4 1.5 %collective-permute-start.8 = (bf16[8,16,1024]{2,1,0:T(8,128)(2,1)S(1)}, bf16[8,16,1024]{2,1,0:T(8,128)(2,1)S(1)}, u32[]{:S(2)}, u32[]{:S(2)}) collective-permute-start(bf16[8,16,1024]{2,1,0:T(8,128)(2,1)S(1)} %get-tuple-element.39), channel_id=1, source_target_pairs={{0,2},{1,3},{2,0},{3,1},{4,6},{5,7},{6,4},{7,5},{8,10},{9,11},{10,... | collective-permute-start | bytes 786440 | tf_op jit(solution)/shard_map/ppermute | solution.py:453
  57.8 4.5 %correlate_next.1 = (f32[8,16,1024]{2,1,0:T(8,128)S(1)}, bf16[8,16,1024]{2,1,0:T(8,128)(2,1)S(1)}) custom-call(bf16[256,8192]{1,0:T(8,128)(2,1)S(1)} %get-tuple-element.36.white_ref, bf16[8448,128]{1,0:T(8,128)(2,1)S(1)} %get-tuple-element.37.table_ref), custom_call_target="tpu_custom_call" | custom-call | flops 4294967296 | bytes 8388608 | tf_op jit(solution)/shard_map/correlate_next/pallas_call | solution.py:350
  62.3 0.7 collective-permute-start.9
  63.1 0.5 collective-permute-done.8.refs_2_
  63.6 5.7 %collective-permute-done.9.refs_3_ = bf16[8,16,1024]{2,1,0:T(8,128)(2,1)S(1)} collective-permute-done((bf16[8,16,1024]{2,1,0:T(8,128)(2,1)S(1)}, bf16[8,16,1024]{2,1,0:T(8,128)(2,1)S(1)}, u32[]{:S(2)}, u32[]{:S(2)}) %collective-permute-start.9) | collective-permute-done | bytes 262176 | tf_op jit(solution)/shard_map/ppermute | solution.py:455
  69.3 0.1 add_line.1
  69.4 18.1 %all_to_all.11.parts_ref = bf16[8,16,2048]{2,1,0:T(8,128)(2,1)S(1)} all-to-all(bf16[8,16,2048]{2,1,0:T(8,128)(2,1)S(1)} %add_line.1), channel_id=1, replica_groups={{0,4,8,12,16,20,24,28},{1,5,9,13,17,21,25,29},{2,6,10,14,18,22,26,30},{..., dimensions={0} | all-to-all | bytes 1048576 | tf_op jit(solution)/shard_map/all_to_all | solution.py:458
  87.4 1.3 %finish.1 = f32[16,2,4,256]{3,2,1,0:T(4,128)} custom-call(bf16[8,16,2048]{2,1,0:T(8,128)(2,1)S(1)} %all_to_all.11.parts_ref), custom_call_target="tpu_custom_call" | custom-call | bytes 1048576 | tf_op jit(solution)/shard_map/finish/pallas_call | solution.py:401
  (5 shorter events, 0.1 us)
Async XLA Ops:
  0.0 21.3 %copy-start = (bf16[512,4096]{1,0:T(8,128)(2,1)S(1)}, bf16[512,4096]{1,0:T(8,128)(2,1)}, u32[]{:S(2)}) copy-start(bf16[512,4096]{1,0:T(8,128)(2,1)} %param.4) | copy-start | bytes 12582916
  0.0 0.8 copy-start.1
  0.8 13.0 %copy-start.3 = (bf16[64]{0:T(256)(128)(2,1)S(1)}, bf16[64]{0:T(256)(128)(2,1)}, u32[]{:S(2)}) copy-start(bf16[64]{0:T(256)(128)(2,1)} %param.5) | copy-start | bytes 388
  0.8 20.4 %copy-start.2 = (s32[16]{0:T(128)S(1)}, s32[16]{0:T(128)}, u32[]{:S(2)}) copy-start(s32[16]{0:T(128)} %off_ref.3) | copy-start | bytes 196
  3.6 17.6 %collective-permute-start.6 = (bf16[16,16,4096]{2,1,0:T(8,128)(2,1)S(1)}, bf16[16,16,4096]{2,1,0:T(8,128)(2,1)S(1)}, u32[]{:S(2)}, u32[]{:S(2)}) collective-permute-start(bf16[16,16,4096]{2,1,0:T(8,128)(2,1)S(1)} %get-tuple-element.27), channel_id=1, source_target_pairs={{0,1},{1,0},{2,3},{3,2},{4,5},{5,4},{6,7},{7,6},{8,9},{9,8},{10,11... | collective-permute-start | bytes 6291464 | tf_op jit(solution)/shard_map/ppermute | solution.py:427
  3.7 6.2 %collective-permute-start = (bf16[17,16,128]{2,1,0:T(8,128)(2,1)S(1)}, bf16[17,16,128]{2,1,0:T(8,128)(2,1)S(1)}, u32[]{:S(2)}, u32[]{:S(2)}) collective-permute-start(bf16[17,16,128]{2,1,0:T(8,128)(2,1)S(1)} %get-tuple-element.24), channel_id=1, source_target_pairs={{1,2},{3,4},{5,6},{7,8},{9,10},{11,12},{13,14},{15,16},{17,18},{19... | collective-permute-start | bytes 208904 | tf_op jit(solution)/shard_map/ppermute | solution.py:426
  7.9 0.7 collective-permute-start.1
  9.9 4.3 %collective-permute-start.4 = (bf16[8,4352]{1,0:T(8,128)(2,1)S(1)}, bf16[8,4352]{1,0:T(8,128)(2,1)S(1)}, u32[]{:S(2)}, u32[]{:S(2)}) collective-permute-start(bf16[8,4352]{1,0:T(8,128)(2,1)S(1)} %extend_sources.1.refs_0_), channel_id=1, source_target_pairs={{0,192},{32,224},{64,0},{96,32},{128,64},{160,96},{192,128},{224,1... | collective-permute-start | bytes 208904 | tf_op jit(solution)/shard_map/ppermute | solution.py:433
  12.3 5.9 %collective-permute-start.3 = (bf16[8,4352]{1,0:T(8,128)(2,1)S(1)}, bf16[8,4352]{1,0:T(8,128)(2,1)S(1)}, u32[]{:S(2)}, u32[]{:S(2)}) collective-permute-start(bf16[8,4352]{1,0:T(8,128)(2,1)S(1)} %extend_sources.1.refs_0_), channel_id=1, source_target_pairs={{0,128},{32,160},{64,192},{96,224},{128,0},{160,32},{192,64},{224,... | collective-permute-start | bytes 208904 | tf_op jit(solution)/shard_map/ppermute | solution.py:433
  12.9 5.9 %collective-permute-start.2 = (bf16[8,4352]{1,0:T(8,128)(2,1)S(1)}, bf16[8,4352]{1,0:T(8,128)(2,1)S(1)}, u32[]{:S(2)}, u32[]{:S(2)}) collective-permute-start(bf16[8,4352]{1,0:T(8,128)(2,1)S(1)} %extend_sources.1.refs_0_), channel_id=1, source_target_pairs={{0,64},{32,96},{64,128},{96,160},{128,192},{160,224},{192,0},{224,... | collective-permute-start | bytes 208904 | tf_op jit(solution)/shard_map/ppermute | solution.py:433
  18.9 6.8 %collective-permute-start.5 = (bf16[8,4352]{1,0:T(8,128)(2,1)S(1)}, bf16[8,4352]{1,0:T(8,128)(2,1)S(1)}, u32[]{:S(2)}, u32[]{:S(2)}) collective-permute-start(bf16[8,4352]{1,0:T(8,128)(2,1)S(1)} %add_pieces.2.refs_0_), channel_id=1, source_target_pairs={{0,32},{32,0},{64,96},{96,64},{128,160},{160,128},{192,224},{224,1... | collective-permute-start | bytes 208904 | tf_op jit(solution)/shard_map/ppermute | solution.py:437
  25.7 2.9 %collective-permute-start.7 = (bf16[8,4352]{1,0:T(8,128)(2,1)S(1)}, bf16[8,4352]{1,0:T(8,128)(2,1)S(1)}, u32[]{:S(2)}, u32[]{:S(2)}) collective-permute-start(bf16[8,4352]{1,0:T(8,128)(2,1)S(1)} %add_pieces.3.mine_ref), channel_id=1, source_target_pairs={{0,1},{1,0},{2,3},{3,2},{4,5},{5,4},{6,7},{7,6},{8,9},{9,8},{10,11... | collective-permute-start | bytes 208904 | tf_op jit(solution)/shard_map/ppermute | solution.py:441
  56.4 7.2 %collective-permute-start.8 = (bf16[8,16,1024]{2,1,0:T(8,128)(2,1)S(1)}, bf16[8,16,1024]{2,1,0:T(8,128)(2,1)S(1)}, u32[]{:S(2)}, u32[]{:S(2)}) collective-permute-start(bf16[8,16,1024]{2,1,0:T(8,128)(2,1)S(1)} %get-tuple-element.39), channel_id=1, source_target_pairs={{0,2},{1,3},{2,0},{3,1},{4,6},{5,7},{6,4},{7,5},{8,10},{9,11},{10,... | collective-permute-start | bytes 786440 | tf_op jit(solution)/shard_map/ppermute | solution.py:453
  62.3 6.9 %collective-permute-start.9 = (bf16[8,16,1024]{2,1,0:T(8,128)(2,1)S(1)}, bf16[8,16,1024]{2,1,0:T(8,128)(2,1)S(1)}, u32[]{:S(2)}, u32[]{:S(2)}) collective-permute-start(bf16[8,16,1024]{2,1,0:T(8,128)(2,1)S(1)} %get-tuple-element.40), channel_id=1, source_target_pairs={{0,2},{1,3},{2,0},{3,1},{4,6},{5,7},{6,4},{7,5},{8,10},{9,11},{10,... | collective-permute-start | bytes 786440 | tf_op jit(solution)/shard_map/ppermute | solution.py:455

commit v7 on v6

--- a/solution.py
+++ b/solution.py
@@ -25,13 +25,16 @@
 ANY = pl.BlockSpec(memory_space=pl.ANY)
 
 
-def call(kernel, name, out, in_specs, scratch=(), out_specs=None, limit=16, flops=0, moved=0):
+def call(
+    kernel, name, out, in_specs, scratch=(), out_specs=None, limit=16, flops=0, moved=0, aliases=None
+):
     return pl.pallas_call(
         kernel,
         out_shape=out,
         in_specs=in_specs,
         out_specs=out_specs or [VMEM] * len(out),
         scratch_shapes=list(scratch),
+        input_output_aliases=aliases or {},
         compiler_params=pltpu.CompilerParams(vmem_limit_bytes=limit * MIB),
         cost_estimate=pl.CostEstimate(flops=flops, bytes_accessed=moved, transcendentals=0),
         name=name,
@@ -141,25 +144,27 @@
     )(*pieces)[0]
 
 
-def filter_rows(offsets, taps, x4, other, low_edge, high_edge):
-    groups, _, sub, half = x4.shape
+def filter_rows(offsets, taps, x4, other, edge, high, first_group, groups, filled=None):
+    all_groups, _, sub, half = x4.shape
+    filled = [] if filled is None else [filled]
     rows = groups * sub
+    chosen = slice(first_group, first_group + groups)
     chunk = 1024
     parts = half // chunk
     total = 2 * parts
 
     def kernel(
-        off_ref, taps_ref, x_ref, other_ref, low_ref, high_ref, out_ref, power_ref,
-        value_buf, sems
+        off_ref, taps_ref, x_ref, other_ref, edge_ref, high_ref, *refs
     ):
+        out_ref, power_ref, value_buf, sems = refs[len(filled) :]
         tile = lax.axis_index("tm")
         core = tile % 2
         matrix = fir_tile(taps_ref[...])
         first_kept = off_ref[tile // 2]
 
         def store(part):
-            cols = pl.ds(part * chunk, chunk)
-            return pltpu.make_async_copy(value_buf.at[part], out_ref.at[:, cols], sems.at[part])
+            place = out_ref.at[pl.ds(first_group * sub, rows), pl.ds(part * chunk, chunk)]
+            return pltpu.make_async_copy(value_buf.at[part], place, sems.at[part])
 
         def run(read_low, read_high, previous):
             power = jnp.zeros((rows, LANE), jnp.float32)
@@ -179,18 +184,18 @@
             power_ref[...] = power
 
         def own(cols):
-            return x_ref[:, core, :, cols]
+            return x_ref[chosen, core, :, cols]
 
         def swapped(cols):
-            return other_ref[:, :, cols]
+            return other_ref[chosen, :, cols]
 
         @pl.when(core == 0)
         def _():
-            run(own, swapped, low_ref[:groups].reshape(rows, LANE))
+            run(own, swapped, edge_ref[chosen].reshape(rows, LANE))
 
         @pl.when(core == 1)
         def _():
-            run(swapped, own, high_ref[...].reshape(rows, LANE))
+            run(swapped, own, high_ref[chosen].reshape(rows, LANE))
 
         for part in range(total):
             store(part).wait()
@@ -198,22 +203,24 @@
     return call(
         kernel,
         "filter_rows",
-        [shape((rows, 2 * half), jnp.float32), shape((rows, LANE), jnp.float32)],
-        [SMEM, VMEM, VMEM, VMEM, VMEM, VMEM],
+        [shape((all_groups * sub, 2 * half), jnp.float32), shape((rows, LANE), jnp.float32)],
+        [SMEM, VMEM, VMEM, VMEM, VMEM, VMEM] + [ANY] * len(filled),
         [pltpu.VMEM((total, rows, chunk), jnp.float32), pltpu.SemaphoreType.DMA((total,))],
         out_specs=[ANY, VMEM],
         limit=40,
         flops=2 * rows * 2 * half * 512,
-        moved=12 * MIB,
-    )(offsets, taps, x4, other, low_edge, high_edge)
-
-
-def filter_sources(offsets, taps, mine, other, power, chips):
+        moved=6 * MIB,
+        aliases={6: 0} if filled else None,
+    )(offsets, taps, x4, other, edge, high, *filled)
+
+
+def filter_sources(offsets, taps, mine, other, powers, chips):
     length = WIN + 2 * MAXLAG
     count = length // LANE
     half = mine.shape[1] - LEFT
 
-    def kernel(off_ref, taps_ref, mine_ref, other_ref, power_ref, out_ref, energy_ref):
+    def kernel(off_ref, taps_ref, mine_ref, other_ref, *refs):
+        *power_refs, out_ref, energy_ref = refs
         tile = lax.axis_index("tm")
         core, chip = tile % 2, tile // 2
         mine_rows = mine_ref[...].astype(jnp.float32)
@@ -247,9 +254,8 @@
                 keep = keep * jnp.where(chip < chips - 1, 1.0, 0.0)
             out_ref[:, j * LANE : (j + 1) * LANE] = piece * keep
         lines = []
-        for r in range(power_ref.shape[0] // LANE):
-            turned = power_ref[r * LANE : (r + 1) * LANE, :].T
-            lines.append(jnp.sum(turned, axis=0, keepdims=True))
+        for power_ref in power_refs:
+            lines.append(jnp.sum(power_ref[...].T, axis=0, keepdims=True))
         repeated = jnp.concatenate([total] * SHIFTS, axis=0)
         lines.append(jnp.sum(repeated.T, axis=0, keepdims=True))
         lines.append(jnp.zeros((8 - len(lines), LANE), jnp.float32))
@@ -260,9 +266,9 @@
         kernel,
         "filter_sources",
         [shape((NS, length), jnp.float32), shape((chips, 8, LANE), jnp.float32)],
-        [SMEM, VMEM, VMEM, VMEM, VMEM],
+        [SMEM, VMEM, VMEM, VMEM] + [VMEM] * len(powers),
         moved=MIB,
-    )(offsets, taps, mine, other, power)
+    )(offsets, taps, mine, other, *powers)
 
 
 def lag_products(white, table_ref, pairs, keep_ref, send_ref, half_groups):
@@ -282,28 +288,32 @@
         send_ref[:, :, cols] = jnp.where(own_low, high, low).astype(jnp.bfloat16)
 
 
-def correlate_first(energies, traces, rows, pairs, half_groups, total_samples):
-    channels, depth = rows.shape
+def correlate_first(energies, traces, row_blocks, pairs, half_groups, total_samples):
+    block_rows, depth = row_blocks[0].shape
+    parts = len(row_blocks)
+    channels = block_rows * parts
     length = traces.shape[1]
     chunk = 1024
     loads = depth // chunk
 
-    def kernel(
-        energy_ref, traces_ref, rows_ref, keep_ref, send_ref, white, table, buf, shifted, sems
-    ):
+    def kernel(energy_ref, traces_ref, *refs):
+        row_refs = refs[:parts]
+        keep_ref, send_ref, white, table, buf, shifted, sems = refs[parts:]
         copies = []
         for i in range(loads):
-            cols = pl.ds(i * chunk, chunk)
-            copies.append(pltpu.make_async_copy(rows_ref.at[:, cols], buf.at[i], sems.at[i]))
+            for r, rows_ref in enumerate(row_refs):
+                source = rows_ref.at[:, pl.ds(i * chunk, chunk)]
+                place = buf.at[i, pl.ds(r * block_rows, block_rows)]
+                copies.append(pltpu.make_async_copy(source, place, sems.at[i * parts + r]))
         for copy in copies:
             copy.start()
         energy = jnp.sum(energy_ref[...], axis=0)
         scale = lax.rsqrt(energy / total_samples + EPS)
         padded = jnp.concatenate([scale, jnp.zeros((LANE - 8, LANE), jnp.float32)], axis=0)
         turned = padded.T
-        parts = channels // LANE
-        gain = jnp.concatenate([turned[:, r : r + 1] for r in range(parts)], axis=0)
-        trace = traces_ref[...] * turned[:NS, parts : parts + 1]
+        blocks = channels // LANE
+        gain = jnp.concatenate([turned[:, r : r + 1] for r in range(blocks)], axis=0)
+        trace = traces_ref[...] * turned[:NS, blocks : blocks + 1]
         trace = trace.astype(jnp.bfloat16).astype(jnp.float32)
         for b in range(SHIFTS):
             moved = trace if b == 0 else pltpu.roll(trace, length - b, 1)
@@ -312,7 +322,8 @@
             cols = slice(j * LANE, (j + 1) * LANE)
             table[cols, :] = shifted[:, cols].T.astype(jnp.bfloat16)
         for i in range(loads):
-            copies[i].wait()
+            for copy in copies[i * parts : (i + 1) * parts]:
+                copy.wait()
             white[:, i * chunk : (i + 1) * chunk] = (buf[i] * gain).astype(jnp.bfloat16)
         lag_products(white, table, pairs, keep_ref, send_ref, half_groups)
 
@@ -327,16 +338,16 @@
             shape((channels, depth), jnp.bfloat16),
             shape((length, LANE), jnp.bfloat16),
         ],
-        [VMEM, VMEM, ANY],
+        [VMEM, VMEM] + [ANY] * parts,
         [
             pltpu.VMEM((loads, channels, chunk), jnp.float32),
             pltpu.VMEM((LANE, length), jnp.float32),
-            pltpu.SemaphoreType.DMA((loads,)),
+            pltpu.SemaphoreType.DMA((loads * parts,)),
         ],
         limit=40,
         flops=2 * channels * depth * cols,
         moved=16 * MIB,
-    )(energies, traces, rows)
+    )(energies, traces, *row_blocks)
 
 
 def correlate_next(white, table, pairs, half_groups):
@@ -433,27 +444,38 @@
         lax.ppermute(piece, "chan", [(i, (i + 2 * d) % groups_chan) for i in range(groups_chan)])
         for d in range(1, groups_chan // 2)
     ]
+    half = chips // 2
+    filtered, power_a = filter_rows(window_offsets, taps, x4, other, edge, high, 0, half)
+    *parts, power_a = lax.optimization_barrier((*parts, power_a))
     piece = add_pieces(piece, *parts)
     arrived = lax.ppermute(piece, "chan", [(i, i ^ 1) for i in range(groups_chan)])
-    filtered, power = filter_rows(window_offsets, taps, x4, other, edge, high)
-    arrived, power = lax.optimization_barrier((arrived, power))
+    filtered, power_b = filter_rows(
+        window_offsets, taps, x4, other, edge, high, half, half, filtered
+    )
+    arrived, power_b = lax.optimization_barrier((arrived, power_b))
     piece = add_pieces(piece, arrived)
     piece_other = lax.ppermute(piece, "tm", swap)
-    traces, energy = filter_sources(window_offsets, taps, piece, piece_other, power, chips)
+    traces, energy = filter_sources(
+        window_offsets, taps, piece, piece_other, [power_a, power_b], chips
+    )
     same = [[2 * k + c for k in range(chips)] for c in range(2)]
     energies = lax.all_to_all(energy, "tm", 0, 0, tiled=True, axis_index_groups=same)
 
     column = tiles // 4
     dots = LAGS // (2 * SHIFTS)
-    first, second = range(dots // 2), range(dots // 2, dots)
-    keep_a, send_a, white, table = correlate_first(
-        energies, traces, filtered, first, column, total_samples
+    splits = [range(0, dots // 4), range(dots // 4, dots * 5 // 8), range(dots * 5 // 8, dots)]
+    line = [(i, i ^ 2) for i in range(tiles)]
+    keep, send, white, table = correlate_first(
+        energies, traces, [filtered], splits[0], column, total_samples
     )
-    line = [(i, i ^ 2) for i in range(tiles)]
-    across_a = lax.ppermute(send_a, "tm", line)
-    keep_b, send_b = correlate_next(white, table, second, column)
-    across_b = lax.ppermute(send_b, "tm", line)
-    summed = add_line([keep_a, keep_b], [across_a, across_b])
+    keeps, arrivals = [keep], [lax.ppermute(send, "tm", line)]
+    for pairs in splits[1:]:
+        if len(keeps) > 1:
+            white, arrivals[-2] = lax.optimization_barrier((white, arrivals[-2]))
+        keep, send = correlate_next(white, table, pairs, column)
+        keeps.append(keep)
+        arrivals.append(lax.ppermute(send, "tm", line))
+    summed = add_line(keeps, arrivals)
     columns = [[4 * z + r for z in range(column)] for r in range(4)]
     parts = lax.all_to_all(summed, "tm", 0, 0, tiled=True, axis_index_groups=columns)
     return finish(parts, 1.0 / math.sqrt(total_samples))

time: 89.1 us -> 87.4 us (0.981)
  waiting for transfers between devices: 13.4 us -> 9.08 us
  Pallas kernels: 22.2 us -> 24 us
  starting transfers between devices: 15.4 us -> 16.4 us
    ppermute x3, waiting for transfers between devices: 5.02 us -> 2.04 us  [shards(): lax.ppermute(piece, 'chan', [(i, (i + 2 * d) % groups_chan) for i in rang...]
    pallas_call x1 -> x2, Pallas kernels: 4.48 us -> 6.8 us  [correlate_next(): call(kernel, 'correlate_next', [shape((half_groups, sub, cols), jnp.float...]
    pallas_call x1, Pallas kernels: 8.13 us -> 5.97 us  [correlate_first(): call(kernel, 'correlate_first', [shape((half_groups, sub, cols), jnp.floa...]
    ppermute x2 -> x3, waiting for transfers between devices: 6.2 us -> 4.36 us  [the longest x2 4.36 us: shards(): arrivals.append(lax.ppermute(send, 'tm', line))]
    pallas_call x1 -> x2, Pallas kernels: 4.36 us -> 5.97 us  [filter_rows(): call(kernel, 'filter_rows', [shape((all_groups * sub, 2 * half), jnp.floa...]
    ppermute x2 -> x3, starting transfers between devices: 2.2 us -> 3.66 us  [the longest x2 2.2 us: shards(): arrivals.append(lax.ppermute(send, 'tm', line))]
  transfers between devices with their start and end apart: 10 -> 11, of which waited for: 7 -> 7; matrix products, arithmetic and copies ran while one was open for 0% -> 0% of each run, Pallas kernels for 10% -> 15%
where the time goes in v7:
time: 87.4 us; the launch traced here: 87.2 us
  blocking collectives  36.8 us (42%)
  Pallas kernels  24 us (27%)
  starting transfers between devices  16.4 us (19%)
  waiting for transfers between devices  9.08 us (10%)
    all_to_all x1, blocking collectives, shards(): lax.all_to_all(energy, 'tm', 0, 0, tiled=True, axis_index_groups=same)  18.7 us
    all_to_all x1, blocking collectives, shards(): lax.all_to_all(summed, 'tm', 0, 0, tiled=True, axis_index_groups=columns)  18.1 us
    pallas_call x2, Pallas kernels, correlate_next(): call(kernel, 'correlate_next', [shape((half_groups, sub, cols), jnp.float...  6.8 us
    pallas_call x1, Pallas kernels, correlate_first(): call(kernel, 'correlate_first', [shape((half_groups, sub, cols), jnp.floa...  5.97 us
    pallas_call x2, Pallas kernels, filter_rows(): call(kernel, 'filter_rows', [shape((all_groups * sub, 2 * half), jnp.floa...  5.97 us
    ppermute x2, waiting for transfers between devices, shards(): arrivals.append(lax.ppermute(send, 'tm', line))  4.36 us
    ppermute x1, starting transfers between devices, shards(): edge = lax.ppermute(edge, 'tm', both_next)  4.18 us
    ppermute x3, starting transfers between devices, shards(): lax.ppermute(piece, 'chan', [(i, (i + 2 * d) % groups_chan) for i in rang...  3.9 us
  transfers between devices with their start and end apart: 11, of which 7 were waited for; matrix products, arithmetic and copies ran while one was open for 0% of the time, Pallas kernels for 15%

profile of v7, /device:TPU:8, one launch (start us, length us, event | category | flops | bytes accessed | tf_op | source)
XLA Modules:
  0.0 87.2 jit_solution(13867159713666452325)
XLA Ops:
  0.0 0.0 copy-start
  0.0 0.0 copy-start.1
  0.0 0.0 copy-start.2
  0.0 0.8 copy-done.2
  0.8 0.0 copy-start.3
  0.8 2.8 %pick_sources.1 = (bf16[8,4096]{1,0:T(8,128)(2,1)S(1)}, bf16[17,16,128]{2,1,0:T(8,128)(2,1)S(1)}, bf16[16,16,128]{2,1,0:T(8,128)(2,1)S(1)}, bf16[16,16,4096]{2,1,0:T(8,128)(2,1)S(1)}) custom-call(s32[2,4]{1,0:T(2,128)S(1)} %copy-done.2, bf16[16,2,16,4096]{3,2,1,0:T(8,128)(2,1)} %bitcast.1), custom_call_target="tpu_custom_call" | custom-call | bytes 2097152 | tf_op jit(solution)/shard_map/pick_sources/pallas_call | solution.py:99
  3.6 0.1 collective-permute-start.5
  3.7 4.2 %collective-permute-start = (bf16[17,16,128]{2,1,0:T(8,128)(2,1)S(1)}, bf16[17,16,128]{2,1,0:T(8,128)(2,1)S(1)}, u32[]{:S(2)}, u32[]{:S(2)}) collective-permute-start(bf16[17,16,128]{2,1,0:T(8,128)(2,1)S(1)} %get-tuple-element.34), channel_id=1, source_target_pairs={{1,2},{3,4},{5,6},{7,8},{9,10},{11,12},{13,14},{15,16},{17,18},{19... | collective-permute-start | bytes 208904 | tf_op jit(solution)/shard_map/ppermute | solution.py:437
  7.9 0.7 collective-permute-start.1
  8.6 0.0 copy-done.3
  8.6 0.0 collective-permute-done.1.high_ref
  8.6 1.3 %collective-permute-done.edge_ref = bf16[17,16,128]{2,1,0:T(8,128)(2,1)S(1)} collective-permute-done((bf16[17,16,128]{2,1,0:T(8,128)(2,1)S(1)}, bf16[17,16,128]{2,1,0:T(8,128)(2,1)S(1)}, u32[]{:S(2)}, u32[]{:S(2)}) %collective-permute-start) | collective-permute-done | bytes 69664 | tf_op jit(solution)/shard_map/ppermute | solution.py:437
  9.9 2.4 %collective-permute-start.4 = (bf16[8,4352]{1,0:T(8,128)(2,1)S(1)}, bf16[8,4352]{1,0:T(8,128)(2,1)S(1)}, u32[]{:S(2)}, u32[]{:S(2)}) collective-permute-start(bf16[8,4352]{1,0:T(8,128)(2,1)S(1)} %extend_sources.1.refs_0_), channel_id=1, source_target_pairs={{0,192},{32,224},{64,0},{96,32},{128,64},{160,96},{192,128},{224,1... | collective-permute-start | bytes 208904 | tf_op jit(solution)/shard_map/ppermute | solution.py:444
  12.3 0.6 collective-permute-start.3
  12.9 0.9 %collective-permute-start.2 = (bf16[8,4352]{1,0:T(8,128)(2,1)S(1)}, bf16[8,4352]{1,0:T(8,128)(2,1)S(1)}, u32[]{:S(2)}, u32[]{:S(2)}) collective-permute-start(bf16[8,4352]{1,0:T(8,128)(2,1)S(1)} %extend_sources.1.refs_0_), channel_id=1, source_target_pairs={{0,64},{32,96},{64,128},{96,160},{128,192},{160,224},{192,0},{224,... | collective-permute-start | bytes 208904 | tf_op jit(solution)/shard_map/ppermute | solution.py:444
  13.8 0.0 collective-permute-done.5.other_ref
  13.8 0.0 copy-done
  13.8 0.0 copy-done.1
  13.8 3.0 %filter_rows.2 = (f32[256,8192]{1,0:T(8,128)}, f32[128,128]{1,0:T(8,128)S(1)}) custom-call(s32[16]{0:T(128)S(1)} %copy-done.1, bf16[1,256]{1,0:T(2,128)(2,1)S(1)} %reshape.6.taps_ref, bf16[16,2,16,4096]{3,2,1,0:T(8,128)(2,1)S(1)} %bitcast.2, bf16[16,16,4096]{2,1,0:T(8,128)(2,1)S(1)} %collective-permute-done.5.other_ref, ...), custom_call_target="tpu_custom_call" | custom-call | flops 1073741824 | bytes 6291456 | tf_op jit(solution)/shard_map/filter_rows/pallas_call | solution.py:203
  16.8 0.0 collective-permute-done.4.refs_3_
  16.8 1.3 %collective-permute-done.3.refs_2_ = bf16[8,4352]{1,0:T(8,128)(2,1)S(1)} collective-permute-done((bf16[8,4352]{1,0:T(8,128)(2,1)S(1)}, bf16[8,4352]{1,0:T(8,128)(2,1)S(1)}, u32[]{:S(2)}, u32[]{:S(2)}) %collective-permute-start.3) | collective-permute-done | bytes 69664 | tf_op jit(solution)/shard_map/ppermute | solution.py:444
  18.1 0.7 collective-permute-done.2.refs_1_
  18.9 2.4 %collective-permute-start.6 = (bf16[8,4352]{1,0:T(8,128)(2,1)S(1)}, bf16[8,4352]{1,0:T(8,128)(2,1)S(1)}, u32[]{:S(2)}, u32[]{:S(2)}) collective-permute-start(bf16[8,4352]{1,0:T(8,128)(2,1)S(1)} %add_pieces.2.refs_0_), channel_id=1, source_target_pairs={{0,32},{32,0},{64,96},{96,64},{128,160},{160,128},{192,224},{224,1... | collective-permute-start | bytes 208904 | tf_op jit(solution)/shard_map/ppermute | solution.py:451
  21.3 3.0 %filter_rows.3 = (f32[256,8192]{1,0:T(8,128)}, f32[128,128]{1,0:T(8,128)S(1)}) custom-call(s32[16]{0:T(128)S(1)} %copy-done.1, bf16[1,256]{1,0:T(2,128)(2,1)S(1)} %reshape.6.taps_ref, bf16[16,2,16,4096]{3,2,1,0:T(8,128)(2,1)S(1)} %bitcast.3, bf16[16,16,4096]{2,1,0:T(8,128)(2,1)S(1)} %collective-permute-done.5.other_ref, ...), custom_call_target="tpu_custom_call", output_to_operand_aliasing={{0}: (6, {})} | custom-call | flops 1073741824 | bytes 6291456 | tf_op jit(solution)/shard_map/filter_rows/pallas_call | solution.py:203
  24.3 0.5 collective-permute-done.6.refs_1_
  24.8 1.5 %collective-permute-start.7 = (bf16[8,4352]{1,0:T(8,128)(2,1)S(1)}, bf16[8,4352]{1,0:T(8,128)(2,1)S(1)}, u32[]{:S(2)}, u32[]{:S(2)}) collective-permute-start(bf16[8,4352]{1,0:T(8,128)(2,1)S(1)} %add_pieces.3.mine_ref), channel_id=1, source_target_pairs={{0,1},{1,0},{2,3},{3,2},{4,5},{5,4},{6,7},{7,6},{8,9},{9,8},{10,11... | collective-permute-start | bytes 208904 | tf_op jit(solution)/shard_map/ppermute | solution.py:457
  26.3 0.9 %collective-permute-done.7.other_ref = bf16[8,4352]{1,0:T(8,128)(2,1)S(1)} collective-permute-done((bf16[8,4352]{1,0:T(8,128)(2,1)S(1)}, bf16[8,4352]{1,0:T(8,128)(2,1)S(1)}, u32[]{:S(2)}, u32[]{:S(2)}) %collective-permute-start.7) | collective-permute-done | bytes 69664 | tf_op jit(solution)/shard_map/ppermute | solution.py:457
  27.2 1.0 %filter_sources.1 = (f32[8,8448]{1,0:T(8,128)S(1)}, f32[16,8,128]{2,1,0:T(8,128)S(1)}) custom-call(s32[16]{0:T(128)S(1)} %copy-done.1, bf16[1,256]{1,0:T(2,128)(2,1)S(1)} %reshape.6.taps_ref, bf16[8,4352]{1,0:T(8,128)(2,1)S(1)} %add_pieces.3.mine_ref, bf16[8,4352]{1,0:T(8,128)(2,1)S(1)} %collective-permute-done.7.other_ref, ...), custom_call_target="tpu_custom_call" | custom-call | bytes 1048576 | tf_op jit(solution)/shard_map/filter_sources/pallas_call | solution.py:265
  28.2 18.7 %all_to_all.10.energy_ref = f32[16,8,128]{2,1,0:T(8,128)S(1)} all-to-all(f32[16,8,128]{2,1,0:T(8,128)S(1)} %get-tuple-element.48), channel_id=1, replica_groups={{0,2,4,6,8,10,12,14,16,18,20,22,24,26,28,30},{1,3,5,7,9,11,13,15,17,19,..., dimensions={0} | all-to-all | bytes 131072 | tf_op jit(solution)/shard_map/all_to_all | solution.py:462
  46.9 6.0 %correlate_first.1 = (f32[8,16,512]{2,1,0:T(8,128)S(1)}, bf16[8,16,512]{2,1,0:T(8,128)(2,1)S(1)}, bf16[256,8192]{1,0:T(8,128)(2,1)S(1)}, bf16[8448,128]{1,0:T(8,128)(2,1)S(1)}) custom-call(f32[16,8,128]{2,1,0:T(8,128)S(1)} %all_to_all.10.energy_ref, f32[8,8448]{1,0:T(8,128)S(1)} %get-tuple-element.49.traces_ref, f32[256,8192]{1,0:T(8,128)} %get-tuple-element.50.refs_0_), custom_call_target="tpu_custom_call" | custom-call | flops 2147483648 | bytes 16777216 | tf_op jit(solution)/shard_map/correlate_first/pallas_call | solution.py:332
  52.8 1.5 %collective-permute-start.8 = (bf16[8,16,512]{2,1,0:T(8,128)(2,1)S(1)}, bf16[8,16,512]{2,1,0:T(8,128)(2,1)S(1)}, u32[]{:S(2)}, u32[]{:S(2)}) collective-permute-start(bf16[8,16,512]{2,1,0:T(8,128)(2,1)S(1)} %get-tuple-element.55), channel_id=1, source_target_pairs={{0,2},{1,3},{2,0},{3,1},{4,6},{5,7},{6,4},{7,5},{8,10},{9,11},{10,... | collective-permute-start | bytes 393224 | tf_op jit(solution)/shard_map/ppermute | solution.py:471
  54.3 3.4 %correlate_next.2 = (f32[8,16,768]{2,1,0:T(8,128)S(1)}, bf16[8,16,768]{2,1,0:T(8,128)(2,1)S(1)}) custom-call(bf16[256,8192]{1,0:T(8,128)(2,1)S(1)} %get-tuple-element.56.white_ref, bf16[8448,128]{1,0:T(8,128)(2,1)S(1)} %get-tuple-element.53.table_ref), custom_call_target="tpu_custom_call" | custom-call | flops 3221225472 | bytes 8388608 | tf_op jit(solution)/shard_map/correlate_next/pallas_call | solution.py:361
  57.7 0.7 collective-permute-start.9
  58.5 0.0 collective-permute-done.8.refs_3_
  58.5 3.4 %correlate_next.3 = (f32[8,16,768]{2,1,0:T(8,128)S(1)}, bf16[8,16,768]{2,1,0:T(8,128)(2,1)S(1)}) custom-call(bf16[256,8192]{1,0:T(8,128)(2,1)S(1)} %get-tuple-element.56.white_ref, bf16[8448,128]{1,0:T(8,128)(2,1)S(1)} %get-tuple-element.53.table_ref), custom_call_target="tpu_custom_call" | custom-call | flops 3221225472 | bytes 8388608 | tf_op jit(solution)/shard_map/correlate_next/pallas_call | solution.py:361
  61.9 1.5 %collective-permute-start.10 = (bf16[8,16,768]{2,1,0:T(8,128)(2,1)S(1)}, bf16[8,16,768]{2,1,0:T(8,128)(2,1)S(1)}, u32[]{:S(2)}, u32[]{:S(2)}) collective-permute-start(bf16[8,16,768]{2,1,0:T(8,128)(2,1)S(1)} %get-tuple-element.60), channel_id=1, source_target_pairs={{0,2},{1,3},{2,0},{3,1},{4,6},{5,7},{6,4},{7,5},{8,10},{9,11},{10,... | collective-permute-start | bytes 589832 | tf_op jit(solution)/shard_map/ppermute | solution.py:477
  63.3 0.7 collective-permute-done.9.refs_4_
  64.0 3.7 %collective-permute-done.10.refs_5_ = bf16[8,16,768]{2,1,0:T(8,128)(2,1)S(1)} collective-permute-done((bf16[8,16,768]{2,1,0:T(8,128)(2,1)S(1)}, bf16[8,16,768]{2,1,0:T(8,128)(2,1)S(1)}, u32[]{:S(2)}, u32[]{:S(2)}) %collective-permute-start.10) | collective-permute-done | bytes 196640 | tf_op jit(solution)/shard_map/ppermute | solution.py:477
  67.7 0.1 add_line.1
  67.8 18.1 %all_to_all.11.parts_ref = bf16[8,16,2048]{2,1,0:T(8,128)(2,1)S(1)} all-to-all(bf16[8,16,2048]{2,1,0:T(8,128)(2,1)S(1)} %add_line.1), channel_id=1, replica_groups={{0,4,8,12,16,20,24,28},{1,5,9,13,17,21,25,29},{2,6,10,14,18,22,26,30},{..., dimensions={0} | all-to-all | bytes 1048576 | tf_op jit(solution)/shard_map/all_to_all | solution.py:480
  85.8 1.3 %finish.1 = f32[16,2,4,256]{3,2,1,0:T(4,128)} custom-call(bf16[8,16,2048]{2,1,0:T(8,128)(2,1)S(1)} %all_to_all.11.parts_ref), custom_call_target="tpu_custom_call" | custom-call | bytes 1048576 | tf_op jit(solution)/shard_map/finish/pallas_call | solution.py:412
  (5 shorter events, 0.1 us)
Async XLA Ops:
  0.0 13.8 %copy-start = (bf16[512,4096]{1,0:T(8,128)(2,1)S(1)}, bf16[512,4096]{1,0:T(8,128)(2,1)}, u32[]{:S(2)}) copy-start(bf16[512,4096]{1,0:T(8,128)(2,1)} %param.4) | copy-start | bytes 12582916
  0.0 13.8 %copy-start.1 = (s32[16]{0:T(128)S(1)}, s32[16]{0:T(128)}, u32[]{:S(2)}) copy-start(s32[16]{0:T(128)} %off_ref.5) | copy-start | bytes 196
  0.0 0.8 copy-start.2
  0.8 7.7 %copy-start.3 = (bf16[64]{0:T(256)(128)(2,1)S(1)}, bf16[64]{0:T(256)(128)(2,1)}, u32[]{:S(2)}) copy-start(bf16[64]{0:T(256)(128)(2,1)} %param.5) | copy-start | bytes 388
  3.6 10.2 %collective-permute-start.5 = (bf16[16,16,4096]{2,1,0:T(8,128)(2,1)S(1)}, bf16[16,16,4096]{2,1,0:T(8,128)(2,1)S(1)}, u32[]{:S(2)}, u32[]{:S(2)}) collective-permute-start(bf16[16,16,4096]{2,1,0:T(8,128)(2,1)S(1)} %get-tuple-element.37), channel_id=1, source_target_pairs={{0,1},{1,0},{2,3},{3,2},{4,5},{5,4},{6,7},{7,6},{8,9},{9,8},{10,11... | collective-permute-start | bytes 6291464 | tf_op jit(solution)/shard_map/ppermute | solution.py:438
  3.7 6.2 %collective-permute-start = (bf16[17,16,128]{2,1,0:T(8,128)(2,1)S(1)}, bf16[17,16,128]{2,1,0:T(8,128)(2,1)S(1)}, u32[]{:S(2)}, u32[]{:S(2)}) collective-permute-start(bf16[17,16,128]{2,1,0:T(8,128)(2,1)S(1)} %get-tuple-element.34), channel_id=1, source_target_pairs={{1,2},{3,4},{5,6},{7,8},{9,10},{11,12},{13,14},{15,16},{17,18},{19... | collective-permute-start | bytes 208904 | tf_op jit(solution)/shard_map/ppermute | solution.py:437
  7.9 0.7 collective-permute-start.1
  9.9 6.9 %collective-permute-start.4 = (bf16[8,4352]{1,0:T(8,128)(2,1)S(1)}, bf16[8,4352]{1,0:T(8,128)(2,1)S(1)}, u32[]{:S(2)}, u32[]{:S(2)}) collective-permute-start(bf16[8,4352]{1,0:T(8,128)(2,1)S(1)} %extend_sources.1.refs_0_), channel_id=1, source_target_pairs={{0,192},{32,224},{64,0},{96,32},{128,64},{160,96},{192,128},{224,1... | collective-permute-start | bytes 208904 | tf_op jit(solution)/shard_map/ppermute | solution.py:444
  12.3 5.9 %collective-permute-start.3 = (bf16[8,4352]{1,0:T(8,128)(2,1)S(1)}, bf16[8,4352]{1,0:T(8,128)(2,1)S(1)}, u32[]{:S(2)}, u32[]{:S(2)}) collective-permute-start(bf16[8,4352]{1,0:T(8,128)(2,1)S(1)} %extend_sources.1.refs_0_), channel_id=1, source_target_pairs={{0,128},{32,160},{64,192},{96,224},{128,0},{160,32},{192,64},{224,... | collective-permute-start | bytes 208904 | tf_op jit(solution)/shard_map/ppermute | solution.py:444
  12.9 5.9 %collective-permute-start.2 = (bf16[8,4352]{1,0:T(8,128)(2,1)S(1)}, bf16[8,4352]{1,0:T(8,128)(2,1)S(1)}, u32[]{:S(2)}, u32[]{:S(2)}) collective-permute-start(bf16[8,4352]{1,0:T(8,128)(2,1)S(1)} %extend_sources.1.refs_0_), channel_id=1, source_target_pairs={{0,64},{32,96},{64,128},{96,160},{128,192},{160,224},{192,0},{224,... | collective-permute-start | bytes 208904 | tf_op jit(solution)/shard_map/ppermute | solution.py:444
  18.9 5.9 %collective-permute-start.6 = (bf16[8,4352]{1,0:T(8,128)(2,1)S(1)}, bf16[8,4352]{1,0:T(8,128)(2,1)S(1)}, u32[]{:S(2)}, u32[]{:S(2)}) collective-permute-start(bf16[8,4352]{1,0:T(8,128)(2,1)S(1)} %add_pieces.2.refs_0_), channel_id=1, source_target_pairs={{0,32},{32,0},{64,96},{96,64},{128,160},{160,128},{192,224},{224,1... | collective-permute-start | bytes 208904 | tf_op jit(solution)/shard_map/ppermute | solution.py:451
  24.8 2.4 %collective-permute-start.7 = (bf16[8,4352]{1,0:T(8,128)(2,1)S(1)}, bf16[8,4352]{1,0:T(8,128)(2,1)S(1)}, u32[]{:S(2)}, u32[]{:S(2)}) collective-permute-start(bf16[8,4352]{1,0:T(8,128)(2,1)S(1)} %add_pieces.3.mine_ref), channel_id=1, source_target_pairs={{0,1},{1,0},{2,3},{3,2},{4,5},{5,4},{6,7},{7,6},{8,9},{9,8},{10,11... | collective-permute-start | bytes 208904 | tf_op jit(solution)/shard_map/ppermute | solution.py:457
  52.8 5.6 %collective-permute-start.8 = (bf16[8,16,512]{2,1,0:T(8,128)(2,1)S(1)}, bf16[8,16,512]{2,1,0:T(8,128)(2,1)S(1)}, u32[]{:S(2)}, u32[]{:S(2)}) collective-permute-start(bf16[8,16,512]{2,1,0:T(8,128)(2,1)S(1)} %get-tuple-element.55), channel_id=1, source_target_pairs={{0,2},{1,3},{2,0},{3,1},{4,6},{5,7},{6,4},{7,5},{8,10},{9,11},{10,... | collective-permute-start | bytes 393224 | tf_op jit(solution)/shard_map/ppermute | solution.py:471
  57.7 6.3 %collective-permute-start.9 = (bf16[8,16,768]{2,1,0:T(8,128)(2,1)S(1)}, bf16[8,16,768]{2,1,0:T(8,128)(2,1)S(1)}, u32[]{:S(2)}, u32[]{:S(2)}) collective-permute-start(bf16[8,16,768]{2,1,0:T(8,128)(2,1)S(1)} %get-tuple-element.59), channel_id=1, source_target_pairs={{0,2},{1,3},{2,0},{3,1},{4,6},{5,7},{6,4},{7,5},{8,10},{9,11},{10,... | collective-permute-start | bytes 589832 | tf_op jit(solution)/shard_map/ppermute | solution.py:477
  61.9 5.8 %collective-permute-start.10 = (bf16[8,16,768]{2,1,0:T(8,128)(2,1)S(1)}, bf16[8,16,768]{2,1,0:T(8,128)(2,1)S(1)}, u32[]{:S(2)}, u32[]{:S(2)}) collective-permute-start(bf16[8,16,768]{2,1,0:T(8,128)(2,1)S(1)} %get-tuple-element.60), channel_id=1, source_target_pairs={{0,2},{1,3},{2,0},{3,1},{4,6},{5,7},{6,4},{7,5},{8,10},{9,11},{10,... | collective-permute-start | bytes 589832 | tf_op jit(solution)/shard_map/ppermute | solution.py:477

commit v8 on v7

--- a/solution.py
+++ b/solution.py
@@ -59,7 +59,7 @@
     groups, _, sub, samples = x4.shape
     channels = groups * 2 * sub
 
-    def kernel(ids_ref, x_ref, own_ref, edge_ref, high_ref, away_ref, buf, sems):
+    def kernel(ids_ref, x_ref, own_ref, tail_ref, away_ref, buf, sems):
         base = lax.axis_index("chan") * channels
         core = lax.axis_index("tm") % 2
         copies = []
@@ -73,11 +73,8 @@
             copies.append(pltpu.make_async_copy(x_ref.at[group, half], buf.at[j], sems.at[j]))
         last = pl.ds(samples - LANE, LANE)
         rest = [
-            pltpu.make_async_copy(
-                x_ref.at[:, 0, :, last], edge_ref.at[pl.ds(0, groups)], sems.at[NS]
-            ),
-            pltpu.make_async_copy(x_ref.at[:, 1, :, last], high_ref, sems.at[NS + 1]),
-            pltpu.make_async_copy(x_ref.at[:, 1 - core], away_ref, sems.at[NS + 2]),
+            pltpu.make_async_copy(x_ref.at[:, :, :, last], tail_ref, sems.at[NS]),
+            pltpu.make_async_copy(x_ref.at[:, 1 - core], away_ref, sems.at[NS + 1]),
         ]
         for copy in copies + rest:
             copy.start()
@@ -89,44 +86,55 @@
             picked = picked[:NS] + picked[NS:]
             own = own + pltpu.roll(picked, (j + NS - inner[j] % NS) % NS, 0)
         own_ref[...] = own.astype(jnp.bfloat16)
-        end = jnp.where(core == 1, own[:, samples - LEFT :], own[:, :LEFT])
         for copy in rest:
             copy.wait()
-        edge_ref[groups] = jnp.concatenate(
-            [end[:, :LANE], end[:, LANE:]], axis=0
-        ).astype(jnp.bfloat16)
 
     return call(
         kernel,
         "pick_sources",
         [
             shape((NS, samples), jnp.bfloat16),
-            shape((groups + 1, sub, LANE), jnp.bfloat16),
-            shape((groups, sub, LANE), jnp.bfloat16),
+            shape((groups, 2, sub, LANE), jnp.bfloat16),
             shape((groups, sub, samples), jnp.bfloat16),
         ],
         [SMEM, ANY],
-        [pltpu.VMEM((NS, sub, samples), jnp.bfloat16), pltpu.SemaphoreType.DMA((NS + 3,))],
+        [pltpu.VMEM((NS, sub, samples), jnp.bfloat16), pltpu.SemaphoreType.DMA((NS + 2,))],
         limit=50,
-        moved=2 * MIB,
+        moved=4 * MIB,
     )(source_channels, x4)
 
 
-def extend_sources(own, edge):
-    samples = own.shape[1]
-    groups = edge.shape[0] - 1
-
-    def kernel(own_ref, edge_ref, out_ref):
-        end = edge_ref[groups].astype(jnp.float32)
-        joined = [own_ref[...].astype(jnp.float32), end[:NS], end[NS:]]
-        out_ref[...] = jnp.concatenate(joined, axis=1).astype(jnp.bfloat16)
+def join_sources(piece, arrived):
+    samples = piece.shape[1]
+
+    def kernel(piece_ref, arrived_ref, out_ref, end_ref):
+        core = lax.axis_index("tm") % 2
+        total = piece_ref[...].astype(jnp.float32) + arrived_ref[...].astype(jnp.float32)
+        out_ref[...] = total.astype(jnp.bfloat16)
+        end = jnp.where(core == 1, total[:, samples - LEFT :], total[:, :LEFT])
+        end_ref[...] = end.astype(jnp.bfloat16)
+
+    return call(
+        kernel,
+        "join_sources",
+        [shape(piece.shape, jnp.bfloat16), shape((NS, LEFT), jnp.bfloat16)],
+        [VMEM, VMEM],
+    )(piece, arrived)
+
+
+def extend_sources(piece, edge):
+    samples = piece.shape[1]
+
+    def kernel(piece_ref, edge_ref, out_ref):
+        out_ref[:, :samples] = piece_ref[...]
+        out_ref[:, samples:] = edge_ref[...]
 
     return call(
         kernel,
         "extend_sources",
         [shape((NS, samples + LEFT), jnp.bfloat16)],
         [VMEM, VMEM],
-    )(own, edge)[0]
+    )(piece, edge)[0]
 
 
 def add_pieces(*pieces):
@@ -191,11 +199,11 @@
 
         @pl.when(core == 0)
         def _():
-            run(own, swapped, edge_ref[chosen].reshape(rows, LANE))
+            run(own, swapped, edge_ref[chosen, 0].reshape(rows, LANE))
 
         @pl.when(core == 1)
         def _():
-            run(swapped, own, high_ref[chosen].reshape(rows, LANE))
+            run(swapped, own, high_ref[chosen, 1].reshape(rows, LANE))
 
         for part in range(total):
             store(part).wait()
@@ -429,31 +437,31 @@
     taps = wide_taps(whiten_taps)
 
     x4 = strain_rate.reshape(chips, 2, sub, samples)
-    own, edge, high, away = pick_sources(source_channels, x4)
+    own, tail, away = pick_sources(source_channels, x4)
 
     swap = [(i, i ^ 1) for i in range(tiles)]
     to_next = [(2 * k - 1, 2 * k) for k in range(1, chips)]
     both_next = to_next + [(b, a) for a, b in to_next]
-    edge = lax.ppermute(edge, "tm", both_next)
     other = lax.ppermute(away, "tm", swap)
-    high = lax.ppermute(high, "tm", [(2 * k - 1, 2 * k + 1) for k in range(1, chips)])
-
-    edge, high = lax.optimization_barrier((edge, high))
-    piece = extend_sources(own, edge)
     parts = [
-        lax.ppermute(piece, "chan", [(i, (i + 2 * d) % groups_chan) for i in range(groups_chan)])
+        lax.ppermute(own, "chan", [(i, (i + 2 * d) % groups_chan) for i in range(groups_chan)])
         for d in range(1, groups_chan // 2)
     ]
+    tail = lax.ppermute(tail, "tm", to_next)
+    *parts, tail = lax.optimization_barrier((*parts, tail))
+    tail_odd = lax.ppermute(tail, "tm", [(2 * k, 2 * k + 1) for k in range(chips)])
+    piece = add_pieces(own, *parts)
+    arrived = lax.ppermute(piece, "chan", [(i, i ^ 1) for i in range(groups_chan)])
     half = chips // 2
-    filtered, power_a = filter_rows(window_offsets, taps, x4, other, edge, high, 0, half)
-    *parts, power_a = lax.optimization_barrier((*parts, power_a))
-    piece = add_pieces(piece, *parts)
-    arrived = lax.ppermute(piece, "chan", [(i, i ^ 1) for i in range(groups_chan)])
+    filtered, power_a = filter_rows(window_offsets, taps, x4, other, tail, tail_odd, 0, half)
+    arrived, power_a = lax.optimization_barrier((arrived, power_a))
+    piece, end = join_sources(piece, arrived)
+    edge = lax.ppermute(end, "tm", both_next)
     filtered, power_b = filter_rows(
-        window_offsets, taps, x4, other, edge, high, half, half, filtered
+        window_offsets, taps, x4, other, tail, tail_odd, half, half, filtered
     )
-    arrived, power_b = lax.optimization_barrier((arrived, power_b))
-    piece = add_pieces(piece, arrived)
+    edge, power_b = lax.optimization_barrier((edge, power_b))
+    piece = extend_sources(piece, edge)
     piece_other = lax.ppermute(piece, "tm", swap)
     traces, energy = filter_sources(
         window_offsets, taps, piece, piece_other, [power_a, power_b], chips

time: 87.4 us -> 90.5 us (1.035)
  starting transfers between devices: 16.4 us -> 19.6 us
  blocking collectives: 36.8 us -> 35 us
  waiting for transfers between devices: 9.08 us -> 10.6 us
    ppermute x5 -> x6, starting transfers between devices: 8.75 us -> 10.7 us  [the longest x3 4.57 us: shards(): lax.ppermute(own, 'chan', [(i, (i + 2 * d) % groups_chan) for i in range(...]
    all_to_all x1, blocking collectives: 18.7 us -> 17 us  [shards(): lax.all_to_all(energy, 'tm', 0, 0, tiled=True, axis_index_groups=same)]
    ppermute x5 -> x6, waiting for transfers between devices: 3.3 us -> 5 us  [the longest x3 4.97 us: shards(): lax.ppermute(own, 'chan', [(i, (i + 2 * d) % groups_chan) for i in range(...]
    ppermute x1, starting transfers between devices: 1.47 us -> 2.57 us  [shards(): piece_other = lax.ppermute(piece, 'tm', swap)]
  transfers between devices with their start and end apart: 11 -> 12, of which waited for: 7 -> 7; matrix products, arithmetic and copies ran while one was open for 0% -> 0% of each run, Pallas kernels for 15% -> 14%
where the time goes in v8:
time: 90.5 us; the launch traced here: 90.1 us
  blocking collectives  35 us (39%)
  Pallas kernels  23.9 us (26%)
  starting transfers between devices  19.6 us (22%)
  waiting for transfers between devices  10.6 us (12%)
    all_to_all x1, blocking collectives, shards(): lax.all_to_all(summed, 'tm', 0, 0, tiled=True, axis_index_groups=columns)  18.1 us
    all_to_all x1, blocking collectives, shards(): lax.all_to_all(energy, 'tm', 0, 0, tiled=True, axis_index_groups=same)  17 us
    pallas_call x2, Pallas kernels, correlate_next(): call(kernel, 'correlate_next', [shape((half_groups, sub, cols), jnp.float...  6.8 us
    pallas_call x1, Pallas kernels, correlate_first(): call(kernel, 'correlate_first', [shape((half_groups, sub, cols), jnp.floa...  5.97 us
    pallas_call x2, Pallas kernels, filter_rows(): call(kernel, 'filter_rows', [shape((all_groups * sub, 2 * half), jnp.floa...  5.89 us
    ppermute x3, waiting for transfers between devices, shards(): lax.ppermute(own, 'chan', [(i, (i + 2 * d) % groups_chan) for i in range(...  4.97 us
    ppermute x3, starting transfers between devices, shards(): lax.ppermute(own, 'chan', [(i, (i + 2 * d) % groups_chan) for i in range(...  4.57 us
    ppermute x2, waiting for transfers between devices, shards(): arrivals.append(lax.ppermute(send, 'tm', line))  4.36 us
  transfers between devices with their start and end apart: 12, of which 7 were waited for; matrix products, arithmetic and copies ran while one was open for 0% of the time, Pallas kernels for 14%

profile of v8, /device:TPU:8, one launch (start us, length us, event | category | flops | bytes accessed | tf_op | source)
XLA Modules:
  0.0 90.1 jit_solution(7640664293856249779)
XLA Ops:
  0.0 0.0 copy-start
  0.0 0.0 copy-start.1
  0.0 0.0 copy-start.2
  0.0 0.8 copy-done.2
  0.8 0.0 copy-start.3
  0.8 2.8 %pick_sources.1 = (bf16[8,4096]{1,0:T(8,128)(2,1)S(1)}, bf16[16,2,16,128]{3,2,1,0:T(8,128)(2,1)S(1)}, bf16[16,16,4096]{2,1,0:T(8,128)(2,1)S(1)}) custom-call(s32[2,4]{1,0:T(2,128)S(1)} %copy-done.2, bf16[16,2,16,4096]{3,2,1,0:T(8,128)(2,1)} %bitcast.1), custom_call_target="tpu_custom_call" | custom-call | bytes 4194304 | tf_op jit(solution)/shard_map/pick_sources/pallas_call | solution.py:92
  3.6 0.1 collective-permute-start.5
  3.7 1.3 %collective-permute-start.3 = (bf16[16,2,16,128]{3,2,1,0:T(8,128)(2,1)S(1)}, bf16[16,2,16,128]{3,2,1,0:T(8,128)(2,1)S(1)}, u32[]{:S(2)}, u32[]{:S(2)}) collective-permute-start(bf16[16,2,16,128]{3,2,1,0:T(8,128)(2,1)S(1)} %get-tuple-element.35), channel_id=1, source_target_pairs={{1,2},{3,4},{5,6},{7,8},{9,10},{11,12},{13,14},{15,16},{17,18},{19... | collective-permute-start | bytes 393224 | tf_op jit(solution)/shard_map/ppermute | solution.py:450
  5.0 2.9 %collective-permute-start.2 = (bf16[8,4096]{1,0:T(8,128)(2,1)S(1)}, bf16[8,4096]{1,0:T(8,128)(2,1)S(1)}, u32[]{:S(2)}, u32[]{:S(2)}) collective-permute-start(bf16[8,4096]{1,0:T(8,128)(2,1)S(1)} %get-tuple-element.34.refs_0_), channel_id=1, source_target_pairs={{0,192},{32,224},{64,0},{96,32},{128,64},{160,96},{192,128},{224,1... | collective-permute-start | bytes 196616 | tf_op jit(solution)/shard_map/ppermute | solution.py:447
  7.9 0.7 collective-permute-start.1
  8.6 0.9 %collective-permute-start = (bf16[8,4096]{1,0:T(8,128)(2,1)S(1)}, bf16[8,4096]{1,0:T(8,128)(2,1)S(1)}, u32[]{:S(2)}, u32[]{:S(2)}) collective-permute-start(bf16[8,4096]{1,0:T(8,128)(2,1)S(1)} %get-tuple-element.34.refs_0_), channel_id=1, source_target_pairs={{0,64},{32,96},{64,128},{96,160},{128,192},{160,224},{192,0},{224,... | collective-permute-start | bytes 196616 | tf_op jit(solution)/shard_map/ppermute | solution.py:447
  9.6 0.2 collective-permute-done.2.refs_3_
  9.8 3.9 %collective-permute-done.1.refs_2_ = bf16[8,4096]{1,0:T(8,128)(2,1)S(1)} collective-permute-done((bf16[8,4096]{1,0:T(8,128)(2,1)S(1)}, bf16[8,4096]{1,0:T(8,128)(2,1)S(1)}, u32[]{:S(2)}, u32[]{:S(2)}) %collective-permute-start.1) | collective-permute-done | bytes 65568 | tf_op jit(solution)/shard_map/ppermute | solution.py:447
  13.7 0.9 collective-permute-done.refs_1_
  14.5 0.0 collective-permute-done.3.edge_ref
  14.5 2.9 %collective-permute-start.6 = (bf16[16,2,16,128]{3,2,1,0:T(8,128)(2,1)S(1)}, bf16[16,2,16,128]{3,2,1,0:T(8,128)(2,1)S(1)}, u32[]{:S(2)}, u32[]{:S(2)}) collective-permute-start(bf16[16,2,16,128]{3,2,1,0:T(8,128)(2,1)S(1)} %collective-permute-done.3.edge_ref), channel_id=1, source_target_pairs={{0,1},{2,3},{4,5},{6,7},{8,9},{10,11},{12,13},{14,15},{16,17},{18,... | collective-permute-start | bytes 393224 | tf_op jit(solution)/shard_map/ppermute | solution.py:452
  17.5 0.0 copy-done.3
  17.6 2.6 %collective-permute-start.4 = (bf16[8,4096]{1,0:T(8,128)(2,1)S(1)}, bf16[8,4096]{1,0:T(8,128)(2,1)S(1)}, u32[]{:S(2)}, u32[]{:S(2)}) collective-permute-start(bf16[8,4096]{1,0:T(8,128)(2,1)S(1)} %add_pieces.1.piece_ref), channel_id=1, source_target_pairs={{0,32},{32,0},{64,96},{96,64},{128,160},{160,128},{192,224},{224,1... | collective-permute-start | bytes 196616 | tf_op jit(solution)/shard_map/ppermute | solution.py:454
  20.1 0.0 collective-permute-done.6.high_ref
  20.1 0.0 collective-permute-done.5.other_ref
  20.1 0.0 copy-done
  20.2 0.0 copy-done.1
  20.2 2.9 %filter_rows.2 = (f32[256,8192]{1,0:T(8,128)}, f32[128,128]{1,0:T(8,128)S(1)}) custom-call(s32[16]{0:T(128)S(1)} %copy-done.1, bf16[1,256]{1,0:T(2,128)(2,1)S(1)} %reshape.6.taps_ref, bf16[16,2,16,4096]{3,2,1,0:T(8,128)(2,1)S(1)} %bitcast.2, bf16[16,16,4096]{2,1,0:T(8,128)(2,1)S(1)} %collective-permute-done.5.other_ref, ...), custom_call_target="tpu_custom_call" | custom-call | flops 1073741824 | bytes 6291456 | tf_op jit(solution)/shard_map/filter_rows/pallas_call | solution.py:211
  23.1 0.3 collective-permute-done.4.arrived_ref
  23.5 1.9 %collective-permute-start.7 = (bf16[8,256]{1,0:T(8,128)(2,1)S(1)}, bf16[8,256]{1,0:T(8,128)(2,1)S(1)}, u32[]{:S(2)}, u32[]{:S(2)}) collective-permute-start(bf16[8,256]{1,0:T(8,128)(2,1)S(1)} %get-tuple-element.44), channel_id=1, source_target_pairs={{1,2},{3,4},{5,6},{7,8},{9,10},{11,12},{13,14},{15,16},{17,18},{19... | collective-permute-start | bytes 12296 | tf_op jit(solution)/shard_map/ppermute | solution.py:459
  25.4 3.0 %filter_rows.3 = (f32[256,8192]{1,0:T(8,128)}, f32[128,128]{1,0:T(8,128)S(1)}) custom-call(s32[16]{0:T(128)S(1)} %copy-done.1, bf16[1,256]{1,0:T(2,128)(2,1)S(1)} %reshape.6.taps_ref, bf16[16,2,16,4096]{3,2,1,0:T(8,128)(2,1)S(1)} %bitcast.3, bf16[16,16,4096]{2,1,0:T(8,128)(2,1)S(1)} %collective-permute-done.5.other_ref, ...), custom_call_target="tpu_custom_call", output_to_operand_aliasing={{0}: (6, {})} | custom-call | flops 1073741824 | bytes 6291456 | tf_op jit(solution)/shard_map/filter_rows/pallas_call | solution.py:211
  28.4 0.0 collective-permute-done.7.edge_ref
  28.4 2.6 %collective-permute-start.8 = (bf16[8,4352]{1,0:T(8,128)(2,1)S(1)}, bf16[8,4352]{1,0:T(8,128)(2,1)S(1)}, u32[]{:S(2)}, u32[]{:S(2)}) collective-permute-start(bf16[8,4352]{1,0:T(8,128)(2,1)S(1)} %extend_sources.1.mine_ref), channel_id=1, source_target_pairs={{0,1},{1,0},{2,3},{3,2},{4,5},{5,4},{6,7},{7,6},{8,9},{9,8},{10,11... | collective-permute-start | bytes 208904 | tf_op jit(solution)/shard_map/ppermute | solution.py:465
  31.0 0.9 %collective-permute-done.8.other_ref = bf16[8,4352]{1,0:T(8,128)(2,1)S(1)} collective-permute-done((bf16[8,4352]{1,0:T(8,128)(2,1)S(1)}, bf16[8,4352]{1,0:T(8,128)(2,1)S(1)}, u32[]{:S(2)}, u32[]{:S(2)}) %collective-permute-start.8) | collective-permute-done | bytes 69664 | tf_op jit(solution)/shard_map/ppermute | solution.py:465
  31.9 1.0 %filter_sources.1 = (f32[8,8448]{1,0:T(8,128)S(1)}, f32[16,8,128]{2,1,0:T(8,128)S(1)}) custom-call(s32[16]{0:T(128)S(1)} %copy-done.1, bf16[1,256]{1,0:T(2,128)(2,1)S(1)} %reshape.6.taps_ref, bf16[8,4352]{1,0:T(8,128)(2,1)S(1)} %extend_sources.1.mine_ref, bf16[8,4352]{1,0:T(8,128)(2,1)S(1)} %collective-permute-done.8.other_ref, ...), custom_call_target="tpu_custom_call" | custom-call | bytes 1048576 | tf_op jit(solution)/shard_map/filter_sources/pallas_call | solution.py:273
  32.9 17.0 %all_to_all.10.energy_ref = f32[16,8,128]{2,1,0:T(8,128)S(1)} all-to-all(f32[16,8,128]{2,1,0:T(8,128)S(1)} %get-tuple-element.50), channel_id=1, replica_groups={{0,2,4,6,8,10,12,14,16,18,20,22,24,26,28,30},{1,3,5,7,9,11,13,15,17,19,..., dimensions={0} | all-to-all | bytes 131072 | tf_op jit(solution)/shard_map/all_to_all | solution.py:470
  49.8 6.0 %correlate_first.1 = (f32[8,16,512]{2,1,0:T(8,128)S(1)}, bf16[8,16,512]{2,1,0:T(8,128)(2,1)S(1)}, bf16[256,8192]{1,0:T(8,128)(2,1)S(1)}, bf16[8448,128]{1,0:T(8,128)(2,1)S(1)}) custom-call(f32[16,8,128]{2,1,0:T(8,128)S(1)} %all_to_all.10.energy_ref, f32[8,8448]{1,0:T(8,128)S(1)} %get-tuple-element.51.traces_ref, f32[256,8192]{1,0:T(8,128)} %get-tuple-element.52.refs_0_), custom_call_target="tpu_custom_call" | custom-call | flops 2147483648 | bytes 16777216 | tf_op jit(solution)/shard_map/correlate_first/pallas_call | solution.py:340
  55.8 1.5 %collective-permute-start.9 = (bf16[8,16,512]{2,1,0:T(8,128)(2,1)S(1)}, bf16[8,16,512]{2,1,0:T(8,128)(2,1)S(1)}, u32[]{:S(2)}, u32[]{:S(2)}) collective-permute-start(bf16[8,16,512]{2,1,0:T(8,128)(2,1)S(1)} %get-tuple-element.57), channel_id=1, source_target_pairs={{0,2},{1,3},{2,0},{3,1},{4,6},{5,7},{6,4},{7,5},{8,10},{9,11},{10,... | collective-permute-start | bytes 393224 | tf_op jit(solution)/shard_map/ppermute | solution.py:479
  57.3 3.4 %correlate_next.2 = (f32[8,16,768]{2,1,0:T(8,128)S(1)}, bf16[8,16,768]{2,1,0:T(8,128)(2,1)S(1)}) custom-call(bf16[256,8192]{1,0:T(8,128)(2,1)S(1)} %get-tuple-element.58.white_ref, bf16[8448,128]{1,0:T(8,128)(2,1)S(1)} %get-tuple-element.55.table_ref), custom_call_target="tpu_custom_call" | custom-call | flops 3221225472 | bytes 8388608 | tf_op jit(solution)/shard_map/correlate_next/pallas_call | solution.py:369
  60.7 0.7 collective-permute-start.10
  61.4 0.0 collective-permute-done.9.refs_3_
  61.4 3.4 %correlate_next.3 = (f32[8,16,768]{2,1,0:T(8,128)S(1)}, bf16[8,16,768]{2,1,0:T(8,128)(2,1)S(1)}) custom-call(bf16[256,8192]{1,0:T(8,128)(2,1)S(1)} %get-tuple-element.58.white_ref, bf16[8448,128]{1,0:T(8,128)(2,1)S(1)} %get-tuple-element.55.table_ref), custom_call_target="tpu_custom_call" | custom-call | flops 3221225472 | bytes 8388608 | tf_op jit(solution)/shard_map/correlate_next/pallas_call | solution.py:369
  64.8 1.5 %collective-permute-start.11 = (bf16[8,16,768]{2,1,0:T(8,128)(2,1)S(1)}, bf16[8,16,768]{2,1,0:T(8,128)(2,1)S(1)}, u32[]{:S(2)}, u32[]{:S(2)}) collective-permute-start(bf16[8,16,768]{2,1,0:T(8,128)(2,1)S(1)} %get-tuple-element.62), channel_id=1, source_target_pairs={{0,2},{1,3},{2,0},{3,1},{4,6},{5,7},{6,4},{7,5},{8,10},{9,11},{10,... | collective-permute-start | bytes 589832 | tf_op jit(solution)/shard_map/ppermute | solution.py:485
  66.3 0.9 collective-permute-done.10.refs_4_
  67.1 3.5 %collective-permute-done.11.refs_5_ = bf16[8,16,768]{2,1,0:T(8,128)(2,1)S(1)} collective-permute-done((bf16[8,16,768]{2,1,0:T(8,128)(2,1)S(1)}, bf16[8,16,768]{2,1,0:T(8,128)(2,1)S(1)}, u32[]{:S(2)}, u32[]{:S(2)}) %collective-permute-start.11) | collective-permute-done | bytes 196640 | tf_op jit(solution)/shard_map/ppermute | solution.py:485
  70.6 0.1 add_line.1
  70.7 18.1 %all_to_all.11.parts_ref = bf16[8,16,2048]{2,1,0:T(8,128)(2,1)S(1)} all-to-all(bf16[8,16,2048]{2,1,0:T(8,128)(2,1)S(1)} %add_line.1), channel_id=1, replica_groups={{0,4,8,12,16,20,24,28},{1,5,9,13,17,21,25,29},{2,6,10,14,18,22,26,30},{..., dimensions={0} | all-to-all | bytes 1048576 | tf_op jit(solution)/shard_map/all_to_all | solution.py:488
  88.8 1.3 %finish.1 = f32[16,2,4,256]{3,2,1,0:T(4,128)} custom-call(bf16[8,16,2048]{2,1,0:T(8,128)(2,1)S(1)} %all_to_all.11.parts_ref), custom_call_target="tpu_custom_call" | custom-call | bytes 1048576 | tf_op jit(solution)/shard_map/finish/pallas_call | solution.py:420
  (5 shorter events, 0.1 us)
Async XLA Ops:
  0.0 20.1 %copy-start = (bf16[512,4096]{1,0:T(8,128)(2,1)S(1)}, bf16[512,4096]{1,0:T(8,128)(2,1)}, u32[]{:S(2)}) copy-start(bf16[512,4096]{1,0:T(8,128)(2,1)} %param.4) | copy-start | bytes 12582916
  0.0 20.2 %copy-start.1 = (s32[16]{0:T(128)S(1)}, s32[16]{0:T(128)}, u32[]{:S(2)}) copy-start(s32[16]{0:T(128)} %off_ref.5) | copy-start | bytes 196
  0.0 0.8 copy-start.2
  0.8 16.7 %copy-start.3 = (bf16[64]{0:T(256)(128)(2,1)S(1)}, bf16[64]{0:T(256)(128)(2,1)}, u32[]{:S(2)}) copy-start(bf16[64]{0:T(256)(128)(2,1)} %param.5) | copy-start | bytes 388
  3.6 16.5 %collective-permute-start.5 = (bf16[16,16,4096]{2,1,0:T(8,128)(2,1)S(1)}, bf16[16,16,4096]{2,1,0:T(8,128)(2,1)S(1)}, u32[]{:S(2)}, u32[]{:S(2)}) collective-permute-start(bf16[16,16,4096]{2,1,0:T(8,128)(2,1)S(1)} %get-tuple-element.39), channel_id=1, source_target_pairs={{0,1},{1,0},{2,3},{3,2},{4,5},{5,4},{6,7},{7,6},{8,9},{9,8},{10,11... | collective-permute-start | bytes 6291464 | tf_op jit(solution)/shard_map/ppermute | solution.py:445
  3.7 10.8 %collective-permute-start.3 = (bf16[16,2,16,128]{3,2,1,0:T(8,128)(2,1)S(1)}, bf16[16,2,16,128]{3,2,1,0:T(8,128)(2,1)S(1)}, u32[]{:S(2)}, u32[]{:S(2)}) collective-permute-start(bf16[16,2,16,128]{3,2,1,0:T(8,128)(2,1)S(1)} %get-tuple-element.35), channel_id=1, source_target_pairs={{1,2},{3,4},{5,6},{7,8},{9,10},{11,12},{13,14},{15,16},{17,18},{19... | collective-permute-start | bytes 393224 | tf_op jit(solution)/shard_map/ppermute | solution.py:450
  5.0 4.8 %collective-permute-start.2 = (bf16[8,4096]{1,0:T(8,128)(2,1)S(1)}, bf16[8,4096]{1,0:T(8,128)(2,1)S(1)}, u32[]{:S(2)}, u32[]{:S(2)}) collective-permute-start(bf16[8,4096]{1,0:T(8,128)(2,1)S(1)} %get-tuple-element.34.refs_0_), channel_id=1, source_target_pairs={{0,192},{32,224},{64,0},{96,32},{128,64},{160,96},{192,128},{224,1... | collective-permute-start | bytes 196616 | tf_op jit(solution)/shard_map/ppermute | solution.py:447
  7.9 5.8 %collective-permute-start.1 = (bf16[8,4096]{1,0:T(8,128)(2,1)S(1)}, bf16[8,4096]{1,0:T(8,128)(2,1)S(1)}, u32[]{:S(2)}, u32[]{:S(2)}) collective-permute-start(bf16[8,4096]{1,0:T(8,128)(2,1)S(1)} %get-tuple-element.34.refs_0_), channel_id=1, source_target_pairs={{0,128},{32,160},{64,192},{96,224},{128,0},{160,32},{192,64},{224,... | collective-permute-start | bytes 196616 | tf_op jit(solution)/shard_map/ppermute | solution.py:447
  8.6 5.9 %collective-permute-start = (bf16[8,4096]{1,0:T(8,128)(2,1)S(1)}, bf16[8,4096]{1,0:T(8,128)(2,1)S(1)}, u32[]{:S(2)}, u32[]{:S(2)}) collective-permute-start(bf16[8,4096]{1,0:T(8,128)(2,1)S(1)} %get-tuple-element.34.refs_0_), channel_id=1, source_target_pairs={{0,64},{32,96},{64,128},{96,160},{128,192},{160,224},{192,0},{224,... | collective-permute-start | bytes 196616 | tf_op jit(solution)/shard_map/ppermute | solution.py:447
  14.5 5.6 %collective-permute-start.6 = (bf16[16,2,16,128]{3,2,1,0:T(8,128)(2,1)S(1)}, bf16[16,2,16,128]{3,2,1,0:T(8,128)(2,1)S(1)}, u32[]{:S(2)}, u32[]{:S(2)}) collective-permute-start(bf16[16,2,16,128]{3,2,1,0:T(8,128)(2,1)S(1)} %collective-permute-done.3.edge_ref), channel_id=1, source_target_pairs={{0,1},{2,3},{4,5},{6,7},{8,9},{10,11},{12,13},{14,15},{16,17},{18,... | collective-permute-start | bytes 393224 | tf_op jit(solution)/shard_map/ppermute | solution.py:452
  17.6 5.9 %collective-permute-start.4 = (bf16[8,4096]{1,0:T(8,128)(2,1)S(1)}, bf16[8,4096]{1,0:T(8,128)(2,1)S(1)}, u32[]{:S(2)}, u32[]{:S(2)}) collective-permute-start(bf16[8,4096]{1,0:T(8,128)(2,1)S(1)} %add_pieces.1.piece_ref), channel_id=1, source_target_pairs={{0,32},{32,0},{64,96},{96,64},{128,160},{160,128},{192,224},{224,1... | collective-permute-start | bytes 196616 | tf_op jit(solution)/shard_map/ppermute | solution.py:454
  23.5 4.9 %collective-permute-start.7 = (bf16[8,256]{1,0:T(8,128)(2,1)S(1)}, bf16[8,256]{1,0:T(8,128)(2,1)S(1)}, u32[]{:S(2)}, u32[]{:S(2)}) collective-permute-start(bf16[8,256]{1,0:T(8,128)(2,1)S(1)} %get-tuple-element.44), channel_id=1, source_target_pairs={{1,2},{3,4},{5,6},{7,8},{9,10},{11,12},{13,14},{15,16},{17,18},{19... | collective-permute-start | bytes 12296 | tf_op jit(solution)/shard_map/ppermute | solution.py:459
  28.4 3.5 %collective-permute-start.8 = (bf16[8,4352]{1,0:T(8,128)(2,1)S(1)}, bf16[8,4352]{1,0:T(8,128)(2,1)S(1)}, u32[]{:S(2)}, u32[]{:S(2)}) collective-permute-start(bf16[8,4352]{1,0:T(8,128)(2,1)S(1)} %extend_sources.1.mine_ref), channel_id=1, source_target_pairs={{0,1},{1,0},{2,3},{3,2},{4,5},{5,4},{6,7},{7,6},{8,9},{9,8},{10,11... | collective-permute-start | bytes 208904 | tf_op jit(solution)/shard_map/ppermute | solution.py:465
  55.8 5.6 %collective-permute-start.9 = (bf16[8,16,512]{2,1,0:T(8,128)(2,1)S(1)}, bf16[8,16,512]{2,1,0:T(8,128)(2,1)S(1)}, u32[]{:S(2)}, u32[]{:S(2)}) collective-permute-start(bf16[8,16,512]{2,1,0:T(8,128)(2,1)S(1)} %get-tuple-element.57), channel_id=1, source_target_pairs={{0,2},{1,3},{2,0},{3,1},{4,6},{5,7},{6,4},{7,5},{8,10},{9,11},{10,... | collective-permute-start | bytes 393224 | tf_op jit(solution)/shard_map/ppermute | solution.py:479
  60.7 6.5 %collective-permute-start.10 = (bf16[8,16,768]{2,1,0:T(8,128)(2,1)S(1)}, bf16[8,16,768]{2,1,0:T(8,128)(2,1)S(1)}, u32[]{:S(2)}, u32[]{:S(2)}) collective-permute-start(bf16[8,16,768]{2,1,0:T(8,128)(2,1)S(1)} %get-tuple-element.61), channel_id=1, source_target_pairs={{0,2},{1,3},{2,0},{3,1},{4,6},{5,7},{6,4},{7,5},{8,10},{9,11},{10,... | collective-permute-start | bytes 589832 | tf_op jit(solution)/shard_map/ppermute | solution.py:485
  64.8 5.8 %collective-permute-start.11 = (bf16[8,16,768]{2,1,0:T(8,128)(2,1)S(1)}, bf16[8,16,768]{2,1,0:T(8,128)(2,1)S(1)}, u32[]{:S(2)}, u32[]{:S(2)}) collective-permute-start(bf16[8,16,768]{2,1,0:T(8,128)(2,1)S(1)} %get-tuple-element.62), channel_id=1, source_target_pairs={{0,2},{1,3},{2,0},{3,1},{4,6},{5,7},{6,4},{7,5},{8,10},{9,11},{10,... | collective-permute-start | bytes 589832 | tf_op jit(solution)/shard_map/ppermute | solution.py:485

commit v9 on v7

--- a/solution.py
+++ b/solution.py
@@ -59,7 +59,7 @@
     groups, _, sub, samples = x4.shape
     channels = groups * 2 * sub
 
-    def kernel(ids_ref, x_ref, own_ref, edge_ref, high_ref, away_ref, buf, sems):
+    def kernel(ids_ref, x_ref, own_ref, edge_ref, away_ref, buf, sems):
         base = lax.axis_index("chan") * channels
         core = lax.axis_index("tm") % 2
         copies = []
@@ -76,7 +76,9 @@
             pltpu.make_async_copy(
                 x_ref.at[:, 0, :, last], edge_ref.at[pl.ds(0, groups)], sems.at[NS]
             ),
-            pltpu.make_async_copy(x_ref.at[:, 1, :, last], high_ref, sems.at[NS + 1]),
+            pltpu.make_async_copy(
+                x_ref.at[:, 1, :, last], edge_ref.at[pl.ds(groups, groups)], sems.at[NS + 1]
+            ),
             pltpu.make_async_copy(x_ref.at[:, 1 - core], away_ref, sems.at[NS + 2]),
         ]
         for copy in copies + rest:
@@ -92,7 +94,7 @@
         end = jnp.where(core == 1, own[:, samples - LEFT :], own[:, :LEFT])
         for copy in rest:
             copy.wait()
-        edge_ref[groups] = jnp.concatenate(
+        edge_ref[2 * groups] = jnp.concatenate(
             [end[:, :LANE], end[:, LANE:]], axis=0
         ).astype(jnp.bfloat16)
 
@@ -101,8 +103,7 @@
         "pick_sources",
         [
             shape((NS, samples), jnp.bfloat16),
-            shape((groups + 1, sub, LANE), jnp.bfloat16),
-            shape((groups, sub, LANE), jnp.bfloat16),
+            shape((2 * groups + 1, sub, LANE), jnp.bfloat16),
             shape((groups, sub, samples), jnp.bfloat16),
         ],
         [SMEM, ANY],
@@ -149,6 +150,7 @@
     filled = [] if filled is None else [filled]
     rows = groups * sub
     chosen = slice(first_group, first_group + groups)
+    chosen_high = slice(all_groups + first_group, all_groups + first_group + groups)
     chunk = 1024
     parts = half // chunk
     total = 2 * parts
@@ -195,7 +197,7 @@
 
         @pl.when(core == 1)
         def _():
-            run(swapped, own, high_ref[chosen].reshape(rows, LANE))
+            run(swapped, own, high_ref[chosen_high].reshape(rows, LANE))
 
         for part in range(total):
             store(part).wait()
@@ -429,16 +431,15 @@
     taps = wide_taps(whiten_taps)
 
     x4 = strain_rate.reshape(chips, 2, sub, samples)
-    own, edge, high, away = pick_sources(source_channels, x4)
+    own, edge, away = pick_sources(source_channels, x4)
 
     swap = [(i, i ^ 1) for i in range(tiles)]
     to_next = [(2 * k - 1, 2 * k) for k in range(1, chips)]
     both_next = to_next + [(b, a) for a, b in to_next]
     edge = lax.ppermute(edge, "tm", both_next)
+    edge, away = lax.optimization_barrier((edge, away))
     other = lax.ppermute(away, "tm", swap)
-    high = lax.ppermute(high, "tm", [(2 * k - 1, 2 * k + 1) for k in range(1, chips)])
-
-    edge, high = lax.optimization_barrier((edge, high))
+    high = lax.ppermute(edge, "tm", [(2 * k, 2 * k + 1) for k in range(chips)])
     piece = extend_sources(own, edge)
     parts = [
         lax.ppermute(piece, "chan", [(i, (i + 2 * d) % groups_chan) for i in range(groups_chan)])
@@ -463,7 +464,7 @@
 
     column = tiles // 4
     dots = LAGS // (2 * SHIFTS)
-    splits = [range(0, dots // 4), range(dots // 4, dots * 5 // 8), range(dots * 5 // 8, dots)]
+    splits = [range(i, i + 2) for i in range(0, dots, 2)]
     line = [(i, i ^ 2) for i in range(tiles)]
     keep, send, white, table = correlate_first(
         energies, traces, [filtered], splits[0], column, total_samples

time: 87.4 us -> 91.4 us (1.046)
  waiting for transfers between devices: 9.08 us -> 15.2 us
  blocking collectives: 36.8 us -> 34.8 us
    ppermute x1, waiting for transfers between devices: 1.26 us -> 5.85 us  [shards(): edge = lax.ppermute(edge, 'tm', both_next)]
    ppermute x1, starting transfers between devices: 4.18 us -> 1.92 us  [shards(): edge = lax.ppermute(edge, 'tm', both_next)]
    ppermute x1, starting transfers between devices: 0.66 us -> 2.41 us  [shards(): high = lax.ppermute(edge, 'tm', [(2 * k, 2 * k + 1) for k in range(chips)])]
    ppermute x1, starting transfers between devices: 1.47 us -> 0.09 us  [shards(): piece_other = lax.ppermute(piece, 'tm', swap)]
    all_to_all x1, blocking collectives: 18.7 us -> 17.6 us  [shards(): lax.all_to_all(energy, 'tm', 0, 0, tiled=True, axis_index_groups=same)]
    ppermute x2 -> x3, starting transfers between devices: 2.2 us -> 3.13 us  [shards(): arrivals.append(lax.ppermute(send, 'tm', line))]
    ppermute x2 -> x3, waiting for transfers between devices: 4.36 us -> 5.16 us  [shards(): arrivals.append(lax.ppermute(send, 'tm', line))]
    pallas_call x2 -> x3, Pallas kernels: 6.8 us -> 6.96 us  [correlate_next(): call(kernel, 'correlate_next', [shape((half_groups, sub, cols), jnp.float...]
  transfers between devices with their start and end apart: 11 -> 12, of which waited for: 7 -> 9; matrix products, arithmetic and copies ran while one was open for 0% -> 0% of each run, Pallas kernels for 15% -> 14%
where the time goes in v9:
time: 91.4 us; the launch traced here: 91.1 us
  blocking collectives  34.8 us (38%)
  Pallas kernels  24.1 us (26%)
  starting transfers between devices  16 us (18%)
  waiting for transfers between devices  15.2 us (17%)
    all_to_all x1, blocking collectives, shards(): lax.all_to_all(energy, 'tm', 0, 0, tiled=True, axis_index_groups=same)  17.6 us
    all_to_all x1, blocking collectives, shards(): lax.all_to_all(summed, 'tm', 0, 0, tiled=True, axis_index_groups=columns)  17.2 us
    pallas_call x3, Pallas kernels, correlate_next(): call(kernel, 'correlate_next', [shape((half_groups, sub, cols), jnp.float...  6.96 us
    pallas_call x1, Pallas kernels, correlate_first(): call(kernel, 'correlate_first', [shape((half_groups, sub, cols), jnp.floa...  5.97 us
    pallas_call x2, Pallas kernels, filter_rows(): call(kernel, 'filter_rows', [shape((all_groups * sub, 2 * half), jnp.floa...  5.89 us
    ppermute x1, waiting for transfers between devices, shards(): edge = lax.ppermute(edge, 'tm', both_next)  5.85 us
    ppermute x3, waiting for transfers between devices, shards(): arrivals.append(lax.ppermute(send, 'tm', line))  5.16 us
    ppermute x3, starting transfers between devices, shards(): lax.ppermute(piece, 'chan', [(i, (i + 2 * d) % groups_chan) for i in rang...  4.52 us
  transfers between devices with their start and end apart: 12, of which 9 were waited for; matrix products, arithmetic and copies ran while one was open for 0% of the time, Pallas kernels for 14%

profile of v9, /device:TPU:8, one launch (start us, length us, event | category | flops | bytes accessed | tf_op | source)
XLA Modules:
  0.0 91.1 jit_solution(10699925628158155482)
XLA Ops:
  0.0 0.0 copy-start
  0.0 0.0 copy-start.1
  0.0 0.0 copy-start.2
  0.0 0.8 copy-done.2
  0.8 0.0 copy-start.3
  0.8 2.8 %pick_sources.1 = (bf16[8,4096]{1,0:T(8,128)(2,1)S(1)}, bf16[33,16,128]{2,1,0:T(8,128)(2,1)S(1)}, bf16[16,16,4096]{2,1,0:T(8,128)(2,1)S(1)}) custom-call(s32[2,4]{1,0:T(2,128)S(1)} %copy-done.2, bf16[16,2,16,4096]{3,2,1,0:T(8,128)(2,1)} %bitcast.1), custom_call_target="tpu_custom_call" | custom-call | bytes 2097152 | tf_op jit(solution)/shard_map/pick_sources/pallas_call | solution.py:101
  3.6 1.9 %collective-permute-start = (bf16[33,16,128]{2,1,0:T(8,128)(2,1)S(1)}, bf16[33,16,128]{2,1,0:T(8,128)(2,1)S(1)}, u32[]{:S(2)}, u32[]{:S(2)}) collective-permute-start(bf16[33,16,128]{2,1,0:T(8,128)(2,1)S(1)} %get-tuple-element.37), channel_id=1, source_target_pairs={{1,2},{3,4},{5,6},{7,8},{9,10},{11,12},{13,14},{15,16},{17,18},{19... | collective-permute-start | bytes 405512 | tf_op jit(solution)/shard_map/ppermute | solution.py:439
  5.5 5.9 %collective-permute-done.edge_ref = bf16[33,16,128]{2,1,0:T(8,128)(2,1)S(1)} collective-permute-done((bf16[33,16,128]{2,1,0:T(8,128)(2,1)S(1)}, bf16[33,16,128]{2,1,0:T(8,128)(2,1)S(1)}, u32[]{:S(2)}, u32[]{:S(2)}) %collective-permute-start) | collective-permute-done | bytes 135200 | tf_op jit(solution)/shard_map/ppermute | solution.py:439
  11.4 0.0 collective-permute-start.4
  11.4 2.4 %collective-permute-start.5 = (bf16[33,16,128]{2,1,0:T(8,128)(2,1)S(1)}, bf16[33,16,128]{2,1,0:T(8,128)(2,1)S(1)}, u32[]{:S(2)}, u32[]{:S(2)}) collective-permute-start(bf16[33,16,128]{2,1,0:T(8,128)(2,1)S(1)} %collective-permute-done.edge_ref), channel_id=1, source_target_pairs={{0,1},{2,3},{4,5},{6,7},{8,9},{10,11},{12,13},{14,15},{16,17},{18,... | collective-permute-start | bytes 405512 | tf_op jit(solution)/shard_map/ppermute | solution.py:442
  13.8 0.0 copy-done.3
  13.9 2.8 %collective-permute-start.3 = (bf16[8,4352]{1,0:T(8,128)(2,1)S(1)}, bf16[8,4352]{1,0:T(8,128)(2,1)S(1)}, u32[]{:S(2)}, u32[]{:S(2)}) collective-permute-start(bf16[8,4352]{1,0:T(8,128)(2,1)S(1)} %extend_sources.1.refs_0_), channel_id=1, source_target_pairs={{0,192},{32,224},{64,0},{96,32},{128,64},{160,96},{192,128},{224,1... | collective-permute-start | bytes 208904 | tf_op jit(solution)/shard_map/ppermute | solution.py:445
  16.7 0.8 collective-permute-start.2
  17.5 0.9 collective-permute-start.1
  18.4 0.0 collective-permute-done.5.high_ref
  18.4 0.0 collective-permute-done.4.other_ref
  18.4 0.0 copy-done
  18.4 0.0 copy-done.1
  18.4 2.9 %filter_rows.2 = (f32[256,8192]{1,0:T(8,128)}, f32[128,128]{1,0:T(8,128)S(1)}) custom-call(s32[16]{0:T(128)S(1)} %copy-done.1, bf16[1,256]{1,0:T(2,128)(2,1)S(1)} %reshape.6.taps_ref, bf16[16,2,16,4096]{3,2,1,0:T(8,128)(2,1)S(1)} %bitcast.2, bf16[16,16,4096]{2,1,0:T(8,128)(2,1)S(1)} %collective-permute-done.4.other_ref, ...), custom_call_target="tpu_custom_call" | custom-call | flops 1073741824 | bytes 6291456 | tf_op jit(solution)/shard_map/filter_rows/pallas_call | solution.py:205
  21.3 0.0 collective-permute-done.3.refs_3_
  21.4 1.2 %collective-permute-done.2.refs_2_ = bf16[8,4352]{1,0:T(8,128)(2,1)S(1)} collective-permute-done((bf16[8,4352]{1,0:T(8,128)(2,1)S(1)}, bf16[8,4352]{1,0:T(8,128)(2,1)S(1)}, u32[]{:S(2)}, u32[]{:S(2)}) %collective-permute-start.2) | collective-permute-done | bytes 69664 | tf_op jit(solution)/shard_map/ppermute | solution.py:445
  22.5 0.7 collective-permute-done.1.refs_1_
  23.3 2.5 %collective-permute-start.6 = (bf16[8,4352]{1,0:T(8,128)(2,1)S(1)}, bf16[8,4352]{1,0:T(8,128)(2,1)S(1)}, u32[]{:S(2)}, u32[]{:S(2)}) collective-permute-start(bf16[8,4352]{1,0:T(8,128)(2,1)S(1)} %add_pieces.2.refs_0_), channel_id=1, source_target_pairs={{0,32},{32,0},{64,96},{96,64},{128,160},{160,128},{192,224},{224,1... | collective-permute-start | bytes 208904 | tf_op jit(solution)/shard_map/ppermute | solution.py:452
  25.8 3.0 %filter_rows.3 = (f32[256,8192]{1,0:T(8,128)}, f32[128,128]{1,0:T(8,128)S(1)}) custom-call(s32[16]{0:T(128)S(1)} %copy-done.1, bf16[1,256]{1,0:T(2,128)(2,1)S(1)} %reshape.6.taps_ref, bf16[16,2,16,4096]{3,2,1,0:T(8,128)(2,1)S(1)} %bitcast.3, bf16[16,16,4096]{2,1,0:T(8,128)(2,1)S(1)} %collective-permute-done.4.other_ref, ...), custom_call_target="tpu_custom_call", output_to_operand_aliasing={{0}: (6, {})} | custom-call | flops 1073741824 | bytes 6291456 | tf_op jit(solution)/shard_map/filter_rows/pallas_call | solution.py:205
  28.8 0.4 collective-permute-done.6.refs_1_
  29.2 0.1 collective-permute-start.7
  29.3 1.2 %collective-permute-done.7.other_ref = bf16[8,4352]{1,0:T(8,128)(2,1)S(1)} collective-permute-done((bf16[8,4352]{1,0:T(8,128)(2,1)S(1)}, bf16[8,4352]{1,0:T(8,128)(2,1)S(1)}, u32[]{:S(2)}, u32[]{:S(2)}) %collective-permute-start.7) | collective-permute-done | bytes 69664 | tf_op jit(solution)/shard_map/ppermute | solution.py:458
  30.6 1.0 %filter_sources.1 = (f32[8,8448]{1,0:T(8,128)S(1)}, f32[16,8,128]{2,1,0:T(8,128)S(1)}) custom-call(s32[16]{0:T(128)S(1)} %copy-done.1, bf16[1,256]{1,0:T(2,128)(2,1)S(1)} %reshape.6.taps_ref, bf16[8,4352]{1,0:T(8,128)(2,1)S(1)} %add_pieces.3.mine_ref, bf16[8,4352]{1,0:T(8,128)(2,1)S(1)} %collective-permute-done.7.other_ref, ...), custom_call_target="tpu_custom_call" | custom-call | bytes 1048576 | tf_op jit(solution)/shard_map/filter_sources/pallas_call | solution.py:267
  31.6 17.6 %all_to_all.10.energy_ref = f32[16,8,128]{2,1,0:T(8,128)S(1)} all-to-all(f32[16,8,128]{2,1,0:T(8,128)S(1)} %get-tuple-element.50), channel_id=1, replica_groups={{0,2,4,6,8,10,12,14,16,18,20,22,24,26,28,30},{1,3,5,7,9,11,13,15,17,19,..., dimensions={0} | all-to-all | bytes 131072 | tf_op jit(solution)/shard_map/all_to_all | solution.py:463
  49.2 6.0 %correlate_first.1 = (f32[8,16,512]{2,1,0:T(8,128)S(1)}, bf16[8,16,512]{2,1,0:T(8,128)(2,1)S(1)}, bf16[256,8192]{1,0:T(8,128)(2,1)S(1)}, bf16[8448,128]{1,0:T(8,128)(2,1)S(1)}) custom-call(f32[16,8,128]{2,1,0:T(8,128)S(1)} %all_to_all.10.energy_ref, f32[8,8448]{1,0:T(8,128)S(1)} %get-tuple-element.51.traces_ref, f32[256,8192]{1,0:T(8,128)} %get-tuple-element.52.refs_0_), custom_call_target="tpu_custom_call" | custom-call | flops 2147483648 | bytes 16777216 | tf_op jit(solution)/shard_map/correlate_first/pallas_call | solution.py:334
  55.2 1.5 %collective-permute-start.8 = (bf16[8,16,512]{2,1,0:T(8,128)(2,1)S(1)}, bf16[8,16,512]{2,1,0:T(8,128)(2,1)S(1)}, u32[]{:S(2)}, u32[]{:S(2)}) collective-permute-start(bf16[8,16,512]{2,1,0:T(8,128)(2,1)S(1)} %get-tuple-element.57), channel_id=1, source_target_pairs={{0,2},{1,3},{2,0},{3,1},{4,6},{5,7},{6,4},{7,5},{8,10},{9,11},{10,... | collective-permute-start | bytes 393224 | tf_op jit(solution)/shard_map/ppermute | solution.py:472
  56.6 2.3 %correlate_next.3 = (f32[8,16,512]{2,1,0:T(8,128)S(1)}, bf16[8,16,512]{2,1,0:T(8,128)(2,1)S(1)}) custom-call(bf16[256,8192]{1,0:T(8,128)(2,1)S(1)} %get-tuple-element.61.white_ref, bf16[8448,128]{1,0:T(8,128)(2,1)S(1)} %get-tuple-element.55.table_ref), custom_call_target="tpu_custom_call" | custom-call | flops 2147483648 | bytes 8388608 | tf_op jit(solution)/shard_map/correlate_next/pallas_call | solution.py:363
  59.0 0.7 collective-permute-start.9
  59.7 0.6 collective-permute-done.8.refs_4_
  60.3 2.3 %correlate_next.4 = (f32[8,16,512]{2,1,0:T(8,128)S(1)}, bf16[8,16,512]{2,1,0:T(8,128)(2,1)S(1)}) custom-call(bf16[256,8192]{1,0:T(8,128)(2,1)S(1)} %get-tuple-element.61.white_ref, bf16[8448,128]{1,0:T(8,128)(2,1)S(1)} %get-tuple-element.55.table_ref), custom_call_target="tpu_custom_call" | custom-call | flops 2147483648 | bytes 8388608 | tf_op jit(solution)/shard_map/correlate_next/pallas_call | solution.py:363
  62.7 2.3 %collective-permute-start.10 = (bf16[8,16,512]{2,1,0:T(8,128)(2,1)S(1)}, bf16[8,16,512]{2,1,0:T(8,128)(2,1)S(1)}, u32[]{:S(2)}, u32[]{:S(2)}) collective-permute-start(bf16[8,16,512]{2,1,0:T(8,128)(2,1)S(1)} %get-tuple-element.65), channel_id=1, source_target_pairs={{0,2},{1,3},{2,0},{3,1},{4,6},{5,7},{6,4},{7,5},{8,10},{9,11},{10,... | collective-permute-start | bytes 393224 | tf_op jit(solution)/shard_map/ppermute | solution.py:478
  65.0 0.2 collective-permute-done.9.refs_5_
  65.2 2.3 %correlate_next.5 = (f32[8,16,512]{2,1,0:T(8,128)S(1)}, bf16[8,16,512]{2,1,0:T(8,128)(2,1)S(1)}) custom-call(bf16[256,8192]{1,0:T(8,128)(2,1)S(1)} %get-tuple-element.61.white_ref, bf16[8448,128]{1,0:T(8,128)(2,1)S(1)} %get-tuple-element.55.table_ref), custom_call_target="tpu_custom_call" | custom-call | flops 2147483648 | bytes 8388608 | tf_op jit(solution)/shard_map/correlate_next/pallas_call | solution.py:363
  67.5 0.1 collective-permute-start.11
  67.6 1.7 %collective-permute-done.10.refs_6_ = bf16[8,16,512]{2,1,0:T(8,128)(2,1)S(1)} collective-permute-done((bf16[8,16,512]{2,1,0:T(8,128)(2,1)S(1)}, bf16[8,16,512]{2,1,0:T(8,128)(2,1)S(1)}, u32[]{:S(2)}, u32[]{:S(2)}) %collective-permute-start.10) | collective-permute-done | bytes 131104 | tf_op jit(solution)/shard_map/ppermute | solution.py:478
  69.3 3.3 %collective-permute-done.11.refs_7_ = bf16[8,16,512]{2,1,0:T(8,128)(2,1)S(1)} collective-permute-done((bf16[8,16,512]{2,1,0:T(8,128)(2,1)S(1)}, bf16[8,16,512]{2,1,0:T(8,128)(2,1)S(1)}, u32[]{:S(2)}, u32[]{:S(2)}) %collective-permute-start.11) | collective-permute-done | bytes 131104 | tf_op jit(solution)/shard_map/ppermute | solution.py:478
  72.5 0.1 add_line.1
  72.6 17.2 %all_to_all.11.parts_ref = bf16[8,16,2048]{2,1,0:T(8,128)(2,1)S(1)} all-to-all(bf16[8,16,2048]{2,1,0:T(8,128)(2,1)S(1)} %add_line.1), channel_id=1, replica_groups={{0,4,8,12,16,20,24,28},{1,5,9,13,17,21,25,29},{2,6,10,14,18,22,26,30},{..., dimensions={0} | all-to-all | bytes 1048576 | tf_op jit(solution)/shard_map/all_to_all | solution.py:481
  89.8 1.3 %finish.1 = f32[16,2,4,256]{3,2,1,0:T(4,128)} custom-call(bf16[8,16,2048]{2,1,0:T(8,128)(2,1)S(1)} %all_to_all.11.parts_ref), custom_call_target="tpu_custom_call" | custom-call | bytes 1048576 | tf_op jit(solution)/shard_map/finish/pallas_call | solution.py:414
  (5 shorter events, 0.1 us)
Async XLA Ops:
  0.0 18.4 %copy-start = (bf16[512,4096]{1,0:T(8,128)(2,1)S(1)}, bf16[512,4096]{1,0:T(8,128)(2,1)}, u32[]{:S(2)}) copy-start(bf16[512,4096]{1,0:T(8,128)(2,1)} %param.4) | copy-start | bytes 12582916
  0.0 18.4 %copy-start.1 = (s32[16]{0:T(128)S(1)}, s32[16]{0:T(128)}, u32[]{:S(2)}) copy-start(s32[16]{0:T(128)} %off_ref.5) | copy-start | bytes 196
  0.0 0.8 copy-start.2
  0.8 13.0 %copy-start.3 = (bf16[64]{0:T(256)(128)(2,1)S(1)}, bf16[64]{0:T(256)(128)(2,1)}, u32[]{:S(2)}) copy-start(bf16[64]{0:T(256)(128)(2,1)} %param.5) | copy-start | bytes 388
  3.6 7.8 %collective-permute-start = (bf16[33,16,128]{2,1,0:T(8,128)(2,1)S(1)}, bf16[33,16,128]{2,1,0:T(8,128)(2,1)S(1)}, u32[]{:S(2)}, u32[]{:S(2)}) collective-permute-start(bf16[33,16,128]{2,1,0:T(8,128)(2,1)S(1)} %get-tuple-element.37), channel_id=1, source_target_pairs={{1,2},{3,4},{5,6},{7,8},{9,10},{11,12},{13,14},{15,16},{17,18},{19... | collective-permute-start | bytes 405512 | tf_op jit(solution)/shard_map/ppermute | solution.py:439
  11.4 7.0 %collective-permute-start.4 = (bf16[16,16,4096]{2,1,0:T(8,128)(2,1)S(1)}, bf16[16,16,4096]{2,1,0:T(8,128)(2,1)S(1)}, u32[]{:S(2)}, u32[]{:S(2)}) collective-permute-start(bf16[16,16,4096]{2,1,0:T(8,128)(2,1)S(1)} %get-tuple-element.40), channel_id=1, source_target_pairs={{0,1},{1,0},{2,3},{3,2},{4,5},{5,4},{6,7},{7,6},{8,9},{9,8},{10,11... | collective-permute-start | bytes 6291464 | tf_op jit(solution)/shard_map/ppermute | solution.py:441
  11.4 7.0 %collective-permute-start.5 = (bf16[33,16,128]{2,1,0:T(8,128)(2,1)S(1)}, bf16[33,16,128]{2,1,0:T(8,128)(2,1)S(1)}, u32[]{:S(2)}, u32[]{:S(2)}) collective-permute-start(bf16[33,16,128]{2,1,0:T(8,128)(2,1)S(1)} %collective-permute-done.edge_ref), channel_id=1, source_target_pairs={{0,1},{2,3},{4,5},{6,7},{8,9},{10,11},{12,13},{14,15},{16,17},{18,... | collective-permute-start | bytes 405512 | tf_op jit(solution)/shard_map/ppermute | solution.py:442
  13.9 7.5 %collective-permute-start.3 = (bf16[8,4352]{1,0:T(8,128)(2,1)S(1)}, bf16[8,4352]{1,0:T(8,128)(2,1)S(1)}, u32[]{:S(2)}, u32[]{:S(2)}) collective-permute-start(bf16[8,4352]{1,0:T(8,128)(2,1)S(1)} %extend_sources.1.refs_0_), channel_id=1, source_target_pairs={{0,192},{32,224},{64,0},{96,32},{128,64},{160,96},{192,128},{224,1... | collective-permute-start | bytes 208904 | tf_op jit(solution)/shard_map/ppermute | solution.py:445
  16.7 5.8 %collective-permute-start.2 = (bf16[8,4352]{1,0:T(8,128)(2,1)S(1)}, bf16[8,4352]{1,0:T(8,128)(2,1)S(1)}, u32[]{:S(2)}, u32[]{:S(2)}) collective-permute-start(bf16[8,4352]{1,0:T(8,128)(2,1)S(1)} %extend_sources.1.refs_0_), channel_id=1, source_target_pairs={{0,128},{32,160},{64,192},{96,224},{128,0},{160,32},{192,64},{224,... | collective-permute-start | bytes 208904 | tf_op jit(solution)/shard_map/ppermute | solution.py:445
  17.5 5.8 %collective-permute-start.1 = (bf16[8,4352]{1,0:T(8,128)(2,1)S(1)}, bf16[8,4352]{1,0:T(8,128)(2,1)S(1)}, u32[]{:S(2)}, u32[]{:S(2)}) collective-permute-start(bf16[8,4352]{1,0:T(8,128)(2,1)S(1)} %extend_sources.1.refs_0_), channel_id=1, source_target_pairs={{0,64},{32,96},{64,128},{96,160},{128,192},{160,224},{192,0},{224,... | collective-permute-start | bytes 208904 | tf_op jit(solution)/shard_map/ppermute | solution.py:445
  23.3 5.9 %collective-permute-start.6 = (bf16[8,4352]{1,0:T(8,128)(2,1)S(1)}, bf16[8,4352]{1,0:T(8,128)(2,1)S(1)}, u32[]{:S(2)}, u32[]{:S(2)}) collective-permute-start(bf16[8,4352]{1,0:T(8,128)(2,1)S(1)} %add_pieces.2.refs_0_), channel_id=1, source_target_pairs={{0,32},{32,0},{64,96},{96,64},{128,160},{160,128},{192,224},{224,1... | collective-permute-start | bytes 208904 | tf_op jit(solution)/shard_map/ppermute | solution.py:452
  29.2 1.3 %collective-permute-start.7 = (bf16[8,4352]{1,0:T(8,128)(2,1)S(1)}, bf16[8,4352]{1,0:T(8,128)(2,1)S(1)}, u32[]{:S(2)}, u32[]{:S(2)}) collective-permute-start(bf16[8,4352]{1,0:T(8,128)(2,1)S(1)} %add_pieces.3.mine_ref), channel_id=1, source_target_pairs={{0,1},{1,0},{2,3},{3,2},{4,5},{5,4},{6,7},{7,6},{8,9},{9,8},{10,11... | collective-permute-start | bytes 208904 | tf_op jit(solution)/shard_map/ppermute | solution.py:458
  55.2 5.1 %collective-permute-start.8 = (bf16[8,16,512]{2,1,0:T(8,128)(2,1)S(1)}, bf16[8,16,512]{2,1,0:T(8,128)(2,1)S(1)}, u32[]{:S(2)}, u32[]{:S(2)}) collective-permute-start(bf16[8,16,512]{2,1,0:T(8,128)(2,1)S(1)} %get-tuple-element.57), channel_id=1, source_target_pairs={{0,2},{1,3},{2,0},{3,1},{4,6},{5,7},{6,4},{7,5},{8,10},{9,11},{10,... | collective-permute-start | bytes 393224 | tf_op jit(solution)/shard_map/ppermute | solution.py:472
  59.0 6.2 %collective-permute-start.9 = (bf16[8,16,512]{2,1,0:T(8,128)(2,1)S(1)}, bf16[8,16,512]{2,1,0:T(8,128)(2,1)S(1)}, u32[]{:S(2)}, u32[]{:S(2)}) collective-permute-start(bf16[8,16,512]{2,1,0:T(8,128)(2,1)S(1)} %get-tuple-element.60), channel_id=1, source_target_pairs={{0,2},{1,3},{2,0},{3,1},{4,6},{5,7},{6,4},{7,5},{8,10},{9,11},{10,... | collective-permute-start | bytes 393224 | tf_op jit(solution)/shard_map/ppermute | solution.py:478
  62.7 6.6 %collective-permute-start.10 = (bf16[8,16,512]{2,1,0:T(8,128)(2,1)S(1)}, bf16[8,16,512]{2,1,0:T(8,128)(2,1)S(1)}, u32[]{:S(2)}, u32[]{:S(2)}) collective-permute-start(bf16[8,16,512]{2,1,0:T(8,128)(2,1)S(1)} %get-tuple-element.65), channel_id=1, source_target_pairs={{0,2},{1,3},{2,0},{3,1},{4,6},{5,7},{6,4},{7,5},{8,10},{9,11},{10,... | collective-permute-start | bytes 393224 | tf_op jit(solution)/shard_map/ppermute | solution.py:478
  67.5 5.1 %collective-permute-start.11 = (bf16[8,16,512]{2,1,0:T(8,128)(2,1)S(1)}, bf16[8,16,512]{2,1,0:T(8,128)(2,1)S(1)}, u32[]{:S(2)}, u32[]{:S(2)}) collective-permute-start(bf16[8,16,512]{2,1,0:T(8,128)(2,1)S(1)} %get-tuple-element.66), channel_id=1, source_target_pairs={{0,2},{1,3},{2,0},{3,1},{4,6},{5,7},{6,4},{7,5},{8,10},{9,11},{10,... | collective-permute-start | bytes 393224 | tf_op jit(solution)/shard_map/ppermute | solution.py:478

commit v10 on v7

--- a/solution.py
+++ b/solution.py
@@ -271,21 +271,20 @@
     )(offsets, taps, mine, other, *powers)
 
 
-def lag_products(white, table_ref, pairs, keep_ref, send_ref, half_groups):
-    rows, depth = white.shape
-    sub = rows // half_groups // 2
+def lag_block(table_ref, start, depth, pair):
+    offset = start + pair * 2 * SHIFTS
+    left = table_ref[offset : offset + depth, :]
+    right = table_ref[offset + SHIFTS : offset + SHIFTS + depth, :]
+    return jnp.concatenate([left, right], axis=1)
+
+
+def split_line(value, cols, keep_ref, send_ref, half_groups):
+    rows, width = value.shape
     own_low = (lax.axis_index("tm") // 2) % 2 == 0
-    for place, pair in enumerate(pairs):
-        offset = pair * 2 * SHIFTS
-        left = table_ref[offset : offset + depth, :]
-        right = table_ref[offset + SHIFTS : offset + SHIFTS + depth, :]
-        lags = jnp.concatenate([left, right], axis=1)
-        value = jnp.dot(white[...], lags, preferred_element_type=jnp.float32)
-        value = value.reshape(half_groups, 2, sub, 2 * LANE)
-        low, high = value[:, 0], value[:, 1]
-        cols = slice(place * 2 * LANE, (place + 1) * 2 * LANE)
-        keep_ref[:, :, cols] = jnp.where(own_low, low, high)
-        send_ref[:, :, cols] = jnp.where(own_low, high, low).astype(jnp.bfloat16)
+    value = value.reshape(half_groups, 2, rows // half_groups // 2, width)
+    low, high = value[:, 0], value[:, 1]
+    keep_ref[:, :, cols] = jnp.where(own_low, low, high)
+    send_ref[:, :, cols] = jnp.where(own_low, high, low).astype(jnp.bfloat16)
 
 
 def correlate_first(energies, traces, row_blocks, pairs, half_groups, total_samples):
@@ -298,7 +297,7 @@
 
     def kernel(energy_ref, traces_ref, *refs):
         row_refs = refs[:parts]
-        keep_ref, send_ref, white, table, buf, shifted, sems = refs[parts:]
+        keep_ref, send_ref, white, table, buf, total, sems = refs[parts:]
         copies = []
         for i in range(loads):
             for r, rows_ref in enumerate(row_refs):
@@ -313,19 +312,44 @@
         turned = padded.T
         blocks = channels // LANE
         gain = jnp.concatenate([turned[:, r : r + 1] for r in range(blocks)], axis=0)
-        trace = traces_ref[...] * turned[:NS, blocks : blocks + 1]
-        trace = trace.astype(jnp.bfloat16).astype(jnp.float32)
-        for b in range(SHIFTS):
-            moved = trace if b == 0 else pltpu.roll(trace, length - b, 1)
-            shifted[b * NS : (b + 1) * NS, :] = moved
-        for j in range(length // LANE):
-            cols = slice(j * LANE, (j + 1) * LANE)
-            table[cols, :] = shifted[:, cols].T.astype(jnp.bfloat16)
+        source_gain = turned[:NS, blocks : blocks + 1]
+        lane = lax.broadcasted_iota(jnp.int32, (NS, LANE), 1)
+
+        def traces_block(j):
+            if j * LANE >= length:
+                return jnp.zeros((NS, LANE), jnp.float32)
+            block = traces_ref[:, j * LANE : (j + 1) * LANE] * source_gain
+            return block.astype(jnp.bfloat16).astype(jnp.float32)
+
+        def build(low, high):
+            for j in range(low // LANE, high // LANE):
+                here, after = traces_block(j), traces_block(j + 1)
+                lines = [here]
+                for b in range(1, SHIFTS):
+                    lines.append(pltpu.roll(jnp.where(lane < b, after, here), LANE - b, 1))
+                turned_block = jnp.concatenate(lines, axis=0).T
+                table[j * LANE : (j + 1) * LANE, :] = turned_block.astype(jnp.bfloat16)
+
+        ahead = chunk + LAGS
+        build(0, ahead)
         for i in range(loads):
             for copy in copies[i * parts : (i + 1) * parts]:
                 copy.wait()
-            white[:, i * chunk : (i + 1) * chunk] = (buf[i] * gain).astype(jnp.bfloat16)
-        lag_products(white, table, pairs, keep_ref, send_ref, half_groups)
+            span = slice(i * chunk, (i + 1) * chunk)
+            white[:, span] = (buf[i] * gain).astype(jnp.bfloat16)
+            if i + 1 < loads:
+                build(i * chunk + ahead, min((i + 1) * chunk + ahead, length))
+            for place, pair in enumerate(pairs):
+                value = jnp.dot(
+                    white[:, span],
+                    lag_block(table, i * chunk, chunk, pair),
+                    preferred_element_type=jnp.float32,
+                )
+                cols = slice(place * 2 * LANE, (place + 1) * 2 * LANE)
+                total[:, cols] = value if i == 0 else total[:, cols] + value
+        for place in range(len(pairs)):
+            cols = slice(place * 2 * LANE, (place + 1) * 2 * LANE)
+            split_line(total[:, cols], cols, keep_ref, send_ref, half_groups)
 
     sub = channels // half_groups // 2
     cols = len(pairs) * 2 * LANE
@@ -341,7 +365,7 @@
         [VMEM, VMEM] + [ANY] * parts,
         [
             pltpu.VMEM((loads, channels, chunk), jnp.float32),
-            pltpu.VMEM((LANE, length), jnp.float32),
+            pltpu.VMEM((channels, len(pairs) * 2 * LANE), jnp.float32),
             pltpu.SemaphoreType.DMA((loads * parts,)),
         ],
         limit=40,
@@ -354,7 +378,11 @@
     channels, depth = white.shape
 
     def kernel(white_ref, table_ref, keep_ref, send_ref):
-        lag_products(white_ref, table_ref, pairs, keep_ref, send_ref, half_groups)
+        for place, pair in enumerate(pairs):
+            lags = lag_block(table_ref, 0, depth, pair)
+            value = jnp.dot(white_ref[...], lags, preferred_element_type=jnp.float32)
+            cols = slice(place * 2 * LANE, (place + 1) * 2 * LANE)
+            split_line(value, cols, keep_ref, send_ref, half_groups)
 
     sub = channels // half_groups // 2
     cols = len(pairs) * 2 * LANE

time: 87.4 us -> 85.5 us (0.978)
  Pallas kernels: 24 us -> 22.2 us
    pallas_call x1, Pallas kernels: 5.97 us -> 4.18 us  [correlate_first(): call(kernel, 'correlate_first', [shape((half_groups, sub, cols), jnp.floa...]
where the time goes in v10:
time: 85.5 us; the launch traced here: 85.4 us
  blocking collectives  36.7 us (43%)
  Pallas kernels  22.2 us (26%)
  starting transfers between devices  16.7 us (20%)
  waiting for transfers between devices  8.74 us (10%)
    all_to_all x1, blocking collectives, shards(): lax.all_to_all(energy, 'tm', 0, 0, tiled=True, axis_index_groups=same)  18.7 us
    all_to_all x1, blocking collectives, shards(): lax.all_to_all(summed, 'tm', 0, 0, tiled=True, axis_index_groups=columns)  18.1 us
    pallas_call x2, Pallas kernels, correlate_next(): call(kernel, 'correlate_next', [shape((half_groups, sub, cols), jnp.float...  6.8 us
    pallas_call x2, Pallas kernels, filter_rows(): call(kernel, 'filter_rows', [shape((all_groups * sub, 2 * half), jnp.floa...  5.97 us
    ppermute x2, waiting for transfers between devices, shards(): arrivals.append(lax.ppermute(send, 'tm', line))  4.36 us
    pallas_call x1, Pallas kernels, correlate_first(): call(kernel, 'correlate_first', [shape((half_groups, sub, cols), jnp.floa...  4.18 us
    ppermute x1, starting transfers between devices, shards(): edge = lax.ppermute(edge, 'tm', both_next)  4.18 us
    ppermute x3, starting transfers between devices, shards(): lax.ppermute(piece, 'chan', [(i, (i + 2 * d) % groups_chan) for i in rang...  3.95 us
  transfers between devices with their start and end apart: 11, of which 7 were waited for; matrix products, arithmetic and copies ran while one was open for 0% of the time, Pallas kernels for 15%

profile of v10, /device:TPU:8, one launch (start us, length us, event | category | flops | bytes accessed | tf_op | source)
XLA Modules:
  0.0 85.4 jit_solution(10550989589607063939)
XLA Ops:
  0.0 0.0 copy-start
  0.0 0.0 copy-start.1
  0.0 0.0 copy-start.2
  0.0 0.8 copy-done.2
  0.8 0.0 copy-start.3
  0.8 2.8 %pick_sources.1 = (bf16[8,4096]{1,0:T(8,128)(2,1)S(1)}, bf16[17,16,128]{2,1,0:T(8,128)(2,1)S(1)}, bf16[16,16,128]{2,1,0:T(8,128)(2,1)S(1)}, bf16[16,16,4096]{2,1,0:T(8,128)(2,1)S(1)}) custom-call(s32[2,4]{1,0:T(2,128)S(1)} %copy-done.2, bf16[16,2,16,4096]{3,2,1,0:T(8,128)(2,1)} %bitcast.1), custom_call_target="tpu_custom_call" | custom-call | bytes 2097152 | tf_op jit(solution)/shard_map/pick_sources/pallas_call | solution.py:99
  3.6 0.1 collective-permute-start.5
  3.7 4.2 %collective-permute-start = (bf16[17,16,128]{2,1,0:T(8,128)(2,1)S(1)}, bf16[17,16,128]{2,1,0:T(8,128)(2,1)S(1)}, u32[]{:S(2)}, u32[]{:S(2)}) collective-permute-start(bf16[17,16,128]{2,1,0:T(8,128)(2,1)S(1)} %get-tuple-element.34), channel_id=1, source_target_pairs={{1,2},{3,4},{5,6},{7,8},{9,10},{11,12},{13,14},{15,16},{17,18},{19... | collective-permute-start | bytes 208904 | tf_op jit(solution)/shard_map/ppermute | solution.py:465
  7.9 0.7 collective-permute-start.1
  8.6 0.0 copy-done.3
  8.6 0.0 collective-permute-done.1.high_ref
  8.6 1.3 %collective-permute-done.edge_ref = bf16[17,16,128]{2,1,0:T(8,128)(2,1)S(1)} collective-permute-done((bf16[17,16,128]{2,1,0:T(8,128)(2,1)S(1)}, bf16[17,16,128]{2,1,0:T(8,128)(2,1)S(1)}, u32[]{:S(2)}, u32[]{:S(2)}) %collective-permute-start) | collective-permute-done | bytes 69664 | tf_op jit(solution)/shard_map/ppermute | solution.py:465
  9.9 2.2 %collective-permute-start.4 = (bf16[8,4352]{1,0:T(8,128)(2,1)S(1)}, bf16[8,4352]{1,0:T(8,128)(2,1)S(1)}, u32[]{:S(2)}, u32[]{:S(2)}) collective-permute-start(bf16[8,4352]{1,0:T(8,128)(2,1)S(1)} %extend_sources.1.refs_0_), channel_id=1, source_target_pairs={{0,192},{32,224},{64,0},{96,32},{128,64},{160,96},{192,128},{224,1... | collective-permute-start | bytes 208904 | tf_op jit(solution)/shard_map/ppermute | solution.py:472
  12.1 0.8 collective-permute-start.3
  12.9 0.9 %collective-permute-start.2 = (bf16[8,4352]{1,0:T(8,128)(2,1)S(1)}, bf16[8,4352]{1,0:T(8,128)(2,1)S(1)}, u32[]{:S(2)}, u32[]{:S(2)}) collective-permute-start(bf16[8,4352]{1,0:T(8,128)(2,1)S(1)} %extend_sources.1.refs_0_), channel_id=1, source_target_pairs={{0,64},{32,96},{64,128},{96,160},{128,192},{160,224},{192,0},{224,... | collective-permute-start | bytes 208904 | tf_op jit(solution)/shard_map/ppermute | solution.py:472
  13.8 0.0 collective-permute-done.5.other_ref
  13.8 0.0 copy-done
  13.8 0.0 copy-done.1
  13.9 3.0 %filter_rows.2 = (f32[256,8192]{1,0:T(8,128)}, f32[128,128]{1,0:T(8,128)S(1)}) custom-call(s32[16]{0:T(128)S(1)} %copy-done.1, bf16[1,256]{1,0:T(2,128)(2,1)S(1)} %reshape.6.taps_ref, bf16[16,2,16,4096]{3,2,1,0:T(8,128)(2,1)S(1)} %bitcast.2, bf16[16,16,4096]{2,1,0:T(8,128)(2,1)S(1)} %collective-permute-done.5.other_ref, ...), custom_call_target="tpu_custom_call" | custom-call | flops 1073741824 | bytes 6291456 | tf_op jit(solution)/shard_map/filter_rows/pallas_call | solution.py:203
  16.8 0.0 collective-permute-done.4.refs_3_
  16.8 1.1 %collective-permute-done.3.refs_2_ = bf16[8,4352]{1,0:T(8,128)(2,1)S(1)} collective-permute-done((bf16[8,4352]{1,0:T(8,128)(2,1)S(1)}, bf16[8,4352]{1,0:T(8,128)(2,1)S(1)}, u32[]{:S(2)}, u32[]{:S(2)}) %collective-permute-start.3) | collective-permute-done | bytes 69664 | tf_op jit(solution)/shard_map/ppermute | solution.py:472
  18.0 0.7 collective-permute-done.2.refs_1_
  18.7 2.5 %collective-permute-start.6 = (bf16[8,4352]{1,0:T(8,128)(2,1)S(1)}, bf16[8,4352]{1,0:T(8,128)(2,1)S(1)}, u32[]{:S(2)}, u32[]{:S(2)}) collective-permute-start(bf16[8,4352]{1,0:T(8,128)(2,1)S(1)} %add_pieces.2.refs_0_), channel_id=1, source_target_pairs={{0,32},{32,0},{64,96},{96,64},{128,160},{160,128},{192,224},{224,1... | collective-permute-start | bytes 208904 | tf_op jit(solution)/shard_map/ppermute | solution.py:479
  21.3 3.0 %filter_rows.3 = (f32[256,8192]{1,0:T(8,128)}, f32[128,128]{1,0:T(8,128)S(1)}) custom-call(s32[16]{0:T(128)S(1)} %copy-done.1, bf16[1,256]{1,0:T(2,128)(2,1)S(1)} %reshape.6.taps_ref, bf16[16,2,16,4096]{3,2,1,0:T(8,128)(2,1)S(1)} %bitcast.3, bf16[16,16,4096]{2,1,0:T(8,128)(2,1)S(1)} %collective-permute-done.5.other_ref, ...), custom_call_target="tpu_custom_call", output_to_operand_aliasing={{0}: (6, {})} | custom-call | flops 1073741824 | bytes 6291456 | tf_op jit(solution)/shard_map/filter_rows/pallas_call | solution.py:203
  24.3 0.4 collective-permute-done.6.refs_1_
  24.6 1.6 %collective-permute-start.7 = (bf16[8,4352]{1,0:T(8,128)(2,1)S(1)}, bf16[8,4352]{1,0:T(8,128)(2,1)S(1)}, u32[]{:S(2)}, u32[]{:S(2)}) collective-permute-start(bf16[8,4352]{1,0:T(8,128)(2,1)S(1)} %add_pieces.3.mine_ref), channel_id=1, source_target_pairs={{0,1},{1,0},{2,3},{3,2},{4,5},{5,4},{6,7},{7,6},{8,9},{9,8},{10,11... | collective-permute-start | bytes 208904 | tf_op jit(solution)/shard_map/ppermute | solution.py:485
  26.3 0.9 %collective-permute-done.7.other_ref = bf16[8,4352]{1,0:T(8,128)(2,1)S(1)} collective-permute-done((bf16[8,4352]{1,0:T(8,128)(2,1)S(1)}, bf16[8,4352]{1,0:T(8,128)(2,1)S(1)}, u32[]{:S(2)}, u32[]{:S(2)}) %collective-permute-start.7) | collective-permute-done | bytes 69664 | tf_op jit(solution)/shard_map/ppermute | solution.py:485
  27.2 1.0 %filter_sources.1 = (f32[8,8448]{1,0:T(8,128)S(1)}, f32[16,8,128]{2,1,0:T(8,128)S(1)}) custom-call(s32[16]{0:T(128)S(1)} %copy-done.1, bf16[1,256]{1,0:T(2,128)(2,1)S(1)} %reshape.6.taps_ref, bf16[8,4352]{1,0:T(8,128)(2,1)S(1)} %add_pieces.3.mine_ref, bf16[8,4352]{1,0:T(8,128)(2,1)S(1)} %collective-permute-done.7.other_ref, ...), custom_call_target="tpu_custom_call" | custom-call | bytes 1048576 | tf_op jit(solution)/shard_map/filter_sources/pallas_call | solution.py:265
  28.2 18.7 %all_to_all.10.energy_ref = f32[16,8,128]{2,1,0:T(8,128)S(1)} all-to-all(f32[16,8,128]{2,1,0:T(8,128)S(1)} %get-tuple-element.48), channel_id=1, replica_groups={{0,2,4,6,8,10,12,14,16,18,20,22,24,26,28,30},{1,3,5,7,9,11,13,15,17,19,..., dimensions={0} | all-to-all | bytes 131072 | tf_op jit(solution)/shard_map/all_to_all | solution.py:490
  46.9 4.2 %correlate_first.1 = (f32[8,16,512]{2,1,0:T(8,128)S(1)}, bf16[8,16,512]{2,1,0:T(8,128)(2,1)S(1)}, bf16[256,8192]{1,0:T(8,128)(2,1)S(1)}, bf16[8448,128]{1,0:T(8,128)(2,1)S(1)}) custom-call(f32[16,8,128]{2,1,0:T(8,128)S(1)} %all_to_all.10.energy_ref, f32[8,8448]{1,0:T(8,128)S(1)} %get-tuple-element.49.traces_ref, f32[256,8192]{1,0:T(8,128)} %get-tuple-element.50.refs_0_), custom_call_target="tpu_custom_call" | custom-call | flops 2147483648 | bytes 16777216 | tf_op jit(solution)/shard_map/correlate_first/pallas_call | solution.py:356
  51.1 1.5 %collective-permute-start.8 = (bf16[8,16,512]{2,1,0:T(8,128)(2,1)S(1)}, bf16[8,16,512]{2,1,0:T(8,128)(2,1)S(1)}, u32[]{:S(2)}, u32[]{:S(2)}) collective-permute-start(bf16[8,16,512]{2,1,0:T(8,128)(2,1)S(1)} %get-tuple-element.55), channel_id=1, source_target_pairs={{0,2},{1,3},{2,0},{3,1},{4,6},{5,7},{6,4},{7,5},{8,10},{9,11},{10,... | collective-permute-start | bytes 393224 | tf_op jit(solution)/shard_map/ppermute | solution.py:499
  52.5 3.4 %correlate_next.2 = (f32[8,16,768]{2,1,0:T(8,128)S(1)}, bf16[8,16,768]{2,1,0:T(8,128)(2,1)S(1)}) custom-call(bf16[256,8192]{1,0:T(8,128)(2,1)S(1)} %get-tuple-element.56.white_ref, bf16[8448,128]{1,0:T(8,128)(2,1)S(1)} %get-tuple-element.53.table_ref), custom_call_target="tpu_custom_call" | custom-call | flops 3221225472 | bytes 8388608 | tf_op jit(solution)/shard_map/correlate_next/pallas_call | solution.py:389
  55.9 0.7 collective-permute-start.9
  56.7 0.0 collective-permute-done.8.refs_3_
  56.7 3.4 %correlate_next.3 = (f32[8,16,768]{2,1,0:T(8,128)S(1)}, bf16[8,16,768]{2,1,0:T(8,128)(2,1)S(1)}) custom-call(bf16[256,8192]{1,0:T(8,128)(2,1)S(1)} %get-tuple-element.56.white_ref, bf16[8448,128]{1,0:T(8,128)(2,1)S(1)} %get-tuple-element.53.table_ref), custom_call_target="tpu_custom_call" | custom-call | flops 3221225472 | bytes 8388608 | tf_op jit(solution)/shard_map/correlate_next/pallas_call | solution.py:389
  60.1 1.5 %collective-permute-start.10 = (bf16[8,16,768]{2,1,0:T(8,128)(2,1)S(1)}, bf16[8,16,768]{2,1,0:T(8,128)(2,1)S(1)}, u32[]{:S(2)}, u32[]{:S(2)}) collective-permute-start(bf16[8,16,768]{2,1,0:T(8,128)(2,1)S(1)} %get-tuple-element.60), channel_id=1, source_target_pairs={{0,2},{1,3},{2,0},{3,1},{4,6},{5,7},{6,4},{7,5},{8,10},{9,11},{10,... | collective-permute-start | bytes 589832 | tf_op jit(solution)/shard_map/ppermute | solution.py:505
  61.5 0.7 collective-permute-done.9.refs_4_
  62.2 3.7 %collective-permute-done.10.refs_5_ = bf16[8,16,768]{2,1,0:T(8,128)(2,1)S(1)} collective-permute-done((bf16[8,16,768]{2,1,0:T(8,128)(2,1)S(1)}, bf16[8,16,768]{2,1,0:T(8,128)(2,1)S(1)}, u32[]{:S(2)}, u32[]{:S(2)}) %collective-permute-start.10) | collective-permute-done | bytes 196640 | tf_op jit(solution)/shard_map/ppermute | solution.py:505
  65.9 0.1 add_line.1
  66.0 18.1 %all_to_all.11.parts_ref = bf16[8,16,2048]{2,1,0:T(8,128)(2,1)S(1)} all-to-all(bf16[8,16,2048]{2,1,0:T(8,128)(2,1)S(1)} %add_line.1), channel_id=1, replica_groups={{0,4,8,12,16,20,24,28},{1,5,9,13,17,21,25,29},{2,6,10,14,18,22,26,30},{..., dimensions={0} | all-to-all | bytes 1048576 | tf_op jit(solution)/shard_map/all_to_all | solution.py:508
  84.1 1.3 %finish.1 = f32[16,2,4,256]{3,2,1,0:T(4,128)} custom-call(bf16[8,16,2048]{2,1,0:T(8,128)(2,1)S(1)} %all_to_all.11.parts_ref), custom_call_target="tpu_custom_call" | custom-call | bytes 1048576 | tf_op jit(solution)/shard_map/finish/pallas_call | solution.py:440
  (5 shorter events, 0.1 us)
Async XLA Ops:
  0.0 13.8 %copy-start = (bf16[512,4096]{1,0:T(8,128)(2,1)S(1)}, bf16[512,4096]{1,0:T(8,128)(2,1)}, u32[]{:S(2)}) copy-start(bf16[512,4096]{1,0:T(8,128)(2,1)} %param.4) | copy-start | bytes 12582916
  0.0 13.8 %copy-start.1 = (s32[16]{0:T(128)S(1)}, s32[16]{0:T(128)}, u32[]{:S(2)}) copy-start(s32[16]{0:T(128)} %off_ref.5) | copy-start | bytes 196
  0.0 0.8 copy-start.2
  0.8 7.7 %copy-start.3 = (bf16[64]{0:T(256)(128)(2,1)S(1)}, bf16[64]{0:T(256)(128)(2,1)}, u32[]{:S(2)}) copy-start(bf16[64]{0:T(256)(128)(2,1)} %param.5) | copy-start | bytes 388
  3.6 10.2 %collective-permute-start.5 = (bf16[16,16,4096]{2,1,0:T(8,128)(2,1)S(1)}, bf16[16,16,4096]{2,1,0:T(8,128)(2,1)S(1)}, u32[]{:S(2)}, u32[]{:S(2)}) collective-permute-start(bf16[16,16,4096]{2,1,0:T(8,128)(2,1)S(1)} %get-tuple-element.37), channel_id=1, source_target_pairs={{0,1},{1,0},{2,3},{3,2},{4,5},{5,4},{6,7},{7,6},{8,9},{9,8},{10,11... | collective-permute-start | bytes 6291464 | tf_op jit(solution)/shard_map/ppermute | solution.py:466
  3.7 6.2 %collective-permute-start = (bf16[17,16,128]{2,1,0:T(8,128)(2,1)S(1)}, bf16[17,16,128]{2,1,0:T(8,128)(2,1)S(1)}, u32[]{:S(2)}, u32[]{:S(2)}) collective-permute-start(bf16[17,16,128]{2,1,0:T(8,128)(2,1)S(1)} %get-tuple-element.34), channel_id=1, source_target_pairs={{1,2},{3,4},{5,6},{7,8},{9,10},{11,12},{13,14},{15,16},{17,18},{19... | collective-permute-start | bytes 208904 | tf_op jit(solution)/shard_map/ppermute | solution.py:465
  7.9 0.7 collective-permute-start.1
  9.9 7.0 %collective-permute-start.4 = (bf16[8,4352]{1,0:T(8,128)(2,1)S(1)}, bf16[8,4352]{1,0:T(8,128)(2,1)S(1)}, u32[]{:S(2)}, u32[]{:S(2)}) collective-permute-start(bf16[8,4352]{1,0:T(8,128)(2,1)S(1)} %extend_sources.1.refs_0_), channel_id=1, source_target_pairs={{0,192},{32,224},{64,0},{96,32},{128,64},{160,96},{192,128},{224,1... | collective-permute-start | bytes 208904 | tf_op jit(solution)/shard_map/ppermute | solution.py:472
  12.1 5.8 %collective-permute-start.3 = (bf16[8,4352]{1,0:T(8,128)(2,1)S(1)}, bf16[8,4352]{1,0:T(8,128)(2,1)S(1)}, u32[]{:S(2)}, u32[]{:S(2)}) collective-permute-start(bf16[8,4352]{1,0:T(8,128)(2,1)S(1)} %extend_sources.1.refs_0_), channel_id=1, source_target_pairs={{0,128},{32,160},{64,192},{96,224},{128,0},{160,32},{192,64},{224,... | collective-permute-start | bytes 208904 | tf_op jit(solution)/shard_map/ppermute | solution.py:472
  12.9 5.8 %collective-permute-start.2 = (bf16[8,4352]{1,0:T(8,128)(2,1)S(1)}, bf16[8,4352]{1,0:T(8,128)(2,1)S(1)}, u32[]{:S(2)}, u32[]{:S(2)}) collective-permute-start(bf16[8,4352]{1,0:T(8,128)(2,1)S(1)} %extend_sources.1.refs_0_), channel_id=1, source_target_pairs={{0,64},{32,96},{64,128},{96,160},{128,192},{160,224},{192,0},{224,... | collective-permute-start | bytes 208904 | tf_op jit(solution)/shard_map/ppermute | solution.py:472
  18.7 5.9 %collective-permute-start.6 = (bf16[8,4352]{1,0:T(8,128)(2,1)S(1)}, bf16[8,4352]{1,0:T(8,128)(2,1)S(1)}, u32[]{:S(2)}, u32[]{:S(2)}) collective-permute-start(bf16[8,4352]{1,0:T(8,128)(2,1)S(1)} %add_pieces.2.refs_0_), channel_id=1, source_target_pairs={{0,32},{32,0},{64,96},{96,64},{128,160},{160,128},{192,224},{224,1... | collective-permute-start | bytes 208904 | tf_op jit(solution)/shard_map/ppermute | solution.py:479
  24.6 2.5 %collective-permute-start.7 = (bf16[8,4352]{1,0:T(8,128)(2,1)S(1)}, bf16[8,4352]{1,0:T(8,128)(2,1)S(1)}, u32[]{:S(2)}, u32[]{:S(2)}) collective-permute-start(bf16[8,4352]{1,0:T(8,128)(2,1)S(1)} %add_pieces.3.mine_ref), channel_id=1, source_target_pairs={{0,1},{1,0},{2,3},{3,2},{4,5},{5,4},{6,7},{7,6},{8,9},{9,8},{10,11... | collective-permute-start | bytes 208904 | tf_op jit(solution)/shard_map/ppermute | solution.py:485
  51.1 5.6 %collective-permute-start.8 = (bf16[8,16,512]{2,1,0:T(8,128)(2,1)S(1)}, bf16[8,16,512]{2,1,0:T(8,128)(2,1)S(1)}, u32[]{:S(2)}, u32[]{:S(2)}) collective-permute-start(bf16[8,16,512]{2,1,0:T(8,128)(2,1)S(1)} %get-tuple-element.55), channel_id=1, source_target_pairs={{0,2},{1,3},{2,0},{3,1},{4,6},{5,7},{6,4},{7,5},{8,10},{9,11},{10,... | collective-permute-start | bytes 393224 | tf_op jit(solution)/shard_map/ppermute | solution.py:499
  55.9 6.3 %collective-permute-start.9 = (bf16[8,16,768]{2,1,0:T(8,128)(2,1)S(1)}, bf16[8,16,768]{2,1,0:T(8,128)(2,1)S(1)}, u32[]{:S(2)}, u32[]{:S(2)}) collective-permute-start(bf16[8,16,768]{2,1,0:T(8,128)(2,1)S(1)} %get-tuple-element.59), channel_id=1, source_target_pairs={{0,2},{1,3},{2,0},{3,1},{4,6},{5,7},{6,4},{7,5},{8,10},{9,11},{10,... | collective-permute-start | bytes 589832 | tf_op jit(solution)/shard_map/ppermute | solution.py:505
  60.1 5.8 %collective-permute-start.10 = (bf16[8,16,768]{2,1,0:T(8,128)(2,1)S(1)}, bf16[8,16,768]{2,1,0:T(8,128)(2,1)S(1)}, u32[]{:S(2)}, u32[]{:S(2)}) collective-permute-start(bf16[8,16,768]{2,1,0:T(8,128)(2,1)S(1)} %get-tuple-element.60), channel_id=1, source_target_pairs={{0,2},{1,3},{2,0},{3,1},{4,6},{5,7},{6,4},{7,5},{8,10},{9,11},{10,... | collective-permute-start | bytes 589832 | tf_op jit(solution)/shard_map/ppermute | solution.py:505

commit v11 on v10

--- a/solution.py
+++ b/solution.py
@@ -59,7 +59,7 @@
     groups, _, sub, samples = x4.shape
     channels = groups * 2 * sub
 
-    def kernel(ids_ref, x_ref, own_ref, edge_ref, high_ref, away_ref, buf, sems):
+    def kernel(ids_ref, x_ref, own_ref, edge_ref, high_ref, away_ref, mine_ref, buf, sems):
         base = lax.axis_index("chan") * channels
         core = lax.axis_index("tm") % 2
         copies = []
@@ -78,6 +78,7 @@
             ),
             pltpu.make_async_copy(x_ref.at[:, 1, :, last], high_ref, sems.at[NS + 1]),
             pltpu.make_async_copy(x_ref.at[:, 1 - core], away_ref, sems.at[NS + 2]),
+            pltpu.make_async_copy(x_ref.at[:, core], mine_ref, sems.at[NS + 3]),
         ]
         for copy in copies + rest:
             copy.start()
@@ -104,10 +105,11 @@
             shape((groups + 1, sub, LANE), jnp.bfloat16),
             shape((groups, sub, LANE), jnp.bfloat16),
             shape((groups, sub, samples), jnp.bfloat16),
+            shape((groups, sub, samples), jnp.bfloat16),
         ],
         [SMEM, ANY],
-        [pltpu.VMEM((NS, sub, samples), jnp.bfloat16), pltpu.SemaphoreType.DMA((NS + 3,))],
-        limit=50,
+        [pltpu.VMEM((NS, sub, samples), jnp.bfloat16), pltpu.SemaphoreType.DMA((NS + 4,))],
+        limit=48,
         moved=2 * MIB,
     )(source_channels, x4)
 
@@ -144,8 +146,8 @@
     )(*pieces)[0]
 
 
-def filter_rows(offsets, taps, x4, other, edge, high, first_group, groups, filled=None):
-    all_groups, _, sub, half = x4.shape
+def filter_rows(offsets, taps, mine, other, edge, high, first_group, groups, filled=None):
+    all_groups, sub, half = mine.shape
     filled = [] if filled is None else [filled]
     rows = groups * sub
     chosen = slice(first_group, first_group + groups)
@@ -154,7 +156,7 @@
     total = 2 * parts
 
     def kernel(
-        off_ref, taps_ref, x_ref, other_ref, edge_ref, high_ref, *refs
+        off_ref, taps_ref, mine_ref, other_ref, edge_ref, high_ref, *refs
     ):
         out_ref, power_ref, value_buf, sems = refs[len(filled) :]
         tile = lax.axis_index("tm")
@@ -184,7 +186,7 @@
             power_ref[...] = power
 
         def own(cols):
-            return x_ref[chosen, core, :, cols]
+            return mine_ref[chosen, :, cols]
 
         def swapped(cols):
             return other_ref[chosen, :, cols]
@@ -207,11 +209,11 @@
         [SMEM, VMEM, VMEM, VMEM, VMEM, VMEM] + [ANY] * len(filled),
         [pltpu.VMEM((total, rows, chunk), jnp.float32), pltpu.SemaphoreType.DMA((total,))],
         out_specs=[ANY, VMEM],
-        limit=40,
+        limit=45,
         flops=2 * rows * 2 * half * 512,
         moved=6 * MIB,
         aliases={6: 0} if filled else None,
-    )(offsets, taps, x4, other, edge, high, *filled)
+    )(offsets, taps, mine, other, edge, high, *filled)
 
 
 def filter_sources(offsets, taps, mine, other, powers, chips):
@@ -423,26 +425,34 @@
 def finish(parts, factor):
     count, sub, cols = parts.shape
 
+    stack = LANE // sub
+
     def kernel(parts_ref, out_ref, turned):
-        blank = jnp.zeros((LANE - sub, LANE), jnp.float32)
+        lane = lax.broadcasted_iota(jnp.int32, (sub, LANE), 1)
         value = parts_ref[0].astype(jnp.float32)
         for i in range(1, count):
             value = value + parts_ref[i].astype(jnp.float32)
         value = value * factor
-        for j in range(cols // LANE):
-            block = jnp.concatenate([value[:, j * LANE : (j + 1) * LANE], blank], axis=0)
-            turned[j * LANE : (j + 1) * LANE, :] = block.T
-        for m in range(NS):
-            for j in range(LAGS // LANE):
-                block = turned[pl.ds(j * LANE * NS + m, LANE, stride=NS), :]
-                out_ref[:, m // SB, m % SB, j * LANE : (j + 1) * LANE] = block.T[:sub]
+        for g in range(cols // LANE // stack):
+            first = g * stack
+            blocks = [value[:, (first + k) * LANE : (first + k + 1) * LANE] for k in range(stack)]
+            turned[...] = jnp.concatenate(blocks, axis=0).T
+            by_source = [turned[pl.ds(m, SHIFTS, stride=NS), :] for m in range(NS)]
+            ordered = jnp.concatenate(by_source, axis=0).T
+            for m in range(NS):
+                line = jnp.zeros((sub, LANE), jnp.float32)
+                for k in range(stack):
+                    block = ordered[k * sub : (k + 1) * sub, :]
+                    moved = pltpu.roll(block, ((k - m) * SHIFTS) % LANE, 1) if k != m else block
+                    line = jnp.where(lane // SHIFTS == k, moved, line)
+                out_ref[:, m // SB, m % SB, g * LANE : (g + 1) * LANE] = line
 
     return call(
         kernel,
         "finish",
         [shape((sub, NSRC, SB, LAGS), jnp.float32)],
         [VMEM],
-        [pltpu.VMEM((NS * LAGS, LANE), jnp.float32)],
+        [pltpu.VMEM((LANE, LANE), jnp.float32)],
         moved=MIB,
     )(parts)[0]
 
@@ -457,7 +467,7 @@
     taps = wide_taps(whiten_taps)
 
     x4 = strain_rate.reshape(chips, 2, sub, samples)
-    own, edge, high, away = pick_sources(source_channels, x4)
+    own, edge, high, away, mine = pick_sources(source_channels, x4)
 
     swap = [(i, i ^ 1) for i in range(tiles)]
     to_next = [(2 * k - 1, 2 * k) for k in range(1, chips)]
@@ -473,12 +483,12 @@
         for d in range(1, groups_chan // 2)
     ]
     half = chips // 2
-    filtered, power_a = filter_rows(window_offsets, taps, x4, other, edge, high, 0, half)
+    filtered, power_a = filter_rows(window_offsets, taps, mine, other, edge, high, 0, half)
     *parts, power_a = lax.optimization_barrier((*parts, power_a))
     piece = add_pieces(piece, *parts)
     arrived = lax.ppermute(piece, "chan", [(i, i ^ 1) for i in range(groups_chan)])
     filtered, power_b = filter_rows(
-        window_offsets, taps, x4, other, edge, high, half, half, filtered
+        window_offsets, taps, mine, other, edge, high, half, half, filtered
     )
     arrived, power_b = lax.optimization_barrier((arrived, power_b))
     piece = add_pieces(piece, arrived)

time: 85.5 us -> 86 us (level)
  no operation moved by 1% of the time
where the time goes in v11:
time: 86 us; the launch traced here: 85.7 us
  blocking collectives  36.7 us (43%)
  Pallas kernels  22.7 us (26%)
  starting transfers between devices  16.4 us (19%)
  waiting for transfers between devices  8.9 us (10%)
    all_to_all x1, blocking collectives, shards(): lax.all_to_all(energy, 'tm', 0, 0, tiled=True, axis_index_groups=same)  18.7 us
    all_to_all x1, blocking collectives, shards(): lax.all_to_all(summed, 'tm', 0, 0, tiled=True, axis_index_groups=columns)  18.1 us
    pallas_call x2, Pallas kernels, correlate_next(): call(kernel, 'correlate_next', [shape((half_groups, sub, cols), jnp.float...  6.8 us
    pallas_call x2, Pallas kernels, filter_rows(): call(kernel, 'filter_rows', [shape((all_groups * sub, 2 * half), jnp.floa...  6 us
    ppermute x2, waiting for transfers between devices, shards(): arrivals.append(lax.ppermute(send, 'tm', line))  4.36 us
    pallas_call x1, Pallas kernels, correlate_first(): call(kernel, 'correlate_first', [shape((half_groups, sub, cols), jnp.floa...  4.18 us
    ppermute x1, starting transfers between devices, shards(): edge = lax.ppermute(edge, 'tm', both_next)  4.18 us
    ppermute x3, starting transfers between devices, shards(): lax.ppermute(piece, 'chan', [(i, (i + 2 * d) % groups_chan) for i in rang...  3.91 us
  transfers between devices with their start and end apart: 11, of which 7 were waited for; matrix products, arithmetic and copies ran while one was open for 0% of the time, Pallas kernels for 15%

profile of v11, /device:TPU:8, one launch (start us, length us, event | category | flops | bytes accessed | tf_op | source)
XLA Modules:
  0.0 85.7 jit_solution(13642450176981403900)
XLA Ops:
  0.0 0.0 copy-start.2
  0.0 0.0 copy-start
  0.0 0.0 copy-start.1
  0.0 0.7 copy-done.1
  0.7 3.4 %pick_sources.1 = (bf16[8,4096]{1,0:T(8,128)(2,1)S(1)}, bf16[17,16,128]{2,1,0:T(8,128)(2,1)S(1)}, bf16[16,16,128]{2,1,0:T(8,128)(2,1)S(1)}, bf16[16,16,4096]{2,1,0:T(8,128)(2,1)S(1)}, bf16[16,16,4096]{2,1,0:T(8,128)(2,1)S(1)}) custom-call(s32[2,4]{1,0:T(2,128)S(1)} %copy-done.1, bf16[16,2,16,4096]{3,2,1,0:T(8,128)(2,1)} %bitcast.1), custom_call_target="tpu_custom_call" | custom-call | bytes 2097152 | tf_op jit(solution)/shard_map/pick_sources/pallas_call | solution.py:100
  4.1 0.1 collective-permute-start.5
  4.2 4.2 %collective-permute-start = (bf16[17,16,128]{2,1,0:T(8,128)(2,1)S(1)}, bf16[17,16,128]{2,1,0:T(8,128)(2,1)S(1)}, u32[]{:S(2)}, u32[]{:S(2)}) collective-permute-start(bf16[17,16,128]{2,1,0:T(8,128)(2,1)S(1)} %get-tuple-element.35), channel_id=1, source_target_pairs={{1,2},{3,4},{5,6},{7,8},{9,10},{11,12},{13,14},{15,16},{17,18},{19... | collective-permute-start | bytes 208904 | tf_op jit(solution)/shard_map/ppermute | solution.py:475
  8.4 0.7 collective-permute-start.1
  9.1 0.0 copy-done.2
  9.1 0.0 collective-permute-done.1.high_ref
  9.1 1.3 %collective-permute-done.edge_ref = bf16[17,16,128]{2,1,0:T(8,128)(2,1)S(1)} collective-permute-done((bf16[17,16,128]{2,1,0:T(8,128)(2,1)S(1)}, bf16[17,16,128]{2,1,0:T(8,128)(2,1)S(1)}, u32[]{:S(2)}, u32[]{:S(2)}) %collective-permute-start) | collective-permute-done | bytes 69664 | tf_op jit(solution)/shard_map/ppermute | solution.py:475
  10.4 2.2 %collective-permute-start.4 = (bf16[8,4352]{1,0:T(8,128)(2,1)S(1)}, bf16[8,4352]{1,0:T(8,128)(2,1)S(1)}, u32[]{:S(2)}, u32[]{:S(2)}) collective-permute-start(bf16[8,4352]{1,0:T(8,128)(2,1)S(1)} %extend_sources.1.refs_0_), channel_id=1, source_target_pairs={{0,192},{32,224},{64,0},{96,32},{128,64},{160,96},{192,128},{224,1... | collective-permute-start | bytes 208904 | tf_op jit(solution)/shard_map/ppermute | solution.py:482
  12.6 0.8 collective-permute-start.3
  13.4 0.9 %collective-permute-start.2 = (bf16[8,4352]{1,0:T(8,128)(2,1)S(1)}, bf16[8,4352]{1,0:T(8,128)(2,1)S(1)}, u32[]{:S(2)}, u32[]{:S(2)}) collective-permute-start(bf16[8,4352]{1,0:T(8,128)(2,1)S(1)} %extend_sources.1.refs_0_), channel_id=1, source_target_pairs={{0,64},{32,96},{64,128},{96,160},{128,192},{160,224},{192,0},{224,... | collective-permute-start | bytes 208904 | tf_op jit(solution)/shard_map/ppermute | solution.py:482
  14.3 0.0 collective-permute-done.5.other_ref
  14.3 0.0 copy-done
  14.3 3.0 %filter_rows.2 = (f32[256,8192]{1,0:T(8,128)}, f32[128,128]{1,0:T(8,128)S(1)}) custom-call(s32[16]{0:T(128)S(1)} %copy-done, bf16[1,256]{1,0:T(2,128)(2,1)S(1)} %reshape.6.taps_ref, bf16[16,16,4096]{2,1,0:T(8,128)(2,1)S(1)} %get-tuple-element.38.mine_ref, bf16[16,16,4096]{2,1,0:T(8,128)(2,1)S(1)} %collective-permute-done.5.other_ref, ...), custom_call_target="tpu_custom_call" | custom-call | flops 1073741824 | bytes 6291456 | tf_op jit(solution)/shard_map/filter_rows/pallas_call | solution.py:205
  17.3 0.0 collective-permute-done.4.refs_3_
  17.3 1.1 %collective-permute-done.3.refs_2_ = bf16[8,4352]{1,0:T(8,128)(2,1)S(1)} collective-permute-done((bf16[8,4352]{1,0:T(8,128)(2,1)S(1)}, bf16[8,4352]{1,0:T(8,128)(2,1)S(1)}, u32[]{:S(2)}, u32[]{:S(2)}) %collective-permute-start.3) | collective-permute-done | bytes 69664 | tf_op jit(solution)/shard_map/ppermute | solution.py:482
  18.5 0.7 collective-permute-done.2.refs_1_
  19.2 2.4 %collective-permute-start.6 = (bf16[8,4352]{1,0:T(8,128)(2,1)S(1)}, bf16[8,4352]{1,0:T(8,128)(2,1)S(1)}, u32[]{:S(2)}, u32[]{:S(2)}) collective-permute-start(bf16[8,4352]{1,0:T(8,128)(2,1)S(1)} %add_pieces.2.refs_0_), channel_id=1, source_target_pairs={{0,32},{32,0},{64,96},{96,64},{128,160},{160,128},{192,224},{224,1... | collective-permute-start | bytes 208904 | tf_op jit(solution)/shard_map/ppermute | solution.py:489
  21.6 3.0 %filter_rows.3 = (f32[256,8192]{1,0:T(8,128)}, f32[128,128]{1,0:T(8,128)S(1)}) custom-call(s32[16]{0:T(128)S(1)} %copy-done, bf16[1,256]{1,0:T(2,128)(2,1)S(1)} %reshape.6.taps_ref, bf16[16,16,4096]{2,1,0:T(8,128)(2,1)S(1)} %get-tuple-element.38.mine_ref, ...), custom_call_target="tpu_custom_call", output_to_operand_aliasing={{0}: (6, {})} | custom-call | flops 1073741824 | bytes 6291456 | tf_op jit(solution)/shard_map/filter_rows/pallas_call | solution.py:205
  24.6 0.5 collective-permute-done.6.refs_1_
  25.2 1.5 %collective-permute-start.7 = (bf16[8,4352]{1,0:T(8,128)(2,1)S(1)}, bf16[8,4352]{1,0:T(8,128)(2,1)S(1)}, u32[]{:S(2)}, u32[]{:S(2)}) collective-permute-start(bf16[8,4352]{1,0:T(8,128)(2,1)S(1)} %add_pieces.3.mine_ref), channel_id=1, source_target_pairs={{0,1},{1,0},{2,3},{3,2},{4,5},{5,4},{6,7},{7,6},{8,9},{9,8},{10,11... | collective-permute-start | bytes 208904 | tf_op jit(solution)/shard_map/ppermute | solution.py:495
  26.7 0.9 %collective-permute-done.7.other_ref = bf16[8,4352]{1,0:T(8,128)(2,1)S(1)} collective-permute-done((bf16[8,4352]{1,0:T(8,128)(2,1)S(1)}, bf16[8,4352]{1,0:T(8,128)(2,1)S(1)}, u32[]{:S(2)}, u32[]{:S(2)}) %collective-permute-start.7) | collective-permute-done | bytes 69664 | tf_op jit(solution)/shard_map/ppermute | solution.py:495
  27.6 1.0 %filter_sources.1 = (f32[8,8448]{1,0:T(8,128)S(1)}, f32[16,8,128]{2,1,0:T(8,128)S(1)}) custom-call(s32[16]{0:T(128)S(1)} %copy-done, bf16[1,256]{1,0:T(2,128)(2,1)S(1)} %reshape.6.taps_ref, bf16[8,4352]{1,0:T(8,128)(2,1)S(1)} %add_pieces.3.mine_ref, bf16[8,4352]{1,0:T(8,128)(2,1)S(1)} %collective-permute-done.7.other_ref, ...), custom_call_target="tpu_custom_call" | custom-call | bytes 1048576 | tf_op jit(solution)/shard_map/filter_sources/pallas_call | solution.py:267
  28.6 18.7 %all_to_all.10.energy_ref = f32[16,8,128]{2,1,0:T(8,128)S(1)} all-to-all(f32[16,8,128]{2,1,0:T(8,128)S(1)} %get-tuple-element.50), channel_id=1, replica_groups={{0,2,4,6,8,10,12,14,16,18,20,22,24,26,28,30},{1,3,5,7,9,11,13,15,17,19,..., dimensions={0} | all-to-all | bytes 131072 | tf_op jit(solution)/shard_map/all_to_all | solution.py:500
  47.2 4.2 %correlate_first.1 = (f32[8,16,512]{2,1,0:T(8,128)S(1)}, bf16[8,16,512]{2,1,0:T(8,128)(2,1)S(1)}, bf16[256,8192]{1,0:T(8,128)(2,1)S(1)}, bf16[8448,128]{1,0:T(8,128)(2,1)S(1)}) custom-call(f32[16,8,128]{2,1,0:T(8,128)S(1)} %all_to_all.10.energy_ref, f32[8,8448]{1,0:T(8,128)S(1)} %get-tuple-element.51.traces_ref, f32[256,8192]{1,0:T(8,128)} %get-tuple-element.52.refs_0_), custom_call_target="tpu_custom_call" | custom-call | flops 2147483648 | bytes 16777216 | tf_op jit(solution)/shard_map/correlate_first/pallas_call | solution.py:358
  51.4 1.5 %collective-permute-start.8 = (bf16[8,16,512]{2,1,0:T(8,128)(2,1)S(1)}, bf16[8,16,512]{2,1,0:T(8,128)(2,1)S(1)}, u32[]{:S(2)}, u32[]{:S(2)}) collective-permute-start(bf16[8,16,512]{2,1,0:T(8,128)(2,1)S(1)} %get-tuple-element.57), channel_id=1, source_target_pairs={{0,2},{1,3},{2,0},{3,1},{4,6},{5,7},{6,4},{7,5},{8,10},{9,11},{10,... | collective-permute-start | bytes 393224 | tf_op jit(solution)/shard_map/ppermute | solution.py:509
  52.9 3.4 %correlate_next.2 = (f32[8,16,768]{2,1,0:T(8,128)S(1)}, bf16[8,16,768]{2,1,0:T(8,128)(2,1)S(1)}) custom-call(bf16[256,8192]{1,0:T(8,128)(2,1)S(1)} %get-tuple-element.58.white_ref, bf16[8448,128]{1,0:T(8,128)(2,1)S(1)} %get-tuple-element.55.table_ref), custom_call_target="tpu_custom_call" | custom-call | flops 3221225472 | bytes 8388608 | tf_op jit(solution)/shard_map/correlate_next/pallas_call | solution.py:391
  56.3 0.7 collective-permute-start.9
  57.0 0.0 collective-permute-done.8.refs_3_
  57.1 3.4 %correlate_next.3 = (f32[8,16,768]{2,1,0:T(8,128)S(1)}, bf16[8,16,768]{2,1,0:T(8,128)(2,1)S(1)}) custom-call(bf16[256,8192]{1,0:T(8,128)(2,1)S(1)} %get-tuple-element.58.white_ref, bf16[8448,128]{1,0:T(8,128)(2,1)S(1)} %get-tuple-element.55.table_ref), custom_call_target="tpu_custom_call" | custom-call | flops 3221225472 | bytes 8388608 | tf_op jit(solution)/shard_map/correlate_next/pallas_call | solution.py:391
  60.5 1.5 %collective-permute-start.10 = (bf16[8,16,768]{2,1,0:T(8,128)(2,1)S(1)}, bf16[8,16,768]{2,1,0:T(8,128)(2,1)S(1)}, u32[]{:S(2)}, u32[]{:S(2)}) collective-permute-start(bf16[8,16,768]{2,1,0:T(8,128)(2,1)S(1)} %get-tuple-element.62), channel_id=1, source_target_pairs={{0,2},{1,3},{2,0},{3,1},{4,6},{5,7},{6,4},{7,5},{8,10},{9,11},{10,... | collective-permute-start | bytes 589832 | tf_op jit(solution)/shard_map/ppermute | solution.py:515
  61.9 0.7 collective-permute-done.9.refs_4_
  62.6 3.7 %collective-permute-done.10.refs_5_ = bf16[8,16,768]{2,1,0:T(8,128)(2,1)S(1)} collective-permute-done((bf16[8,16,768]{2,1,0:T(8,128)(2,1)S(1)}, bf16[8,16,768]{2,1,0:T(8,128)(2,1)S(1)}, u32[]{:S(2)}, u32[]{:S(2)}) %collective-permute-start.10) | collective-permute-done | bytes 196640 | tf_op jit(solution)/shard_map/ppermute | solution.py:515
  66.3 0.1 add_line.1
  66.4 18.1 %all_to_all.11.parts_ref = bf16[8,16,2048]{2,1,0:T(8,128)(2,1)S(1)} all-to-all(bf16[8,16,2048]{2,1,0:T(8,128)(2,1)S(1)} %add_line.1), channel_id=1, replica_groups={{0,4,8,12,16,20,24,28},{1,5,9,13,17,21,25,29},{2,6,10,14,18,22,26,30},{..., dimensions={0} | all-to-all | bytes 1048576 | tf_op jit(solution)/shard_map/all_to_all | solution.py:518
  84.4 1.2 %finish.1 = f32[16,2,4,256]{3,2,1,0:T(4,128)} custom-call(bf16[8,16,2048]{2,1,0:T(8,128)(2,1)S(1)} %all_to_all.11.parts_ref), custom_call_target="tpu_custom_call" | custom-call | bytes 1048576 | tf_op jit(solution)/shard_map/finish/pallas_call | solution.py:450
  (5 shorter events, 0.1 us)
Async XLA Ops:
  0.0 9.1 %copy-start.2 = (bf16[64]{0:T(256)(128)(2,1)S(1)}, bf16[64]{0:T(256)(128)(2,1)}, u32[]{:S(2)}) copy-start(bf16[64]{0:T(256)(128)(2,1)} %param.5) | copy-start | bytes 388
  0.0 14.3 %copy-start = (s32[16]{0:T(128)S(1)}, s32[16]{0:T(128)}, u32[]{:S(2)}) copy-start(s32[16]{0:T(128)} %off_ref.5) | copy-start | bytes 196
  0.0 0.7 copy-start.1
  4.1 10.2 %collective-permute-start.5 = (bf16[16,16,4096]{2,1,0:T(8,128)(2,1)S(1)}, bf16[16,16,4096]{2,1,0:T(8,128)(2,1)S(1)}, u32[]{:S(2)}, u32[]{:S(2)}) collective-permute-start(bf16[16,16,4096]{2,1,0:T(8,128)(2,1)S(1)} %get-tuple-element.39), channel_id=1, source_target_pairs={{0,1},{1,0},{2,3},{3,2},{4,5},{5,4},{6,7},{7,6},{8,9},{9,8},{10,11... | collective-permute-start | bytes 6291464 | tf_op jit(solution)/shard_map/ppermute | solution.py:476
  4.2 6.2 %collective-permute-start = (bf16[17,16,128]{2,1,0:T(8,128)(2,1)S(1)}, bf16[17,16,128]{2,1,0:T(8,128)(2,1)S(1)}, u32[]{:S(2)}, u32[]{:S(2)}) collective-permute-start(bf16[17,16,128]{2,1,0:T(8,128)(2,1)S(1)} %get-tuple-element.35), channel_id=1, source_target_pairs={{1,2},{3,4},{5,6},{7,8},{9,10},{11,12},{13,14},{15,16},{17,18},{19... | collective-permute-start | bytes 208904 | tf_op jit(solution)/shard_map/ppermute | solution.py:475
  8.4 0.7 collective-permute-start.1
  10.4 6.9 %collective-permute-start.4 = (bf16[8,4352]{1,0:T(8,128)(2,1)S(1)}, bf16[8,4352]{1,0:T(8,128)(2,1)S(1)}, u32[]{:S(2)}, u32[]{:S(2)}) collective-permute-start(bf16[8,4352]{1,0:T(8,128)(2,1)S(1)} %extend_sources.1.refs_0_), channel_id=1, source_target_pairs={{0,192},{32,224},{64,0},{96,32},{128,64},{160,96},{192,128},{224,1... | collective-permute-start | bytes 208904 | tf_op jit(solution)/shard_map/ppermute | solution.py:482
  12.6 5.8 %collective-permute-start.3 = (bf16[8,4352]{1,0:T(8,128)(2,1)S(1)}, bf16[8,4352]{1,0:T(8,128)(2,1)S(1)}, u32[]{:S(2)}, u32[]{:S(2)}) collective-permute-start(bf16[8,4352]{1,0:T(8,128)(2,1)S(1)} %extend_sources.1.refs_0_), channel_id=1, source_target_pairs={{0,128},{32,160},{64,192},{96,224},{128,0},{160,32},{192,64},{224,... | collective-permute-start | bytes 208904 | tf_op jit(solution)/shard_map/ppermute | solution.py:482
  13.4 5.8 %collective-permute-start.2 = (bf16[8,4352]{1,0:T(8,128)(2,1)S(1)}, bf16[8,4352]{1,0:T(8,128)(2,1)S(1)}, u32[]{:S(2)}, u32[]{:S(2)}) collective-permute-start(bf16[8,4352]{1,0:T(8,128)(2,1)S(1)} %extend_sources.1.refs_0_), channel_id=1, source_target_pairs={{0,64},{32,96},{64,128},{96,160},{128,192},{160,224},{192,0},{224,... | collective-permute-start | bytes 208904 | tf_op jit(solution)/shard_map/ppermute | solution.py:482
  19.2 5.9 %collective-permute-start.6 = (bf16[8,4352]{1,0:T(8,128)(2,1)S(1)}, bf16[8,4352]{1,0:T(8,128)(2,1)S(1)}, u32[]{:S(2)}, u32[]{:S(2)}) collective-permute-start(bf16[8,4352]{1,0:T(8,128)(2,1)S(1)} %add_pieces.2.refs_0_), channel_id=1, source_target_pairs={{0,32},{32,0},{64,96},{96,64},{128,160},{160,128},{192,224},{224,1... | collective-permute-start | bytes 208904 | tf_op jit(solution)/shard_map/ppermute | solution.py:489
  25.2 2.4 %collective-permute-start.7 = (bf16[8,4352]{1,0:T(8,128)(2,1)S(1)}, bf16[8,4352]{1,0:T(8,128)(2,1)S(1)}, u32[]{:S(2)}, u32[]{:S(2)}) collective-permute-start(bf16[8,4352]{1,0:T(8,128)(2,1)S(1)} %add_pieces.3.mine_ref), channel_id=1, source_target_pairs={{0,1},{1,0},{2,3},{3,2},{4,5},{5,4},{6,7},{7,6},{8,9},{9,8},{10,11... | collective-permute-start | bytes 208904 | tf_op jit(solution)/shard_map/ppermute | solution.py:495
  51.4 5.6 %collective-permute-start.8 = (bf16[8,16,512]{2,1,0:T(8,128)(2,1)S(1)}, bf16[8,16,512]{2,1,0:T(8,128)(2,1)S(1)}, u32[]{:S(2)}, u32[]{:S(2)}) collective-permute-start(bf16[8,16,512]{2,1,0:T(8,128)(2,1)S(1)} %get-tuple-element.57), channel_id=1, source_target_pairs={{0,2},{1,3},{2,0},{3,1},{4,6},{5,7},{6,4},{7,5},{8,10},{9,11},{10,... | collective-permute-start | bytes 393224 | tf_op jit(solution)/shard_map/ppermute | solution.py:509
  56.3 6.3 %collective-permute-start.9 = (bf16[8,16,768]{2,1,0:T(8,128)(2,1)S(1)}, bf16[8,16,768]{2,1,0:T(8,128)(2,1)S(1)}, u32[]{:S(2)}, u32[]{:S(2)}) collective-permute-start(bf16[8,16,768]{2,1,0:T(8,128)(2,1)S(1)} %get-tuple-element.61), channel_id=1, source_target_pairs={{0,2},{1,3},{2,0},{3,1},{4,6},{5,7},{6,4},{7,5},{8,10},{9,11},{10,... | collective-permute-start | bytes 589832 | tf_op jit(solution)/shard_map/ppermute | solution.py:515
  60.5 5.8 %collective-permute-start.10 = (bf16[8,16,768]{2,1,0:T(8,128)(2,1)S(1)}, bf16[8,16,768]{2,1,0:T(8,128)(2,1)S(1)}, u32[]{:S(2)}, u32[]{:S(2)}) collective-permute-start(bf16[8,16,768]{2,1,0:T(8,128)(2,1)S(1)} %get-tuple-element.62), channel_id=1, source_target_pairs={{0,2},{1,3},{2,0},{3,1},{4,6},{5,7},{6,4},{7,5},{8,10},{9,11},{10,... | collective-permute-start | bytes 589832 | tf_op jit(solution)/shard_map/ppermute | solution.py:515

commit v12 on v11

--- a/solution.py
+++ b/solution.py
@@ -59,7 +59,7 @@
     groups, _, sub, samples = x4.shape
     channels = groups * 2 * sub
 
-    def kernel(ids_ref, x_ref, own_ref, edge_ref, high_ref, away_ref, mine_ref, buf, sems):
+    def kernel(ids_ref, x_ref, own_ref, edge_ref, high_ref, away_ref, buf, sems):
         base = lax.axis_index("chan") * channels
         core = lax.axis_index("tm") % 2
         copies = []
@@ -78,7 +78,6 @@
             ),
             pltpu.make_async_copy(x_ref.at[:, 1, :, last], high_ref, sems.at[NS + 1]),
             pltpu.make_async_copy(x_ref.at[:, 1 - core], away_ref, sems.at[NS + 2]),
-            pltpu.make_async_copy(x_ref.at[:, core], mine_ref, sems.at[NS + 3]),
         ]
         for copy in copies + rest:
             copy.start()
@@ -105,11 +104,10 @@
             shape((groups + 1, sub, LANE), jnp.bfloat16),
             shape((groups, sub, LANE), jnp.bfloat16),
             shape((groups, sub, samples), jnp.bfloat16),
-            shape((groups, sub, samples), jnp.bfloat16),
         ],
         [SMEM, ANY],
-        [pltpu.VMEM((NS, sub, samples), jnp.bfloat16), pltpu.SemaphoreType.DMA((NS + 4,))],
-        limit=48,
+        [pltpu.VMEM((NS, sub, samples), jnp.bfloat16), pltpu.SemaphoreType.DMA((NS + 3,))],
+        limit=50,
         moved=2 * MIB,
     )(source_channels, x4)
 
@@ -146,74 +144,74 @@
     )(*pieces)[0]
 
 
-def filter_rows(offsets, taps, mine, other, edge, high, first_group, groups, filled=None):
-    all_groups, sub, half = mine.shape
-    filled = [] if filled is None else [filled]
+def filter_rows(offsets, taps, x4, other, edges, part, filled=None):
+    groups, _, sub, half = x4.shape
     rows = groups * sub
-    chosen = slice(first_group, first_group + groups)
     chunk = 1024
-    parts = half // chunk
-    total = 2 * parts
-
-    def kernel(
-        off_ref, taps_ref, mine_ref, other_ref, edge_ref, high_ref, *refs
-    ):
-        out_ref, power_ref, value_buf, sems = refs[len(filled) :]
+    count = half // chunk
+    extra = list(edges) + ([] if filled is None else [filled])
+
+    def kernel(off_ref, taps_ref, x_ref, other_ref, *refs):
+        edge_refs = refs[: len(edges)]
+        out_ref, power_ref, value_buf, sems = refs[len(extra) :]
         tile = lax.axis_index("tm")
         core = tile % 2
         matrix = fir_tile(taps_ref[...])
         first_kept = off_ref[tile // 2]
 
-        def store(part):
-            place = out_ref.at[pl.ds(first_group * sub, rows), pl.ds(part * chunk, chunk)]
-            return pltpu.make_async_copy(value_buf.at[part], place, sems.at[part])
-
-        def run(read_low, read_high, previous):
+        def store(index):
+            place = out_ref.at[:, pl.ds(part * half + index * chunk, chunk)]
+            return pltpu.make_async_copy(value_buf.at[index], place, sems.at[index])
+
+        def run(read, previous):
             power = jnp.zeros((rows, LANE), jnp.float32)
-            for part in range(total):
-                read = read_low if part < parts else read_high
+            for index in range(count):
                 for j in range(chunk // LANE):
-                    first = (part % parts) * chunk + j * LANE
+                    first = index * chunk + j * LANE
                     current = read(slice(first, first + LANE)).reshape(rows, LANE)
                     framed = jnp.concatenate([previous, current], axis=1)
                     value = jnp.dot(framed, matrix, preferred_element_type=jnp.float32)
                     power = power + value * value
-                    place = lax.broadcasted_iota(jnp.int32, (1, LANE), 1) + part * chunk + j * LANE
+                    place = lax.broadcasted_iota(jnp.int32, (1, LANE), 1) + part * half + first
                     value = value * jnp.where(place >= first_kept, 1.0, 0.0)
-                    value_buf[part, :, j * LANE : (j + 1) * LANE] = value
+                    value_buf[index, :, j * LANE : (j + 1) * LANE] = value
                     previous = current
-                store(part).start()
+                store(index).start()
             power_ref[...] = power
 
         def own(cols):
-            return mine_ref[chosen, :, cols]
+            return x_ref[:, core, :, cols]
 
         def swapped(cols):
-            return other_ref[chosen, :, cols]
-
-        @pl.when(core == 0)
-        def _():
-            run(own, swapped, edge_ref[chosen].reshape(rows, LANE))
-
-        @pl.when(core == 1)
-        def _():
-            run(swapped, own, high_ref[chosen].reshape(rows, LANE))
-
-        for part in range(total):
-            store(part).wait()
+            return other_ref[:, :, cols]
+
+        last = slice(half - LANE, half)
+        readers = (own, swapped)
+        for index in range(2):
+            low, high = readers[index], readers[1 - index]
+
+            @pl.when(core == index)
+            def _(index=index, low=low, high=high):
+                if part == 1:
+                    run(high, low(last).reshape(rows, LANE))
+                else:
+                    run(low, edge_refs[index][:groups].reshape(rows, LANE))
+
+        for index in range(count):
+            store(index).wait()
 
     return call(
         kernel,
         "filter_rows",
-        [shape((all_groups * sub, 2 * half), jnp.float32), shape((rows, LANE), jnp.float32)],
-        [SMEM, VMEM, VMEM, VMEM, VMEM, VMEM] + [ANY] * len(filled),
-        [pltpu.VMEM((total, rows, chunk), jnp.float32), pltpu.SemaphoreType.DMA((total,))],
+        [shape((rows, 2 * half), jnp.float32), shape((rows, LANE), jnp.float32)],
+        [SMEM, VMEM, VMEM, VMEM] + [VMEM] * len(edges) + ([] if filled is None else [ANY]),
+        [pltpu.VMEM((count, rows, chunk), jnp.float32), pltpu.SemaphoreType.DMA((count,))],
         out_specs=[ANY, VMEM],
-        limit=45,
-        flops=2 * rows * 2 * half * 512,
+        limit=40,
+        flops=rows * 2 * half * 512,
         moved=6 * MIB,
-        aliases={6: 0} if filled else None,
-    )(offsets, taps, mine, other, edge, high, *filled)
+        aliases=None if filled is None else {4 + len(edges): 0},
+    )(offsets, taps, x4, other, *extra)
 
 
 def filter_sources(offsets, taps, mine, other, powers, chips):
@@ -256,8 +254,9 @@
                 keep = keep * jnp.where(chip < chips - 1, 1.0, 0.0)
             out_ref[:, j * LANE : (j + 1) * LANE] = piece * keep
         lines = []
-        for power_ref in power_refs:
-            lines.append(jnp.sum(power_ref[...].T, axis=0, keepdims=True))
+        for r in range(power_refs[0].shape[0] // LANE):
+            block = sum(ref[r * LANE : (r + 1) * LANE, :] for ref in power_refs)
+            lines.append(jnp.sum(block.T, axis=0, keepdims=True))
         repeated = jnp.concatenate([total] * SHIFTS, axis=0)
         lines.append(jnp.sum(repeated.T, axis=0, keepdims=True))
         lines.append(jnp.zeros((8 - len(lines), LANE), jnp.float32))
@@ -467,7 +466,7 @@
     taps = wide_taps(whiten_taps)
 
     x4 = strain_rate.reshape(chips, 2, sub, samples)
-    own, edge, high, away, mine = pick_sources(source_channels, x4)
+    own, edge, high, away = pick_sources(source_channels, x4)
 
     swap = [(i, i ^ 1) for i in range(tiles)]
     to_next = [(2 * k - 1, 2 * k) for k in range(1, chips)]
@@ -476,19 +475,17 @@
     other = lax.ppermute(away, "tm", swap)
     high = lax.ppermute(high, "tm", [(2 * k - 1, 2 * k + 1) for k in range(1, chips)])
 
-    edge, high = lax.optimization_barrier((edge, high))
     piece = extend_sources(own, edge)
     parts = [
         lax.ppermute(piece, "chan", [(i, (i + 2 * d) % groups_chan) for i in range(groups_chan)])
         for d in range(1, groups_chan // 2)
     ]
-    half = chips // 2
-    filtered, power_a = filter_rows(window_offsets, taps, mine, other, edge, high, 0, half)
+    filtered, power_a = filter_rows(window_offsets, taps, x4, other, [], 1)
     *parts, power_a = lax.optimization_barrier((*parts, power_a))
     piece = add_pieces(piece, *parts)
     arrived = lax.ppermute(piece, "chan", [(i, i ^ 1) for i in range(groups_chan)])
     filtered, power_b = filter_rows(
-        window_offsets, taps, mine, other, edge, high, half, half, filtered
+        window_offsets, taps, x4, other, [edge, high], 0, filtered
     )
     arrived, power_b = lax.optimization_barrier((arrived, power_b))
     piece = add_pieces(piece, arrived)

time: 86 us -> 84.8 us (0.986)
  waiting for transfers between devices: 8.9 us -> 10.9 us
  starting transfers between devices: 16.4 us -> 15 us
  blocking collectives: 36.7 us -> 35.6 us
    ppermute x3, waiting for transfers between devices: 1.87 us -> 3.49 us  [shards(): lax.ppermute(piece, 'chan', [(i, (i + 2 * d) % groups_chan) for i in rang...]
    ppermute x1, starting transfers between devices: 1.5 us -> 0.09 us  [shards(): piece_other = lax.ppermute(piece, 'tm', swap)]
    all_to_all x1, blocking collectives: 18.7 us -> 17.5 us  [shards(): lax.all_to_all(energy, 'tm', 0, 0, tiled=True, axis_index_groups=same)]
where the time goes in v12:
time: 84.8 us; the launch traced here: 84.6 us
  blocking collectives  35.6 us (42%)
  Pallas kernels  22.1 us (26%)
  starting transfers between devices  15 us (18%)
  waiting for transfers between devices  10.9 us (13%)
  local copies, waits for them, and re-layouts  0.85 us (1%)
    all_to_all x1, blocking collectives, shards(): lax.all_to_all(summed, 'tm', 0, 0, tiled=True, axis_index_groups=columns)  18.1 us
    all_to_all x1, blocking collectives, shards(): lax.all_to_all(energy, 'tm', 0, 0, tiled=True, axis_index_groups=same)  17.5 us
    pallas_call x2, Pallas kernels, correlate_next(): call(kernel, 'correlate_next', [shape((half_groups, sub, cols), jnp.float...  6.8 us
    pallas_call x2, Pallas kernels, filter_rows(): call(kernel, 'filter_rows', [shape((rows, 2 * half), jnp.float32), shape(...  6.02 us
    ppermute x2, waiting for transfers between devices, shards(): arrivals.append(lax.ppermute(send, 'tm', line))  4.36 us
    pallas_call x1, Pallas kernels, correlate_first(): call(kernel, 'correlate_first', [shape((half_groups, sub, cols), jnp.floa...  4.19 us
    ppermute x1, starting transfers between devices, shards(): edge = lax.ppermute(edge, 'tm', both_next)  4.18 us
    ppermute x3, starting transfers between devices, shards(): lax.ppermute(piece, 'chan', [(i, (i + 2 * d) % groups_chan) for i in rang...  3.9 us
  transfers between devices with their start and end apart: 11, of which 7 were waited for; matrix products, arithmetic and copies ran while one was open for 0% of the time, Pallas kernels for 15%

profile of v12, /device:TPU:8, one launch (start us, length us, event | category | flops | bytes accessed | tf_op | source)
XLA Modules:
  0.0 84.6 jit_solution(8574135410513306256)
XLA Ops:
  0.0 0.0 copy-start
  0.0 0.0 copy-start.1
  0.0 0.0 copy-start.2
  0.0 0.8 copy-done.2
  0.8 0.0 copy-start.3
  0.8 2.8 %pick_sources.1 = (bf16[8,4096]{1,0:T(8,128)(2,1)S(1)}, bf16[17,16,128]{2,1,0:T(8,128)(2,1)S(1)}, bf16[16,16,128]{2,1,0:T(8,128)(2,1)S(1)}, bf16[16,16,4096]{2,1,0:T(8,128)(2,1)S(1)}) custom-call(s32[2,4]{1,0:T(2,128)S(1)} %copy-done.2, bf16[16,2,16,4096]{3,2,1,0:T(8,128)(2,1)} %bitcast.1), custom_call_target="tpu_custom_call" | custom-call | bytes 2097152 | tf_op jit(solution)/shard_map/pick_sources/pallas_call | solution.py:99
  3.6 0.1 collective-permute-start.4
  3.7 4.2 %collective-permute-start = (bf16[17,16,128]{2,1,0:T(8,128)(2,1)S(1)}, bf16[17,16,128]{2,1,0:T(8,128)(2,1)S(1)}, u32[]{:S(2)}, u32[]{:S(2)}) collective-permute-start(bf16[17,16,128]{2,1,0:T(8,128)(2,1)S(1)} %get-tuple-element.32), channel_id=1, source_target_pairs={{1,2},{3,4},{5,6},{7,8},{9,10},{11,12},{13,14},{15,16},{17,18},{19... | collective-permute-start | bytes 208904 | tf_op jit(solution)/shard_map/ppermute | solution.py:474
  7.9 0.7 collective-permute-start.6
  8.6 0.0 copy-done.3
  8.6 1.3 %collective-permute-done.edge_ref.refs_0_ = bf16[17,16,128]{2,1,0:T(8,128)(2,1)S(1)} collective-permute-done((bf16[17,16,128]{2,1,0:T(8,128)(2,1)S(1)}, bf16[17,16,128]{2,1,0:T(8,128)(2,1)S(1)}, u32[]{:S(2)}, u32[]{:S(2)}) %collective-permute-start) | collective-permute-done | bytes 69664 | tf_op jit(solution)/shard_map/ppermute | solution.py:474
  9.9 2.4 %collective-permute-start.3 = (bf16[8,4352]{1,0:T(8,128)(2,1)S(1)}, bf16[8,4352]{1,0:T(8,128)(2,1)S(1)}, u32[]{:S(2)}, u32[]{:S(2)}) collective-permute-start(bf16[8,4352]{1,0:T(8,128)(2,1)S(1)} %extend_sources.1.refs_0_), channel_id=1, source_target_pairs={{0,192},{32,224},{64,0},{96,32},{128,64},{160,96},{192,128},{224,1... | collective-permute-start | bytes 208904 | tf_op jit(solution)/shard_map/ppermute | solution.py:480
  12.3 0.6 collective-permute-start.2
  12.9 0.9 %collective-permute-start.1 = (bf16[8,4352]{1,0:T(8,128)(2,1)S(1)}, bf16[8,4352]{1,0:T(8,128)(2,1)S(1)}, u32[]{:S(2)}, u32[]{:S(2)}) collective-permute-start(bf16[8,4352]{1,0:T(8,128)(2,1)S(1)} %extend_sources.1.refs_0_), channel_id=1, source_target_pairs={{0,64},{32,96},{64,128},{96,160},{128,192},{160,224},{192,0},{224,... | collective-permute-start | bytes 208904 | tf_op jit(solution)/shard_map/ppermute | solution.py:480
  13.8 0.0 collective-permute-done.4.other_ref
  13.8 0.0 copy-done
  13.8 0.0 copy-done.1
  13.8 3.0 %filter_rows.2 = (f32[256,8192]{1,0:T(8,128)}, f32[256,128]{1,0:T(8,128)S(1)}) custom-call(s32[16]{0:T(128)S(1)} %copy-done.1, bf16[1,256]{1,0:T(2,128)(2,1)S(1)} %reshape.6.taps_ref, bf16[16,2,16,4096]{3,2,1,0:T(8,128)(2,1)S(1)} %bitcast.2, bf16[16,16,4096]{2,1,0:T(8,128)(2,1)S(1)} %collective-permute-done.4.other_ref), custom_call_target="tpu_custom_call" | custom-call | flops 1073741824 | bytes 6291456 | tf_op jit(solution)/shard_map/filter_rows/pallas_call | solution.py:203
  16.8 0.0 collective-permute-done.3.refs_3_
  16.8 1.8 %collective-permute-done.2.refs_2_ = bf16[8,4352]{1,0:T(8,128)(2,1)S(1)} collective-permute-done((bf16[8,4352]{1,0:T(8,128)(2,1)S(1)}, bf16[8,4352]{1,0:T(8,128)(2,1)S(1)}, u32[]{:S(2)}, u32[]{:S(2)}) %collective-permute-start.2) | collective-permute-done | bytes 69664 | tf_op jit(solution)/shard_map/ppermute | solution.py:480
  18.6 1.7 %collective-permute-done.1.refs_1_ = bf16[8,4352]{1,0:T(8,128)(2,1)S(1)} collective-permute-done((bf16[8,4352]{1,0:T(8,128)(2,1)S(1)}, bf16[8,4352]{1,0:T(8,128)(2,1)S(1)}, u32[]{:S(2)}, u32[]{:S(2)}) %collective-permute-start.1) | collective-permute-done | bytes 69664 | tf_op jit(solution)/shard_map/ppermute | solution.py:480
  20.4 2.4 %collective-permute-start.5 = (bf16[8,4352]{1,0:T(8,128)(2,1)S(1)}, bf16[8,4352]{1,0:T(8,128)(2,1)S(1)}, u32[]{:S(2)}, u32[]{:S(2)}) collective-permute-start(bf16[8,4352]{1,0:T(8,128)(2,1)S(1)} %add_pieces.2.refs_0_), channel_id=1, source_target_pairs={{0,32},{32,0},{64,96},{96,64},{128,160},{160,128},{192,224},{224,1... | collective-permute-start | bytes 208904 | tf_op jit(solution)/shard_map/ppermute | solution.py:486
  22.7 0.0 collective-permute-done.6.refs_1_
  22.7 3.0 %filter_rows.3 = (f32[256,8192]{1,0:T(8,128)}, f32[256,128]{1,0:T(8,128)S(1)}) custom-call(s32[16]{0:T(128)S(1)} %copy-done.1, bf16[1,256]{1,0:T(2,128)(2,1)S(1)} %reshape.6.taps_ref, bf16[16,2,16,4096]{3,2,1,0:T(8,128)(2,1)S(1)} %bitcast.3, bf16[16,16,4096]{2,1,0:T(8,128)(2,1)S(1)} %collective-permute-done.4.other_ref, ...), custom_call_target="tpu_custom_call", output_to_operand_aliasing={{0}: (6, {})} | custom-call | flops 1073741824 | bytes 6291456 | tf_op jit(solution)/shard_map/filter_rows/pallas_call | solution.py:203
  25.8 0.5 collective-permute-done.5.refs_1_
  26.3 0.1 collective-permute-start.7
  26.4 1.2 %collective-permute-done.7.other_ref = bf16[8,4352]{1,0:T(8,128)(2,1)S(1)} collective-permute-done((bf16[8,4352]{1,0:T(8,128)(2,1)S(1)}, bf16[8,4352]{1,0:T(8,128)(2,1)S(1)}, u32[]{:S(2)}, u32[]{:S(2)}) %collective-permute-start.7) | collective-permute-done | bytes 69664 | tf_op jit(solution)/shard_map/ppermute | solution.py:492
  27.6 1.0 %filter_sources.1 = (f32[8,8448]{1,0:T(8,128)S(1)}, f32[16,8,128]{2,1,0:T(8,128)S(1)}) custom-call(s32[16]{0:T(128)S(1)} %copy-done.1, bf16[1,256]{1,0:T(2,128)(2,1)S(1)} %reshape.6.taps_ref, bf16[8,4352]{1,0:T(8,128)(2,1)S(1)} %add_pieces.3.mine_ref, bf16[8,4352]{1,0:T(8,128)(2,1)S(1)} %collective-permute-done.7.other_ref, ...), custom_call_target="tpu_custom_call" | custom-call | bytes 1048576 | tf_op jit(solution)/shard_map/filter_sources/pallas_call | solution.py:266
  28.6 17.5 %all_to_all.10.energy_ref = f32[16,8,128]{2,1,0:T(8,128)S(1)} all-to-all(f32[16,8,128]{2,1,0:T(8,128)S(1)} %get-tuple-element.44), channel_id=1, replica_groups={{0,2,4,6,8,10,12,14,16,18,20,22,24,26,28,30},{1,3,5,7,9,11,13,15,17,19,..., dimensions={0} | all-to-all | bytes 131072 | tf_op jit(solution)/shard_map/all_to_all | solution.py:497
  46.2 4.2 %correlate_first.1 = (f32[8,16,512]{2,1,0:T(8,128)S(1)}, bf16[8,16,512]{2,1,0:T(8,128)(2,1)S(1)}, bf16[256,8192]{1,0:T(8,128)(2,1)S(1)}, bf16[8448,128]{1,0:T(8,128)(2,1)S(1)}) custom-call(f32[16,8,128]{2,1,0:T(8,128)S(1)} %all_to_all.10.energy_ref, f32[8,8448]{1,0:T(8,128)S(1)} %get-tuple-element.45.traces_ref, f32[256,8192]{1,0:T(8,128)} %get-tuple-element.46.refs_0_), custom_call_target="tpu_custom_call" | custom-call | flops 2147483648 | bytes 16777216 | tf_op jit(solution)/shard_map/correlate_first/pallas_call | solution.py:357
  50.4 1.5 %collective-permute-start.8 = (bf16[8,16,512]{2,1,0:T(8,128)(2,1)S(1)}, bf16[8,16,512]{2,1,0:T(8,128)(2,1)S(1)}, u32[]{:S(2)}, u32[]{:S(2)}) collective-permute-start(bf16[8,16,512]{2,1,0:T(8,128)(2,1)S(1)} %get-tuple-element.51), channel_id=1, source_target_pairs={{0,2},{1,3},{2,0},{3,1},{4,6},{5,7},{6,4},{7,5},{8,10},{9,11},{10,... | collective-permute-start | bytes 393224 | tf_op jit(solution)/shard_map/ppermute | solution.py:506
  51.8 3.4 %correlate_next.2 = (f32[8,16,768]{2,1,0:T(8,128)S(1)}, bf16[8,16,768]{2,1,0:T(8,128)(2,1)S(1)}) custom-call(bf16[256,8192]{1,0:T(8,128)(2,1)S(1)} %get-tuple-element.52.white_ref, bf16[8448,128]{1,0:T(8,128)(2,1)S(1)} %get-tuple-element.49.table_ref), custom_call_target="tpu_custom_call" | custom-call | flops 3221225472 | bytes 8388608 | tf_op jit(solution)/shard_map/correlate_next/pallas_call | solution.py:390
  55.2 0.7 collective-permute-start.9
  56.0 0.0 collective-permute-done.8.refs_3_
  56.0 3.4 %correlate_next.3 = (f32[8,16,768]{2,1,0:T(8,128)S(1)}, bf16[8,16,768]{2,1,0:T(8,128)(2,1)S(1)}) custom-call(bf16[256,8192]{1,0:T(8,128)(2,1)S(1)} %get-tuple-element.52.white_ref, bf16[8448,128]{1,0:T(8,128)(2,1)S(1)} %get-tuple-element.49.table_ref), custom_call_target="tpu_custom_call" | custom-call | flops 3221225472 | bytes 8388608 | tf_op jit(solution)/shard_map/correlate_next/pallas_call | solution.py:390
  59.4 1.5 %collective-permute-start.10 = (bf16[8,16,768]{2,1,0:T(8,128)(2,1)S(1)}, bf16[8,16,768]{2,1,0:T(8,128)(2,1)S(1)}, u32[]{:S(2)}, u32[]{:S(2)}) collective-permute-start(bf16[8,16,768]{2,1,0:T(8,128)(2,1)S(1)} %get-tuple-element.56), channel_id=1, source_target_pairs={{0,2},{1,3},{2,0},{3,1},{4,6},{5,7},{6,4},{7,5},{8,10},{9,11},{10,... | collective-permute-start | bytes 589832 | tf_op jit(solution)/shard_map/ppermute | solution.py:512
  60.8 0.9 %collective-permute-done.9.refs_4_ = bf16[8,16,768]{2,1,0:T(8,128)(2,1)S(1)} collective-permute-done((bf16[8,16,768]{2,1,0:T(8,128)(2,1)S(1)}, bf16[8,16,768]{2,1,0:T(8,128)(2,1)S(1)}, u32[]{:S(2)}, u32[]{:S(2)}) %collective-permute-start.9) | collective-permute-done | bytes 196640 | tf_op jit(solution)/shard_map/ppermute | solution.py:512
  61.7 3.5 %collective-permute-done.10.refs_5_ = bf16[8,16,768]{2,1,0:T(8,128)(2,1)S(1)} collective-permute-done((bf16[8,16,768]{2,1,0:T(8,128)(2,1)S(1)}, bf16[8,16,768]{2,1,0:T(8,128)(2,1)S(1)}, u32[]{:S(2)}, u32[]{:S(2)}) %collective-permute-start.10) | collective-permute-done | bytes 196640 | tf_op jit(solution)/shard_map/ppermute | solution.py:512
  65.2 0.1 add_line.1
  65.3 18.1 %all_to_all.11.parts_ref = bf16[8,16,2048]{2,1,0:T(8,128)(2,1)S(1)} all-to-all(bf16[8,16,2048]{2,1,0:T(8,128)(2,1)S(1)} %add_line.1), channel_id=1, replica_groups={{0,4,8,12,16,20,24,28},{1,5,9,13,17,21,25,29},{2,6,10,14,18,22,26,30},{..., dimensions={0} | all-to-all | bytes 1048576 | tf_op jit(solution)/shard_map/all_to_all | solution.py:515
  83.4 1.2 %finish.1 = f32[16,2,4,256]{3,2,1,0:T(4,128)} custom-call(bf16[8,16,2048]{2,1,0:T(8,128)(2,1)S(1)} %all_to_all.11.parts_ref), custom_call_target="tpu_custom_call" | custom-call | bytes 1048576 | tf_op jit(solution)/shard_map/finish/pallas_call | solution.py:449
  (5 shorter events, 0.1 us)
Async XLA Ops:
  0.0 13.8 %copy-start = (bf16[512,4096]{1,0:T(8,128)(2,1)S(1)}, bf16[512,4096]{1,0:T(8,128)(2,1)}, u32[]{:S(2)}) copy-start(bf16[512,4096]{1,0:T(8,128)(2,1)} %param.4) | copy-start | bytes 12582916
  0.0 13.8 %copy-start.1 = (s32[16]{0:T(128)S(1)}, s32[16]{0:T(128)}, u32[]{:S(2)}) copy-start(s32[16]{0:T(128)} %off_ref.5) | copy-start | bytes 196
  0.0 0.8 copy-start.2
  0.8 7.7 %copy-start.3 = (bf16[64]{0:T(256)(128)(2,1)S(1)}, bf16[64]{0:T(256)(128)(2,1)}, u32[]{:S(2)}) copy-start(bf16[64]{0:T(256)(128)(2,1)} %param.5) | copy-start | bytes 388
  3.6 10.2 %collective-permute-start.4 = (bf16[16,16,4096]{2,1,0:T(8,128)(2,1)S(1)}, bf16[16,16,4096]{2,1,0:T(8,128)(2,1)S(1)}, u32[]{:S(2)}, u32[]{:S(2)}) collective-permute-start(bf16[16,16,4096]{2,1,0:T(8,128)(2,1)S(1)} %get-tuple-element.33), channel_id=1, source_target_pairs={{0,1},{1,0},{2,3},{3,2},{4,5},{5,4},{6,7},{7,6},{8,9},{9,8},{10,11... | collective-permute-start | bytes 6291464 | tf_op jit(solution)/shard_map/ppermute | solution.py:475
  3.7 6.2 %collective-permute-start = (bf16[17,16,128]{2,1,0:T(8,128)(2,1)S(1)}, bf16[17,16,128]{2,1,0:T(8,128)(2,1)S(1)}, u32[]{:S(2)}, u32[]{:S(2)}) collective-permute-start(bf16[17,16,128]{2,1,0:T(8,128)(2,1)S(1)} %get-tuple-element.32), channel_id=1, source_target_pairs={{1,2},{3,4},{5,6},{7,8},{9,10},{11,12},{13,14},{15,16},{17,18},{19... | collective-permute-start | bytes 208904 | tf_op jit(solution)/shard_map/ppermute | solution.py:474
  7.9 14.8 %collective-permute-start.6 = (bf16[16,16,128]{2,1,0:T(8,128)(2,1)S(1)}, bf16[16,16,128]{2,1,0:T(8,128)(2,1)S(1)}, u32[]{:S(2)}, u32[]{:S(2)}) collective-permute-start(bf16[16,16,128]{2,1,0:T(8,128)(2,1)S(1)} %get-tuple-element.38), channel_id=1, source_target_pairs={{1,3},{3,5},{5,7},{7,9},{9,11},{11,13},{13,15},{15,17},{17,19},{19... | collective-permute-start | bytes 196616 | tf_op jit(solution)/shard_map/ppermute | solution.py:476
  9.9 6.9 %collective-permute-start.3 = (bf16[8,4352]{1,0:T(8,128)(2,1)S(1)}, bf16[8,4352]{1,0:T(8,128)(2,1)S(1)}, u32[]{:S(2)}, u32[]{:S(2)}) collective-permute-start(bf16[8,4352]{1,0:T(8,128)(2,1)S(1)} %extend_sources.1.refs_0_), channel_id=1, source_target_pairs={{0,192},{32,224},{64,0},{96,32},{128,64},{160,96},{192,128},{224,1... | collective-permute-start | bytes 208904 | tf_op jit(solution)/shard_map/ppermute | solution.py:480
  12.3 6.4 %collective-permute-start.2 = (bf16[8,4352]{1,0:T(8,128)(2,1)S(1)}, bf16[8,4352]{1,0:T(8,128)(2,1)S(1)}, u32[]{:S(2)}, u32[]{:S(2)}) collective-permute-start(bf16[8,4352]{1,0:T(8,128)(2,1)S(1)} %extend_sources.1.refs_0_), channel_id=1, source_target_pairs={{0,128},{32,160},{64,192},{96,224},{128,0},{160,32},{192,64},{224,... | collective-permute-start | bytes 208904 | tf_op jit(solution)/shard_map/ppermute | solution.py:480
  12.9 7.4 %collective-permute-start.1 = (bf16[8,4352]{1,0:T(8,128)(2,1)S(1)}, bf16[8,4352]{1,0:T(8,128)(2,1)S(1)}, u32[]{:S(2)}, u32[]{:S(2)}) collective-permute-start(bf16[8,4352]{1,0:T(8,128)(2,1)S(1)} %extend_sources.1.refs_0_), channel_id=1, source_target_pairs={{0,64},{32,96},{64,128},{96,160},{128,192},{160,224},{192,0},{224,... | collective-permute-start | bytes 208904 | tf_op jit(solution)/shard_map/ppermute | solution.py:480
  20.4 5.9 %collective-permute-start.5 = (bf16[8,4352]{1,0:T(8,128)(2,1)S(1)}, bf16[8,4352]{1,0:T(8,128)(2,1)S(1)}, u32[]{:S(2)}, u32[]{:S(2)}) collective-permute-start(bf16[8,4352]{1,0:T(8,128)(2,1)S(1)} %add_pieces.2.refs_0_), channel_id=1, source_target_pairs={{0,32},{32,0},{64,96},{96,64},{128,160},{160,128},{192,224},{224,1... | collective-permute-start | bytes 208904 | tf_op jit(solution)/shard_map/ppermute | solution.py:486
  26.3 1.3 %collective-permute-start.7 = (bf16[8,4352]{1,0:T(8,128)(2,1)S(1)}, bf16[8,4352]{1,0:T(8,128)(2,1)S(1)}, u32[]{:S(2)}, u32[]{:S(2)}) collective-permute-start(bf16[8,4352]{1,0:T(8,128)(2,1)S(1)} %add_pieces.3.mine_ref), channel_id=1, source_target_pairs={{0,1},{1,0},{2,3},{3,2},{4,5},{5,4},{6,7},{7,6},{8,9},{9,8},{10,11... | collective-permute-start | bytes 208904 | tf_op jit(solution)/shard_map/ppermute | solution.py:492
  50.4 5.6 %collective-permute-start.8 = (bf16[8,16,512]{2,1,0:T(8,128)(2,1)S(1)}, bf16[8,16,512]{2,1,0:T(8,128)(2,1)S(1)}, u32[]{:S(2)}, u32[]{:S(2)}) collective-permute-start(bf16[8,16,512]{2,1,0:T(8,128)(2,1)S(1)} %get-tuple-element.51), channel_id=1, source_target_pairs={{0,2},{1,3},{2,0},{3,1},{4,6},{5,7},{6,4},{7,5},{8,10},{9,11},{10,... | collective-permute-start | bytes 393224 | tf_op jit(solution)/shard_map/ppermute | solution.py:506
  55.2 6.5 %collective-permute-start.9 = (bf16[8,16,768]{2,1,0:T(8,128)(2,1)S(1)}, bf16[8,16,768]{2,1,0:T(8,128)(2,1)S(1)}, u32[]{:S(2)}, u32[]{:S(2)}) collective-permute-start(bf16[8,16,768]{2,1,0:T(8,128)(2,1)S(1)} %get-tuple-element.55), channel_id=1, source_target_pairs={{0,2},{1,3},{2,0},{3,1},{4,6},{5,7},{6,4},{7,5},{8,10},{9,11},{10,... | collective-permute-start | bytes 589832 | tf_op jit(solution)/shard_map/ppermute | solution.py:512
  59.4 5.8 %collective-permute-start.10 = (bf16[8,16,768]{2,1,0:T(8,128)(2,1)S(1)}, bf16[8,16,768]{2,1,0:T(8,128)(2,1)S(1)}, u32[]{:S(2)}, u32[]{:S(2)}) collective-permute-start(bf16[8,16,768]{2,1,0:T(8,128)(2,1)S(1)} %get-tuple-element.56), channel_id=1, source_target_pairs={{0,2},{1,3},{2,0},{3,1},{4,6},{5,7},{6,4},{7,5},{8,10},{9,11},{10,... | collective-permute-start | bytes 589832 | tf_op jit(solution)/shard_map/ppermute | solution.py:512

commit v13 on v12

--- a/solution.py
+++ b/solution.py
@@ -472,6 +472,7 @@
     to_next = [(2 * k - 1, 2 * k) for k in range(1, chips)]
     both_next = to_next + [(b, a) for a, b in to_next]
     edge = lax.ppermute(edge, "tm", both_next)
+    edge, away = lax.optimization_barrier((edge, away))
     other = lax.ppermute(away, "tm", swap)
     high = lax.ppermute(high, "tm", [(2 * k - 1, 2 * k + 1) for k in range(1, chips)])
 

time: 84.8 us -> 86.9 us (1.025)
  blocking collectives: 35.6 us -> 36.5 us
    ppermute x1, waiting for transfers between devices: 1.27 us -> 3.7 us  [shards(): edge = lax.ppermute(edge, 'tm', both_next)]
    ppermute x1, starting transfers between devices: 4.18 us -> 1.92 us  [shards(): edge = lax.ppermute(edge, 'tm', both_next)]
    ppermute x3, waiting for transfers between devices: 3.49 us -> 1.97 us  [shards(): lax.ppermute(piece, 'chan', [(i, (i + 2 * d) % groups_chan) for i in rang...]
    ppermute x1, starting transfers between devices: 0.09 us -> 1.49 us  [shards(): piece_other = lax.ppermute(piece, 'tm', swap)]
    all_to_all x1, blocking collectives: 17.5 us -> 18.5 us  [shards(): lax.all_to_all(energy, 'tm', 0, 0, tiled=True, axis_index_groups=same)]
where the time goes in v13:
time: 86.9 us; the launch traced here: 86.7 us
  blocking collectives  36.5 us (42%)
  Pallas kernels  22.1 us (25%)
  starting transfers between devices  15.6 us (18%)
  waiting for transfers between devices  11.4 us (13%)
    all_to_all x1, blocking collectives, shards(): lax.all_to_all(energy, 'tm', 0, 0, tiled=True, axis_index_groups=same)  18.5 us
    all_to_all x1, blocking collectives, shards(): lax.all_to_all(summed, 'tm', 0, 0, tiled=True, axis_index_groups=columns)  18.1 us
    pallas_call x2, Pallas kernels, correlate_next(): call(kernel, 'correlate_next', [shape((half_groups, sub, cols), jnp.float...  6.8 us
    pallas_call x2, Pallas kernels, filter_rows(): call(kernel, 'filter_rows', [shape((rows, 2 * half), jnp.float32), shape(...  6.02 us
    ppermute x3, starting transfers between devices, shards(): lax.ppermute(piece, 'chan', [(i, (i + 2 * d) % groups_chan) for i in rang...  4.75 us
    ppermute x2, waiting for transfers between devices, shards(): arrivals.append(lax.ppermute(send, 'tm', line))  4.36 us
    pallas_call x1, Pallas kernels, correlate_first(): call(kernel, 'correlate_first', [shape((half_groups, sub, cols), jnp.floa...  4.19 us
    ppermute x1, waiting for transfers between devices, shards(): edge = lax.ppermute(edge, 'tm', both_next)  3.7 us
  transfers between devices with their start and end apart: 11, of which 7 were waited for; matrix products, arithmetic and copies ran while one was open for 0% of the time, Pallas kernels for 15%

profile of v13, /device:TPU:8, one launch (start us, length us, event | category | flops | bytes accessed | tf_op | source)
XLA Modules:
  0.0 86.7 jit_solution(3052448180431430572)
XLA Ops:
  0.0 0.0 copy-start
  0.0 0.0 copy-start.1
  0.0 0.0 copy-start.2
  0.0 0.8 copy-done.2
  0.8 0.0 copy-start.3
  0.8 2.8 %pick_sources.1 = (bf16[8,4096]{1,0:T(8,128)(2,1)S(1)}, bf16[17,16,128]{2,1,0:T(8,128)(2,1)S(1)}, bf16[16,16,128]{2,1,0:T(8,128)(2,1)S(1)}, bf16[16,16,4096]{2,1,0:T(8,128)(2,1)S(1)}) custom-call(s32[2,4]{1,0:T(2,128)S(1)} %copy-done.2, bf16[16,2,16,4096]{3,2,1,0:T(8,128)(2,1)} %bitcast.1), custom_call_target="tpu_custom_call" | custom-call | bytes 2097152 | tf_op jit(solution)/shard_map/pick_sources/pallas_call | solution.py:99
  3.6 1.9 %collective-permute-start = (bf16[17,16,128]{2,1,0:T(8,128)(2,1)S(1)}, bf16[17,16,128]{2,1,0:T(8,128)(2,1)S(1)}, u32[]{:S(2)}, u32[]{:S(2)}) collective-permute-start(bf16[17,16,128]{2,1,0:T(8,128)(2,1)S(1)} %get-tuple-element.34), channel_id=1, source_target_pairs={{1,2},{3,4},{5,6},{7,8},{9,10},{11,12},{13,14},{15,16},{17,18},{19... | collective-permute-start | bytes 208904 | tf_op jit(solution)/shard_map/ppermute | solution.py:474
  5.5 3.7 %collective-permute-done.edge_ref.refs_0_ = bf16[17,16,128]{2,1,0:T(8,128)(2,1)S(1)} collective-permute-done((bf16[17,16,128]{2,1,0:T(8,128)(2,1)S(1)}, bf16[17,16,128]{2,1,0:T(8,128)(2,1)S(1)}, u32[]{:S(2)}, u32[]{:S(2)}) %collective-permute-start) | collective-permute-done | bytes 69664 | tf_op jit(solution)/shard_map/ppermute | solution.py:474
  9.2 0.7 collective-permute-start.4
  10.0 0.7 collective-permute-start.6
  10.6 0.0 copy-done.3
  10.7 3.2 %collective-permute-start.3 = (bf16[8,4352]{1,0:T(8,128)(2,1)S(1)}, bf16[8,4352]{1,0:T(8,128)(2,1)S(1)}, u32[]{:S(2)}, u32[]{:S(2)}) collective-permute-start(bf16[8,4352]{1,0:T(8,128)(2,1)S(1)} %extend_sources.1.refs_0_), channel_id=1, source_target_pairs={{0,192},{32,224},{64,0},{96,32},{128,64},{160,96},{192,128},{224,1... | collective-permute-start | bytes 208904 | tf_op jit(solution)/shard_map/ppermute | solution.py:481
  13.9 0.6 collective-permute-start.2
  14.4 1.0 %collective-permute-start.1 = (bf16[8,4352]{1,0:T(8,128)(2,1)S(1)}, bf16[8,4352]{1,0:T(8,128)(2,1)S(1)}, u32[]{:S(2)}, u32[]{:S(2)}) collective-permute-start(bf16[8,4352]{1,0:T(8,128)(2,1)S(1)} %extend_sources.1.refs_0_), channel_id=1, source_target_pairs={{0,64},{32,96},{64,128},{96,160},{128,192},{160,224},{192,0},{224,... | collective-permute-start | bytes 208904 | tf_op jit(solution)/shard_map/ppermute | solution.py:481
  15.4 0.0 collective-permute-done.4.other_ref
  15.4 0.0 copy-done
  15.4 0.0 copy-done.1
  15.4 3.0 %filter_rows.2 = (f32[256,8192]{1,0:T(8,128)}, f32[256,128]{1,0:T(8,128)S(1)}) custom-call(s32[16]{0:T(128)S(1)} %copy-done.1, bf16[1,256]{1,0:T(2,128)(2,1)S(1)} %reshape.6.taps_ref, bf16[16,2,16,4096]{3,2,1,0:T(8,128)(2,1)S(1)} %bitcast.2, bf16[16,16,4096]{2,1,0:T(8,128)(2,1)S(1)} %collective-permute-done.4.other_ref), custom_call_target="tpu_custom_call" | custom-call | flops 1073741824 | bytes 6291456 | tf_op jit(solution)/shard_map/filter_rows/pallas_call | solution.py:203
  18.5 0.0 collective-permute-done.3.refs_3_
  18.5 1.3 %collective-permute-done.2.refs_2_ = bf16[8,4352]{1,0:T(8,128)(2,1)S(1)} collective-permute-done((bf16[8,4352]{1,0:T(8,128)(2,1)S(1)}, bf16[8,4352]{1,0:T(8,128)(2,1)S(1)}, u32[]{:S(2)}, u32[]{:S(2)}) %collective-permute-start.2) | collective-permute-done | bytes 69664 | tf_op jit(solution)/shard_map/ppermute | solution.py:481
  19.7 0.7 collective-permute-done.1.refs_1_
  20.5 2.4 %collective-permute-start.5 = (bf16[8,4352]{1,0:T(8,128)(2,1)S(1)}, bf16[8,4352]{1,0:T(8,128)(2,1)S(1)}, u32[]{:S(2)}, u32[]{:S(2)}) collective-permute-start(bf16[8,4352]{1,0:T(8,128)(2,1)S(1)} %add_pieces.2.refs_0_), channel_id=1, source_target_pairs={{0,32},{32,0},{64,96},{96,64},{128,160},{160,128},{192,224},{224,1... | collective-permute-start | bytes 208904 | tf_op jit(solution)/shard_map/ppermute | solution.py:487
  22.9 0.0 collective-permute-done.6.refs_1_
  22.9 3.0 %filter_rows.3 = (f32[256,8192]{1,0:T(8,128)}, f32[256,128]{1,0:T(8,128)S(1)}) custom-call(s32[16]{0:T(128)S(1)} %copy-done.1, bf16[1,256]{1,0:T(2,128)(2,1)S(1)} %reshape.6.taps_ref, bf16[16,2,16,4096]{3,2,1,0:T(8,128)(2,1)S(1)} %bitcast.3, bf16[16,16,4096]{2,1,0:T(8,128)(2,1)S(1)} %collective-permute-done.4.other_ref, ...), custom_call_target="tpu_custom_call", output_to_operand_aliasing={{0}: (6, {})} | custom-call | flops 1073741824 | bytes 6291456 | tf_op jit(solution)/shard_map/filter_rows/pallas_call | solution.py:203
  25.9 0.5 collective-permute-done.5.refs_1_
  26.4 1.5 %collective-permute-start.7 = (bf16[8,4352]{1,0:T(8,128)(2,1)S(1)}, bf16[8,4352]{1,0:T(8,128)(2,1)S(1)}, u32[]{:S(2)}, u32[]{:S(2)}) collective-permute-start(bf16[8,4352]{1,0:T(8,128)(2,1)S(1)} %add_pieces.3.mine_ref), channel_id=1, source_target_pairs={{0,1},{1,0},{2,3},{3,2},{4,5},{5,4},{6,7},{7,6},{8,9},{9,8},{10,11... | collective-permute-start | bytes 208904 | tf_op jit(solution)/shard_map/ppermute | solution.py:493
  27.9 0.9 %collective-permute-done.7.other_ref = bf16[8,4352]{1,0:T(8,128)(2,1)S(1)} collective-permute-done((bf16[8,4352]{1,0:T(8,128)(2,1)S(1)}, bf16[8,4352]{1,0:T(8,128)(2,1)S(1)}, u32[]{:S(2)}, u32[]{:S(2)}) %collective-permute-start.7) | collective-permute-done | bytes 69664 | tf_op jit(solution)/shard_map/ppermute | solution.py:493
  28.8 1.0 %filter_sources.1 = (f32[8,8448]{1,0:T(8,128)S(1)}, f32[16,8,128]{2,1,0:T(8,128)S(1)}) custom-call(s32[16]{0:T(128)S(1)} %copy-done.1, bf16[1,256]{1,0:T(2,128)(2,1)S(1)} %reshape.6.taps_ref, bf16[8,4352]{1,0:T(8,128)(2,1)S(1)} %add_pieces.3.mine_ref, bf16[8,4352]{1,0:T(8,128)(2,1)S(1)} %collective-permute-done.7.other_ref, ...), custom_call_target="tpu_custom_call" | custom-call | bytes 1048576 | tf_op jit(solution)/shard_map/filter_sources/pallas_call | solution.py:266
  29.8 18.5 %all_to_all.10.energy_ref = f32[16,8,128]{2,1,0:T(8,128)S(1)} all-to-all(f32[16,8,128]{2,1,0:T(8,128)S(1)} %get-tuple-element.48), channel_id=1, replica_groups={{0,2,4,6,8,10,12,14,16,18,20,22,24,26,28,30},{1,3,5,7,9,11,13,15,17,19,..., dimensions={0} | all-to-all | bytes 131072 | tf_op jit(solution)/shard_map/all_to_all | solution.py:498
  48.3 4.2 %correlate_first.1 = (f32[8,16,512]{2,1,0:T(8,128)S(1)}, bf16[8,16,512]{2,1,0:T(8,128)(2,1)S(1)}, bf16[256,8192]{1,0:T(8,128)(2,1)S(1)}, bf16[8448,128]{1,0:T(8,128)(2,1)S(1)}) custom-call(f32[16,8,128]{2,1,0:T(8,128)S(1)} %all_to_all.10.energy_ref, f32[8,8448]{1,0:T(8,128)S(1)} %get-tuple-element.49.traces_ref, f32[256,8192]{1,0:T(8,128)} %get-tuple-element.50.refs_0_), custom_call_target="tpu_custom_call" | custom-call | flops 2147483648 | bytes 16777216 | tf_op jit(solution)/shard_map/correlate_first/pallas_call | solution.py:357
  52.5 1.5 %collective-permute-start.8 = (bf16[8,16,512]{2,1,0:T(8,128)(2,1)S(1)}, bf16[8,16,512]{2,1,0:T(8,128)(2,1)S(1)}, u32[]{:S(2)}, u32[]{:S(2)}) collective-permute-start(bf16[8,16,512]{2,1,0:T(8,128)(2,1)S(1)} %get-tuple-element.55), channel_id=1, source_target_pairs={{0,2},{1,3},{2,0},{3,1},{4,6},{5,7},{6,4},{7,5},{8,10},{9,11},{10,... | collective-permute-start | bytes 393224 | tf_op jit(solution)/shard_map/ppermute | solution.py:507
  53.9 3.4 %correlate_next.2 = (f32[8,16,768]{2,1,0:T(8,128)S(1)}, bf16[8,16,768]{2,1,0:T(8,128)(2,1)S(1)}) custom-call(bf16[256,8192]{1,0:T(8,128)(2,1)S(1)} %get-tuple-element.56.white_ref, bf16[8448,128]{1,0:T(8,128)(2,1)S(1)} %get-tuple-element.53.table_ref), custom_call_target="tpu_custom_call" | custom-call | flops 3221225472 | bytes 8388608 | tf_op jit(solution)/shard_map/correlate_next/pallas_call | solution.py:390
  57.3 0.7 collective-permute-start.9
  58.1 0.0 collective-permute-done.8.refs_3_
  58.1 3.4 %correlate_next.3 = (f32[8,16,768]{2,1,0:T(8,128)S(1)}, bf16[8,16,768]{2,1,0:T(8,128)(2,1)S(1)}) custom-call(bf16[256,8192]{1,0:T(8,128)(2,1)S(1)} %get-tuple-element.56.white_ref, bf16[8448,128]{1,0:T(8,128)(2,1)S(1)} %get-tuple-element.53.table_ref), custom_call_target="tpu_custom_call" | custom-call | flops 3221225472 | bytes 8388608 | tf_op jit(solution)/shard_map/correlate_next/pallas_call | solution.py:390
  61.5 1.5 %collective-permute-start.10 = (bf16[8,16,768]{2,1,0:T(8,128)(2,1)S(1)}, bf16[8,16,768]{2,1,0:T(8,128)(2,1)S(1)}, u32[]{:S(2)}, u32[]{:S(2)}) collective-permute-start(bf16[8,16,768]{2,1,0:T(8,128)(2,1)S(1)} %get-tuple-element.60), channel_id=1, source_target_pairs={{0,2},{1,3},{2,0},{3,1},{4,6},{5,7},{6,4},{7,5},{8,10},{9,11},{10,... | collective-permute-start | bytes 589832 | tf_op jit(solution)/shard_map/ppermute | solution.py:513
  63.0 0.9 %collective-permute-done.9.refs_4_ = bf16[8,16,768]{2,1,0:T(8,128)(2,1)S(1)} collective-permute-done((bf16[8,16,768]{2,1,0:T(8,128)(2,1)S(1)}, bf16[8,16,768]{2,1,0:T(8,128)(2,1)S(1)}, u32[]{:S(2)}, u32[]{:S(2)}) %collective-permute-start.9) | collective-permute-done | bytes 196640 | tf_op jit(solution)/shard_map/ppermute | solution.py:513
  63.8 3.5 %collective-permute-done.10.refs_5_ = bf16[8,16,768]{2,1,0:T(8,128)(2,1)S(1)} collective-permute-done((bf16[8,16,768]{2,1,0:T(8,128)(2,1)S(1)}, bf16[8,16,768]{2,1,0:T(8,128)(2,1)S(1)}, u32[]{:S(2)}, u32[]{:S(2)}) %collective-permute-start.10) | collective-permute-done | bytes 196640 | tf_op jit(solution)/shard_map/ppermute | solution.py:513
  67.3 0.1 add_line.1
  67.4 18.1 %all_to_all.11.parts_ref = bf16[8,16,2048]{2,1,0:T(8,128)(2,1)S(1)} all-to-all(bf16[8,16,2048]{2,1,0:T(8,128)(2,1)S(1)} %add_line.1), channel_id=1, replica_groups={{0,4,8,12,16,20,24,28},{1,5,9,13,17,21,25,29},{2,6,10,14,18,22,26,30},{..., dimensions={0} | all-to-all | bytes 1048576 | tf_op jit(solution)/shard_map/all_to_all | solution.py:516
  85.5 1.2 %finish.1 = f32[16,2,4,256]{3,2,1,0:T(4,128)} custom-call(bf16[8,16,2048]{2,1,0:T(8,128)(2,1)S(1)} %all_to_all.11.parts_ref), custom_call_target="tpu_custom_call" | custom-call | bytes 1048576 | tf_op jit(solution)/shard_map/finish/pallas_call | solution.py:449
  (5 shorter events, 0.1 us)
Async XLA Ops:
  0.0 15.4 %copy-start = (bf16[512,4096]{1,0:T(8,128)(2,1)S(1)}, bf16[512,4096]{1,0:T(8,128)(2,1)}, u32[]{:S(2)}) copy-start(bf16[512,4096]{1,0:T(8,128)(2,1)} %param.4) | copy-start | bytes 12582916
  0.0 15.4 %copy-start.1 = (s32[16]{0:T(128)S(1)}, s32[16]{0:T(128)}, u32[]{:S(2)}) copy-start(s32[16]{0:T(128)} %off_ref.5) | copy-start | bytes 196
  0.0 0.8 copy-start.2
  0.8 9.8 %copy-start.3 = (bf16[64]{0:T(256)(128)(2,1)S(1)}, bf16[64]{0:T(256)(128)(2,1)}, u32[]{:S(2)}) copy-start(bf16[64]{0:T(256)(128)(2,1)} %param.5) | copy-start | bytes 388
  3.6 5.6 %collective-permute-start = (bf16[17,16,128]{2,1,0:T(8,128)(2,1)S(1)}, bf16[17,16,128]{2,1,0:T(8,128)(2,1)S(1)}, u32[]{:S(2)}, u32[]{:S(2)}) collective-permute-start(bf16[17,16,128]{2,1,0:T(8,128)(2,1)S(1)} %get-tuple-element.34), channel_id=1, source_target_pairs={{1,2},{3,4},{5,6},{7,8},{9,10},{11,12},{13,14},{15,16},{17,18},{19... | collective-permute-start | bytes 208904 | tf_op jit(solution)/shard_map/ppermute | solution.py:474
  9.2 6.2 %collective-permute-start.4 = (bf16[16,16,4096]{2,1,0:T(8,128)(2,1)S(1)}, bf16[16,16,4096]{2,1,0:T(8,128)(2,1)S(1)}, u32[]{:S(2)}, u32[]{:S(2)}) collective-permute-start(bf16[16,16,4096]{2,1,0:T(8,128)(2,1)S(1)} %get-tuple-element.37), channel_id=1, source_target_pairs={{0,1},{1,0},{2,3},{3,2},{4,5},{5,4},{6,7},{7,6},{8,9},{9,8},{10,11... | collective-permute-start | bytes 6291464 | tf_op jit(solution)/shard_map/ppermute | solution.py:476
  10.0 12.9 %collective-permute-start.6 = (bf16[16,16,128]{2,1,0:T(8,128)(2,1)S(1)}, bf16[16,16,128]{2,1,0:T(8,128)(2,1)S(1)}, u32[]{:S(2)}, u32[]{:S(2)}) collective-permute-start(bf16[16,16,128]{2,1,0:T(8,128)(2,1)S(1)} %get-tuple-element.42), channel_id=1, source_target_pairs={{1,3},{3,5},{5,7},{7,9},{9,11},{11,13},{13,15},{15,17},{17,19},{19... | collective-permute-start | bytes 196616 | tf_op jit(solution)/shard_map/ppermute | solution.py:477
  10.7 7.8 %collective-permute-start.3 = (bf16[8,4352]{1,0:T(8,128)(2,1)S(1)}, bf16[8,4352]{1,0:T(8,128)(2,1)S(1)}, u32[]{:S(2)}, u32[]{:S(2)}) collective-permute-start(bf16[8,4352]{1,0:T(8,128)(2,1)S(1)} %extend_sources.1.refs_0_), channel_id=1, source_target_pairs={{0,192},{32,224},{64,0},{96,32},{128,64},{160,96},{192,128},{224,1... | collective-permute-start | bytes 208904 | tf_op jit(solution)/shard_map/ppermute | solution.py:481
  13.9 5.9 %collective-permute-start.2 = (bf16[8,4352]{1,0:T(8,128)(2,1)S(1)}, bf16[8,4352]{1,0:T(8,128)(2,1)S(1)}, u32[]{:S(2)}, u32[]{:S(2)}) collective-permute-start(bf16[8,4352]{1,0:T(8,128)(2,1)S(1)} %extend_sources.1.refs_0_), channel_id=1, source_target_pairs={{0,128},{32,160},{64,192},{96,224},{128,0},{160,32},{192,64},{224,... | collective-permute-start | bytes 208904 | tf_op jit(solution)/shard_map/ppermute | solution.py:481
  14.4 6.0 %collective-permute-start.1 = (bf16[8,4352]{1,0:T(8,128)(2,1)S(1)}, bf16[8,4352]{1,0:T(8,128)(2,1)S(1)}, u32[]{:S(2)}, u32[]{:S(2)}) collective-permute-start(bf16[8,4352]{1,0:T(8,128)(2,1)S(1)} %extend_sources.1.refs_0_), channel_id=1, source_target_pairs={{0,64},{32,96},{64,128},{96,160},{128,192},{160,224},{192,0},{224,... | collective-permute-start | bytes 208904 | tf_op jit(solution)/shard_map/ppermute | solution.py:481
  20.5 5.9 %collective-permute-start.5 = (bf16[8,4352]{1,0:T(8,128)(2,1)S(1)}, bf16[8,4352]{1,0:T(8,128)(2,1)S(1)}, u32[]{:S(2)}, u32[]{:S(2)}) collective-permute-start(bf16[8,4352]{1,0:T(8,128)(2,1)S(1)} %add_pieces.2.refs_0_), channel_id=1, source_target_pairs={{0,32},{32,0},{64,96},{96,64},{128,160},{160,128},{192,224},{224,1... | collective-permute-start | bytes 208904 | tf_op jit(solution)/shard_map/ppermute | solution.py:487
  26.4 2.4 %collective-permute-start.7 = (bf16[8,4352]{1,0:T(8,128)(2,1)S(1)}, bf16[8,4352]{1,0:T(8,128)(2,1)S(1)}, u32[]{:S(2)}, u32[]{:S(2)}) collective-permute-start(bf16[8,4352]{1,0:T(8,128)(2,1)S(1)} %add_pieces.3.mine_ref), channel_id=1, source_target_pairs={{0,1},{1,0},{2,3},{3,2},{4,5},{5,4},{6,7},{7,6},{8,9},{9,8},{10,11... | collective-permute-start | bytes 208904 | tf_op jit(solution)/shard_map/ppermute | solution.py:493
  52.5 5.6 %collective-permute-start.8 = (bf16[8,16,512]{2,1,0:T(8,128)(2,1)S(1)}, bf16[8,16,512]{2,1,0:T(8,128)(2,1)S(1)}, u32[]{:S(2)}, u32[]{:S(2)}) collective-permute-start(bf16[8,16,512]{2,1,0:T(8,128)(2,1)S(1)} %get-tuple-element.55), channel_id=1, source_target_pairs={{0,2},{1,3},{2,0},{3,1},{4,6},{5,7},{6,4},{7,5},{8,10},{9,11},{10,... | collective-permute-start | bytes 393224 | tf_op jit(solution)/shard_map/ppermute | solution.py:507
  57.3 6.5 %collective-permute-start.9 = (bf16[8,16,768]{2,1,0:T(8,128)(2,1)S(1)}, bf16[8,16,768]{2,1,0:T(8,128)(2,1)S(1)}, u32[]{:S(2)}, u32[]{:S(2)}) collective-permute-start(bf16[8,16,768]{2,1,0:T(8,128)(2,1)S(1)} %get-tuple-element.59), channel_id=1, source_target_pairs={{0,2},{1,3},{2,0},{3,1},{4,6},{5,7},{6,4},{7,5},{8,10},{9,11},{10,... | collective-permute-start | bytes 589832 | tf_op jit(solution)/shard_map/ppermute | solution.py:513
  61.5 5.8 %collective-permute-start.10 = (bf16[8,16,768]{2,1,0:T(8,128)(2,1)S(1)}, bf16[8,16,768]{2,1,0:T(8,128)(2,1)S(1)}, u32[]{:S(2)}, u32[]{:S(2)}) collective-permute-start(bf16[8,16,768]{2,1,0:T(8,128)(2,1)S(1)} %get-tuple-element.60), channel_id=1, source_target_pairs={{0,2},{1,3},{2,0},{3,1},{4,6},{5,7},{6,4},{7,5},{8,10},{9,11},{10,... | collective-permute-start | bytes 589832 | tf_op jit(solution)/shard_map/ppermute | solution.py:513

commit v14 on v12

--- a/solution.py
+++ b/solution.py
@@ -147,7 +147,7 @@
 def filter_rows(offsets, taps, x4, other, edges, part, filled=None):
     groups, _, sub, half = x4.shape
     rows = groups * sub
-    chunk = 1024
+    chunk = 512
     count = half // chunk
     extra = list(edges) + ([] if filled is None else [filled])
 

time: 84.8 us -> 84.8 us (level)
  no operation moved by 1% of the time
where the time goes in v14:
time: 84.8 us
  blocking collectives  35.9 us (42%)
  Pallas kernels  21.9 us (26%)
  starting transfers between devices  15 us (18%)
  waiting for transfers between devices  11 us (13%)
  local copies, waits for them, and re-layouts  0.85 us (1%)
    all_to_all x1, blocking collectives, shards(): lax.all_to_all(summed, 'tm', 0, 0, tiled=True, axis_index_groups=columns)  18.4 us
    all_to_all x1, blocking collectives, shards(): lax.all_to_all(energy, 'tm', 0, 0, tiled=True, axis_index_groups=same)  17.5 us
    pallas_call x2, Pallas kernels, correlate_next(): call(kernel, 'correlate_next', [shape((half_groups, sub, cols), jnp.float...  6.8 us
    pallas_call x2, Pallas kernels, filter_rows(): call(kernel, 'filter_rows', [shape((rows, 2 * half), jnp.float32), shape(...  5.83 us
    ppermute x2, waiting for transfers between devices, shards(): arrivals.append(lax.ppermute(send, 'tm', line))  4.36 us
    ppermute x1, starting transfers between devices, shards(): edge = lax.ppermute(edge, 'tm', both_next)  4.18 us
    pallas_call x1, Pallas kernels, correlate_first(): call(kernel, 'correlate_first', [shape((half_groups, sub, cols), jnp.floa...  4.17 us
    ppermute x3, starting transfers between devices, shards(): lax.ppermute(piece, 'chan', [(i, (i + 2 * d) % groups_chan) for i in rang...  3.96 us
  transfers between devices with their start and end apart: 11, of which 7 were waited for; matrix products, arithmetic and copies ran while one was open for 0% of the time, Pallas kernels for 15%

profile of v14, /device:TPU:8, one launch (start us, length us, event | category | flops | bytes accessed | tf_op | source)
XLA Modules:
  0.0 84.8 jit_solution(3584808288493214751)
XLA Ops:
  0.0 0.0 copy-start
  0.0 0.0 copy-start.1
  0.0 0.0 copy-start.2
  0.0 0.8 copy-done.2
  0.8 0.0 copy-start.3
  0.8 2.8 %pick_sources.1 = (bf16[8,4096]{1,0:T(8,128)(2,1)S(1)}, bf16[17,16,128]{2,1,0:T(8,128)(2,1)S(1)}, bf16[16,16,128]{2,1,0:T(8,128)(2,1)S(1)}, bf16[16,16,4096]{2,1,0:T(8,128)(2,1)S(1)}) custom-call(s32[2,4]{1,0:T(2,128)S(1)} %copy-done.2, bf16[16,2,16,4096]{3,2,1,0:T(8,128)(2,1)} %bitcast.1), custom_call_target="tpu_custom_call" | custom-call | bytes 2097152 | tf_op jit(solution)/shard_map/pick_sources/pallas_call | solution.py:99
  3.6 0.1 collective-permute-start.4
  3.7 4.2 %collective-permute-start = (bf16[17,16,128]{2,1,0:T(8,128)(2,1)S(1)}, bf16[17,16,128]{2,1,0:T(8,128)(2,1)S(1)}, u32[]{:S(2)}, u32[]{:S(2)}) collective-permute-start(bf16[17,16,128]{2,1,0:T(8,128)(2,1)S(1)} %get-tuple-element.32), channel_id=1, source_target_pairs={{1,2},{3,4},{5,6},{7,8},{9,10},{11,12},{13,14},{15,16},{17,18},{19... | collective-permute-start | bytes 208904 | tf_op jit(solution)/shard_map/ppermute | solution.py:474
  7.9 0.7 collective-permute-start.6
  8.6 0.0 copy-done.3
  8.6 1.3 %collective-permute-done.edge_ref.refs_0_ = bf16[17,16,128]{2,1,0:T(8,128)(2,1)S(1)} collective-permute-done((bf16[17,16,128]{2,1,0:T(8,128)(2,1)S(1)}, bf16[17,16,128]{2,1,0:T(8,128)(2,1)S(1)}, u32[]{:S(2)}, u32[]{:S(2)}) %collective-permute-start) | collective-permute-done | bytes 69664 | tf_op jit(solution)/shard_map/ppermute | solution.py:474
  9.9 2.4 %collective-permute-start.3 = (bf16[8,4352]{1,0:T(8,128)(2,1)S(1)}, bf16[8,4352]{1,0:T(8,128)(2,1)S(1)}, u32[]{:S(2)}, u32[]{:S(2)}) collective-permute-start(bf16[8,4352]{1,0:T(8,128)(2,1)S(1)} %extend_sources.1.refs_0_), channel_id=1, source_target_pairs={{0,192},{32,224},{64,0},{96,32},{128,64},{160,96},{192,128},{224,1... | collective-permute-start | bytes 208904 | tf_op jit(solution)/shard_map/ppermute | solution.py:480
  12.3 0.6 collective-permute-start.2
  12.9 0.9 %collective-permute-start.1 = (bf16[8,4352]{1,0:T(8,128)(2,1)S(1)}, bf16[8,4352]{1,0:T(8,128)(2,1)S(1)}, u32[]{:S(2)}, u32[]{:S(2)}) collective-permute-start(bf16[8,4352]{1,0:T(8,128)(2,1)S(1)} %extend_sources.1.refs_0_), channel_id=1, source_target_pairs={{0,64},{32,96},{64,128},{96,160},{128,192},{160,224},{192,0},{224,... | collective-permute-start | bytes 208904 | tf_op jit(solution)/shard_map/ppermute | solution.py:480
  13.8 0.0 collective-permute-done.4.other_ref
  13.9 0.0 copy-done
  13.9 0.0 copy-done.1
  13.9 2.9 %filter_rows.2 = (f32[256,8192]{1,0:T(8,128)}, f32[256,128]{1,0:T(8,128)S(1)}) custom-call(s32[16]{0:T(128)S(1)} %copy-done.1, bf16[1,256]{1,0:T(2,128)(2,1)S(1)} %reshape.6.taps_ref, bf16[16,2,16,4096]{3,2,1,0:T(8,128)(2,1)S(1)} %bitcast.2, bf16[16,16,4096]{2,1,0:T(8,128)(2,1)S(1)} %collective-permute-done.4.other_ref), custom_call_target="tpu_custom_call" | custom-call | flops 1073741824 | bytes 6291456 | tf_op jit(solution)/shard_map/filter_rows/pallas_call | solution.py:203
  16.8 0.0 collective-permute-done.3.refs_3_
  16.8 1.8 %collective-permute-done.2.refs_2_ = bf16[8,4352]{1,0:T(8,128)(2,1)S(1)} collective-permute-done((bf16[8,4352]{1,0:T(8,128)(2,1)S(1)}, bf16[8,4352]{1,0:T(8,128)(2,1)S(1)}, u32[]{:S(2)}, u32[]{:S(2)}) %collective-permute-start.2) | collective-permute-done | bytes 69664 | tf_op jit(solution)/shard_map/ppermute | solution.py:480
  18.6 1.7 %collective-permute-done.1.refs_1_ = bf16[8,4352]{1,0:T(8,128)(2,1)S(1)} collective-permute-done((bf16[8,4352]{1,0:T(8,128)(2,1)S(1)}, bf16[8,4352]{1,0:T(8,128)(2,1)S(1)}, u32[]{:S(2)}, u32[]{:S(2)}) %collective-permute-start.1) | collective-permute-done | bytes 69664 | tf_op jit(solution)/shard_map/ppermute | solution.py:480
  20.4 2.4 %collective-permute-start.5 = (bf16[8,4352]{1,0:T(8,128)(2,1)S(1)}, bf16[8,4352]{1,0:T(8,128)(2,1)S(1)}, u32[]{:S(2)}, u32[]{:S(2)}) collective-permute-start(bf16[8,4352]{1,0:T(8,128)(2,1)S(1)} %add_pieces.2.refs_0_), channel_id=1, source_target_pairs={{0,32},{32,0},{64,96},{96,64},{128,160},{160,128},{192,224},{224,1... | collective-permute-start | bytes 208904 | tf_op jit(solution)/shard_map/ppermute | solution.py:486
  22.7 0.0 collective-permute-done.6.refs_1_
  22.7 2.9 %filter_rows.3 = (f32[256,8192]{1,0:T(8,128)}, f32[256,128]{1,0:T(8,128)S(1)}) custom-call(s32[16]{0:T(128)S(1)} %copy-done.1, bf16[1,256]{1,0:T(2,128)(2,1)S(1)} %reshape.6.taps_ref, bf16[16,2,16,4096]{3,2,1,0:T(8,128)(2,1)S(1)} %bitcast.3, bf16[16,16,4096]{2,1,0:T(8,128)(2,1)S(1)} %collective-permute-done.4.other_ref, ...), custom_call_target="tpu_custom_call", output_to_operand_aliasing={{0}: (6, {})} | custom-call | flops 1073741824 | bytes 6291456 | tf_op jit(solution)/shard_map/filter_rows/pallas_call | solution.py:203
  25.7 0.6 collective-permute-done.5.refs_1_
  26.3 0.1 collective-permute-start.7
  26.4 1.2 %collective-permute-done.7.other_ref = bf16[8,4352]{1,0:T(8,128)(2,1)S(1)} collective-permute-done((bf16[8,4352]{1,0:T(8,128)(2,1)S(1)}, bf16[8,4352]{1,0:T(8,128)(2,1)S(1)}, u32[]{:S(2)}, u32[]{:S(2)}) %collective-permute-start.7) | collective-permute-done | bytes 69664 | tf_op jit(solution)/shard_map/ppermute | solution.py:492
  27.6 1.0 %filter_sources.1 = (f32[8,8448]{1,0:T(8,128)S(1)}, f32[16,8,128]{2,1,0:T(8,128)S(1)}) custom-call(s32[16]{0:T(128)S(1)} %copy-done.1, bf16[1,256]{1,0:T(2,128)(2,1)S(1)} %reshape.6.taps_ref, bf16[8,4352]{1,0:T(8,128)(2,1)S(1)} %add_pieces.3.mine_ref, bf16[8,4352]{1,0:T(8,128)(2,1)S(1)} %collective-permute-done.7.other_ref, ...), custom_call_target="tpu_custom_call" | custom-call | bytes 1048576 | tf_op jit(solution)/shard_map/filter_sources/pallas_call | solution.py:266
  28.6 17.5 %all_to_all.10.energy_ref = f32[16,8,128]{2,1,0:T(8,128)S(1)} all-to-all(f32[16,8,128]{2,1,0:T(8,128)S(1)} %get-tuple-element.44), channel_id=1, replica_groups={{0,2,4,6,8,10,12,14,16,18,20,22,24,26,28,30},{1,3,5,7,9,11,13,15,17,19,..., dimensions={0} | all-to-all | bytes 131072 | tf_op jit(solution)/shard_map/all_to_all | solution.py:497
  46.1 4.2 %correlate_first.1 = (f32[8,16,512]{2,1,0:T(8,128)S(1)}, bf16[8,16,512]{2,1,0:T(8,128)(2,1)S(1)}, bf16[256,8192]{1,0:T(8,128)(2,1)S(1)}, bf16[8448,128]{1,0:T(8,128)(2,1)S(1)}) custom-call(f32[16,8,128]{2,1,0:T(8,128)S(1)} %all_to_all.10.energy_ref, f32[8,8448]{1,0:T(8,128)S(1)} %get-tuple-element.45.traces_ref, f32[256,8192]{1,0:T(8,128)} %get-tuple-element.46.refs_0_), custom_call_target="tpu_custom_call" | custom-call | flops 2147483648 | bytes 16777216 | tf_op jit(solution)/shard_map/correlate_first/pallas_call | solution.py:357
  50.3 1.5 %collective-permute-start.8 = (bf16[8,16,512]{2,1,0:T(8,128)(2,1)S(1)}, bf16[8,16,512]{2,1,0:T(8,128)(2,1)S(1)}, u32[]{:S(2)}, u32[]{:S(2)}) collective-permute-start(bf16[8,16,512]{2,1,0:T(8,128)(2,1)S(1)} %get-tuple-element.51), channel_id=1, source_target_pairs={{0,2},{1,3},{2,0},{3,1},{4,6},{5,7},{6,4},{7,5},{8,10},{9,11},{10,... | collective-permute-start | bytes 393224 | tf_op jit(solution)/shard_map/ppermute | solution.py:506
  51.8 3.4 %correlate_next.2 = (f32[8,16,768]{2,1,0:T(8,128)S(1)}, bf16[8,16,768]{2,1,0:T(8,128)(2,1)S(1)}) custom-call(bf16[256,8192]{1,0:T(8,128)(2,1)S(1)} %get-tuple-element.52.white_ref, bf16[8448,128]{1,0:T(8,128)(2,1)S(1)} %get-tuple-element.49.table_ref), custom_call_target="tpu_custom_call" | custom-call | flops 3221225472 | bytes 8388608 | tf_op jit(solution)/shard_map/correlate_next/pallas_call | solution.py:390
  55.2 0.7 collective-permute-start.9
  55.9 0.0 collective-permute-done.8.refs_3_
  55.9 3.4 %correlate_next.3 = (f32[8,16,768]{2,1,0:T(8,128)S(1)}, bf16[8,16,768]{2,1,0:T(8,128)(2,1)S(1)}) custom-call(bf16[256,8192]{1,0:T(8,128)(2,1)S(1)} %get-tuple-element.52.white_ref, bf16[8448,128]{1,0:T(8,128)(2,1)S(1)} %get-tuple-element.49.table_ref), custom_call_target="tpu_custom_call" | custom-call | flops 3221225472 | bytes 8388608 | tf_op jit(solution)/shard_map/correlate_next/pallas_call | solution.py:390
  59.3 1.5 %collective-permute-start.10 = (bf16[8,16,768]{2,1,0:T(8,128)(2,1)S(1)}, bf16[8,16,768]{2,1,0:T(8,128)(2,1)S(1)}, u32[]{:S(2)}, u32[]{:S(2)}) collective-permute-start(bf16[8,16,768]{2,1,0:T(8,128)(2,1)S(1)} %get-tuple-element.56), channel_id=1, source_target_pairs={{0,2},{1,3},{2,0},{3,1},{4,6},{5,7},{6,4},{7,5},{8,10},{9,11},{10,... | collective-permute-start | bytes 589832 | tf_op jit(solution)/shard_map/ppermute | solution.py:512
  60.8 0.8 collective-permute-done.9.refs_4_
  61.7 3.5 %collective-permute-done.10.refs_5_ = bf16[8,16,768]{2,1,0:T(8,128)(2,1)S(1)} collective-permute-done((bf16[8,16,768]{2,1,0:T(8,128)(2,1)S(1)}, bf16[8,16,768]{2,1,0:T(8,128)(2,1)S(1)}, u32[]{:S(2)}, u32[]{:S(2)}) %collective-permute-start.10) | collective-permute-done | bytes 196640 | tf_op jit(solution)/shard_map/ppermute | solution.py:512
  65.2 0.1 add_line.1
  65.3 18.4 %all_to_all.11.parts_ref = bf16[8,16,2048]{2,1,0:T(8,128)(2,1)S(1)} all-to-all(bf16[8,16,2048]{2,1,0:T(8,128)(2,1)S(1)} %add_line.1), channel_id=1, replica_groups={{0,4,8,12,16,20,24,28},{1,5,9,13,17,21,25,29},{2,6,10,14,18,22,26,30},{..., dimensions={0} | all-to-all | bytes 1048576 | tf_op jit(solution)/shard_map/all_to_all | solution.py:515
  83.6 1.2 %finish.1 = f32[16,2,4,256]{3,2,1,0:T(4,128)} custom-call(bf16[8,16,2048]{2,1,0:T(8,128)(2,1)S(1)} %all_to_all.11.parts_ref), custom_call_target="tpu_custom_call" | custom-call | bytes 1048576 | tf_op jit(solution)/shard_map/finish/pallas_call | solution.py:449
  (5 shorter events, 0.1 us)
Async XLA Ops:
  0.0 13.9 %copy-start = (bf16[512,4096]{1,0:T(8,128)(2,1)S(1)}, bf16[512,4096]{1,0:T(8,128)(2,1)}, u32[]{:S(2)}) copy-start(bf16[512,4096]{1,0:T(8,128)(2,1)} %param.4) | copy-start | bytes 12582916
  0.0 13.9 %copy-start.1 = (s32[16]{0:T(128)S(1)}, s32[16]{0:T(128)}, u32[]{:S(2)}) copy-start(s32[16]{0:T(128)} %off_ref.5) | copy-start | bytes 196
  0.0 0.8 copy-start.2
  0.8 7.7 %copy-start.3 = (bf16[64]{0:T(256)(128)(2,1)S(1)}, bf16[64]{0:T(256)(128)(2,1)}, u32[]{:S(2)}) copy-start(bf16[64]{0:T(256)(128)(2,1)} %param.5) | copy-start | bytes 388
  3.6 10.2 %collective-permute-start.4 = (bf16[16,16,4096]{2,1,0:T(8,128)(2,1)S(1)}, bf16[16,16,4096]{2,1,0:T(8,128)(2,1)S(1)}, u32[]{:S(2)}, u32[]{:S(2)}) collective-permute-start(bf16[16,16,4096]{2,1,0:T(8,128)(2,1)S(1)} %get-tuple-element.33), channel_id=1, source_target_pairs={{0,1},{1,0},{2,3},{3,2},{4,5},{5,4},{6,7},{7,6},{8,9},{9,8},{10,11... | collective-permute-start | bytes 6291464 | tf_op jit(solution)/shard_map/ppermute | solution.py:475
  3.7 6.2 %collective-permute-start = (bf16[17,16,128]{2,1,0:T(8,128)(2,1)S(1)}, bf16[17,16,128]{2,1,0:T(8,128)(2,1)S(1)}, u32[]{:S(2)}, u32[]{:S(2)}) collective-permute-start(bf16[17,16,128]{2,1,0:T(8,128)(2,1)S(1)} %get-tuple-element.32), channel_id=1, source_target_pairs={{1,2},{3,4},{5,6},{7,8},{9,10},{11,12},{13,14},{15,16},{17,18},{19... | collective-permute-start | bytes 208904 | tf_op jit(solution)/shard_map/ppermute | solution.py:474
  7.9 14.8 %collective-permute-start.6 = (bf16[16,16,128]{2,1,0:T(8,128)(2,1)S(1)}, bf16[16,16,128]{2,1,0:T(8,128)(2,1)S(1)}, u32[]{:S(2)}, u32[]{:S(2)}) collective-permute-start(bf16[16,16,128]{2,1,0:T(8,128)(2,1)S(1)} %get-tuple-element.38), channel_id=1, source_target_pairs={{1,3},{3,5},{5,7},{7,9},{9,11},{11,13},{13,15},{15,17},{17,19},{19... | collective-permute-start | bytes 196616 | tf_op jit(solution)/shard_map/ppermute | solution.py:476
  9.9 6.9 %collective-permute-start.3 = (bf16[8,4352]{1,0:T(8,128)(2,1)S(1)}, bf16[8,4352]{1,0:T(8,128)(2,1)S(1)}, u32[]{:S(2)}, u32[]{:S(2)}) collective-permute-start(bf16[8,4352]{1,0:T(8,128)(2,1)S(1)} %extend_sources.1.refs_0_), channel_id=1, source_target_pairs={{0,192},{32,224},{64,0},{96,32},{128,64},{160,96},{192,128},{224,1... | collective-permute-start | bytes 208904 | tf_op jit(solution)/shard_map/ppermute | solution.py:480
  12.3 6.4 %collective-permute-start.2 = (bf16[8,4352]{1,0:T(8,128)(2,1)S(1)}, bf16[8,4352]{1,0:T(8,128)(2,1)S(1)}, u32[]{:S(2)}, u32[]{:S(2)}) collective-permute-start(bf16[8,4352]{1,0:T(8,128)(2,1)S(1)} %extend_sources.1.refs_0_), channel_id=1, source_target_pairs={{0,128},{32,160},{64,192},{96,224},{128,0},{160,32},{192,64},{224,... | collective-permute-start | bytes 208904 | tf_op jit(solution)/shard_map/ppermute | solution.py:480
  12.9 7.4 %collective-permute-start.1 = (bf16[8,4352]{1,0:T(8,128)(2,1)S(1)}, bf16[8,4352]{1,0:T(8,128)(2,1)S(1)}, u32[]{:S(2)}, u32[]{:S(2)}) collective-permute-start(bf16[8,4352]{1,0:T(8,128)(2,1)S(1)} %extend_sources.1.refs_0_), channel_id=1, source_target_pairs={{0,64},{32,96},{64,128},{96,160},{128,192},{160,224},{192,0},{224,... | collective-permute-start | bytes 208904 | tf_op jit(solution)/shard_map/ppermute | solution.py:480
  20.4 5.9 %collective-permute-start.5 = (bf16[8,4352]{1,0:T(8,128)(2,1)S(1)}, bf16[8,4352]{1,0:T(8,128)(2,1)S(1)}, u32[]{:S(2)}, u32[]{:S(2)}) collective-permute-start(bf16[8,4352]{1,0:T(8,128)(2,1)S(1)} %add_pieces.2.refs_0_), channel_id=1, source_target_pairs={{0,32},{32,0},{64,96},{96,64},{128,160},{160,128},{192,224},{224,1... | collective-permute-start | bytes 208904 | tf_op jit(solution)/shard_map/ppermute | solution.py:486
  26.3 1.3 %collective-permute-start.7 = (bf16[8,4352]{1,0:T(8,128)(2,1)S(1)}, bf16[8,4352]{1,0:T(8,128)(2,1)S(1)}, u32[]{:S(2)}, u32[]{:S(2)}) collective-permute-start(bf16[8,4352]{1,0:T(8,128)(2,1)S(1)} %add_pieces.3.mine_ref), channel_id=1, source_target_pairs={{0,1},{1,0},{2,3},{3,2},{4,5},{5,4},{6,7},{7,6},{8,9},{9,8},{10,11... | collective-permute-start | bytes 208904 | tf_op jit(solution)/shard_map/ppermute | solution.py:492
  50.3 5.6 %collective-permute-start.8 = (bf16[8,16,512]{2,1,0:T(8,128)(2,1)S(1)}, bf16[8,16,512]{2,1,0:T(8,128)(2,1)S(1)}, u32[]{:S(2)}, u32[]{:S(2)}) collective-permute-start(bf16[8,16,512]{2,1,0:T(8,128)(2,1)S(1)} %get-tuple-element.51), channel_id=1, source_target_pairs={{0,2},{1,3},{2,0},{3,1},{4,6},{5,7},{6,4},{7,5},{8,10},{9,11},{10,... | collective-permute-start | bytes 393224 | tf_op jit(solution)/shard_map/ppermute | solution.py:506
  55.2 6.5 %collective-permute-start.9 = (bf16[8,16,768]{2,1,0:T(8,128)(2,1)S(1)}, bf16[8,16,768]{2,1,0:T(8,128)(2,1)S(1)}, u32[]{:S(2)}, u32[]{:S(2)}) collective-permute-start(bf16[8,16,768]{2,1,0:T(8,128)(2,1)S(1)} %get-tuple-element.55), channel_id=1, source_target_pairs={{0,2},{1,3},{2,0},{3,1},{4,6},{5,7},{6,4},{7,5},{8,10},{9,11},{10,... | collective-permute-start | bytes 589832 | tf_op jit(solution)/shard_map/ppermute | solution.py:512
  59.3 5.8 %collective-permute-start.10 = (bf16[8,16,768]{2,1,0:T(8,128)(2,1)S(1)}, bf16[8,16,768]{2,1,0:T(8,128)(2,1)S(1)}, u32[]{:S(2)}, u32[]{:S(2)}) collective-permute-start(bf16[8,16,768]{2,1,0:T(8,128)(2,1)S(1)} %get-tuple-element.56), channel_id=1, source_target_pairs={{0,2},{1,3},{2,0},{3,1},{4,6},{5,7},{6,4},{7,5},{8,10},{9,11},{10,... | collective-permute-start | bytes 589832 | tf_op jit(solution)/shard_map/ppermute | solution.py:512
